TPU v7x, 32 devices: a whole 2x2x4 slice. The times are simulated.
32 devices in a mesh: groups: 2 (over x), rows: 16 (over z, y, core).
Axes of the slice: x: 2, y: 2, z: 4, core: 2. Of those that a mesh axis runs over, the one named last changes fastest.
Arguments:
- genotypes: bfloat16 [32768, 4096], P(('groups', 'rows')), parts along dimension 0, may hold values from -6 to 6
- sample_factors: float32 [32768, 64], P(('groups', 'rows')), parts along dimension 0, may hold values from -2.1213203 to 2.1213203
- snp_factors: float32 [20480, 64], P(('groups', 'rows')), parts along dimension 0, may hold values from -2.1213203 to 2.1213203
- coverage: int32 [32, 64], P('groups'), parts along dimension 0, may hold values from 0 to 159, as said below
Outputs:
- new_samples: float32 [32768, 64], P(('groups', 'rows')), parts along dimension 0
- new_snps: float32 [20480, 64], P(('groups', 'rows')), parts along dimension 0
There are 2 independent parts, one for each index of `groups`. A program takes and returns all parts, laid end to end along the dimension named above; each array names one. Nothing has to cross between parts.
Inputs may be any that keep to these rules, and one draw needn't show every extreme that they name: `coverage`: each row lists 64 distinct SNP blocks in ascending order, exactly 4 of them among blocks o * 10 to (o + 1) * 10 - 1 for every o; every SNP block is listed by at least one batch.
All inputs are finite; a program needn't handle non-finite values.
Results may differ from a plain program's by a relative error of at most 0.0067.
Values may be sent and summed in bfloat16 or wider, within the bound.
No kernel may reach another device: no remote copies, remote signals or barrier semaphores. Data moves between devices by JAX's collectives and lax.ppermute only.
A program may use at most 128 MiB of HBM per device.

v0:
```python
import math

import jax
import jax.numpy as jnp
from jax import lax
from jax.sharding import PartitionSpec as P

ROUNDS = 2


weight_decay = 0.02


def on_device(genotypes, sample_factors, snp_factors, coverage):
    devices = lax.axis_size("rows")
    position = lax.axis_index("rows")
    samples_here = genotypes.shape[0]
    rank_width = sample_factors.shape[1]
    covered = coverage.shape[1]
    tile_size = genotypes.shape[1] // covered
    per_owner = covered // devices
    own_blocks = snp_factors.shape[0] // tile_size
    own_list = lax.dynamic_index_in_dim(coverage, position, 0, keepdims=False)
    local_list = (
        lax.dynamic_slice_in_dim(coverage, position * per_owner, per_owner, 1)
        - position * own_blocks
    )
    one_hot = (
        local_list[:, :, None] == jnp.arange(own_blocks, dtype=jnp.int32)[None, None, :]
    ).astype(jnp.float32)
    observers = jnp.sum(one_hot, axis=(0, 1))
    snp_step = 0.5 * math.sqrt(rank_width) / (samples_here * observers)
    sample_step = 0.5 * math.sqrt(rank_width) / (covered * tile_size)
    samples = sample_factors
    snps = snp_factors
    for iteration in range(ROUNDS):
        snp_bf16 = snps.astype(jnp.bfloat16).reshape(own_blocks, tile_size, rank_width)
        gathered = lax.all_gather(snp_bf16, "rows", axis=0, tiled=True)
        panels = gathered[own_list].reshape(covered * tile_size, rank_width)
        predicted = lax.dot_general(
            samples.astype(jnp.bfloat16),
            panels,
            (((1,), (1,)), ((), ())),
            preferred_element_type=jnp.float32,
        )
        residual = (genotypes.astype(jnp.float32) - predicted).astype(jnp.bfloat16)
        gradient = jnp.dot(residual, panels, preferred_element_type=jnp.float32)
        samples = (1.0 - weight_decay) * samples + sample_step * gradient
        sample_bf16 = samples.astype(jnp.bfloat16)
        predicted = lax.dot_general(
            sample_bf16, panels, (((1,), (1,)), ((), ())), preferred_element_type=jnp.float32
        )
        residual = (genotypes.astype(jnp.float32) - predicted).astype(jnp.bfloat16)
        snp_gradient = lax.dot_general(
            residual, sample_bf16, (((0,), (0,)), ((), ())), preferred_element_type=jnp.float32
        )
        incoming_terms = lax.all_to_all(
            snp_gradient.reshape(devices, per_owner, tile_size, rank_width).astype(jnp.bfloat16),
            "rows",
            split_axis=0,
            concat_axis=0,
            tiled=True,
        ).astype(jnp.float32)
        summed = jnp.einsum(
            "bpk,bptr->ktr", one_hot, incoming_terms, precision=lax.Precision.HIGHEST
        )
        snps = (1.0 - weight_decay) * snps + (snp_step[:, None, None] * summed).reshape(
            own_blocks * tile_size, rank_width
        )
    return (samples, snps)


def solution(mesh):
    placed = (
        P(("groups", "rows"), None),
        P(("groups", "rows"), None),
        P(("groups", "rows"), None),
        P("groups", None),
    )
    return jax.shard_map(
        on_device,
        mesh=mesh,
        in_specs=placed,
        out_specs=(P(("groups", "rows"), None), P(("groups", "rows"), None)),
        check_vma=False,
    )
```

profile of v0, /device:TPU:0, one launch (start us, length us, event | category | flops | bytes accessed | tf_op | source)
XLA Modules:
  0.0 190.6 jit_solution(12273409029608411657)
XLA Ops:
  7.2 1.1 copy.32
  8.3 0.7 convert_element_type.52
  9.0 12.1 %copy.31 = bf16[1024,4096]{0,1:T(8,128)(2,1)} copy(bf16[1024,4096]{1,0:T(8,128)(2,1)} %param.4) | data formatting | bytes 16777216 | tf_op args[0]
  21.1 35.6 %all-gather.3.cloned.1.call-done = bf16[160,64,64]{2,1,0:T(8,128)(2,1)} async-done(((bf16[10,64,64]{2,1,0:T(8,128)(2,1)}), bf16[160,64,64]{2,1,0:T(8,128)(2,1)}) %all-gather.3.cloned.1.call-update) | async-done | bytes 1310736 | tf_op jit(solution)/shard_map/all_gather | solution.py:38
  56.8 2.5 %gather_fusion = bf16[64,64,64]{2,1,0:T(8,128)(2,1)S(1)} fusion(bf16[160,64,64]{2,1,0:T(8,128)(2,1)} %all-gather.3.cloned.1.call-done, s32[1024]{0:T(1024)S(1)} %pad_clamp_fusion), kind=kCustom, calls=%fused_computation | custom fusion | bytes 1048832 | tf_op jit(solution)/shard_map/gather | solution.py:39
  59.3 7.2 %fusion.11 = f32[1024,64]{0,1:T(8,128)S(1)} fusion(bf16[4096,64]{1,0:T(8,128)(2,1)S(1)} %bitcast.58, bf16[1024,4096]{0,1:T(8,128)(2,1)} %copy.31, f32[1024,64]{0,1:T(8,128)S(1)} %copy-done.1), kind=kOutput, calls=%fused_computation.21 | convolution fusion | flops 1086586880 | bytes 9437184 | tf_op jit(solution)/shard_map/dot_general | solution.py:47
  66.5 8.1 %convolution_convert_fusion.1 = bf16[4096,64]{0,1:T(8,128)(2,1)S(1)} fusion(bf16[1024,4096]{0,1:T(8,128)(2,1)} %copy.31, bf16[4096,64]{1,0:T(8,128)(2,1)S(1)} %bitcast.59, f32[1024,64]{0,1:T(8,128)S(1)} %fusion.11), kind=kOutput, calls=%fused_computation.11 | convolution fusion | flops 1086717952 | bytes 9699328 | tf_op jit(solution)/shard_map/dot_general | solution.py:54
  74.6 1.1 convert_element_type.59
  75.7 1.9 copy.36
  77.6 1.5 reshape.84
  79.2 3.6 %all-to-all-start = ((bf16[16,2,8192]{2,1,0:T(2,128)(2,1)}), bf16[16,2,8192]{2,1,0:T(2,128)(2,1)S(1)}, u32[]{:S(2)}, u32[]{:S(2)}) async-start(bf16[16,2,8192]{2,1,0:T(2,128)(2,1)} %reshape.84), calls=%async_computation | async-start | bytes 1048576 | tf_op jit(solution)/shard_map/all_to_all | solution.py:57
  82.8 0.2 all-gather.5.cloned.1.call-start
  83.0 0.1 constant_dynamic-slice_fusion
  83.1 0.1 copy.50
  83.2 0.1 convert_reduce_fusion
  83.3 13.9 %all-to-all-done = bf16[16,2,8192]{2,1,0:T(2,128)(2,1)S(1)} async-done(((bf16[16,2,8192]{2,1,0:T(2,128)(2,1)}), bf16[16,2,8192]{2,1,0:T(2,128)(2,1)S(1)}, u32[]{:S(2)}, u32[]{:S(2)}) %all-to-all-start) | async-done | bytes 524320 | tf_op jit(solution)/shard_map/all_to_all | solution.py:57
  97.2 0.7 reshape.85
  97.9 0.7 fusion.7
  98.6 0.1 copy.38
  98.7 0.7 fusion.18
  99.4 42.7 %all-gather.5.cloned.1.call-done = bf16[160,64,64]{2,1,0:T(8,128)(2,1)} async-done(((bf16[10,64,64]{2,1,0:T(8,128)(2,1)}), bf16[160,64,64]{2,1,0:T(8,128)(2,1)}) %all-gather.5.cloned.1.call-update) | async-done | bytes 1310736 | tf_op jit(solution)/shard_map/all_gather | solution.py:38
  142.1 2.5 %gather_fusion.1 = bf16[64,64,64]{2,1,0:T(8,128)(2,1)S(1)} fusion(bf16[160,64,64]{2,1,0:T(8,128)(2,1)} %all-gather.5.cloned.1.call-done, s32[1024]{0:T(1024)S(1)} %pad_clamp_fusion), kind=kCustom, calls=%fused_computation.1 | custom fusion | bytes 1048832 | tf_op jit(solution)/shard_map/gather | solution.py:39
  144.6 7.1 %fusion.10 = f32[1024,64]{0,1:T(8,128)S(1)} fusion(bf16[4096,64]{1,0:T(8,128)(2,1)S(1)} %bitcast.56, bf16[1024,4096]{0,1:T(8,128)(2,1)} %copy.31, f32[1024,64]{0,1:T(8,128)S(1)} %fusion.11), kind=kOutput, calls=%fused_computation.20 | convolution fusion | flops 1086586880 | bytes 9437184 | tf_op jit(solution)/shard_map/dot_general | solution.py:47
  151.7 8.2 %convolution_convert_fusion = bf16[4096,64]{0,1:T(8,128)(2,1)S(1)} fusion(bf16[1024,4096]{0,1:T(8,128)(2,1)} %copy.31, bf16[4096,64]{1,0:T(8,128)(2,1)S(1)} %bitcast.57, f32[1024,64]{0,1:T(8,128)S(1)} %fusion.10), kind=kOutput, calls=%fused_computation.10 | convolution fusion | flops 1086717952 | bytes 9699328 | tf_op jit(solution)/shard_map/dot_general | solution.py:54
  160.0 1.1 convert_element_type.65
  161.1 1.9 copy.41
  163.0 0.7 reshape.86
  163.7 17.6 %all_to_all.10 = bf16[16,2,8192]{2,1,0:T(2,128)(2,1)S(1)} all-to-all(bf16[16,2,8192]{2,1,0:T(2,128)(2,1)S(1)} %reshape.86), channel_id=1, replica_groups=mesh['groups'=2,'rows'=16] {'rows'}, dimensions={0} | all-to-all | bytes 1048576 | tf_op jit(solution)/shard_map/all_to_all | solution.py:57
  181.4 0.7 reshape.87
  182.0 0.7 fusion.6
  182.7 0.1 copy.43
  182.9 0.8 copy.44
  (14 shorter events, 0.2 us)
Async XLA Ops:
  7.2 49.6 %all-gather.3.cloned.1.call-start = ((), (), s32[]{:S(2)}) async-start(), calls=%async_computation.2 | async-start | bytes 2785280 | tf_op jit(solution)/shard_map/all_gather | solution.py:38
  9.0 12.1 %copy-start = (s32[16,64]{1,0:T(8,128)S(1)}, s32[16,64]{1,0:T(8,128)}, u32[]{:S(2)}) copy-start(s32[16,64]{1,0:T(8,128)} %param.7) | copy-start | bytes 12292
  9.0 50.3 %copy-start.1 = (f32[1024,64]{0,1:T(8,128)S(1)}, f32[1024,64]{0,1:T(8,128)}, u32[]{:S(2)}) copy-start(f32[1024,64]{0,1:T(8,128)} %param.5) | copy-start | bytes 786436
  79.2 18.0 %all-to-all-start = ((bf16[16,2,8192]{2,1,0:T(2,128)(2,1)}), bf16[16,2,8192]{2,1,0:T(2,128)(2,1)S(1)}, u32[]{:S(2)}, u32[]{:S(2)}) async-start(bf16[16,2,8192]{2,1,0:T(2,128)(2,1)} %reshape.84), calls=%async_computation | async-start | bytes 1048576 | tf_op jit(solution)/shard_map/all_to_all | solution.py:57
  82.8 59.3 %all-gather.5.cloned.1.call-start = ((), (), s32[]{:S(2)}) async-start(), calls=%async_computation.3 | async-start | bytes 2785280 | tf_op jit(solution)/shard_map/all_gather | solution.py:38
  151.7 12.0 %copy-start.2 = (f32[1024,64]{0,1:T(8,128)}, f32[1024,64]{0,1:T(8,128)S(1)}, u32[]{:S(2)}) copy-start(f32[1024,64]{0,1:T(8,128)S(1)} %fusion.10) | copy-start | bytes 786436
Sparse Core Ops, SparseCore 0:
  10.9 45.8 all-gather.2
  99.5 42.4 all-gather.4
where the time goes:
time: 191 us
  waiting for transfers between devices  92.2 us (48%)
  matrix products  32.1 us (17%)
  local copies, waits for them, and re-layouts  29 us (15%)
  blocking collectives  17.6 us (9%)
  between operations  14.2 us (7%)
  starting transfers between devices  3.83 us (2%)
    all_gather x2, waiting for transfers between devices, on_device(): gathered = lax.all_gather(snp_bf16, 'rows', axis=0, tiled=True)  78.3 us
    unnamed x14, local copies, waits for them, and re-layouts  17.6 us
    all_to_all x1, blocking collectives, on_device(): lax.all_to_all(snp_gradient.reshape(devices, per_owner, tile_size, rank_w...  17.6 us
    dot_general x2, matrix products, on_device(): lax.dot_general(residual, sample_bf16, (((0,), (0,)), ((), ())), preferre...  16.4 us
    dot_general x2, matrix products, on_device(): gradient = jnp.dot(residual, panels, preferred_element_type=jnp.float32)  14.3 us
    all_to_all x1, waiting for transfers between devices, on_device(): lax.all_to_all(snp_gradient.reshape(devices, per_owner, tile_size, rank_w...  13.9 us
    convert_element_type x4, local copies, waits for them, and re-layouts, on_device(): snp_gradient.reshape(devices, per_owner, tile_size, rank_width)  6.07 us
    gather x2, local copies, waits for them, and re-layouts, on_device(): panels = gathered[own_list].reshape(covered * tile_size, rank_width)  4.97 us
  transfers between devices with their start and end apart: 3, of which 3 were waited for; matrix products, arithmetic and copies ran while one was open for 7% of the time, Pallas kernels for 0%

commit v1 on v0

v1 whole, which is shorter than its diff:
```python
import functools
import math

import jax
import jax.numpy as jnp
from jax import lax
from jax.experimental import pallas as pl
from jax.experimental.pallas import tpu as pltpu
from jax.sharding import PartitionSpec as P

ROUNDS = 2

weight_decay = 0.02

PLANE = 4
NT = (((1,), (1,)), ((), ()))
NN = (((1,), (0,)), ((), ()))
VMEM_LIMIT = 24 * 1024 * 1024


def dot(a, b, dims):
    return lax.dot_general(a, b, dims, preferred_element_type=jnp.float32)


def split3(x):
    hi = x.astype(jnp.bfloat16)
    rest = x - hi.astype(jnp.float32)
    mid = rest.astype(jnp.bfloat16)
    lo = (rest - mid.astype(jnp.float32)).astype(jnp.bfloat16)
    return hi, mid, lo


def low_half(rows):
    return lax.broadcasted_iota(jnp.int32, (rows, 128), 1) < 64


def double(x, low):
    turned = pltpu.roll(x, 64, 1)
    return jnp.where(low, x, turned), jnp.where(low, turned, x)


def owner_at(pos, planes, ahead, mate):
    plane = lax.rem(lax.shift_right_logical(pos, 2) + ahead, planes)
    return plane * PLANE + lax.bitwise_xor(lax.bitwise_and(pos, 3), mate)


def load_kernel(geno, samples, geno_out, samples_out, sems):
    copies = [
        pltpu.make_async_copy(samples, samples_out, sems.at[0]),
        pltpu.make_async_copy(geno, geno_out, sems.at[1]),
    ]
    for copy in copies:
        copy.start()
    for copy in copies:
        copy.wait()


def table_kernel(planes, per_owner, own_blocks, pos_ref, cov, table):
    pos = pos_ref[0]
    for mate in range(PLANE):
        batch = owner_at(pos, planes, 0, mate)
        for ahead in range(planes):
            owner = owner_at(pos, planes, ahead, 0)
            for p in range(per_owner):
                table[mate * planes + ahead, p] = cov[batch, owner * per_owner + p] - owner * own_blocks


def pick_kernel(planes, per_owner, own_blocks, table, *refs):
    held, packets, blocks = refs[:planes], refs[planes:-1], refs[-1]
    low = low_half(held[0].shape[0])
    for ahead in range(planes):
        for j in range(own_blocks // 2):
            x = held[ahead][:, 128 * j:128 * (j + 1)].astype(jnp.float32)
            blocks[ahead, 2 * j], blocks[ahead, 2 * j + 1] = double(x, low)
    for ahead in range(planes):
        for mate in range(PLANE):
            for q in range(per_owner // 2):
                first = table[mate * planes + ahead, 2 * q]
                second = table[mate * planes + ahead, 2 * q + 1]
                pair = jnp.where(low, blocks[ahead, first], blocks[ahead, second])
                packets[mate][ahead, :, 128 * q:128 * (q + 1)] = pair.astype(jnp.bfloat16)


def plane_sum_kernel(planes, per_owner, own_blocks, table, *refs):
    terms, sums, total = refs[:PLANE], refs[PLANE:-1], refs[-1]
    low = low_half(terms[0].shape[1])
    total[...] = jnp.zeros_like(total)
    for ahead in range(planes):
        for mate in range(PLANE):
            for q in range(per_owner // 2):
                first = table[mate * planes + ahead, 2 * q]
                second = table[mate * planes + ahead, 2 * q + 1]
                pair = terms[mate][ahead, :, 128 * q:128 * (q + 1)].astype(jnp.float32)
                total[ahead, first] += jnp.where(low, pair, 0.0)
                total[ahead, second] += jnp.where(low, 0.0, pair)
    for ahead in range(planes):
        for j in range(own_blocks // 2):
            first, second = total[ahead, 2 * j], total[ahead, 2 * j + 1]
            both = jnp.where(low, first, second) + pltpu.roll(jnp.where(low, second, first), 64, 1)
            sums[ahead][:, 128 * j:128 * (j + 1)] = both.astype(sums[ahead].dtype)


def columns_of(pos, planes, ahead, mate, width):
    return pl.ds(pl.multiple_of(owner_at(pos, planes, ahead, mate) * width, width), width)


def product_kernel(planes, mates, first, rows, pos_ref, geno, *refs):
    refs = list(refs)
    packets = [refs.pop(0) for _ in mates]
    before = None if first else (refs.pop(0), refs.pop(0))
    gradient, gram = refs
    pos = pos_ref[0]
    width = packets[0].shape[2]
    total = None if first else before[1][...]
    for packet in packets:
        for ahead in range(planes):
            term = dot(packet[ahead], packet[ahead], NT)
            total = term if total is None else total + term
    gram[...] = total
    for i in range(geno.shape[0] // rows):
        here = slice(i * rows, (i + 1) * rows)
        total = None if first else before[0][:, here]
        for mate, packet in zip(mates, packets):
            for ahead in range(planes):
                term = dot(packet[ahead], geno[here, columns_of(pos, planes, ahead, mate, width)], NT)
                total = term if total is None else total + term
        gradient[:, here] = total


def sample_kernel(sample_step, samples, gradient, gram, new_samples, new_bf16, new_gram):
    old = samples[...]
    old_bf16 = old.astype(jnp.bfloat16)
    total = gradient[...]
    for part in split3(gram[...]):
        total -= dot(part, old_bf16, NN)
    new = (1.0 - weight_decay) * old + sample_step * total
    new_samples[...] = new
    rounded = new.astype(jnp.bfloat16)
    new_bf16[...] = rounded
    new_gram[...] = dot(rounded, rounded, NT)


def term_kernel(planes, mate, pos_ref, geno, samples, gram, packet, terms):
    pos = pos_ref[0]
    width = packet.shape[2]
    parts = split3(gram[...])
    for ahead in range(planes):
        term = dot(samples[...], geno[:, columns_of(pos, planes, ahead, mate, width)], NN)
        for part in parts:
            term -= dot(part, packet[ahead], NN)
        terms[ahead] = term.astype(jnp.bfloat16)


def on_device(genotypes, sample_factors, snp_factors, coverage):
    devices = lax.axis_size("rows")
    planes = devices // PLANE
    position = lax.axis_index("rows").astype(jnp.int32)
    samples_here, snps_here = genotypes.shape
    rank = sample_factors.shape[1]
    covered = coverage.shape[1]
    tile_size = snps_here // covered
    per_owner = covered // devices
    own_snps = snp_factors.shape[0]
    own_blocks = own_snps // tile_size
    width = per_owner * tile_size
    assert tile_size == 64 and per_owner % 2 == 0 and own_blocks % 2 == 0
    assert devices % PLANE == 0

    local_list = (
        lax.dynamic_slice_in_dim(coverage, position * per_owner, per_owner, 1)
        - position * own_blocks
    )
    one_hot = local_list[:, :, None] == jnp.arange(own_blocks, dtype=jnp.int32)[None, None, :]
    observers = jnp.sum(one_hot.astype(jnp.float32), axis=(0, 1))
    snp_step = 0.5 * math.sqrt(rank) / (samples_here * observers)
    snp_step = jnp.broadcast_to(snp_step[:, None], (own_blocks, tile_size)).reshape(1, own_snps)
    sample_step = 0.5 * math.sqrt(rank) / (covered * tile_size)

    smem = pl.BlockSpec(memory_space=pltpu.SMEM)
    vmem = pl.BlockSpec(memory_space=pltpu.VMEM)
    hbm = pl.BlockSpec(memory_space=pltpu.HBM)
    params = pltpu.CompilerParams(vmem_limit_bytes=VMEM_LIMIT)
    pos = position.reshape(1)
    packet = jax.ShapeDtypeStruct((planes, rank, width), jnp.bfloat16)
    dense_blocks = pltpu.VMEM((planes, own_blocks, rank, 128), jnp.float32)
    by_samples = jax.ShapeDtypeStruct((rank, samples_here), jnp.float32)
    square = jax.ShapeDtypeStruct((rank, rank), jnp.float32)
    sizes = (planes, per_owner, own_blocks)

    def cost(flops, bytes_accessed):
        return pl.CostEstimate(flops=flops, bytes_accessed=bytes_accessed, transcendentals=0)

    table = pl.pallas_call(
        functools.partial(table_kernel, *sizes),
        out_shape=jax.ShapeDtypeStruct((PLANE * planes, per_owner), jnp.int32),
        in_specs=[smem, smem],
        out_specs=smem,
        compiler_params=params,
        name="block_table",
    )(pos, coverage)
    geno, samples = pl.pallas_call(
        load_kernel,
        out_shape=(
            pltpu.VMEM((samples_here, snps_here), jnp.bfloat16),
            pltpu.VMEM((rank, samples_here), jnp.float32),
        ),
        in_specs=[hbm, hbm],
        out_specs=(vmem, vmem),
        scratch_shapes=[pltpu.SemaphoreType.DMA((2,))],
        compiler_params=pltpu.CompilerParams(
            vmem_limit_bytes=58 * 1024 * 1024 - 2 * samples_here * snps_here
        ),
        cost_estimate=cost(0, 2 * samples_here * snps_here),
        name="load_batch",
    )(genotypes, sample_factors.T)

    def pick(held):
        return pl.pallas_call(
            functools.partial(pick_kernel, *sizes),
            out_shape=(packet,) * PLANE,
            in_specs=[smem] + [vmem] * planes,
            out_specs=(vmem,) * PLANE,
            scratch_shapes=[dense_blocks],
            compiler_params=params,
            name="pick_blocks",
        )(table, *held)

    def plane_sum(terms):
        return pl.pallas_call(
            functools.partial(plane_sum_kernel, *sizes),
            out_shape=tuple(
                jax.ShapeDtypeStruct((rank, own_snps), jnp.bfloat16 if ahead else jnp.float32)
                for ahead in range(planes)
            ),
            in_specs=[smem] + [vmem] * PLANE,
            out_specs=(vmem,) * planes,
            scratch_shapes=[dense_blocks],
            compiler_params=params,
            name="plane_sum",
        )(table, *terms)

    def product(mates, panels, before):
        share = len(mates) * samples_here * snps_here // PLANE
        return pl.pallas_call(
            functools.partial(product_kernel, planes, mates, before is None, 256),
            out_shape=(by_samples, square),
            in_specs=[smem] + [vmem] * (1 + len(mates) + (0 if before is None else 2)),
            out_specs=(vmem, vmem),
            compiler_params=params,
            cost_estimate=cost(8 * rank * share, 2 * share),
            name="panel_product",
        )(pos, geno, *[panels[mate] for mate in mates], *(before or ()))

    def sample_update(samples, gradient, gram):
        return pl.pallas_call(
            functools.partial(sample_kernel, sample_step),
            out_shape=(by_samples, jax.ShapeDtypeStruct((rank, samples_here), jnp.bfloat16), square),
            in_specs=[vmem] * 3,
            out_specs=(vmem,) * 3,
            compiler_params=params,
            name="sample_update",
        )(samples, gradient, gram)

    def terms_for(mate, samples_bf16, gram, panel):
        share = samples_here * snps_here // PLANE
        return pl.pallas_call(
            functools.partial(term_kernel, planes, mate),
            out_shape=packet,
            in_specs=[smem] + [vmem] * 4,
            out_specs=vmem,
            compiler_params=params,
            cost_estimate=cost(8 * rank * share, 2 * share),
            name="mate_terms",
        )(pos, geno, samples_bf16, gram, panel)

    def along(x, shift):
        if shift % planes == 0:
            return x
        pairs = [(r, ((r // PLANE + shift) % planes) * PLANE + r % PLANE) for r in range(devices)]
        return lax.ppermute(x, "rows", pairs)

    def to_mate(x, mate):
        if mate == 0:
            return x
        return lax.ppermute(x, "rows", [(r, r ^ mate) for r in range(devices)])

    snps = snp_factors.T
    for iteration in range(ROUNDS):
        own = snps.astype(jnp.bfloat16)
        held = [along(own, planes - ahead) for ahead in range(planes)]
        packets = pick(held)
        panels = [to_mate(packets[mate], mate) for mate in range(PLANE)]
        partial = product([0], panels, None)
        partial = product([1], panels, partial)
        partial = product([2, 3], panels, partial)
        samples, samples_bf16, sample_gram = sample_update(samples, *partial)
        terms = [None] * PLANE
        for mate in (2, 3, 1, 0):
            terms[mate] = to_mate(terms_for(mate, samples_bf16, sample_gram, panels[mate]), mate)
        sums = plane_sum(terms)
        total = sums[0]
        for ahead in range(1, planes):
            total = total + along(sums[ahead], ahead).astype(jnp.float32)
        snps = (1.0 - weight_decay) * snps + snp_step * total
    return (samples.T, snps.T)


def solution(mesh):
    placed = (
        P(("groups", "rows"), None),
        P(("groups", "rows"), None),
        P(("groups", "rows"), None),
        P("groups", None),
    )
    return jax.shard_map(
        on_device,
        mesh=mesh,
        in_specs=placed,
        out_specs=(P(("groups", "rows"), None), P(("groups", "rows"), None)),
        check_vma=False,
    )
```

time: 191 us -> 87.7 us (0.46)
  waiting for transfers between devices: 92.2 us -> 28.4 us
  matrix products: 32.1 us -> 0 us
  starting transfers between devices: 3.83 us -> 29.4 us
  local copies, waits for them, and re-layouts: 29 us -> 5.1 us
  Pallas kernels: 0 us -> 21.8 us
  blocking collectives: 17.6 us -> 0 us
  between operations: 14.2 us -> 0.87 us
    all_gather x2 -> x0, waiting for transfers between devices: 78.3 us -> none  [on_device(): gathered = lax.all_gather(snp_bf16, 'rows', axis=0, tiled=True)]
    dot_general x6 -> x0, matrix products: 32.1 us -> none  [the longest x2 16.4 us: on_device(): lax.dot_general(residual, sample_bf16, (((0,), (0,)), ((), ())), preferre...]
    ppermute x0 -> x24, starting transfers between devices: none -> 29.4 us  [the longest x12 21.1 us: along(): return lax.ppermute(x, 'rows', pairs)]
    ppermute x0 -> x24, waiting for transfers between devices: none -> 28.4 us  [the longest x12 16.7 us: along(): return lax.ppermute(x, 'rows', pairs)]
    pallas_call x0 -> x22, Pallas kernels: none -> 21.8 us  [the longest x6 6.11 us: product(): pl.pallas_call(functools.partial(product_kernel, planes, mates, before is...]
    all_to_all x1 -> x0, blocking collectives: 17.6 us -> none  [on_device(): lax.all_to_all(snp_gradient.reshape(devices, per_owner, tile_size, rank_w...]
    all_to_all x1 -> x0, waiting for transfers between devices: 13.9 us -> none  [on_device(): lax.all_to_all(snp_gradient.reshape(devices, per_owner, tile_size, rank_w...]
    unnamed x14 -> x13, local copies, waits for them, and re-layouts: 17.6 us -> 4.18 us
  transfers between devices with their start and end apart: 3 -> 24, of which waited for: 3 -> 14; matrix products, arithmetic and copies ran while one was open for 7% -> 1% of each run, Pallas kernels for 0% -> 14%
where the time goes in v1:
time: 87.7 us; the launch traced here: 87.4 us
  starting transfers between devices  29.4 us (34%)
  waiting for transfers between devices  28.4 us (32%)
  Pallas kernels  21.8 us (25%)
  local copies, waits for them, and re-layouts  5.1 us (6%)
  other arithmetic  1.88 us (2%)
    ppermute x12, starting transfers between devices, along(): return lax.ppermute(x, 'rows', pairs)  21.1 us
    ppermute x12, waiting for transfers between devices, along(): return lax.ppermute(x, 'rows', pairs)  16.7 us
    ppermute x12, waiting for transfers between devices, to_mate(): return lax.ppermute(x, 'rows', [(r, r ^ mate) for r in range(devices)])  11.7 us
    ppermute x12, starting transfers between devices, to_mate(): return lax.ppermute(x, 'rows', [(r, r ^ mate) for r in range(devices)])  8.25 us
    pallas_call x6, Pallas kernels, product(): pl.pallas_call(functools.partial(product_kernel, planes, mates, before is...  6.11 us
    pallas_call x8, Pallas kernels, terms_for(): pl.pallas_call(functools.partial(term_kernel, planes, mate), out_shape=pa...  4.9 us
    unnamed x13, local copies, waits for them, and re-layouts  4.18 us
    pallas_call x1, Pallas kernels, on_device(): pl.pallas_call(load_kernel, out_shape=(pltpu.VMEM((samples_here, snps_her...  3.5 us
  transfers between devices with their start and end apart: 24, of which 14 were waited for; matrix products, arithmetic and copies ran while one was open for 1% of the time, Pallas kernels for 14%

profile of v1, /device:TPU:0, one launch (start us, length us, event | category | flops | bytes accessed | tf_op | source)
XLA Modules:
  0.0 87.4 jit_solution(3196370617228039359)
XLA Ops:
  1.6 3.1 %collective-permute-start.2 = (bf16[64,640]{1,0:T(8,128)(2,1)S(1)}, bf16[64,640]{1,0:T(8,128)(2,1)S(1)}, u32[]{:S(2)}, u32[]{:S(2)}) collective-permute-start(bf16[64,640]{1,0:T(8,128)(2,1)S(1)} %convert_bitcast_fusion.refs_0_), channel_id=1, source_target_pairs={{0,4},{1,5},{2,6},{3,7},{4,8},{5,9},{6,10},{7,11},{8,12},{9,13},{1... | collective-permute-start | bytes 245768 | tf_op jit(solution)/shard_map/ppermute | solution.py:280
  4.6 2.6 %collective-permute-start.1 = (bf16[64,640]{1,0:T(8,128)(2,1)S(1)}, bf16[64,640]{1,0:T(8,128)(2,1)S(1)}, u32[]{:S(2)}, u32[]{:S(2)}) collective-permute-start(bf16[64,640]{1,0:T(8,128)(2,1)S(1)} %convert_bitcast_fusion.refs_0_), channel_id=1, source_target_pairs={{0,8},{1,9},{2,10},{3,11},{4,12},{5,13},{6,14},{7,15},{8,0},{9,1},... | collective-permute-start | bytes 245768 | tf_op jit(solution)/shard_map/ppermute | solution.py:280
  7.2 1.3 %collective-permute-start = (bf16[64,640]{1,0:T(8,128)(2,1)S(1)}, bf16[64,640]{1,0:T(8,128)(2,1)S(1)}, u32[]{:S(2)}, u32[]{:S(2)}) collective-permute-start(bf16[64,640]{1,0:T(8,128)(2,1)S(1)} %convert_bitcast_fusion.refs_0_), channel_id=1, source_target_pairs={{0,12},{1,13},{2,14},{3,15},{4,0},{5,1},{6,2},{7,3},{8,4},{9,5},{1... | collective-permute-start | bytes 245768 | tf_op jit(solution)/shard_map/ppermute | solution.py:280
  10.1 1.5 %block_table.1.table = s32[16,4]{1,0:T(8,128)S(1)} custom-call(s32[1]{0:T(128)} %bitcast.1.pos_ref, s32[16,64]{1,0:T(8,128)S(1)} %copy-done.2), custom_call_target="tpu_custom_call" | custom-call | tf_op jit(solution)/shard_map/block_table/pallas_call | solution.py:193
  13.9 1.6 %collective-permute-start.3 = (bf16[4,64,256]{2,1,0:T(8,128)(2,1)S(1)}, bf16[4,64,256]{2,1,0:T(8,128)(2,1)S(1)}, u32[]{:S(2)}, u32[]{:S(2)}) collective-permute-start(bf16[4,64,256]{2,1,0:T(8,128)(2,1)S(1)} %get-tuple-element.40), channel_id=1, source_target_pairs={{0,2},{1,3},{2,0},{3,1},{4,6},{5,7},{6,4},{7,5},{8,10},{9,11},{10,... | collective-permute-start | bytes 393224 | tf_op jit(solution)/shard_map/ppermute | solution.py:285
  16.1 3.5 %load_batch.1 = (bf16[1024,4096]{1,0:T(8,128)(2,1)S(1)}, f32[64,1024]{1,0:T(8,128)S(1)}) custom-call(bf16[1024,4096]{1,0:T(8,128)(2,1)} %geno.1, f32[64,1024]{1,0:T(8,128)} %bitcast.12), custom_call_target="tpu_custom_call" | custom-call | bytes 8388608 | tf_op jit(solution)/shard_map/load_batch/pallas_call | solution.py:201
  21.2 1.5 %panel_product.8 = (f32[64,1024]{1,0:T(8,128)S(1)}, f32[64,64]{1,0:T(8,128)S(1)}) custom-call(s32[1]{0:T(128)} %bitcast.1.pos_ref, bf16[1024,4096]{1,0:T(8,128)(2,1)S(1)} %get-tuple-element.39.geno, bf16[4,64,256]{2,1,0:T(8,128)(2,1)S(1)} %collective-permute-done.3.refs_0_.packet, bf16[4,64,256]{2,1,0:T(8,128)(2,1)S(1)} %collective-permute-done.4.refs_1_.packet, ...), custom_call_target="tpu_custom_call" | custom-call | flops 1073741824 | bytes 4194304 | tf_op jit(solution)/shard_map/panel_product/pallas_call | solution.py:244
  24.9 1.5 %collective-permute-start.7 = (bf16[4,64,256]{2,1,0:T(8,128)(2,1)S(1)}, bf16[4,64,256]{2,1,0:T(8,128)(2,1)S(1)}, u32[]{:S(2)}, u32[]{:S(2)}) collective-permute-start(bf16[4,64,256]{2,1,0:T(8,128)(2,1)S(1)} %mate_terms.10), channel_id=1, source_target_pairs={{0,2},{1,3},{2,0},{3,1},{4,6},{5,7},{6,4},{7,5},{8,10},{9,11},{10,... | collective-permute-start | bytes 393224 | tf_op jit(solution)/shard_map/ppermute | solution.py:285
  27.8 2.9 %collective-permute-done.7.refs_2_ = bf16[4,64,256]{2,1,0:T(8,128)(2,1)S(1)} collective-permute-done((bf16[4,64,256]{2,1,0:T(8,128)(2,1)S(1)}, bf16[4,64,256]{2,1,0:T(8,128)(2,1)S(1)}, u32[]{:S(2)}, u32[]{:S(2)}) %collective-permute-start.7) | collective-permute-done | bytes 131104 | tf_op jit(solution)/shard_map/ppermute | solution.py:285
  30.8 2.1 %collective-permute-done.8.refs_3_ = bf16[4,64,256]{2,1,0:T(8,128)(2,1)S(1)} collective-permute-done((bf16[4,64,256]{2,1,0:T(8,128)(2,1)S(1)}, bf16[4,64,256]{2,1,0:T(8,128)(2,1)S(1)}, u32[]{:S(2)}, u32[]{:S(2)}) %collective-permute-start.8) | collective-permute-done | bytes 131104 | tf_op jit(solution)/shard_map/ppermute | solution.py:285
  32.9 1.3 %plane_sum.2 = (f32[64,640]{1,0:T(8,128)S(1)}, bf16[64,640]{1,0:T(8,128)(2,1)S(1)}, bf16[64,640]{1,0:T(8,128)(2,1)S(1)}, bf16[64,640]{1,0:T(8,128)(2,1)S(1)}) custom-call(s32[16,4]{1,0:T(8,128)S(1)} %block_table.1.table, bf16[4,64,256]{2,1,0:T(8,128)(2,1)S(1)} %mate_terms.8.refs_0_, bf16[4,64,256]{2,1,0:T(8,128)(2,1)S(1)} %collective-permute-done.6.refs_1_, ...), custom_call_target="tpu_custom_call" | custom-call | tf_op jit(solution)/shard_map/plane_sum/pallas_call | solution.py:229
  34.2 2.4 %collective-permute-start.9 = (bf16[64,640]{1,0:T(8,128)(2,1)S(1)}, bf16[64,640]{1,0:T(8,128)(2,1)S(1)}, u32[]{:S(2)}, u32[]{:S(2)}) collective-permute-start(bf16[64,640]{1,0:T(8,128)(2,1)S(1)} %get-tuple-element.54), channel_id=1, source_target_pairs={{0,4},{1,5},{2,6},{3,7},{4,8},{5,9},{6,10},{7,11},{8,12},{9,13},{1... | collective-permute-start | bytes 245768 | tf_op jit(solution)/shard_map/ppermute | solution.py:280
  36.5 1.4 %collective-permute-start.10 = (bf16[64,640]{1,0:T(8,128)(2,1)S(1)}, bf16[64,640]{1,0:T(8,128)(2,1)S(1)}, u32[]{:S(2)}, u32[]{:S(2)}) collective-permute-start(bf16[64,640]{1,0:T(8,128)(2,1)S(1)} %get-tuple-element.55), channel_id=1, source_target_pairs={{0,8},{1,9},{2,10},{3,11},{4,12},{5,13},{6,14},{7,15},{8,0},{9,1},... | collective-permute-start | bytes 245768 | tf_op jit(solution)/shard_map/ppermute | solution.py:280
  39.1 2.3 %collective-permute-done.9 = bf16[64,640]{1,0:T(8,128)(2,1)S(1)} collective-permute-done((bf16[64,640]{1,0:T(8,128)(2,1)S(1)}, bf16[64,640]{1,0:T(8,128)(2,1)S(1)}, u32[]{:S(2)}, u32[]{:S(2)}) %collective-permute-start.9) | collective-permute-done | bytes 81952 | tf_op jit(solution)/shard_map/ppermute | solution.py:280
  41.4 2.7 %collective-permute-done.10 = bf16[64,640]{1,0:T(8,128)(2,1)S(1)} collective-permute-done((bf16[64,640]{1,0:T(8,128)(2,1)S(1)}, bf16[64,640]{1,0:T(8,128)(2,1)S(1)}, u32[]{:S(2)}, u32[]{:S(2)}) %collective-permute-start.10) | collective-permute-done | bytes 81952 | tf_op jit(solution)/shard_map/ppermute | solution.py:280
  44.3 2.1 %collective-permute-start.14 = (bf16[64,640]{1,0:T(8,128)(2,1)S(1)}, bf16[64,640]{1,0:T(8,128)(2,1)S(1)}, u32[]{:S(2)}, u32[]{:S(2)}) collective-permute-start(bf16[64,640]{1,0:T(8,128)(2,1)S(1)} %get-tuple-element.74.refs_0_), channel_id=1, source_target_pairs={{0,4},{1,5},{2,6},{3,7},{4,8},{5,9},{6,10},{7,11},{8,12},{9,13},{1... | collective-permute-start | bytes 245768 | tf_op jit(solution)/shard_map/ppermute | solution.py:280
  46.5 1.1 %collective-permute-start.13 = (bf16[64,640]{1,0:T(8,128)(2,1)S(1)}, bf16[64,640]{1,0:T(8,128)(2,1)S(1)}, u32[]{:S(2)}, u32[]{:S(2)}) collective-permute-start(bf16[64,640]{1,0:T(8,128)(2,1)S(1)} %get-tuple-element.74.refs_0_), channel_id=1, source_target_pairs={{0,8},{1,9},{2,10},{3,11},{4,12},{5,13},{6,14},{7,15},{8,0},{9,1},... | collective-permute-start | bytes 245768 | tf_op jit(solution)/shard_map/ppermute | solution.py:280
  47.6 1.3 %collective-permute-start.12 = (bf16[64,640]{1,0:T(8,128)(2,1)S(1)}, bf16[64,640]{1,0:T(8,128)(2,1)S(1)}, u32[]{:S(2)}, u32[]{:S(2)}) collective-permute-start(bf16[64,640]{1,0:T(8,128)(2,1)S(1)} %get-tuple-element.74.refs_0_), channel_id=1, source_target_pairs={{0,12},{1,13},{2,14},{3,15},{4,0},{5,1},{6,2},{7,3},{8,4},{9,5},{1... | collective-permute-start | bytes 245768 | tf_op jit(solution)/shard_map/ppermute | solution.py:280
  48.9 2.6 %collective-permute-done.14.refs_3_ = bf16[64,640]{1,0:T(8,128)(2,1)S(1)} collective-permute-done((bf16[64,640]{1,0:T(8,128)(2,1)S(1)}, bf16[64,640]{1,0:T(8,128)(2,1)S(1)}, u32[]{:S(2)}, u32[]{:S(2)}) %collective-permute-start.14) | collective-permute-done | bytes 81952 | tf_op jit(solution)/shard_map/ppermute | solution.py:280
  51.5 2.4 %collective-permute-done.13.refs_2_ = bf16[64,640]{1,0:T(8,128)(2,1)S(1)} collective-permute-done((bf16[64,640]{1,0:T(8,128)(2,1)S(1)}, bf16[64,640]{1,0:T(8,128)(2,1)S(1)}, u32[]{:S(2)}, u32[]{:S(2)}) %collective-permute-start.13) | collective-permute-done | bytes 81952 | tf_op jit(solution)/shard_map/ppermute | solution.py:280
  55.0 1.6 %collective-permute-start.15 = (bf16[4,64,256]{2,1,0:T(8,128)(2,1)S(1)}, bf16[4,64,256]{2,1,0:T(8,128)(2,1)S(1)}, u32[]{:S(2)}, u32[]{:S(2)}) collective-permute-start(bf16[4,64,256]{2,1,0:T(8,128)(2,1)S(1)} %get-tuple-element.57), channel_id=1, source_target_pairs={{0,2},{1,3},{2,0},{3,1},{4,6},{5,7},{6,4},{7,5},{8,10},{9,11},{10,... | collective-permute-start | bytes 393224 | tf_op jit(solution)/shard_map/ppermute | solution.py:285
  56.9 3.4 %copy-done.1 = bf16[1024,4096]{1,0:T(8,128)(2,1)S(1)} copy-done((bf16[1024,4096]{1,0:T(8,128)(2,1)S(1)}, bf16[1024,4096]{1,0:T(8,128)(2,1)}, u32[]{:S(2)}) %copy-start.1) | copy-done | bytes 8388632
  61.9 1.4 %collective-permute-done.16.refs_1_.packet = bf16[4,64,256]{2,1,0:T(8,128)(2,1)S(1)} collective-permute-done((bf16[4,64,256]{2,1,0:T(8,128)(2,1)S(1)}, bf16[4,64,256]{2,1,0:T(8,128)(2,1)S(1)}, u32[]{:S(2)}, u32[]{:S(2)}) %collective-permute-start.16) | collective-permute-done | bytes 131104 | tf_op jit(solution)/shard_map/ppermute | solution.py:285
  63.3 1.5 %panel_product.11 = (f32[64,1024]{1,0:T(8,128)S(1)}, f32[64,64]{1,0:T(8,128)S(1)}) custom-call(s32[1]{0:T(128)} %bitcast.1.pos_ref, bf16[1024,4096]{1,0:T(8,128)(2,1)S(1)} %copy-done.1, bf16[4,64,256]{2,1,0:T(8,128)(2,1)S(1)} %collective-permute-done.15.refs_0_.packet, bf16[4,64,256]{2,1,0:T(8,128)(2,1)S(1)} %collective-permute-done.16.refs_1_.packet, ...), custom_call_target="tpu_custom_call" | custom-call | flops 1073741824 | bytes 4194304 | tf_op jit(solution)/shard_map/panel_product/pallas_call | solution.py:244
  67.3 1.6 %collective-permute-start.19 = (bf16[4,64,256]{2,1,0:T(8,128)(2,1)S(1)}, bf16[4,64,256]{2,1,0:T(8,128)(2,1)S(1)}, u32[]{:S(2)}, u32[]{:S(2)}) collective-permute-start(bf16[4,64,256]{2,1,0:T(8,128)(2,1)S(1)} %mate_terms.14), channel_id=1, source_target_pairs={{0,2},{1,3},{2,0},{3,1},{4,6},{5,7},{6,4},{7,5},{8,10},{9,11},{10,... | collective-permute-start | bytes 393224 | tf_op jit(solution)/shard_map/ppermute | solution.py:285
  70.2 3.1 %collective-permute-done.19.refs_2_ = bf16[4,64,256]{2,1,0:T(8,128)(2,1)S(1)} collective-permute-done((bf16[4,64,256]{2,1,0:T(8,128)(2,1)S(1)}, bf16[4,64,256]{2,1,0:T(8,128)(2,1)S(1)}, u32[]{:S(2)}, u32[]{:S(2)}) %collective-permute-start.19) | collective-permute-done | bytes 131104 | tf_op jit(solution)/shard_map/ppermute | solution.py:285
  73.3 2.1 %collective-permute-done.20.refs_3_ = bf16[4,64,256]{2,1,0:T(8,128)(2,1)S(1)} collective-permute-done((bf16[4,64,256]{2,1,0:T(8,128)(2,1)S(1)}, bf16[4,64,256]{2,1,0:T(8,128)(2,1)S(1)}, u32[]{:S(2)}, u32[]{:S(2)}) %collective-permute-start.20) | collective-permute-done | bytes 131104 | tf_op jit(solution)/shard_map/ppermute | solution.py:285
  75.5 1.3 %plane_sum.3 = (f32[64,640]{1,0:T(8,128)S(1)}, bf16[64,640]{1,0:T(8,128)(2,1)S(1)}, bf16[64,640]{1,0:T(8,128)(2,1)S(1)}, bf16[64,640]{1,0:T(8,128)(2,1)S(1)}) custom-call(s32[16,4]{1,0:T(8,128)S(1)} %block_table.1.table, bf16[4,64,256]{2,1,0:T(8,128)(2,1)S(1)} %mate_terms.12.refs_0_, bf16[4,64,256]{2,1,0:T(8,128)(2,1)S(1)} %collective-permute-done.18.refs_1_, ...), custom_call_target="tpu_custom_call" | custom-call | tf_op jit(solution)/shard_map/plane_sum/pallas_call | solution.py:229
  76.7 2.3 %collective-permute-start.21 = (bf16[64,640]{1,0:T(8,128)(2,1)S(1)}, bf16[64,640]{1,0:T(8,128)(2,1)S(1)}, u32[]{:S(2)}, u32[]{:S(2)}) collective-permute-start(bf16[64,640]{1,0:T(8,128)(2,1)S(1)} %get-tuple-element.71), channel_id=1, source_target_pairs={{0,4},{1,5},{2,6},{3,7},{4,8},{5,9},{6,10},{7,11},{8,12},{9,13},{1... | collective-permute-start | bytes 245768 | tf_op jit(solution)/shard_map/ppermute | solution.py:280
  80.1 1.3 %collective-permute-start.23 = (bf16[64,640]{1,0:T(8,128)(2,1)S(1)}, bf16[64,640]{1,0:T(8,128)(2,1)S(1)}, u32[]{:S(2)}, u32[]{:S(2)}) collective-permute-start(bf16[64,640]{1,0:T(8,128)(2,1)S(1)} %get-tuple-element.73), channel_id=1, source_target_pairs={{0,12},{1,13},{2,14},{3,15},{4,0},{5,1},{6,2},{7,3},{8,4},{9,5},{1... | collective-permute-start | bytes 245768 | tf_op jit(solution)/shard_map/ppermute | solution.py:280
  81.4 2.5 %collective-permute-done.21 = bf16[64,640]{1,0:T(8,128)(2,1)S(1)} collective-permute-done((bf16[64,640]{1,0:T(8,128)(2,1)S(1)}, bf16[64,640]{1,0:T(8,128)(2,1)S(1)}, u32[]{:S(2)}, u32[]{:S(2)}) %collective-permute-start.21) | collective-permute-done | bytes 81952 | tf_op jit(solution)/shard_map/ppermute | solution.py:280
  84.0 2.7 %collective-permute-done.22 = bf16[64,640]{1,0:T(8,128)(2,1)S(1)} collective-permute-done((bf16[64,640]{1,0:T(8,128)(2,1)S(1)}, bf16[64,640]{1,0:T(8,128)(2,1)S(1)}, u32[]{:S(2)}, u32[]{:S(2)}) %collective-permute-start.22) | collective-permute-done | bytes 81952 | tf_op jit(solution)/shard_map/ppermute | solution.py:280
  (61 shorter events, 20.4 us)
Async XLA Ops:
  1.6 10.1 %collective-permute-start.2 = (bf16[64,640]{1,0:T(8,128)(2,1)S(1)}, bf16[64,640]{1,0:T(8,128)(2,1)S(1)}, u32[]{:S(2)}, u32[]{:S(2)}) collective-permute-start(bf16[64,640]{1,0:T(8,128)(2,1)S(1)} %convert_bitcast_fusion.refs_0_), channel_id=1, source_target_pairs={{0,4},{1,5},{2,6},{3,7},{4,8},{5,9},{6,10},{7,11},{8,12},{9,13},{1... | collective-permute-start | bytes 245768 | tf_op jit(solution)/shard_map/ppermute | solution.py:280
  4.6 8.1 %collective-permute-start.1 = (bf16[64,640]{1,0:T(8,128)(2,1)S(1)}, bf16[64,640]{1,0:T(8,128)(2,1)S(1)}, u32[]{:S(2)}, u32[]{:S(2)}) collective-permute-start(bf16[64,640]{1,0:T(8,128)(2,1)S(1)} %convert_bitcast_fusion.refs_0_), channel_id=1, source_target_pairs={{0,8},{1,9},{2,10},{3,11},{4,12},{5,13},{6,14},{7,15},{8,0},{9,1},... | collective-permute-start | bytes 245768 | tf_op jit(solution)/shard_map/ppermute | solution.py:280
  7.2 5.7 %collective-permute-start = (bf16[64,640]{1,0:T(8,128)(2,1)S(1)}, bf16[64,640]{1,0:T(8,128)(2,1)S(1)}, u32[]{:S(2)}, u32[]{:S(2)}) collective-permute-start(bf16[64,640]{1,0:T(8,128)(2,1)S(1)} %convert_bitcast_fusion.refs_0_), channel_id=1, source_target_pairs={{0,12},{1,13},{2,14},{3,15},{4,0},{5,1},{6,2},{7,3},{8,4},{9,5},{1... | collective-permute-start | bytes 245768 | tf_op jit(solution)/shard_map/ppermute | solution.py:280
  9.4 0.7 copy-start.2
  13.9 7.3 %collective-permute-start.3 = (bf16[4,64,256]{2,1,0:T(8,128)(2,1)S(1)}, bf16[4,64,256]{2,1,0:T(8,128)(2,1)S(1)}, u32[]{:S(2)}, u32[]{:S(2)}) collective-permute-start(bf16[4,64,256]{2,1,0:T(8,128)(2,1)S(1)} %get-tuple-element.40), channel_id=1, source_target_pairs={{0,2},{1,3},{2,0},{3,1},{4,6},{5,7},{6,4},{7,5},{8,10},{9,11},{10,... | collective-permute-start | bytes 393224 | tf_op jit(solution)/shard_map/ppermute | solution.py:285
  15.4 5.8 %collective-permute-start.4 = (bf16[4,64,256]{2,1,0:T(8,128)(2,1)S(1)}, bf16[4,64,256]{2,1,0:T(8,128)(2,1)S(1)}, u32[]{:S(2)}, u32[]{:S(2)}) collective-permute-start(bf16[4,64,256]{2,1,0:T(8,128)(2,1)S(1)} %get-tuple-element.41), channel_id=1, source_target_pairs={{0,3},{1,2},{2,1},{3,0},{4,7},{5,6},{6,5},{7,4},{8,11},{9,10},{10,... | collective-permute-start | bytes 393224 | tf_op jit(solution)/shard_map/ppermute | solution.py:285
  15.4 4.9 %collective-permute-start.5 = (bf16[4,64,256]{2,1,0:T(8,128)(2,1)S(1)}, bf16[4,64,256]{2,1,0:T(8,128)(2,1)S(1)}, u32[]{:S(2)}, u32[]{:S(2)}) collective-permute-start(bf16[4,64,256]{2,1,0:T(8,128)(2,1)S(1)} %get-tuple-element.42), channel_id=1, source_target_pairs={{0,1},{1,0},{2,3},{3,2},{4,5},{5,4},{6,7},{7,6},{8,9},{9,8},{10,11... | collective-permute-start | bytes 393224 | tf_op jit(solution)/shard_map/ppermute | solution.py:285
  19.6 7.6 %copy-start = (bf16[1024,4096]{1,0:T(8,128)(2,1)}, bf16[1024,4096]{1,0:T(8,128)(2,1)S(1)}, u32[]{:S(2)}) copy-start(bf16[1024,4096]{1,0:T(8,128)(2,1)S(1)} %get-tuple-element.39.geno) | copy-start | bytes 25165828
  23.7 4.1 %collective-permute-start.6 = (bf16[4,64,256]{2,1,0:T(8,128)(2,1)S(1)}, bf16[4,64,256]{2,1,0:T(8,128)(2,1)S(1)}, u32[]{:S(2)}, u32[]{:S(2)}) collective-permute-start(bf16[4,64,256]{2,1,0:T(8,128)(2,1)S(1)} %mate_terms.9), channel_id=1, source_target_pairs={{0,1},{1,0},{2,3},{3,2},{4,5},{5,4},{6,7},{7,6},{8,9},{9,8},{10,11... | collective-permute-start | bytes 393224 | tf_op jit(solution)/shard_map/ppermute | solution.py:285
  24.9 19.4 %copy-start.3 = (f32[640,64]{0,1:T(8,128)S(1)}, f32[640,64]{0,1:T(8,128)}, u32[]{:S(2)}) copy-start(f32[640,64]{0,1:T(8,128)} %param.6) | copy-start | bytes 491524
  24.9 5.9 %collective-permute-start.7 = (bf16[4,64,256]{2,1,0:T(8,128)(2,1)S(1)}, bf16[4,64,256]{2,1,0:T(8,128)(2,1)S(1)}, u32[]{:S(2)}, u32[]{:S(2)}) collective-permute-start(bf16[4,64,256]{2,1,0:T(8,128)(2,1)S(1)} %mate_terms.10), channel_id=1, source_target_pairs={{0,2},{1,3},{2,0},{3,1},{4,6},{5,7},{6,4},{7,5},{8,10},{9,11},{10,... | collective-permute-start | bytes 393224 | tf_op jit(solution)/shard_map/ppermute | solution.py:285
  27.0 5.9 %collective-permute-start.8 = (bf16[4,64,256]{2,1,0:T(8,128)(2,1)S(1)}, bf16[4,64,256]{2,1,0:T(8,128)(2,1)S(1)}, u32[]{:S(2)}, u32[]{:S(2)}) collective-permute-start(bf16[4,64,256]{2,1,0:T(8,128)(2,1)S(1)} %mate_terms.11), channel_id=1, source_target_pairs={{0,3},{1,2},{2,1},{3,0},{4,7},{5,6},{6,5},{7,4},{8,11},{9,10},{10,... | collective-permute-start | bytes 393224 | tf_op jit(solution)/shard_map/ppermute | solution.py:285
  34.2 7.2 %collective-permute-start.9 = (bf16[64,640]{1,0:T(8,128)(2,1)S(1)}, bf16[64,640]{1,0:T(8,128)(2,1)S(1)}, u32[]{:S(2)}, u32[]{:S(2)}) collective-permute-start(bf16[64,640]{1,0:T(8,128)(2,1)S(1)} %get-tuple-element.54), channel_id=1, source_target_pairs={{0,4},{1,5},{2,6},{3,7},{4,8},{5,9},{6,10},{7,11},{8,12},{9,13},{1... | collective-permute-start | bytes 245768 | tf_op jit(solution)/shard_map/ppermute | solution.py:280
  36.5 7.6 %collective-permute-start.10 = (bf16[64,640]{1,0:T(8,128)(2,1)S(1)}, bf16[64,640]{1,0:T(8,128)(2,1)S(1)}, u32[]{:S(2)}, u32[]{:S(2)}) collective-permute-start(bf16[64,640]{1,0:T(8,128)(2,1)S(1)} %get-tuple-element.55), channel_id=1, source_target_pairs={{0,8},{1,9},{2,10},{3,11},{4,12},{5,13},{6,14},{7,15},{8,0},{9,1},... | collective-permute-start | bytes 245768 | tf_op jit(solution)/shard_map/ppermute | solution.py:280
  38.0 6.3 %collective-permute-start.11 = (bf16[64,640]{1,0:T(8,128)(2,1)S(1)}, bf16[64,640]{1,0:T(8,128)(2,1)S(1)}, u32[]{:S(2)}, u32[]{:S(2)}) collective-permute-start(bf16[64,640]{1,0:T(8,128)(2,1)S(1)} %get-tuple-element.56), channel_id=1, source_target_pairs={{0,12},{1,13},{2,14},{3,15},{4,0},{5,1},{6,2},{7,3},{8,4},{9,5},{1... | collective-permute-start | bytes 245768 | tf_op jit(solution)/shard_map/ppermute | solution.py:280
  44.3 7.2 %collective-permute-start.14 = (bf16[64,640]{1,0:T(8,128)(2,1)S(1)}, bf16[64,640]{1,0:T(8,128)(2,1)S(1)}, u32[]{:S(2)}, u32[]{:S(2)}) collective-permute-start(bf16[64,640]{1,0:T(8,128)(2,1)S(1)} %get-tuple-element.74.refs_0_), channel_id=1, source_target_pairs={{0,4},{1,5},{2,6},{3,7},{4,8},{5,9},{6,10},{7,11},{8,12},{9,13},{1... | collective-permute-start | bytes 245768 | tf_op jit(solution)/shard_map/ppermute | solution.py:280
  46.5 7.5 %collective-permute-start.13 = (bf16[64,640]{1,0:T(8,128)(2,1)S(1)}, bf16[64,640]{1,0:T(8,128)(2,1)S(1)}, u32[]{:S(2)}, u32[]{:S(2)}) collective-permute-start(bf16[64,640]{1,0:T(8,128)(2,1)S(1)} %get-tuple-element.74.refs_0_), channel_id=1, source_target_pairs={{0,8},{1,9},{2,10},{3,11},{4,12},{5,13},{6,14},{7,15},{8,0},{9,1},... | collective-permute-start | bytes 245768 | tf_op jit(solution)/shard_map/ppermute | solution.py:280
  47.6 6.4 %collective-permute-start.12 = (bf16[64,640]{1,0:T(8,128)(2,1)S(1)}, bf16[64,640]{1,0:T(8,128)(2,1)S(1)}, u32[]{:S(2)}, u32[]{:S(2)}) collective-permute-start(bf16[64,640]{1,0:T(8,128)(2,1)S(1)} %get-tuple-element.74.refs_0_), channel_id=1, source_target_pairs={{0,12},{1,13},{2,14},{3,15},{4,0},{5,1},{6,2},{7,3},{8,4},{9,5},{1... | collective-permute-start | bytes 245768 | tf_op jit(solution)/shard_map/ppermute | solution.py:280
  54.9 6.1 %collective-permute-start.17 = (bf16[4,64,256]{2,1,0:T(8,128)(2,1)S(1)}, bf16[4,64,256]{2,1,0:T(8,128)(2,1)S(1)}, u32[]{:S(2)}, u32[]{:S(2)}) collective-permute-start(bf16[4,64,256]{2,1,0:T(8,128)(2,1)S(1)} %get-tuple-element.59), channel_id=1, source_target_pairs={{0,1},{1,0},{2,3},{3,2},{4,5},{5,4},{6,7},{7,6},{8,9},{9,8},{10,11... | collective-permute-start | bytes 393224 | tf_op jit(solution)/shard_map/ppermute | solution.py:285
  55.0 6.9 %collective-permute-start.15 = (bf16[4,64,256]{2,1,0:T(8,128)(2,1)S(1)}, bf16[4,64,256]{2,1,0:T(8,128)(2,1)S(1)}, u32[]{:S(2)}, u32[]{:S(2)}) collective-permute-start(bf16[4,64,256]{2,1,0:T(8,128)(2,1)S(1)} %get-tuple-element.57), channel_id=1, source_target_pairs={{0,2},{1,3},{2,0},{3,1},{4,6},{5,7},{6,4},{7,5},{8,10},{9,11},{10,... | collective-permute-start | bytes 393224 | tf_op jit(solution)/shard_map/ppermute | solution.py:285
  56.6 6.6 %collective-permute-start.16 = (bf16[4,64,256]{2,1,0:T(8,128)(2,1)S(1)}, bf16[4,64,256]{2,1,0:T(8,128)(2,1)S(1)}, u32[]{:S(2)}, u32[]{:S(2)}) collective-permute-start(bf16[4,64,256]{2,1,0:T(8,128)(2,1)S(1)} %get-tuple-element.58), channel_id=1, source_target_pairs={{0,3},{1,2},{2,1},{3,0},{4,7},{5,6},{6,5},{7,4},{8,11},{9,10},{10,... | collective-permute-start | bytes 393224 | tf_op jit(solution)/shard_map/ppermute | solution.py:285
  56.9 3.4 %copy-start.1 = (bf16[1024,4096]{1,0:T(8,128)(2,1)S(1)}, bf16[1024,4096]{1,0:T(8,128)(2,1)}, u32[]{:S(2)}) copy-start(bf16[1024,4096]{1,0:T(8,128)(2,1)} %copy-done) | copy-start | bytes 25165828
  61.1 4.7 %slice-start = ((s8[8388608]{0:T(1024)(128)(4,1)}), s8[4194304]{0:T(1024)(128)(4,1)S(1)}, s32[]{:S(2)}) async-start(s8[8388608]{0:T(1024)(128)(4,1)} %bitcast.10), calls=%async_computation | async-start | bytes 8388608
  63.3 2.5 %slice-start.1 = ((s8[8388608]{0:T(1024)(128)(4,1)}), s8[4194304]{0:T(1024)(128)(4,1)S(1)}, s32[]{:S(2)}) async-start(s8[8388608]{0:T(1024)(128)(4,1)} %bitcast.10), calls=%async_computation.1 | async-start | bytes 8388608
  66.3 3.9 %collective-permute-start.18 = (bf16[4,64,256]{2,1,0:T(8,128)(2,1)S(1)}, bf16[4,64,256]{2,1,0:T(8,128)(2,1)S(1)}, u32[]{:S(2)}, u32[]{:S(2)}) collective-permute-start(bf16[4,64,256]{2,1,0:T(8,128)(2,1)S(1)} %mate_terms.13), channel_id=1, source_target_pairs={{0,1},{1,0},{2,3},{3,2},{4,5},{5,4},{6,7},{7,6},{8,9},{9,8},{10,11... | collective-permute-start | bytes 393224 | tf_op jit(solution)/shard_map/ppermute | solution.py:285
  67.3 6.0 %collective-permute-start.19 = (bf16[4,64,256]{2,1,0:T(8,128)(2,1)S(1)}, bf16[4,64,256]{2,1,0:T(8,128)(2,1)S(1)}, u32[]{:S(2)}, u32[]{:S(2)}) collective-permute-start(bf16[4,64,256]{2,1,0:T(8,128)(2,1)S(1)} %mate_terms.14), channel_id=1, source_target_pairs={{0,2},{1,3},{2,0},{3,1},{4,6},{5,7},{6,4},{7,5},{8,10},{9,11},{10,... | collective-permute-start | bytes 393224 | tf_op jit(solution)/shard_map/ppermute | solution.py:285
  69.5 5.9 %collective-permute-start.20 = (bf16[4,64,256]{2,1,0:T(8,128)(2,1)S(1)}, bf16[4,64,256]{2,1,0:T(8,128)(2,1)S(1)}, u32[]{:S(2)}, u32[]{:S(2)}) collective-permute-start(bf16[4,64,256]{2,1,0:T(8,128)(2,1)S(1)} %mate_terms.15), channel_id=1, source_target_pairs={{0,3},{1,2},{2,1},{3,0},{4,7},{5,6},{6,5},{7,4},{8,11},{9,10},{10,... | collective-permute-start | bytes 393224 | tf_op jit(solution)/shard_map/ppermute | solution.py:285
  76.7 7.2 %collective-permute-start.21 = (bf16[64,640]{1,0:T(8,128)(2,1)S(1)}, bf16[64,640]{1,0:T(8,128)(2,1)S(1)}, u32[]{:S(2)}, u32[]{:S(2)}) collective-permute-start(bf16[64,640]{1,0:T(8,128)(2,1)S(1)} %get-tuple-element.71), channel_id=1, source_target_pairs={{0,4},{1,5},{2,6},{3,7},{4,8},{5,9},{6,10},{7,11},{8,12},{9,13},{1... | collective-permute-start | bytes 245768 | tf_op jit(solution)/shard_map/ppermute | solution.py:280
  79.0 7.7 %collective-permute-start.22 = (bf16[64,640]{1,0:T(8,128)(2,1)S(1)}, bf16[64,640]{1,0:T(8,128)(2,1)S(1)}, u32[]{:S(2)}, u32[]{:S(2)}) collective-permute-start(bf16[64,640]{1,0:T(8,128)(2,1)S(1)} %get-tuple-element.72), channel_id=1, source_target_pairs={{0,8},{1,9},{2,10},{3,11},{4,12},{5,13},{6,14},{7,15},{8,0},{9,1},... | collective-permute-start | bytes 245768 | tf_op jit(solution)/shard_map/ppermute | solution.py:280
  80.1 6.6 %collective-permute-start.23 = (bf16[64,640]{1,0:T(8,128)(2,1)S(1)}, bf16[64,640]{1,0:T(8,128)(2,1)S(1)}, u32[]{:S(2)}, u32[]{:S(2)}) collective-permute-start(bf16[64,640]{1,0:T(8,128)(2,1)S(1)} %get-tuple-element.73), channel_id=1, source_target_pairs={{0,12},{1,13},{2,14},{3,15},{4,0},{5,1},{6,2},{7,3},{8,4},{9,5},{1... | collective-permute-start | bytes 245768 | tf_op jit(solution)/shard_map/ppermute | solution.py:280

commit v2 on v1

--- a/solution.py
+++ b/solution.py
@@ -63,6 +63,60 @@
             owner = owner_at(pos, planes, ahead, 0)
             for p in range(per_owner):
                 table[mate * planes + ahead, p] = cov[batch, owner * per_owner + p] - owner * own_blocks
+
+
+def write_sends(cov, pos, blocks, send, per_owner):
+    own_blocks = blocks.shape[0]
+    low = low_half(blocks.shape[1])
+
+    def batch(b, carry):
+        for q in range(per_owner // 2):
+            first = cov[b, pos * per_owner + 2 * q] - pos * own_blocks
+            second = cov[b, pos * per_owner + 2 * q + 1] - pos * own_blocks
+            pair = jnp.where(low, blocks[first], blocks[second])
+            send[b, :, 128 * q:128 * (q + 1)] = pair.astype(send.dtype)
+        return carry
+
+    lax.fori_loop(0, send.shape[0], batch, 0, unroll=4)
+
+
+def pack_kernel(per_owner, pos_ref, cov, snps, send, upper, blocks):
+    own_blocks, rows = blocks.shape[0], blocks.shape[1]
+    low = low_half(rows)
+    upper[...] = snps[rows:, :]
+    for j in range(own_blocks // 2):
+        blocks[2 * j], blocks[2 * j + 1] = double(snps[rows:, 128 * j:128 * (j + 1)], low)
+    write_sends(cov, pos_ref[0], blocks, send, per_owner)
+
+
+def owner_kernel(per_owner, last, pos_ref, cov, steps, incoming, snps, new_snps, *rest):
+    pos = pos_ref[0]
+    total = rest[-1]
+    own_blocks = total.shape[0]
+    low = low_half(total.shape[1])
+    total[...] = jnp.zeros_like(total)
+
+    def batch(b, carry):
+        for q in range(per_owner // 2):
+            first = cov[b, pos * per_owner + 2 * q] - pos * own_blocks
+            second = cov[b, pos * per_owner + 2 * q + 1] - pos * own_blocks
+            pair = incoming[b, :, 128 * q:128 * (q + 1)].astype(jnp.float32)
+            total[first] += jnp.where(low, pair, 0.0)
+            total[second] += jnp.where(low, 0.0, pair)
+        return carry
+
+    lax.fori_loop(0, incoming.shape[0], batch, 0, unroll=4)
+    for j in range(own_blocks // 2):
+        first, second = total[2 * j], total[2 * j + 1]
+        first = (first + pltpu.roll(first, 64, 1)) * steps[2 * j]
+        second = (second + pltpu.roll(second, 64, 1)) * steps[2 * j + 1]
+        columns = slice(128 * j, 128 * (j + 1))
+        updated = (1.0 - weight_decay) * snps[:, columns] + jnp.where(low, first, second)
+        new_snps[:, columns] = updated
+        if not last:
+            total[2 * j], total[2 * j + 1] = double(updated, low)
+    if not last:
+        write_sends(cov, pos, total, rest[0], per_owner)
 
 
 def pick_kernel(planes, per_owner, own_blocks, table, *refs):
@@ -104,26 +158,30 @@
     return pl.ds(pl.multiple_of(owner_at(pos, planes, ahead, mate) * width, width), width)
 
 
-def product_kernel(planes, mates, first, rows, pos_ref, geno, *refs):
+def panel_of(pos, planes, ahead, mate, packet, upper):
+    return jnp.concatenate([packet[ahead], upper[owner_at(pos, planes, ahead, mate)]], axis=0)
+
+
+def product_kernel(planes, mates, first, rows, pos_ref, geno, upper, *refs):
     refs = list(refs)
     packets = [refs.pop(0) for _ in mates]
     before = None if first else (refs.pop(0), refs.pop(0))
     gradient, gram = refs
     pos = pos_ref[0]
     width = packets[0].shape[2]
+    places = [(mate, packet, ahead) for mate, packet in zip(mates, packets) for ahead in range(planes)]
+    panels = [panel_of(pos, planes, ahead, mate, packet, upper) for mate, packet, ahead in places]
     total = None if first else before[1][...]
-    for packet in packets:
-        for ahead in range(planes):
-            term = dot(packet[ahead], packet[ahead], NT)
-            total = term if total is None else total + term
+    for panel in panels:
+        term = dot(panel, panel, NT)
+        total = term if total is None else total + term
     gram[...] = total
     for i in range(geno.shape[0] // rows):
         here = slice(i * rows, (i + 1) * rows)
         total = None if first else before[0][:, here]
-        for mate, packet in zip(mates, packets):
-            for ahead in range(planes):
-                term = dot(packet[ahead], geno[here, columns_of(pos, planes, ahead, mate, width)], NT)
-                total = term if total is None else total + term
+        for (mate, packet, ahead), panel in zip(places, panels):
+            term = dot(panel, geno[here, columns_of(pos, planes, ahead, mate, width)], NT)
+            total = term if total is None else total + term
         gradient[:, here] = total
 
 
@@ -140,15 +198,24 @@
     new_gram[...] = dot(rounded, rounded, NT)
 
 
-def term_kernel(planes, mate, pos_ref, geno, samples, gram, packet, terms):
+def term_kernel(planes, mate, others, pos_ref, geno, samples, gram, packet, upper, *refs):
+    terms, direct = refs[-2:]
     pos = pos_ref[0]
-    width = packet.shape[2]
+    half, width = packet.shape[1], packet.shape[2]
     parts = split3(gram[...])
     for ahead in range(planes):
+        panel = panel_of(pos, planes, ahead, mate, packet, upper)
         term = dot(samples[...], geno[:, columns_of(pos, planes, ahead, mate, width)], NN)
         for part in parts:
-            term -= dot(part, packet[ahead], NN)
-        terms[ahead] = term.astype(jnp.bfloat16)
+            term -= dot(part, panel, NN)
+        term = term.astype(jnp.bfloat16)
+        terms[ahead] = term[:half]
+        if others:
+            direct[owner_at(pos, planes, ahead, mate)] = term[half:]
+            for other, piece in zip(others, refs):
+                direct[owner_at(pos, planes, ahead, other)] = piece[ahead]
+        else:
+            direct[ahead] = term[half:]
 
 
 def on_device(genotypes, sample_factors, snp_factors, coverage):
@@ -165,6 +232,7 @@
     width = per_owner * tile_size
     assert tile_size == 64 and per_owner % 2 == 0 and own_blocks % 2 == 0
     assert devices % PLANE == 0
+    half = rank // 2
 
     local_list = (
         lax.dynamic_slice_in_dim(coverage, position * per_owner, per_owner, 1)
@@ -173,7 +241,7 @@
     one_hot = local_list[:, :, None] == jnp.arange(own_blocks, dtype=jnp.int32)[None, None, :]
     observers = jnp.sum(one_hot.astype(jnp.float32), axis=(0, 1))
     snp_step = 0.5 * math.sqrt(rank) / (samples_here * observers)
-    snp_step = jnp.broadcast_to(snp_step[:, None], (own_blocks, tile_size)).reshape(1, own_snps)
+    snp_steps = jnp.broadcast_to(snp_step[:, None], (own_blocks, tile_size)).reshape(1, own_snps)
     sample_step = 0.5 * math.sqrt(rank) / (covered * tile_size)
 
     smem = pl.BlockSpec(memory_space=pltpu.SMEM)
@@ -181,8 +249,11 @@
     hbm = pl.BlockSpec(memory_space=pltpu.HBM)
     params = pltpu.CompilerParams(vmem_limit_bytes=VMEM_LIMIT)
     pos = position.reshape(1)
-    packet = jax.ShapeDtypeStruct((planes, rank, width), jnp.bfloat16)
-    dense_blocks = pltpu.VMEM((planes, own_blocks, rank, 128), jnp.float32)
+    packet = jax.ShapeDtypeStruct((planes, half, width), jnp.bfloat16)
+    direct = jax.ShapeDtypeStruct((devices, half, width), jnp.bfloat16)
+    dense_blocks = pltpu.VMEM((planes, own_blocks, half, 128), jnp.float32)
+    owner_blocks = pltpu.VMEM((own_blocks, half, 128), jnp.float32)
+    half_snps = jax.ShapeDtypeStruct((half, own_snps), jnp.float32)
     by_samples = jax.ShapeDtypeStruct((rank, samples_here), jnp.float32)
     square = jax.ShapeDtypeStruct((rank, rank), jnp.float32)
     sizes = (planes, per_owner, own_blocks)
@@ -229,7 +300,7 @@
         return pl.pallas_call(
             functools.partial(plane_sum_kernel, *sizes),
             out_shape=tuple(
-                jax.ShapeDtypeStruct((rank, own_snps), jnp.bfloat16 if ahead else jnp.float32)
+                jax.ShapeDtypeStruct((half, own_snps), jnp.bfloat16 if ahead else jnp.float32)
                 for ahead in range(planes)
             ),
             in_specs=[smem] + [vmem] * PLANE,
@@ -239,17 +310,43 @@
             name="plane_sum",
         )(table, *terms)
 
-    def product(mates, panels, before):
+    def pack(snps):
+        return pl.pallas_call(
+            functools.partial(pack_kernel, per_owner),
+            out_shape=(direct, half_snps),
+            in_specs=[smem, smem, vmem],
+            out_specs=(vmem, vmem),
+            scratch_shapes=[owner_blocks],
+            compiler_params=params,
+            name="pack_blocks",
+        )(pos, coverage, snps)
+
+    def owner_update(incoming, snps, last):
+        results = pl.pallas_call(
+            functools.partial(owner_kernel, per_owner, last),
+            out_shape=(half_snps,) if last else (half_snps, direct),
+            in_specs=[smem, smem, smem, vmem, vmem],
+            out_specs=(vmem,) if last else (vmem, vmem),
+            scratch_shapes=[owner_blocks],
+            compiler_params=params,
+            name="owner_update",
+        )(pos, coverage, snp_step, incoming, snps)
+        return results[0], None if last else results[1]
+
+    def resident():
+        return pltpu.with_memory_space_constraint(geno, pltpu.VMEM)
+
+    def product(mates, panels, upper, before):
         share = len(mates) * samples_here * snps_here // PLANE
         return pl.pallas_call(
             functools.partial(product_kernel, planes, mates, before is None, 256),
             out_shape=(by_samples, square),
-            in_specs=[smem] + [vmem] * (1 + len(mates) + (0 if before is None else 2)),
+            in_specs=[smem] + [vmem] * (2 + len(mates) + (0 if before is None else 2)),
             out_specs=(vmem, vmem),
             compiler_params=params,
             cost_estimate=cost(8 * rank * share, 2 * share),
             name="panel_product",
-        )(pos, geno, *[panels[mate] for mate in mates], *(before or ()))
+        )(pos, resident(), upper, *[panels[mate] for mate in mates], *(before or ()))
 
     def sample_update(samples, gradient, gram):
         return pl.pallas_call(
@@ -261,17 +358,20 @@
             name="sample_update",
         )(samples, gradient, gram)
 
-    def terms_for(mate, samples_bf16, gram, panel):
+    def terms_for(mate, samples_bf16, gram, panel, upper, others, pieces):
         share = samples_here * snps_here // PLANE
         return pl.pallas_call(
-            functools.partial(term_kernel, planes, mate),
-            out_shape=packet,
-            in_specs=[smem] + [vmem] * 4,
-            out_specs=vmem,
+            functools.partial(term_kernel, planes, mate, others),
+            out_shape=(packet, direct if others else packet),
+            in_specs=[smem] + [vmem] * (5 + len(pieces)),
+            out_specs=(vmem, vmem),
             compiler_params=params,
             cost_estimate=cost(8 * rank * share, 2 * share),
             name="mate_terms",
-        )(pos, geno, samples_bf16, gram, panel)
+        )(pos, resident(), samples_bf16, gram, panel, upper, *pieces)
+
+    def exchange(x):
+        return lax.all_to_all(x, "rows", split_axis=0, concat_axis=0, tiled=True)
 
     def along(x, shift):
         if shift % planes == 0:
@@ -284,25 +384,37 @@
             return x
         return lax.ppermute(x, "rows", [(r, r ^ mate) for r in range(devices)])
 
-    snps = snp_factors.T
+    lower = snp_factors.T[:half]
+    outgoing, upper = pack(snp_factors.T)
     for iteration in range(ROUNDS):
-        own = snps.astype(jnp.bfloat16)
+        own = lower.astype(jnp.bfloat16)
         held = [along(own, planes - ahead) for ahead in range(planes)]
+        upper_panels = exchange(outgoing)
         packets = pick(held)
         panels = [to_mate(packets[mate], mate) for mate in range(PLANE)]
-        partial = product([0], panels, None)
-        partial = product([1], panels, partial)
-        partial = product([2, 3], panels, partial)
+        partial = product([0], panels, upper_panels, None)
+        partial = product([1], panels, upper_panels, partial)
+        partial = product([2, 3], panels, upper_panels, partial)
         samples, samples_bf16, sample_gram = sample_update(samples, *partial)
-        terms = [None] * PLANE
-        for mate in (2, 3, 1, 0):
-            terms[mate] = to_mate(terms_for(mate, samples_bf16, sample_gram, panels[mate]), mate)
-        sums = plane_sum(terms)
+        terms, pieces = {}, []
+        order = (2, 3, 1, 0)
+        for mate in order:
+            last = mate == order[-1]
+            own_terms, piece = terms_for(
+                mate, samples_bf16, sample_gram, panels[mate], upper_panels,
+                order[:-1] if last else (), pieces if last else [],
+            )
+            terms[mate] = to_mate(own_terms, mate)
+            pieces.append(piece)
+        outgoing = pieces[-1]
+        incoming = exchange(outgoing)
+        sums = plane_sum([terms[mate] for mate in range(PLANE)])
         total = sums[0]
         for ahead in range(1, planes):
             total = total + along(sums[ahead], ahead).astype(jnp.float32)
-        snps = (1.0 - weight_decay) * snps + snp_step * total
-    return (samples.T, snps.T)
+        lower = (1.0 - weight_decay) * lower + snp_steps * total
+        upper, outgoing = owner_update(incoming, upper, iteration == ROUNDS - 1)
+    return (samples.T, jnp.concatenate([lower, upper], axis=0).T)
 
 
 def solution(mesh):

time: 87.7 us -> 128 us (1.46)
  starting transfers between devices: 29.4 us -> 48.7 us
  local copies, waits for them, and re-layouts: 5.1 us -> 15.6 us
  Pallas kernels: 21.8 us -> 27.5 us
  waiting for transfers between devices: 28.4 us -> 33.5 us
    all_to_all x0 -> x4, starting transfers between devices: none -> 18.8 us  [exchange(): return lax.all_to_all(x, 'rows', split_axis=0, concat_axis=0, tiled=True)]
    all_to_all x0 -> x4, waiting for transfers between devices: none -> 9.87 us  [exchange(): return lax.all_to_all(x, 'rows', split_axis=0, concat_axis=0, tiled=True)]
    unnamed x13 -> x25, local copies, waits for them, and re-layouts: 4.18 us -> 13.8 us
    pallas_call x8 -> x11, Pallas kernels: 4.9 us -> 11 us  [the longest x8 6.28 us: terms_for(): pl.pallas_call(functools.partial(term_kernel, planes, mate, others), out_...]
    ppermute x12, waiting for transfers between devices: 16.7 us -> 13 us  [along(): return lax.ppermute(x, 'rows', pairs)]
  transfers between devices with their start and end apart: 24 -> 28, of which waited for: 14 -> 16; matrix products, arithmetic and copies ran while one was open for 1% -> 2% of each run, Pallas kernels for 14% -> 10%
where the time goes in v2:
time: 128 us; the launch traced here: 127 us
  starting transfers between devices  48.7 us (38%)
  waiting for transfers between devices  33.5 us (26%)
  Pallas kernels  27.5 us (21%)
  local copies, waits for them, and re-layouts  15.6 us (12%)
    ppermute x12, starting transfers between devices, along(): return lax.ppermute(x, 'rows', pairs)  21.6 us
    all_to_all x4, starting transfers between devices, exchange(): return lax.all_to_all(x, 'rows', split_axis=0, concat_axis=0, tiled=True)  18.8 us
    unnamed x25, local copies, waits for them, and re-layouts  13.8 us
    ppermute x12, waiting for transfers between devices, along(): return lax.ppermute(x, 'rows', pairs)  13 us
    ppermute x12, waiting for transfers between devices, to_mate(): return lax.ppermute(x, 'rows', [(r, r ^ mate) for r in range(devices)])  10.6 us
    all_to_all x4, waiting for transfers between devices, exchange(): return lax.all_to_all(x, 'rows', split_axis=0, concat_axis=0, tiled=True)  9.87 us
    ppermute x12, starting transfers between devices, to_mate(): return lax.ppermute(x, 'rows', [(r, r ^ mate) for r in range(devices)])  8.26 us
    pallas_call x8, Pallas kernels, terms_for(): pl.pallas_call(functools.partial(term_kernel, planes, mate, others), out_...  6.28 us
  transfers between devices with their start and end apart: 28, of which 16 were waited for; matrix products, arithmetic and copies ran while one was open for 2% of the time, Pallas kernels for 10%

profile of v2, /device:TPU:0, one launch (start us, length us, event | category | flops | bytes accessed | tf_op | source)
XLA Modules:
  0.0 127.1 jit_solution(11608110709576548879)
XLA Ops:
  2.2 1.6 %pack_blocks.1 = (bf16[16,32,256]{2,1,0:T(8,128)(2,1)}, f32[32,640]{1,0:T(8,128)S(1)}) custom-call(s32[1]{0:T(128)} %bitcast.1.pos_ref, s32[16,64]{1,0:T(8,128)S(1)} %copy-done.5, f32[64,640]{1,0:T(8,128)S(1)} %bitcast.11), custom_call_target="tpu_custom_call" | custom-call | tf_op jit(solution)/shard_map/pack_blocks/pallas_call | solution.py:314
  3.9 7.4 %all-to-all-start = ((bf16[16,32,256]{2,1,0:T(8,128)(2,1)}), bf16[16,32,256]{2,1,0:T(8,128)(2,1)S(1)}, u32[]{:S(2)}, u32[]{:S(2)}) async-start(bf16[16,32,256]{2,1,0:T(8,128)(2,1)} %get-tuple-element.60), calls=%async_computation | async-start | bytes 524288 | tf_op jit(solution)/shard_map/all_to_all | solution.py:374
  12.2 1.9 %collective-permute-start.2 = (bf16[32,640]{1,0:T(8,128)(2,1)S(1)}, bf16[32,640]{1,0:T(8,128)(2,1)S(1)}, u32[]{:S(2)}, u32[]{:S(2)}) collective-permute-start(bf16[32,640]{1,0:T(8,128)(2,1)S(1)} %slice.7.refs_0_), channel_id=1, source_target_pairs={{0,4},{1,5},{2,6},{3,7},{4,8},{5,9},{6,10},{7,11},{8,12},{9,13},{1... | collective-permute-start | bytes 122888 | tf_op jit(solution)/shard_map/ppermute | solution.py:380
  14.1 2.4 %collective-permute-start.1 = (bf16[32,640]{1,0:T(8,128)(2,1)S(1)}, bf16[32,640]{1,0:T(8,128)(2,1)S(1)}, u32[]{:S(2)}, u32[]{:S(2)}) collective-permute-start(bf16[32,640]{1,0:T(8,128)(2,1)S(1)} %slice.7.refs_0_), channel_id=1, source_target_pairs={{0,8},{1,9},{2,10},{3,11},{4,12},{5,13},{6,14},{7,15},{8,0},{9,1},... | collective-permute-start | bytes 122888 | tf_op jit(solution)/shard_map/ppermute | solution.py:380
  18.6 1.5 %block_table.1.table = s32[16,4]{1,0:T(8,128)S(1)} custom-call(s32[1]{0:T(128)} %bitcast.1.pos_ref, s32[16,64]{1,0:T(8,128)S(1)} %copy-done.6), custom_call_target="tpu_custom_call" | custom-call | tf_op jit(solution)/shard_map/block_table/pallas_call | solution.py:264
  20.2 1.6 %collective-permute-done.2.refs_3_ = bf16[32,640]{1,0:T(8,128)(2,1)S(1)} collective-permute-done((bf16[32,640]{1,0:T(8,128)(2,1)S(1)}, bf16[32,640]{1,0:T(8,128)(2,1)S(1)}, u32[]{:S(2)}, u32[]{:S(2)}) %collective-permute-start.2) | collective-permute-done | bytes 40992 | tf_op jit(solution)/shard_map/ppermute | solution.py:380
  21.8 2.2 %collective-permute-done.1.refs_2_ = bf16[32,640]{1,0:T(8,128)(2,1)S(1)} collective-permute-done((bf16[32,640]{1,0:T(8,128)(2,1)S(1)}, bf16[32,640]{1,0:T(8,128)(2,1)S(1)}, u32[]{:S(2)}, u32[]{:S(2)}) %collective-permute-start.1) | collective-permute-done | bytes 40992 | tf_op jit(solution)/shard_map/ppermute | solution.py:380
  25.8 3.5 %load_batch.1 = (bf16[1024,4096]{1,0:T(8,128)(2,1)S(1)}, f32[64,1024]{1,0:T(8,128)S(1)}) custom-call(bf16[1024,4096]{1,0:T(8,128)(2,1)} %geno.1, f32[64,1024]{1,0:T(8,128)} %bitcast.13), custom_call_target="tpu_custom_call" | custom-call | bytes 8388608 | tf_op jit(solution)/shard_map/load_batch/pallas_call | solution.py:272
  29.3 3.3 %copy-done = bf16[1024,4096]{1,0:T(8,128)(2,1)} copy-done((bf16[1024,4096]{1,0:T(8,128)(2,1)}, bf16[1024,4096]{1,0:T(8,128)(2,1)S(1)}, u32[]{:S(2)}) %copy-start) | copy-done | bytes 8388632
  32.6 1.5 %collective-permute-start.3 = (bf16[4,32,256]{2,1,0:T(8,128)(2,1)S(1)}, bf16[4,32,256]{2,1,0:T(8,128)(2,1)S(1)}, u32[]{:S(2)}, u32[]{:S(2)}) collective-permute-start(bf16[4,32,256]{2,1,0:T(8,128)(2,1)S(1)} %get-tuple-element.61), channel_id=1, source_target_pairs={{0,2},{1,3},{2,0},{3,1},{4,6},{5,7},{6,4},{7,5},{8,10},{9,11},{10,... | collective-permute-start | bytes 196616 | tf_op jit(solution)/shard_map/ppermute | solution.py:385
  34.4 3.4 %copy-done.1 = bf16[1024,4096]{1,0:T(8,128)(2,1)S(1)} copy-done((bf16[1024,4096]{1,0:T(8,128)(2,1)S(1)}, bf16[1024,4096]{1,0:T(8,128)(2,1)}, u32[]{:S(2)}) %copy-start.1) | copy-done | bytes 8388632
  39.5 1.5 %panel_product.8 = (f32[64,1024]{1,0:T(8,128)S(1)}, f32[64,64]{1,0:T(8,128)S(1)}) custom-call(s32[1]{0:T(128)} %bitcast.1.pos_ref, bf16[1024,4096]{1,0:T(8,128)(2,1)S(1)} %copy-done.1, bf16[16,32,256]{2,1,0:T(8,128)(2,1)S(1)} %all-to-all-done.upper, bf16[4,32,256]{2,1,0:T(8,128)(2,1)S(1)} %collective-permute-done.3.refs_0_.packet, ...), custom_call_target="tpu_custom_call" | custom-call | flops 1073741824 | bytes 4194304 | tf_op jit(solution)/shard_map/panel_product/pallas_call | solution.py:341
  45.5 4.2 %all-to-all-start.1 = ((bf16[16,32,256]{2,1,0:T(8,128)(2,1)}), bf16[16,32,256]{2,1,0:T(8,128)(2,1)S(1)}, u32[]{:S(2)}, u32[]{:S(2)}) async-start(bf16[16,32,256]{2,1,0:T(8,128)(2,1)} %get-tuple-element.77), calls=%async_computation.1 | async-start | bytes 524288 | tf_op jit(solution)/shard_map/all_to_all | solution.py:374
  49.9 9.9 %all-to-all-done.1.incoming = bf16[16,32,256]{2,1,0:T(8,128)(2,1)S(1)} async-done(((bf16[16,32,256]{2,1,0:T(8,128)(2,1)}), bf16[16,32,256]{2,1,0:T(8,128)(2,1)S(1)}, u32[]{:S(2)}, u32[]{:S(2)}) %all-to-all-start.1) | async-done | bytes 262176 | tf_op jit(solution)/shard_map/all_to_all | solution.py:374
  59.7 2.0 %owner_update.2 = (f32[32,640]{1,0:T(8,128)S(1)}, bf16[16,32,256]{2,1,0:T(8,128)(2,1)}) custom-call(s32[1]{0:T(128)} %bitcast.1.pos_ref, s32[16,64]{1,0:T(8,128)S(1)} %copy-done.7, f32[10]{0:T(128)S(1)} %multiply_divide_fusion.steps, bf16[16,32,256]{2,1,0:T(8,128)(2,1)S(1)} %all-to-all-done.1.incoming, f32[32,640]{1,0:T(8,128)S(1)} %get-tuple-element.78.snps), custom_call_target="tpu_custom_call" | custom-call | tf_op jit(solution)/shard_map/owner_update/pallas_call | solution.py:325
  61.7 3.5 %all-to-all-start.2 = ((bf16[16,32,256]{2,1,0:T(8,128)(2,1)}), bf16[16,32,256]{2,1,0:T(8,128)(2,1)S(1)}, u32[]{:S(2)}, u32[]{:S(2)}) async-start(bf16[16,32,256]{2,1,0:T(8,128)(2,1)} %get-tuple-element.79), calls=%async_computation.2 | async-start | bytes 524288 | tf_op jit(solution)/shard_map/all_to_all | solution.py:374
  65.3 1.8 %collective-permute-start.7 = (bf16[4,32,256]{2,1,0:T(8,128)(2,1)S(1)}, bf16[4,32,256]{2,1,0:T(8,128)(2,1)S(1)}, u32[]{:S(2)}, u32[]{:S(2)}) collective-permute-start(bf16[4,32,256]{2,1,0:T(8,128)(2,1)S(1)} %get-tuple-element.82), channel_id=1, source_target_pairs={{0,2},{1,3},{2,0},{3,1},{4,6},{5,7},{6,4},{7,5},{8,10},{9,11},{10,... | collective-permute-start | bytes 196616 | tf_op jit(solution)/shard_map/ppermute | solution.py:385
  67.5 4.5 %collective-permute-done.7.refs_2_ = bf16[4,32,256]{2,1,0:T(8,128)(2,1)S(1)} collective-permute-done((bf16[4,32,256]{2,1,0:T(8,128)(2,1)S(1)}, bf16[4,32,256]{2,1,0:T(8,128)(2,1)S(1)}, u32[]{:S(2)}, u32[]{:S(2)}) %collective-permute-start.7) | collective-permute-done | bytes 65568 | tf_op jit(solution)/shard_map/ppermute | solution.py:385
  73.8 1.7 %collective-permute-start.9 = (bf16[32,640]{1,0:T(8,128)(2,1)S(1)}, bf16[32,640]{1,0:T(8,128)(2,1)S(1)}, u32[]{:S(2)}, u32[]{:S(2)}) collective-permute-start(bf16[32,640]{1,0:T(8,128)(2,1)S(1)} %get-tuple-element.85), channel_id=1, source_target_pairs={{0,4},{1,5},{2,6},{3,7},{4,8},{5,9},{6,10},{7,11},{8,12},{9,13},{1... | collective-permute-start | bytes 122888 | tf_op jit(solution)/shard_map/ppermute | solution.py:380
  75.6 3.1 %collective-permute-start.10 = (bf16[32,640]{1,0:T(8,128)(2,1)S(1)}, bf16[32,640]{1,0:T(8,128)(2,1)S(1)}, u32[]{:S(2)}, u32[]{:S(2)}) collective-permute-start(bf16[32,640]{1,0:T(8,128)(2,1)S(1)} %get-tuple-element.86), channel_id=1, source_target_pairs={{0,8},{1,9},{2,10},{3,11},{4,12},{5,13},{6,14},{7,15},{8,0},{9,1},... | collective-permute-start | bytes 122888 | tf_op jit(solution)/shard_map/ppermute | solution.py:380
  80.1 1.7 %collective-permute-done.10 = bf16[32,640]{1,0:T(8,128)(2,1)S(1)} collective-permute-done((bf16[32,640]{1,0:T(8,128)(2,1)S(1)}, bf16[32,640]{1,0:T(8,128)(2,1)S(1)}, u32[]{:S(2)}, u32[]{:S(2)}) %collective-permute-start.10) | collective-permute-done | bytes 40992 | tf_op jit(solution)/shard_map/ppermute | solution.py:380
  83.3 3.0 %collective-permute-start.13 = (bf16[32,640]{1,0:T(8,128)(2,1)S(1)}, bf16[32,640]{1,0:T(8,128)(2,1)S(1)}, u32[]{:S(2)}, u32[]{:S(2)}) collective-permute-start(bf16[32,640]{1,0:T(8,128)(2,1)S(1)} %get-tuple-element.114.refs_0_), channel_id=1, source_target_pairs={{0,8},{1,9},{2,10},{3,11},{4,12},{5,13},{6,14},{7,15},{8,0},{9,1},... | collective-permute-start | bytes 122888 | tf_op jit(solution)/shard_map/ppermute | solution.py:380
  86.8 2.0 %collective-permute-done.14.refs_3_ = bf16[32,640]{1,0:T(8,128)(2,1)S(1)} collective-permute-done((bf16[32,640]{1,0:T(8,128)(2,1)S(1)}, bf16[32,640]{1,0:T(8,128)(2,1)S(1)}, u32[]{:S(2)}, u32[]{:S(2)}) %collective-permute-start.14) | collective-permute-done | bytes 40992 | tf_op jit(solution)/shard_map/ppermute | solution.py:380
  91.5 1.6 %collective-permute-start.16 = (bf16[4,32,256]{2,1,0:T(8,128)(2,1)S(1)}, bf16[4,32,256]{2,1,0:T(8,128)(2,1)S(1)}, u32[]{:S(2)}, u32[]{:S(2)}) collective-permute-start(bf16[4,32,256]{2,1,0:T(8,128)(2,1)S(1)} %get-tuple-element.89), channel_id=1, source_target_pairs={{0,3},{1,2},{2,1},{3,0},{4,7},{5,6},{6,5},{7,4},{8,11},{9,10},{10,... | collective-permute-start | bytes 196616 | tf_op jit(solution)/shard_map/ppermute | solution.py:385
  93.0 3.4 %copy-done.2 = bf16[1024,4096]{1,0:T(8,128)(2,1)S(1)} copy-done((bf16[1024,4096]{1,0:T(8,128)(2,1)S(1)}, bf16[1024,4096]{1,0:T(8,128)(2,1)}, u32[]{:S(2)}) %copy-start.2) | copy-done | bytes 8388632
  98.1 1.5 %panel_product.11 = (f32[64,1024]{1,0:T(8,128)S(1)}, f32[64,64]{1,0:T(8,128)S(1)}) custom-call(s32[1]{0:T(128)} %bitcast.1.pos_ref, bf16[1024,4096]{1,0:T(8,128)(2,1)S(1)} %copy-done.2, bf16[16,32,256]{2,1,0:T(8,128)(2,1)S(1)} %all-to-all-done.2.upper, bf16[4,32,256]{2,1,0:T(8,128)(2,1)S(1)} %collective-permute-done.15.refs_0_.packet, ...), custom_call_target="tpu_custom_call" | custom-call | flops 1073741824 | bytes 4194304 | tf_op jit(solution)/shard_map/panel_product/pallas_call | solution.py:341
  104.1 3.7 %all-to-all-start.3 = ((bf16[16,32,256]{2,1,0:T(8,128)(2,1)}), bf16[16,32,256]{2,1,0:T(8,128)(2,1)S(1)}, u32[]{:S(2)}, u32[]{:S(2)}) async-start(bf16[16,32,256]{2,1,0:T(8,128)(2,1)} %get-tuple-element.112), calls=%async_computation.3 | async-start | bytes 524288 | tf_op jit(solution)/shard_map/all_to_all | solution.py:374
  107.8 1.9 %collective-permute-start.19 = (bf16[4,32,256]{2,1,0:T(8,128)(2,1)S(1)}, bf16[4,32,256]{2,1,0:T(8,128)(2,1)S(1)}, u32[]{:S(2)}, u32[]{:S(2)}) collective-permute-start(bf16[4,32,256]{2,1,0:T(8,128)(2,1)S(1)} %get-tuple-element.106), channel_id=1, source_target_pairs={{0,2},{1,3},{2,0},{3,1},{4,6},{5,7},{6,4},{7,5},{8,10},{9,11},{10,... | collective-permute-start | bytes 196616 | tf_op jit(solution)/shard_map/ppermute | solution.py:385
  110.0 4.7 %collective-permute-done.19.refs_2_ = bf16[4,32,256]{2,1,0:T(8,128)(2,1)S(1)} collective-permute-done((bf16[4,32,256]{2,1,0:T(8,128)(2,1)S(1)}, bf16[4,32,256]{2,1,0:T(8,128)(2,1)S(1)}, u32[]{:S(2)}, u32[]{:S(2)}) %collective-permute-start.19) | collective-permute-done | bytes 65568 | tf_op jit(solution)/shard_map/ppermute | solution.py:385
  116.5 1.7 %collective-permute-start.21 = (bf16[32,640]{1,0:T(8,128)(2,1)S(1)}, bf16[32,640]{1,0:T(8,128)(2,1)S(1)}, u32[]{:S(2)}, u32[]{:S(2)}) collective-permute-start(bf16[32,640]{1,0:T(8,128)(2,1)S(1)} %get-tuple-element.109), channel_id=1, source_target_pairs={{0,4},{1,5},{2,6},{3,7},{4,8},{5,9},{6,10},{7,11},{8,12},{9,13},{1... | collective-permute-start | bytes 122888 | tf_op jit(solution)/shard_map/ppermute | solution.py:380
  118.2 3.1 %collective-permute-start.22 = (bf16[32,640]{1,0:T(8,128)(2,1)S(1)}, bf16[32,640]{1,0:T(8,128)(2,1)S(1)}, u32[]{:S(2)}, u32[]{:S(2)}) collective-permute-start(bf16[32,640]{1,0:T(8,128)(2,1)S(1)} %get-tuple-element.110), channel_id=1, source_target_pairs={{0,8},{1,9},{2,10},{3,11},{4,12},{5,13},{6,14},{7,15},{8,0},{9,1},... | collective-permute-start | bytes 122888 | tf_op jit(solution)/shard_map/ppermute | solution.py:380
  122.7 1.8 %collective-permute-done.22 = bf16[32,640]{1,0:T(8,128)(2,1)S(1)} collective-permute-done((bf16[32,640]{1,0:T(8,128)(2,1)S(1)}, bf16[32,640]{1,0:T(8,128)(2,1)S(1)}, u32[]{:S(2)}, u32[]{:S(2)}) %collective-permute-start.22) | collective-permute-done | bytes 40992 | tf_op jit(solution)/shard_map/ppermute | solution.py:380
  (86 shorter events, 33.6 us)
Async XLA Ops:
  3.9 30.6 %all-to-all-start = ((bf16[16,32,256]{2,1,0:T(8,128)(2,1)}), bf16[16,32,256]{2,1,0:T(8,128)(2,1)S(1)}, u32[]{:S(2)}, u32[]{:S(2)}) async-start(bf16[16,32,256]{2,1,0:T(8,128)(2,1)} %get-tuple-element.60), calls=%async_computation | async-start | bytes 524288 | tf_op jit(solution)/shard_map/all_to_all | solution.py:374
  12.2 9.6 %collective-permute-start.2 = (bf16[32,640]{1,0:T(8,128)(2,1)S(1)}, bf16[32,640]{1,0:T(8,128)(2,1)S(1)}, u32[]{:S(2)}, u32[]{:S(2)}) collective-permute-start(bf16[32,640]{1,0:T(8,128)(2,1)S(1)} %slice.7.refs_0_), channel_id=1, source_target_pairs={{0,4},{1,5},{2,6},{3,7},{4,8},{5,9},{6,10},{7,11},{8,12},{9,13},{1... | collective-permute-start | bytes 122888 | tf_op jit(solution)/shard_map/ppermute | solution.py:380
  14.1 9.9 %collective-permute-start.1 = (bf16[32,640]{1,0:T(8,128)(2,1)S(1)}, bf16[32,640]{1,0:T(8,128)(2,1)S(1)}, u32[]{:S(2)}, u32[]{:S(2)}) collective-permute-start(bf16[32,640]{1,0:T(8,128)(2,1)S(1)} %slice.7.refs_0_), channel_id=1, source_target_pairs={{0,8},{1,9},{2,10},{3,11},{4,12},{5,13},{6,14},{7,15},{8,0},{9,1},... | collective-permute-start | bytes 122888 | tf_op jit(solution)/shard_map/ppermute | solution.py:380
  16.4 7.5 %collective-permute-start = (bf16[32,640]{1,0:T(8,128)(2,1)S(1)}, bf16[32,640]{1,0:T(8,128)(2,1)S(1)}, u32[]{:S(2)}, u32[]{:S(2)}) collective-permute-start(bf16[32,640]{1,0:T(8,128)(2,1)S(1)} %slice.7.refs_0_), channel_id=1, source_target_pairs={{0,12},{1,13},{2,14},{3,15},{4,0},{5,1},{6,2},{7,3},{8,4},{9,5},{1... | collective-permute-start | bytes 122888 | tf_op jit(solution)/shard_map/ppermute | solution.py:380
  24.8 13.8 %collective-permute-start.5 = (bf16[4,32,256]{2,1,0:T(8,128)(2,1)S(1)}, bf16[4,32,256]{2,1,0:T(8,128)(2,1)S(1)}, u32[]{:S(2)}, u32[]{:S(2)}) collective-permute-start(bf16[4,32,256]{2,1,0:T(8,128)(2,1)S(1)} %get-tuple-element.63), channel_id=1, source_target_pairs={{0,1},{1,0},{2,3},{3,2},{4,5},{5,4},{6,7},{7,6},{8,9},{9,8},{10,11... | collective-permute-start | bytes 196616 | tf_op jit(solution)/shard_map/ppermute | solution.py:385
  32.6 6.9 %collective-permute-start.3 = (bf16[4,32,256]{2,1,0:T(8,128)(2,1)S(1)}, bf16[4,32,256]{2,1,0:T(8,128)(2,1)S(1)}, u32[]{:S(2)}, u32[]{:S(2)}) collective-permute-start(bf16[4,32,256]{2,1,0:T(8,128)(2,1)S(1)} %get-tuple-element.61), channel_id=1, source_target_pairs={{0,2},{1,3},{2,0},{3,1},{4,6},{5,7},{6,4},{7,5},{8,10},{9,11},{10,... | collective-permute-start | bytes 196616 | tf_op jit(solution)/shard_map/ppermute | solution.py:385
  34.0 5.4 %collective-permute-start.4 = (bf16[4,32,256]{2,1,0:T(8,128)(2,1)S(1)}, bf16[4,32,256]{2,1,0:T(8,128)(2,1)S(1)}, u32[]{:S(2)}, u32[]{:S(2)}) collective-permute-start(bf16[4,32,256]{2,1,0:T(8,128)(2,1)S(1)} %get-tuple-element.62), channel_id=1, source_target_pairs={{0,3},{1,2},{2,1},{3,0},{4,7},{5,6},{6,5},{7,4},{8,11},{9,10},{10,... | collective-permute-start | bytes 196616 | tf_op jit(solution)/shard_map/ppermute | solution.py:385
  34.4 3.4 %copy-start.1 = (bf16[1024,4096]{1,0:T(8,128)(2,1)S(1)}, bf16[1024,4096]{1,0:T(8,128)(2,1)}, u32[]{:S(2)}) copy-start(bf16[1024,4096]{1,0:T(8,128)(2,1)} %copy-done) | copy-start | bytes 25165828
  43.5 16.2 %copy-start.7 = (s32[16,64]{1,0:T(8,128)S(1)}, s32[16,64]{1,0:T(8,128)}, u32[]{:S(2)}) copy-start(s32[16,64]{1,0:T(8,128)} %cov.7) | copy-start | bytes 12292
  43.5 39.2 %copy-start.4 = (f32[640,64]{0,1:T(8,128)S(1)}, f32[640,64]{0,1:T(8,128)}, u32[]{:S(2)}) copy-start(f32[640,64]{0,1:T(8,128)} %param.6) | copy-start | bytes 491524
  45.5 14.3 %all-to-all-start.1 = ((bf16[16,32,256]{2,1,0:T(8,128)(2,1)}), bf16[16,32,256]{2,1,0:T(8,128)(2,1)S(1)}, u32[]{:S(2)}, u32[]{:S(2)}) async-start(bf16[16,32,256]{2,1,0:T(8,128)(2,1)} %get-tuple-element.77), calls=%async_computation.1 | async-start | bytes 524288 | tf_op jit(solution)/shard_map/all_to_all | solution.py:374
  61.7 31.3 %all-to-all-start.2 = ((bf16[16,32,256]{2,1,0:T(8,128)(2,1)}), bf16[16,32,256]{2,1,0:T(8,128)(2,1)S(1)}, u32[]{:S(2)}, u32[]{:S(2)}) async-start(bf16[16,32,256]{2,1,0:T(8,128)(2,1)} %get-tuple-element.79), calls=%async_computation.2 | async-start | bytes 524288 | tf_op jit(solution)/shard_map/all_to_all | solution.py:374
  65.3 6.7 %collective-permute-start.7 = (bf16[4,32,256]{2,1,0:T(8,128)(2,1)S(1)}, bf16[4,32,256]{2,1,0:T(8,128)(2,1)S(1)}, u32[]{:S(2)}, u32[]{:S(2)}) collective-permute-start(bf16[4,32,256]{2,1,0:T(8,128)(2,1)S(1)} %get-tuple-element.82), channel_id=1, source_target_pairs={{0,2},{1,3},{2,0},{3,1},{4,6},{5,7},{6,4},{7,5},{8,10},{9,11},{10,... | collective-permute-start | bytes 196616 | tf_op jit(solution)/shard_map/ppermute | solution.py:385
  67.1 5.6 %collective-permute-start.8 = (bf16[4,32,256]{2,1,0:T(8,128)(2,1)S(1)}, bf16[4,32,256]{2,1,0:T(8,128)(2,1)S(1)}, u32[]{:S(2)}, u32[]{:S(2)}) collective-permute-start(bf16[4,32,256]{2,1,0:T(8,128)(2,1)S(1)} %get-tuple-element.83), channel_id=1, source_target_pairs={{0,3},{1,2},{2,1},{3,0},{4,7},{5,6},{6,5},{7,4},{8,11},{9,10},{10,... | collective-permute-start | bytes 196616 | tf_op jit(solution)/shard_map/ppermute | solution.py:385
  67.1 5.6 %collective-permute-start.6 = (bf16[4,32,256]{2,1,0:T(8,128)(2,1)S(1)}, bf16[4,32,256]{2,1,0:T(8,128)(2,1)S(1)}, u32[]{:S(2)}, u32[]{:S(2)}) collective-permute-start(bf16[4,32,256]{2,1,0:T(8,128)(2,1)S(1)} %get-tuple-element.81), channel_id=1, source_target_pairs={{0,1},{1,0},{2,3},{3,2},{4,5},{5,4},{6,7},{7,6},{8,9},{9,8},{10,11... | collective-permute-start | bytes 196616 | tf_op jit(solution)/shard_map/ppermute | solution.py:385
  73.8 6.3 %collective-permute-start.9 = (bf16[32,640]{1,0:T(8,128)(2,1)S(1)}, bf16[32,640]{1,0:T(8,128)(2,1)S(1)}, u32[]{:S(2)}, u32[]{:S(2)}) collective-permute-start(bf16[32,640]{1,0:T(8,128)(2,1)S(1)} %get-tuple-element.85), channel_id=1, source_target_pairs={{0,4},{1,5},{2,6},{3,7},{4,8},{5,9},{6,10},{7,11},{8,12},{9,13},{1... | collective-permute-start | bytes 122888 | tf_op jit(solution)/shard_map/ppermute | solution.py:380
  75.6 6.2 %collective-permute-start.10 = (bf16[32,640]{1,0:T(8,128)(2,1)S(1)}, bf16[32,640]{1,0:T(8,128)(2,1)S(1)}, u32[]{:S(2)}, u32[]{:S(2)}) collective-permute-start(bf16[32,640]{1,0:T(8,128)(2,1)S(1)} %get-tuple-element.86), channel_id=1, source_target_pairs={{0,8},{1,9},{2,10},{3,11},{4,12},{5,13},{6,14},{7,15},{8,0},{9,1},... | collective-permute-start | bytes 122888 | tf_op jit(solution)/shard_map/ppermute | solution.py:380
  78.7 4.0 %collective-permute-start.11 = (bf16[32,640]{1,0:T(8,128)(2,1)S(1)}, bf16[32,640]{1,0:T(8,128)(2,1)S(1)}, u32[]{:S(2)}, u32[]{:S(2)}) collective-permute-start(bf16[32,640]{1,0:T(8,128)(2,1)S(1)} %get-tuple-element.87), channel_id=1, source_target_pairs={{0,12},{1,13},{2,14},{3,15},{4,0},{5,1},{6,2},{7,3},{8,4},{9,5},{1... | collective-permute-start | bytes 122888 | tf_op jit(solution)/shard_map/ppermute | solution.py:380
  82.7 6.0 %collective-permute-start.14 = (bf16[32,640]{1,0:T(8,128)(2,1)S(1)}, bf16[32,640]{1,0:T(8,128)(2,1)S(1)}, u32[]{:S(2)}, u32[]{:S(2)}) collective-permute-start(bf16[32,640]{1,0:T(8,128)(2,1)S(1)} %get-tuple-element.114.refs_0_), channel_id=1, source_target_pairs={{0,4},{1,5},{2,6},{3,7},{4,8},{5,9},{6,10},{7,11},{8,12},{9,13},{1... | collective-permute-start | bytes 122888 | tf_op jit(solution)/shard_map/ppermute | solution.py:380
  83.3 5.9 %collective-permute-start.13 = (bf16[32,640]{1,0:T(8,128)(2,1)S(1)}, bf16[32,640]{1,0:T(8,128)(2,1)S(1)}, u32[]{:S(2)}, u32[]{:S(2)}) collective-permute-start(bf16[32,640]{1,0:T(8,128)(2,1)S(1)} %get-tuple-element.114.refs_0_), channel_id=1, source_target_pairs={{0,8},{1,9},{2,10},{3,11},{4,12},{5,13},{6,14},{7,15},{8,0},{9,1},... | collective-permute-start | bytes 122888 | tf_op jit(solution)/shard_map/ppermute | solution.py:380
  86.2 4.0 %collective-permute-start.12 = (bf16[32,640]{1,0:T(8,128)(2,1)S(1)}, bf16[32,640]{1,0:T(8,128)(2,1)S(1)}, u32[]{:S(2)}, u32[]{:S(2)}) collective-permute-start(bf16[32,640]{1,0:T(8,128)(2,1)S(1)} %get-tuple-element.114.refs_0_), channel_id=1, source_target_pairs={{0,12},{1,13},{2,14},{3,15},{4,0},{5,1},{6,2},{7,3},{8,4},{9,5},{1... | collective-permute-start | bytes 122888 | tf_op jit(solution)/shard_map/ppermute | solution.py:380
  91.1 6.1 %collective-permute-start.17 = (bf16[4,32,256]{2,1,0:T(8,128)(2,1)S(1)}, bf16[4,32,256]{2,1,0:T(8,128)(2,1)S(1)}, u32[]{:S(2)}, u32[]{:S(2)}) collective-permute-start(bf16[4,32,256]{2,1,0:T(8,128)(2,1)S(1)} %get-tuple-element.90), channel_id=1, source_target_pairs={{0,1},{1,0},{2,3},{3,2},{4,5},{5,4},{6,7},{7,6},{8,9},{9,8},{10,11... | collective-permute-start | bytes 196616 | tf_op jit(solution)/shard_map/ppermute | solution.py:385
  91.2 6.9 %collective-permute-start.15 = (bf16[4,32,256]{2,1,0:T(8,128)(2,1)S(1)}, bf16[4,32,256]{2,1,0:T(8,128)(2,1)S(1)}, u32[]{:S(2)}, u32[]{:S(2)}) collective-permute-start(bf16[4,32,256]{2,1,0:T(8,128)(2,1)S(1)} %get-tuple-element.88), channel_id=1, source_target_pairs={{0,2},{1,3},{2,0},{3,1},{4,6},{5,7},{6,4},{7,5},{8,10},{9,11},{10,... | collective-permute-start | bytes 196616 | tf_op jit(solution)/shard_map/ppermute | solution.py:385
  91.5 6.6 %collective-permute-start.16 = (bf16[4,32,256]{2,1,0:T(8,128)(2,1)S(1)}, bf16[4,32,256]{2,1,0:T(8,128)(2,1)S(1)}, u32[]{:S(2)}, u32[]{:S(2)}) collective-permute-start(bf16[4,32,256]{2,1,0:T(8,128)(2,1)S(1)} %get-tuple-element.89), channel_id=1, source_target_pairs={{0,3},{1,2},{2,1},{3,0},{4,7},{5,6},{6,5},{7,4},{8,11},{9,10},{10,... | collective-permute-start | bytes 196616 | tf_op jit(solution)/shard_map/ppermute | solution.py:385
  93.0 3.4 %copy-start.2 = (bf16[1024,4096]{1,0:T(8,128)(2,1)S(1)}, bf16[1024,4096]{1,0:T(8,128)(2,1)}, u32[]{:S(2)}) copy-start(bf16[1024,4096]{1,0:T(8,128)(2,1)} %copy-done) | copy-start | bytes 25165828
  104.1 21.2 %all-to-all-start.3 = ((bf16[16,32,256]{2,1,0:T(8,128)(2,1)}), bf16[16,32,256]{2,1,0:T(8,128)(2,1)S(1)}, u32[]{:S(2)}, u32[]{:S(2)}) async-start(bf16[16,32,256]{2,1,0:T(8,128)(2,1)} %get-tuple-element.112), calls=%async_computation.3 | async-start | bytes 524288 | tf_op jit(solution)/shard_map/all_to_all | solution.py:374
  107.8 6.9 %collective-permute-start.19 = (bf16[4,32,256]{2,1,0:T(8,128)(2,1)S(1)}, bf16[4,32,256]{2,1,0:T(8,128)(2,1)S(1)}, u32[]{:S(2)}, u32[]{:S(2)}) collective-permute-start(bf16[4,32,256]{2,1,0:T(8,128)(2,1)S(1)} %get-tuple-element.106), channel_id=1, source_target_pairs={{0,2},{1,3},{2,0},{3,1},{4,6},{5,7},{6,4},{7,5},{8,10},{9,11},{10,... | collective-permute-start | bytes 196616 | tf_op jit(solution)/shard_map/ppermute | solution.py:385
  109.7 5.6 %collective-permute-start.20 = (bf16[4,32,256]{2,1,0:T(8,128)(2,1)S(1)}, bf16[4,32,256]{2,1,0:T(8,128)(2,1)S(1)}, u32[]{:S(2)}, u32[]{:S(2)}) collective-permute-start(bf16[4,32,256]{2,1,0:T(8,128)(2,1)S(1)} %get-tuple-element.107), channel_id=1, source_target_pairs={{0,3},{1,2},{2,1},{3,0},{4,7},{5,6},{6,5},{7,4},{8,11},{9,10},{10,... | collective-permute-start | bytes 196616 | tf_op jit(solution)/shard_map/ppermute | solution.py:385
  109.7 5.6 %collective-permute-start.18 = (bf16[4,32,256]{2,1,0:T(8,128)(2,1)S(1)}, bf16[4,32,256]{2,1,0:T(8,128)(2,1)S(1)}, u32[]{:S(2)}, u32[]{:S(2)}) collective-permute-start(bf16[4,32,256]{2,1,0:T(8,128)(2,1)S(1)} %get-tuple-element.105), channel_id=1, source_target_pairs={{0,1},{1,0},{2,3},{3,2},{4,5},{5,4},{6,7},{7,6},{8,9},{9,8},{10,11... | collective-permute-start | bytes 196616 | tf_op jit(solution)/shard_map/ppermute | solution.py:385
  116.5 6.2 %collective-permute-start.21 = (bf16[32,640]{1,0:T(8,128)(2,1)S(1)}, bf16[32,640]{1,0:T(8,128)(2,1)S(1)}, u32[]{:S(2)}, u32[]{:S(2)}) collective-permute-start(bf16[32,640]{1,0:T(8,128)(2,1)S(1)} %get-tuple-element.109), channel_id=1, source_target_pairs={{0,4},{1,5},{2,6},{3,7},{4,8},{5,9},{6,10},{7,11},{8,12},{9,13},{1... | collective-permute-start | bytes 122888 | tf_op jit(solution)/shard_map/ppermute | solution.py:380
  118.2 6.4 %collective-permute-start.22 = (bf16[32,640]{1,0:T(8,128)(2,1)S(1)}, bf16[32,640]{1,0:T(8,128)(2,1)S(1)}, u32[]{:S(2)}, u32[]{:S(2)}) collective-permute-start(bf16[32,640]{1,0:T(8,128)(2,1)S(1)} %get-tuple-element.110), channel_id=1, source_target_pairs={{0,8},{1,9},{2,10},{3,11},{4,12},{5,13},{6,14},{7,15},{8,0},{9,1},... | collective-permute-start | bytes 122888 | tf_op jit(solution)/shard_map/ppermute | solution.py:380
  121.2 4.0 %collective-permute-start.23 = (bf16[32,640]{1,0:T(8,128)(2,1)S(1)}, bf16[32,640]{1,0:T(8,128)(2,1)S(1)}, u32[]{:S(2)}, u32[]{:S(2)}) collective-permute-start(bf16[32,640]{1,0:T(8,128)(2,1)S(1)} %get-tuple-element.111), channel_id=1, source_target_pairs={{0,12},{1,13},{2,14},{3,15},{4,0},{5,1},{6,2},{7,3},{8,4},{9,5},{1... | collective-permute-start | bytes 122888 | tf_op jit(solution)/shard_map/ppermute | solution.py:380
  (8 other events, 17.4 us)

commit v3 on v1

v3 whole, which is shorter than its diff:
```python
import functools
import math

import jax
import jax.numpy as jnp
from jax import lax
from jax.experimental import pallas as pl
from jax.experimental.pallas import tpu as pltpu
from jax.sharding import PartitionSpec as P

ROUNDS = 2

weight_decay = 0.02

PLANE = 4
NT = (((1,), (1,)), ((), ()))
NN = (((1,), (0,)), ((), ()))
VMEM_LIMIT = 24 * 1024 * 1024


def dot(a, b, dims):
    return lax.dot_general(a, b, dims, preferred_element_type=jnp.float32)


def split3(x):
    hi = x.astype(jnp.bfloat16)
    rest = x - hi.astype(jnp.float32)
    mid = rest.astype(jnp.bfloat16)
    lo = (rest - mid.astype(jnp.float32)).astype(jnp.bfloat16)
    return hi, mid, lo


def low_half(rows):
    return lax.broadcasted_iota(jnp.int32, (rows, 128), 1) < 64


def double(x, low):
    turned = pltpu.roll(x, 64, 1)
    return jnp.where(low, x, turned), jnp.where(low, turned, x)


def load_kernel(geno, samples, geno_out, samples_out, sems):
    copies = [
        pltpu.make_async_copy(samples, samples_out, sems.at[0]),
        pltpu.make_async_copy(geno, geno_out, sems.at[1]),
    ]
    for copy in copies:
        copy.start()
    for copy in copies:
        copy.wait()


def table_kernel(planes, per_owner, own_blocks, pos_ref, cov, table):
    place = lax.bitwise_and(pos_ref[0], PLANE - 1)
    for mate in range(PLANE):
        batch = lax.bitwise_xor(pos_ref[0], mate)
        for plane in range(planes):
            owner = plane * PLANE + place
            for p in range(per_owner):
                table[mate * planes + plane, p] = cov[batch, owner * per_owner + p] - owner * own_blocks


def pick_kernel(planes, per_owner, own_blocks, pos_ref, table, held, packets, blocks):
    place = lax.bitwise_and(pos_ref[0], PLANE - 1)
    low = low_half(held.shape[1])
    for plane in range(planes):
        for j in range(own_blocks // 2):
            x = held[plane, :, 128 * j:128 * (j + 1)].astype(jnp.float32)
            blocks[plane, 2 * j], blocks[plane, 2 * j + 1] = double(x, low)
    for plane in range(planes):
        for mate in range(PLANE):
            for q in range(per_owner // 2):
                first = table[mate * planes + plane, 2 * q]
                second = table[mate * planes + plane, 2 * q + 1]
                pair = jnp.where(low, blocks[plane, first], blocks[plane, second])
                to = lax.bitwise_xor(place, mate)
                packets[to, plane, :, 128 * q:128 * (q + 1)] = pair.astype(jnp.bfloat16)


def plane_sum_kernel(planes, per_owner, own_blocks, table, *refs):
    terms, sums, total = refs[:PLANE], refs[PLANE], refs[-1]
    low = low_half(terms[0].shape[1])
    total[...] = jnp.zeros_like(total)
    for plane in range(planes):
        for mate in range(PLANE):
            for q in range(per_owner // 2):
                first = table[mate * planes + plane, 2 * q]
                second = table[mate * planes + plane, 2 * q + 1]
                pair = terms[mate][plane, :, 128 * q:128 * (q + 1)].astype(jnp.float32)
                total[plane, first] += jnp.where(low, pair, 0.0)
                total[plane, second] += jnp.where(low, 0.0, pair)
    for plane in range(planes):
        for j in range(own_blocks // 2):
            first, second = total[plane, 2 * j], total[plane, 2 * j + 1]
            both = jnp.where(low, first, second) + pltpu.roll(jnp.where(low, second, first), 64, 1)
            sums[plane, :, 128 * j:128 * (j + 1)] = both.astype(jnp.bfloat16)


def columns_of(plane, place, width):
    return pl.ds(pl.multiple_of((plane * PLANE + place) * width, width), width)


def product_kernel(mates, first, rows, pos_ref, geno, packets, *refs):
    before, (geno_out, gradient, gram) = refs[:-3], refs[-3:]
    place = lax.bitwise_and(pos_ref[0], PLANE - 1)
    planes, width = packets.shape[1], packets.shape[3]
    places = [(plane, lax.bitwise_xor(place, mate)) for mate in mates for plane in range(planes)]
    total = None if first else before[1][...]
    for plane, at in places:
        term = dot(packets[at, plane], packets[at, plane], NT)
        total = term if total is None else total + term
    gram[...] = total
    for i in range(geno.shape[0] // rows):
        here = slice(i * rows, (i + 1) * rows)
        total = None if first else before[0][:, here]
        for plane, at in places:
            term = dot(packets[at, plane], geno[here, columns_of(plane, at, width)], NT)
            total = term if total is None else total + term
        gradient[:, here] = total


def sample_kernel(sample_step, samples, gradient, gram, new_samples, new_bf16, new_gram):
    old = samples[...]
    old_bf16 = old.astype(jnp.bfloat16)
    total = gradient[...]
    for part in split3(gram[...]):
        total -= dot(part, old_bf16, NN)
    new = (1.0 - weight_decay) * old + sample_step * total
    new_samples[...] = new
    rounded = new.astype(jnp.bfloat16)
    new_bf16[...] = rounded
    new_gram[...] = dot(rounded, rounded, NT)


def term_kernel(mate, pos_ref, geno, samples, gram, packets, geno_out, terms):
    place = lax.bitwise_and(pos_ref[0], PLANE - 1)
    at = lax.bitwise_xor(place, mate)
    planes, width = packets.shape[1], packets.shape[3]
    parts = split3(gram[...])
    for plane in range(planes):
        term = dot(samples[...], geno[:, columns_of(plane, at, width)], NN)
        for part in parts:
            term -= dot(part, packets[at, plane], NN)
        terms[plane] = term.astype(jnp.bfloat16)


def on_device(genotypes, sample_factors, snp_factors, coverage):
    devices = lax.axis_size("rows")
    planes = devices // PLANE
    position = lax.axis_index("rows").astype(jnp.int32)
    samples_here, snps_here = genotypes.shape
    rank = sample_factors.shape[1]
    covered = coverage.shape[1]
    tile_size = snps_here // covered
    per_owner = covered // devices
    own_snps = snp_factors.shape[0]
    own_blocks = own_snps // tile_size
    width = per_owner * tile_size
    assert tile_size == 64 and per_owner % 2 == 0 and own_blocks % 2 == 0
    assert devices % PLANE == 0

    local_list = (
        lax.dynamic_slice_in_dim(coverage, position * per_owner, per_owner, 1)
        - position * own_blocks
    )
    one_hot = local_list[:, :, None] == jnp.arange(own_blocks, dtype=jnp.int32)[None, None, :]
    observers = jnp.sum(one_hot.astype(jnp.float32), axis=(0, 1))
    snp_step = 0.5 * math.sqrt(rank) / (samples_here * observers)
    snp_step = jnp.broadcast_to(snp_step[:, None], (own_blocks, tile_size)).reshape(1, own_snps)
    sample_step = 0.5 * math.sqrt(rank) / (covered * tile_size)

    smem = pl.BlockSpec(memory_space=pltpu.SMEM)
    vmem = pl.BlockSpec(memory_space=pltpu.VMEM)
    hbm = pl.BlockSpec(memory_space=pltpu.HBM)
    params = pltpu.CompilerParams(vmem_limit_bytes=VMEM_LIMIT)
    pos = position.reshape(1)
    packet = jax.ShapeDtypeStruct((planes, rank, width), jnp.bfloat16)
    packets_shape = jax.ShapeDtypeStruct((PLANE, planes, rank, width), jnp.bfloat16)
    dense_blocks = pltpu.VMEM((planes, own_blocks, rank, 128), jnp.float32)
    by_samples = jax.ShapeDtypeStruct((rank, samples_here), jnp.float32)
    square = jax.ShapeDtypeStruct((rank, rank), jnp.float32)
    sizes = (planes, per_owner, own_blocks)

    def cost(flops, bytes_accessed):
        return pl.CostEstimate(flops=flops, bytes_accessed=bytes_accessed, transcendentals=0)

    table = pl.pallas_call(
        functools.partial(table_kernel, *sizes),
        out_shape=jax.ShapeDtypeStruct((PLANE * planes, per_owner), jnp.int32),
        in_specs=[smem, smem],
        out_specs=smem,
        compiler_params=params,
        name="block_table",
    )(pos, coverage)
    geno, samples = pl.pallas_call(
        load_kernel,
        out_shape=(
            pltpu.VMEM((samples_here, snps_here), jnp.bfloat16),
            pltpu.VMEM((rank, samples_here), jnp.float32),
        ),
        in_specs=[hbm, hbm],
        out_specs=(vmem, vmem),
        scratch_shapes=[pltpu.SemaphoreType.DMA((2,))],
        compiler_params=pltpu.CompilerParams(
            vmem_limit_bytes=58 * 1024 * 1024 - 2 * samples_here * snps_here
        ),
        cost_estimate=cost(0, 2 * samples_here * snps_here),
        name="load_batch",
    )(genotypes, sample_factors.T)

    resident = pltpu.VMEM((samples_here, snps_here), jnp.bfloat16)

    def pick(held):
        return pl.pallas_call(
            functools.partial(pick_kernel, *sizes),
            out_shape=packets_shape,
            in_specs=[smem, smem, vmem],
            out_specs=vmem,
            scratch_shapes=[dense_blocks],
            compiler_params=params,
            name="pick_blocks",
        )(pos, table, held)

    def plane_sum(terms):
        return pl.pallas_call(
            functools.partial(plane_sum_kernel, *sizes),
            out_shape=jax.ShapeDtypeStruct((planes, rank, own_snps), jnp.bfloat16),
            in_specs=[smem] + [vmem] * PLANE,
            out_specs=vmem,
            scratch_shapes=[dense_blocks],
            compiler_params=params,
            name="plane_sum",
        )(table, *terms)

    def product(mates, geno, packets, before):
        share = len(mates) * samples_here * snps_here // PLANE
        return pl.pallas_call(
            functools.partial(product_kernel, mates, not before, 256),
            out_shape=(resident, by_samples, square),
            in_specs=[smem] + [vmem] * (2 + len(before)),
            out_specs=(vmem,) * 3,
            input_output_aliases={1: 0},
            compiler_params=params,
            cost_estimate=cost(8 * rank * share, 2 * share),
            name="panel_product",
        )(pos, geno, packets, *before)

    def sample_update(samples, gradient, gram):
        return pl.pallas_call(
            functools.partial(sample_kernel, sample_step),
            out_shape=(by_samples, jax.ShapeDtypeStruct((rank, samples_here), jnp.bfloat16), square),
            in_specs=[vmem] * 3,
            out_specs=(vmem,) * 3,
            compiler_params=params,
            name="sample_update",
        )(samples, gradient, gram)

    def terms_for(mate, geno, samples_bf16, gram, packets):
        share = samples_here * snps_here // PLANE
        return pl.pallas_call(
            functools.partial(term_kernel, mate),
            out_shape=(resident, packet),
            in_specs=[smem] + [vmem] * 4,
            out_specs=(vmem, vmem),
            input_output_aliases={1: 0},
            compiler_params=params,
            cost_estimate=cost(8 * rank * share, 2 * share),
            name="mate_terms",
        )(pos, geno, samples_bf16, gram, packets)

    def across_planes(x):
        groups = [[plane * PLANE + place for plane in range(planes)] for place in range(PLANE)]
        return lax.all_to_all(x, "rows", 0, 0, axis_index_groups=groups, tiled=True)

    def across_mates(x):
        groups = [[plane * PLANE + place for place in range(PLANE)] for plane in range(planes)]
        return lax.all_to_all(x, "rows", 0, 0, axis_index_groups=groups, tiled=True)

    def to_mate(x, mate):
        if mate == 0:
            return x
        return lax.ppermute(x, "rows", [(r, r ^ mate) for r in range(devices)])

    snps = snp_factors.T
    for iteration in range(ROUNDS):
        own = jnp.broadcast_to(snps.astype(jnp.bfloat16), (planes, rank, own_snps))
        packets = pick(across_planes(own))
        panels = across_mates(packets)
        geno, *partial = product([0], geno, packets, ())
        geno, *partial = product([1, 2, 3], geno, panels, partial)
        samples, samples_bf16, sample_gram = sample_update(samples, *partial)
        terms = [None] * PLANE
        for mate in (2, 3, 1, 0):
            geno, own_terms = terms_for(mate, geno, samples_bf16, sample_gram, panels)
            terms[mate] = to_mate(own_terms, mate)
        sums = across_planes(plane_sum(terms))
        total = jnp.sum(sums.astype(jnp.float32), axis=0)
        snps = (1.0 - weight_decay) * snps + snp_step * total
    return (samples.T, snps.T)


def solution(mesh):
    placed = (
        P(("groups", "rows"), None),
        P(("groups", "rows"), None),
        P(("groups", "rows"), None),
        P("groups", None),
    )
    return jax.shard_map(
        on_device,
        mesh=mesh,
        in_specs=placed,
        out_specs=(P(("groups", "rows"), None), P(("groups", "rows"), None)),
        check_vma=False,
    )
```

time: 87.7 us -> 150 us (1.71)
  local copies, waits for them, and re-layouts: 5.1 us -> 48.4 us
  blocking collectives: 0 us -> 26.2 us
  starting transfers between devices: 29.4 us -> 20.8 us
  Pallas kernels: 21.8 us -> 25.9 us
  waiting for transfers between devices: 28.4 us -> 24.9 us
    unnamed x13 -> x35, local copies, waits for them, and re-layouts: 4.18 us -> 47.4 us
    all_to_all x0 -> x2, blocking collectives: none -> 26.2 us  [across_planes(): return lax.all_to_all(x, 'rows', 0, 0, axis_index_groups=groups, tiled=True)]
    ppermute x12 -> x0, starting transfers between devices: 21.1 us -> none  [along(): return lax.ppermute(x, 'rows', pairs)]
    all_to_all x0 -> x4, waiting for transfers between devices: none -> 19.2 us  [the longest x2 18.9 us: across_planes(): return lax.all_to_all(x, 'rows', 0, 0, axis_index_groups=groups, tiled=True)]
    ppermute x12 -> x0, waiting for transfers between devices: 16.7 us -> none  [along(): return lax.ppermute(x, 'rows', pairs)]
    all_to_all x0 -> x4, starting transfers between devices: none -> 16.7 us  [the longest x2 9.77 us: across_planes(): return lax.all_to_all(x, 'rows', 0, 0, axis_index_groups=groups, tiled=True)]
    ppermute x12 -> x6, waiting for transfers between devices: 11.7 us -> 5.67 us  [to_mate(): return lax.ppermute(x, 'rows', [(r, r ^ mate) for r in range(devices)])]
    ppermute x12 -> x6, starting transfers between devices: 8.25 us -> 4.1 us  [to_mate(): return lax.ppermute(x, 'rows', [(r, r ^ mate) for r in range(devices)])]
  transfers between devices with their start and end apart: 24 -> 10, of which waited for: 14 -> 5; matrix products, arithmetic and copies ran while one was open for 1% -> 0% of each run, Pallas kernels for 14% -> 7%
where the time goes in v3:
time: 150 us; the launch traced here: 149 us
  local copies, waits for them, and re-layouts  48.4 us (32%)
  blocking collectives  26.2 us (17%)
  Pallas kernels  25.9 us (17%)
  waiting for transfers between devices  24.9 us (17%)
  starting transfers between devices  20.8 us (14%)
  other arithmetic  1.93 us (1%)
    unnamed x35, local copies, waits for them, and re-layouts  47.4 us
    all_to_all x2, blocking collectives, across_planes(): return lax.all_to_all(x, 'rows', 0, 0, axis_index_groups=groups, tiled=True)  26.2 us
    all_to_all x2, waiting for transfers between devices, across_planes(): return lax.all_to_all(x, 'rows', 0, 0, axis_index_groups=groups, tiled=True)  18.9 us
    all_to_all x2, starting transfers between devices, across_planes(): return lax.all_to_all(x, 'rows', 0, 0, axis_index_groups=groups, tiled=True)  9.77 us
    pallas_call x4, Pallas kernels, product(): pl.pallas_call(functools.partial(product_kernel, mates, not before, 256),...  7.91 us
    all_to_all x2, starting transfers between devices, across_mates(): return lax.all_to_all(x, 'rows', 0, 0, axis_index_groups=groups, tiled=True)  6.94 us
    ppermute x6, waiting for transfers between devices, to_mate(): return lax.ppermute(x, 'rows', [(r, r ^ mate) for r in range(devices)])  5.67 us
    pallas_call x8, Pallas kernels, terms_for(): pl.pallas_call(functools.partial(term_kernel, mate), out_shape=(resident,...  4.78 us
  transfers between devices with their start and end apart: 10, of which 5 were waited for; matrix products, arithmetic and copies ran while one was open for 0% of the time, Pallas kernels for 7%

profile of v3, /device:TPU:0, one launch (start us, length us, event | category | flops | bytes accessed | tf_op | source)
XLA Modules:
  0.0 149.1 jit_solution(13103335215858117971)
XLA Ops:
  2.3 6.3 %all-to-all-start = ((bf16[4,64,640]{2,1,0:T(8,128)(2,1)}), bf16[4,64,640]{2,1,0:T(8,128)(2,1)S(1)}, u32[]{:S(2)}, u32[]{:S(2)}) async-start(bf16[4,64,640]{2,1,0:T(8,128)(2,1)} %broadcast_in_dim.6), calls=%async_computation | async-start | bytes 655360 | tf_op jit(solution)/shard_map/all_to_all | solution.py:273
  10.9 8.1 %all-to-all-done.held = bf16[4,64,640]{2,1,0:T(8,128)(2,1)S(1)} async-done(((bf16[4,64,640]{2,1,0:T(8,128)(2,1)}), bf16[4,64,640]{2,1,0:T(8,128)(2,1)S(1)}, u32[]{:S(2)}, u32[]{:S(2)}) %all-to-all-start) | async-done | bytes 327712 | tf_op jit(solution)/shard_map/all_to_all | solution.py:273
  18.9 1.8 %pick_blocks.2.packets = bf16[4,4,64,256]{3,2,1,0:T(8,128)(2,1)} custom-call(s32[1]{0:T(128)} %bitcast.1.pos_ref, s32[16,4]{1,0:T(8,128)S(1)} %block_table.1.table, bf16[4,64,640]{2,1,0:T(8,128)(2,1)S(1)} %all-to-all-done.held), custom_call_target="tpu_custom_call" | custom-call | tf_op jit(solution)/shard_map/pick_blocks/pallas_call | solution.py:214
  20.7 3.5 %all-to-all-start.1 = ((bf16[4,4,64,256]{3,2,1,0:T(8,128)(2,1)}), bf16[4,4,64,256]{3,2,1,0:T(8,128)(2,1)S(1)}, u32[]{:S(2)}, u32[]{:S(2)}) async-start(bf16[4,4,64,256]{3,2,1,0:T(8,128)(2,1)} %pick_blocks.2.packets), calls=%async_computation.1 | async-start | bytes 1048576 | tf_op jit(solution)/shard_map/all_to_all | solution.py:277
  24.2 3.5 %load_batch.1 = (bf16[1024,4096]{1,0:T(8,128)(2,1)S(1)}, f32[64,1024]{1,0:T(8,128)S(1)}) custom-call(bf16[1024,4096]{1,0:T(8,128)(2,1)} %geno.1, f32[64,1024]{1,0:T(8,128)} %bitcast.17), custom_call_target="tpu_custom_call" | custom-call | bytes 8388608 | tf_op jit(solution)/shard_map/load_batch/pallas_call | solution.py:195
  27.7 3.3 %copy-done = bf16[1024,4096]{1,0:T(8,128)(2,1)} copy-done((bf16[1024,4096]{1,0:T(8,128)(2,1)}, bf16[1024,4096]{1,0:T(8,128)(2,1)S(1)}, u32[]{:S(2)}) %copy-start) | copy-done | bytes 8388632
  31.0 3.4 %copy-done.1 = bf16[1024,4096]{1,0:T(8,128)(2,1)S(1)} copy-done((bf16[1024,4096]{1,0:T(8,128)(2,1)S(1)}, bf16[1024,4096]{1,0:T(8,128)(2,1)}, u32[]{:S(2)}) %copy-start.1) | copy-done | bytes 8388632
  34.4 1.8 %panel_product.4 = (bf16[1024,4096]{1,0:T(8,128)(2,1)S(1)}, f32[64,1024]{1,0:T(8,128)S(1)}, f32[64,64]{1,0:T(8,128)S(1)}) custom-call(s32[1]{0:T(128)} %bitcast.1.pos_ref, bf16[1024,4096]{1,0:T(8,128)(2,1)S(1)} %copy-done.1, bf16[4,4,64,256]{3,2,1,0:T(8,128)(2,1)} %pick_blocks.2.packets), custom_call_target="tpu_custom_call", output_to_operand_aliasing={{0}: (1, {})} | custom-call | flops 536870912 | bytes 2097152 | tf_op jit(solution)/shard_map/panel_product/pallas_call | solution.py:237
  36.2 3.3 %copy-done.2 = bf16[1024,4096]{1,0:T(8,128)(2,1)} copy-done((bf16[1024,4096]{1,0:T(8,128)(2,1)}, bf16[1024,4096]{1,0:T(8,128)(2,1)S(1)}, u32[]{:S(2)}) %copy-start.2) | copy-done | bytes 8388632
  39.5 3.4 %copy-done.3 = bf16[1024,4096]{1,0:T(8,128)(2,1)S(1)} copy-done((bf16[1024,4096]{1,0:T(8,128)(2,1)S(1)}, bf16[1024,4096]{1,0:T(8,128)(2,1)}, u32[]{:S(2)}) %copy-start.3) | copy-done | bytes 8388632
  42.9 2.1 %panel_product.5 = (bf16[1024,4096]{1,0:T(8,128)(2,1)S(1)}, f32[64,1024]{1,0:T(8,128)S(1)}, f32[64,64]{1,0:T(8,128)S(1)}) custom-call(s32[1]{0:T(128)} %bitcast.1.pos_ref, bf16[1024,4096]{1,0:T(8,128)(2,1)S(1)} %copy-done.3, bf16[4,4,64,256]{3,2,1,0:T(8,128)(2,1)S(1)} %all-to-all-done.1.packets, ...), custom_call_target="tpu_custom_call", output_to_operand_aliasing={{0}: (1, {})} | custom-call | flops 1610612736 | bytes 6291456 | tf_op jit(solution)/shard_map/panel_product/pallas_call | solution.py:237
  45.0 3.3 %copy-done.4 = bf16[1024,4096]{1,0:T(8,128)(2,1)} copy-done((bf16[1024,4096]{1,0:T(8,128)(2,1)}, bf16[1024,4096]{1,0:T(8,128)(2,1)S(1)}, u32[]{:S(2)}) %copy-start.4) | copy-done | bytes 8388632
  48.7 3.4 %copy-done.5 = bf16[1024,4096]{1,0:T(8,128)(2,1)S(1)} copy-done((bf16[1024,4096]{1,0:T(8,128)(2,1)S(1)}, bf16[1024,4096]{1,0:T(8,128)(2,1)}, u32[]{:S(2)}) %copy-start.5) | copy-done | bytes 8388632
  53.9 3.3 %copy-done.6 = bf16[1024,4096]{1,0:T(8,128)(2,1)} copy-done((bf16[1024,4096]{1,0:T(8,128)(2,1)}, bf16[1024,4096]{1,0:T(8,128)(2,1)S(1)}, u32[]{:S(2)}) %copy-start.6) | copy-done | bytes 8388632
  57.7 1.7 %collective-permute-start.1 = (bf16[4,64,256]{2,1,0:T(8,128)(2,1)S(1)}, bf16[4,64,256]{2,1,0:T(8,128)(2,1)S(1)}, u32[]{:S(2)}, u32[]{:S(2)}) collective-permute-start(bf16[4,64,256]{2,1,0:T(8,128)(2,1)S(1)} %get-tuple-element.54), channel_id=1, source_target_pairs={{0,2},{1,3},{2,0},{3,1},{4,6},{5,7},{6,4},{7,5},{8,10},{9,11},{10,... | collective-permute-start | bytes 393224 | tf_op jit(solution)/shard_map/ppermute | solution.py:282
  59.5 3.4 %copy-done.7 = bf16[1024,4096]{1,0:T(8,128)(2,1)S(1)} copy-done((bf16[1024,4096]{1,0:T(8,128)(2,1)S(1)}, bf16[1024,4096]{1,0:T(8,128)(2,1)}, u32[]{:S(2)}) %copy-start.7) | copy-done | bytes 8388632
  63.5 3.3 %copy-done.8 = bf16[1024,4096]{1,0:T(8,128)(2,1)} copy-done((bf16[1024,4096]{1,0:T(8,128)(2,1)}, bf16[1024,4096]{1,0:T(8,128)(2,1)S(1)}, u32[]{:S(2)}) %copy-start.8) | copy-done | bytes 8388632
  66.8 2.0 %plane_sum.2 = bf16[4,64,640]{2,1,0:T(8,128)(2,1)} custom-call(s32[16,4]{1,0:T(8,128)S(1)} %block_table.1.table, bf16[4,64,256]{2,1,0:T(8,128)(2,1)S(1)} %get-tuple-element.52.refs_0_, bf16[4,64,256]{2,1,0:T(8,128)(2,1)S(1)} %collective-permute-done.refs_1_, bf16[4,64,256]{2,1,0:T(8,128)(2,1)S(1)} %collective-permute-done.1.refs_2_, ...), custom_call_target="tpu_custom_call" | custom-call | tf_op jit(solution)/shard_map/plane_sum/pallas_call | solution.py:225
  68.8 3.5 %all-to-all-start.2 = ((bf16[4,64,640]{2,1,0:T(8,128)(2,1)}), bf16[4,64,640]{2,1,0:T(8,128)(2,1)S(1)}, u32[]{:S(2)}, u32[]{:S(2)}) async-start(bf16[4,64,640]{2,1,0:T(8,128)(2,1)} %plane_sum.2), calls=%async_computation.2 | async-start | bytes 655360 | tf_op jit(solution)/shard_map/all_to_all | solution.py:273
  72.6 10.8 %all-to-all-done.2 = bf16[4,64,640]{2,1,0:T(8,128)(2,1)S(1)} async-done(((bf16[4,64,640]{2,1,0:T(8,128)(2,1)}), bf16[4,64,640]{2,1,0:T(8,128)(2,1)S(1)}, u32[]{:S(2)}, u32[]{:S(2)}) %all-to-all-start.2) | async-done | bytes 327712 | tf_op jit(solution)/shard_map/all_to_all | solution.py:273
  83.5 12.7 %all_to_all.30.held = bf16[4,64,640]{2,1,0:T(8,128)(2,1)S(1)} all-to-all(bf16[4,64,640]{2,1,0:T(8,128)(2,1)S(1)} %broadcast_in_dim.16), channel_id=1, replica_groups={{0,4,8,12},{1,5,9,13},{2,6,10,14},{3,7,11,15},{16,20,24,28},{17,21,25,2..., dimensions={0} | all-to-all | bytes 655360 | tf_op jit(solution)/shard_map/all_to_all | solution.py:273
  96.3 1.8 %pick_blocks.3.packets = bf16[4,4,64,256]{3,2,1,0:T(8,128)(2,1)} custom-call(s32[1]{0:T(128)} %bitcast.1.pos_ref, s32[16,4]{1,0:T(8,128)S(1)} %block_table.1.table, bf16[4,64,640]{2,1,0:T(8,128)(2,1)S(1)} %all_to_all.30.held), custom_call_target="tpu_custom_call" | custom-call | tf_op jit(solution)/shard_map/pick_blocks/pallas_call | solution.py:214
  98.1 3.5 %all-to-all-start.4 = ((bf16[4,4,64,256]{3,2,1,0:T(8,128)(2,1)}), bf16[4,4,64,256]{3,2,1,0:T(8,128)(2,1)S(1)}, u32[]{:S(2)}, u32[]{:S(2)}) async-start(bf16[4,4,64,256]{3,2,1,0:T(8,128)(2,1)} %pick_blocks.3.packets), calls=%async_computation.4 | async-start | bytes 1048576 | tf_op jit(solution)/shard_map/all_to_all | solution.py:277
  101.5 3.4 %copy-done.9 = bf16[1024,4096]{1,0:T(8,128)(2,1)S(1)} copy-done((bf16[1024,4096]{1,0:T(8,128)(2,1)S(1)}, bf16[1024,4096]{1,0:T(8,128)(2,1)}, u32[]{:S(2)}) %copy-start.9) | copy-done | bytes 8388632
  104.9 1.8 %panel_product.6 = (bf16[1024,4096]{1,0:T(8,128)(2,1)S(1)}, f32[64,1024]{1,0:T(8,128)S(1)}, f32[64,64]{1,0:T(8,128)S(1)}) custom-call(s32[1]{0:T(128)} %bitcast.1.pos_ref, bf16[1024,4096]{1,0:T(8,128)(2,1)S(1)} %copy-done.9, bf16[4,4,64,256]{3,2,1,0:T(8,128)(2,1)} %pick_blocks.3.packets), custom_call_target="tpu_custom_call", output_to_operand_aliasing={{0}: (1, {})} | custom-call | flops 536870912 | bytes 2097152 | tf_op jit(solution)/shard_map/panel_product/pallas_call | solution.py:237
  106.8 3.3 %copy-done.10 = bf16[1024,4096]{1,0:T(8,128)(2,1)} copy-done((bf16[1024,4096]{1,0:T(8,128)(2,1)}, bf16[1024,4096]{1,0:T(8,128)(2,1)S(1)}, u32[]{:S(2)}) %copy-start.10) | copy-done | bytes 8388632
  110.3 3.4 %copy-done.11 = bf16[1024,4096]{1,0:T(8,128)(2,1)S(1)} copy-done((bf16[1024,4096]{1,0:T(8,128)(2,1)S(1)}, bf16[1024,4096]{1,0:T(8,128)(2,1)}, u32[]{:S(2)}) %copy-start.11) | copy-done | bytes 8388632
  113.7 2.1 %panel_product.7 = (bf16[1024,4096]{1,0:T(8,128)(2,1)S(1)}, f32[64,1024]{1,0:T(8,128)S(1)}, f32[64,64]{1,0:T(8,128)S(1)}) custom-call(s32[1]{0:T(128)} %bitcast.1.pos_ref, bf16[1024,4096]{1,0:T(8,128)(2,1)S(1)} %copy-done.11, bf16[4,4,64,256]{3,2,1,0:T(8,128)(2,1)S(1)} %all-to-all-done.4.packets, ...), custom_call_target="tpu_custom_call", output_to_operand_aliasing={{0}: (1, {})} | custom-call | flops 1610612736 | bytes 6291456 | tf_op jit(solution)/shard_map/panel_product/pallas_call | solution.py:237
  115.9 3.3 %copy-done.12 = bf16[1024,4096]{1,0:T(8,128)(2,1)} copy-done((bf16[1024,4096]{1,0:T(8,128)(2,1)}, bf16[1024,4096]{1,0:T(8,128)(2,1)S(1)}, u32[]{:S(2)}) %copy-start.12) | copy-done | bytes 8388632
  120.1 3.4 %copy-done.13 = bf16[1024,4096]{1,0:T(8,128)(2,1)S(1)} copy-done((bf16[1024,4096]{1,0:T(8,128)(2,1)S(1)}, bf16[1024,4096]{1,0:T(8,128)(2,1)}, u32[]{:S(2)}) %copy-start.13) | copy-done | bytes 8388632
  127.9 4.0 %collective-permute-done.4.refs_2_ = bf16[4,64,256]{2,1,0:T(8,128)(2,1)S(1)} collective-permute-done((bf16[4,64,256]{2,1,0:T(8,128)(2,1)S(1)}, bf16[4,64,256]{2,1,0:T(8,128)(2,1)S(1)}, u32[]{:S(2)}, u32[]{:S(2)}) %collective-permute-start.4) | collective-permute-done | bytes 131104 | tf_op jit(solution)/shard_map/ppermute | solution.py:282
  134.8 13.5 %all_to_all.31 = bf16[4,64,640]{2,1,0:T(8,128)(2,1)S(1)} all-to-all(bf16[4,64,640]{2,1,0:T(8,128)(2,1)S(1)} %plane_sum.3), channel_id=1, replica_groups={{0,4,8,12},{1,5,9,13},{2,6,10,14},{3,7,11,15},{16,20,24,28},{17,21,25,2..., dimensions={0} | all-to-all | bytes 655360 | tf_op jit(solution)/shard_map/all_to_all | solution.py:273
  (58 shorter events, 17.1 us)
Async XLA Ops:
  2.3 16.6 %all-to-all-start = ((bf16[4,64,640]{2,1,0:T(8,128)(2,1)}), bf16[4,64,640]{2,1,0:T(8,128)(2,1)S(1)}, u32[]{:S(2)}, u32[]{:S(2)}) async-start(bf16[4,64,640]{2,1,0:T(8,128)(2,1)} %broadcast_in_dim.6), calls=%async_computation | async-start | bytes 655360 | tf_op jit(solution)/shard_map/all_to_all | solution.py:273
  8.6 0.7 copy-start.14
  20.7 18.8 %all-to-all-start.1 = ((bf16[4,4,64,256]{3,2,1,0:T(8,128)(2,1)}), bf16[4,4,64,256]{3,2,1,0:T(8,128)(2,1)S(1)}, u32[]{:S(2)}, u32[]{:S(2)}) async-start(bf16[4,4,64,256]{3,2,1,0:T(8,128)(2,1)} %pick_blocks.2.packets), calls=%async_computation.1 | async-start | bytes 1048576 | tf_op jit(solution)/shard_map/all_to_all | solution.py:277
  27.7 3.3 %copy-start = (bf16[1024,4096]{1,0:T(8,128)(2,1)}, bf16[1024,4096]{1,0:T(8,128)(2,1)S(1)}, u32[]{:S(2)}) copy-start(bf16[1024,4096]{1,0:T(8,128)(2,1)S(1)} %get-tuple-element.38.geno) | copy-start | bytes 25165828
  31.0 3.4 %copy-start.1 = (bf16[1024,4096]{1,0:T(8,128)(2,1)S(1)}, bf16[1024,4096]{1,0:T(8,128)(2,1)}, u32[]{:S(2)}) copy-start(bf16[1024,4096]{1,0:T(8,128)(2,1)} %copy-done) | copy-start | bytes 25165828
  36.2 3.3 %copy-start.2 = (bf16[1024,4096]{1,0:T(8,128)(2,1)}, bf16[1024,4096]{1,0:T(8,128)(2,1)S(1)}, u32[]{:S(2)}) copy-start(bf16[1024,4096]{1,0:T(8,128)(2,1)S(1)} %get-tuple-element.39.geno) | copy-start | bytes 25165828
  39.5 3.4 %copy-start.3 = (bf16[1024,4096]{1,0:T(8,128)(2,1)S(1)}, bf16[1024,4096]{1,0:T(8,128)(2,1)}, u32[]{:S(2)}) copy-start(bf16[1024,4096]{1,0:T(8,128)(2,1)} %copy-done.2) | copy-start | bytes 25165828
  45.0 3.3 %copy-start.4 = (bf16[1024,4096]{1,0:T(8,128)(2,1)}, bf16[1024,4096]{1,0:T(8,128)(2,1)S(1)}, u32[]{:S(2)}) copy-start(bf16[1024,4096]{1,0:T(8,128)(2,1)S(1)} %get-tuple-element.45.geno) | copy-start | bytes 25165828
  48.7 3.4 %copy-start.5 = (bf16[1024,4096]{1,0:T(8,128)(2,1)S(1)}, bf16[1024,4096]{1,0:T(8,128)(2,1)}, u32[]{:S(2)}) copy-start(bf16[1024,4096]{1,0:T(8,128)(2,1)} %copy-done.4) | copy-start | bytes 25165828
  52.7 6.7 %copy-start.15 = (s32[16,64]{1,0:T(8,128)S(1)}, s32[16,64]{1,0:T(8,128)}, u32[]{:S(2)}) copy-start(s32[16,64]{1,0:T(8,128)} %cov.1) | copy-start | bytes 12292
  53.3 30.2 %copy-start.16 = (f32[640,64]{0,1:T(8,128)S(1)}, f32[640,64]{0,1:T(8,128)}, u32[]{:S(2)}) copy-start(f32[640,64]{0,1:T(8,128)} %param.6) | copy-start | bytes 491524
  53.9 3.3 %copy-start.6 = (bf16[1024,4096]{1,0:T(8,128)(2,1)}, bf16[1024,4096]{1,0:T(8,128)(2,1)S(1)}, u32[]{:S(2)}) copy-start(bf16[1024,4096]{1,0:T(8,128)(2,1)S(1)} %get-tuple-element.50.geno) | copy-start | bytes 25165828
  57.2 9.6 %collective-permute-start = (bf16[4,64,256]{2,1,0:T(8,128)(2,1)S(1)}, bf16[4,64,256]{2,1,0:T(8,128)(2,1)S(1)}, u32[]{:S(2)}, u32[]{:S(2)}) collective-permute-start(bf16[4,64,256]{2,1,0:T(8,128)(2,1)S(1)} %get-tuple-element.53), channel_id=1, source_target_pairs={{0,1},{1,0},{2,3},{3,2},{4,5},{5,4},{6,7},{7,6},{8,9},{9,8},{10,11... | collective-permute-start | bytes 393224 | tf_op jit(solution)/shard_map/ppermute | solution.py:282
  57.7 9.1 %collective-permute-start.1 = (bf16[4,64,256]{2,1,0:T(8,128)(2,1)S(1)}, bf16[4,64,256]{2,1,0:T(8,128)(2,1)S(1)}, u32[]{:S(2)}, u32[]{:S(2)}) collective-permute-start(bf16[4,64,256]{2,1,0:T(8,128)(2,1)S(1)} %get-tuple-element.54), channel_id=1, source_target_pairs={{0,2},{1,3},{2,0},{3,1},{4,6},{5,7},{6,4},{7,5},{8,10},{9,11},{10,... | collective-permute-start | bytes 393224 | tf_op jit(solution)/shard_map/ppermute | solution.py:282
  59.4 7.4 %collective-permute-start.2 = (bf16[4,64,256]{2,1,0:T(8,128)(2,1)S(1)}, bf16[4,64,256]{2,1,0:T(8,128)(2,1)S(1)}, u32[]{:S(2)}, u32[]{:S(2)}) collective-permute-start(bf16[4,64,256]{2,1,0:T(8,128)(2,1)S(1)} %get-tuple-element.55), channel_id=1, source_target_pairs={{0,3},{1,2},{2,1},{3,0},{4,7},{5,6},{6,5},{7,4},{8,11},{9,10},{10,... | collective-permute-start | bytes 393224 | tf_op jit(solution)/shard_map/ppermute | solution.py:282
  59.5 3.4 %copy-start.7 = (bf16[1024,4096]{1,0:T(8,128)(2,1)S(1)}, bf16[1024,4096]{1,0:T(8,128)(2,1)}, u32[]{:S(2)}) copy-start(bf16[1024,4096]{1,0:T(8,128)(2,1)} %copy-done.6) | copy-start | bytes 25165828
  63.5 3.3 %copy-start.8 = (bf16[1024,4096]{1,0:T(8,128)(2,1)}, bf16[1024,4096]{1,0:T(8,128)(2,1)S(1)}, u32[]{:S(2)}) copy-start(bf16[1024,4096]{1,0:T(8,128)(2,1)S(1)} %get-tuple-element.51.geno) | copy-start | bytes 25165828
  68.8 14.6 %all-to-all-start.2 = ((bf16[4,64,640]{2,1,0:T(8,128)(2,1)}), bf16[4,64,640]{2,1,0:T(8,128)(2,1)S(1)}, u32[]{:S(2)}, u32[]{:S(2)}) async-start(bf16[4,64,640]{2,1,0:T(8,128)(2,1)} %plane_sum.2), calls=%async_computation.2 | async-start | bytes 655360 | tf_op jit(solution)/shard_map/all_to_all | solution.py:273
  98.1 12.3 %all-to-all-start.4 = ((bf16[4,4,64,256]{3,2,1,0:T(8,128)(2,1)}), bf16[4,4,64,256]{3,2,1,0:T(8,128)(2,1)S(1)}, u32[]{:S(2)}, u32[]{:S(2)}) async-start(bf16[4,4,64,256]{3,2,1,0:T(8,128)(2,1)} %pick_blocks.3.packets), calls=%async_computation.4 | async-start | bytes 1048576 | tf_op jit(solution)/shard_map/all_to_all | solution.py:277
  101.5 3.4 %copy-start.9 = (bf16[1024,4096]{1,0:T(8,128)(2,1)S(1)}, bf16[1024,4096]{1,0:T(8,128)(2,1)}, u32[]{:S(2)}) copy-start(bf16[1024,4096]{1,0:T(8,128)(2,1)} %copy-done.8) | copy-start | bytes 25165828
  106.7 3.3 %copy-start.10 = (bf16[1024,4096]{1,0:T(8,128)(2,1)}, bf16[1024,4096]{1,0:T(8,128)(2,1)S(1)}, u32[]{:S(2)}) copy-start(bf16[1024,4096]{1,0:T(8,128)(2,1)S(1)} %get-tuple-element.56.geno) | copy-start | bytes 25165828
  110.3 3.4 %copy-start.11 = (bf16[1024,4096]{1,0:T(8,128)(2,1)S(1)}, bf16[1024,4096]{1,0:T(8,128)(2,1)}, u32[]{:S(2)}) copy-start(bf16[1024,4096]{1,0:T(8,128)(2,1)} %copy-done.10) | copy-start | bytes 25165828
  115.9 3.3 %copy-start.12 = (bf16[1024,4096]{1,0:T(8,128)(2,1)}, bf16[1024,4096]{1,0:T(8,128)(2,1)S(1)}, u32[]{:S(2)}) copy-start(bf16[1024,4096]{1,0:T(8,128)(2,1)S(1)} %get-tuple-element.62.geno) | copy-start | bytes 25165828
  120.1 3.4 %copy-start.13 = (bf16[1024,4096]{1,0:T(8,128)(2,1)S(1)}, bf16[1024,4096]{1,0:T(8,128)(2,1)}, u32[]{:S(2)}) copy-start(bf16[1024,4096]{1,0:T(8,128)(2,1)} %copy-done.12) | copy-start | bytes 25165828
  125.3 2.5 %collective-permute-start.3 = (bf16[4,64,256]{2,1,0:T(8,128)(2,1)S(1)}, bf16[4,64,256]{2,1,0:T(8,128)(2,1)S(1)}, u32[]{:S(2)}, u32[]{:S(2)}) collective-permute-start(bf16[4,64,256]{2,1,0:T(8,128)(2,1)S(1)} %get-tuple-element.69), channel_id=1, source_target_pairs={{0,1},{1,0},{2,3},{3,2},{4,5},{5,4},{6,7},{7,6},{8,9},{9,8},{10,11... | collective-permute-start | bytes 393224 | tf_op jit(solution)/shard_map/ppermute | solution.py:282
  125.5 6.3 %collective-permute-start.4 = (bf16[4,64,256]{2,1,0:T(8,128)(2,1)S(1)}, bf16[4,64,256]{2,1,0:T(8,128)(2,1)S(1)}, u32[]{:S(2)}, u32[]{:S(2)}) collective-permute-start(bf16[4,64,256]{2,1,0:T(8,128)(2,1)S(1)} %get-tuple-element.70), channel_id=1, source_target_pairs={{0,2},{1,3},{2,0},{3,1},{4,6},{5,7},{6,4},{7,5},{8,10},{9,11},{10,... | collective-permute-start | bytes 393224 | tf_op jit(solution)/shard_map/ppermute | solution.py:282
  127.2 6.3 %collective-permute-start.5 = (bf16[4,64,256]{2,1,0:T(8,128)(2,1)S(1)}, bf16[4,64,256]{2,1,0:T(8,128)(2,1)S(1)}, u32[]{:S(2)}, u32[]{:S(2)}) collective-permute-start(bf16[4,64,256]{2,1,0:T(8,128)(2,1)S(1)} %get-tuple-element.71), channel_id=1, source_target_pairs={{0,3},{1,2},{2,1},{3,0},{4,7},{5,6},{6,5},{7,4},{8,11},{9,10},{10,... | collective-permute-start | bytes 393224 | tf_op jit(solution)/shard_map/ppermute | solution.py:282

commit v4 on v1

v4 whole, which is shorter than its diff:
```python
import functools
import math

import jax
import jax.numpy as jnp
from jax import lax
from jax.experimental import pallas as pl
from jax.experimental.pallas import tpu as pltpu
from jax.sharding import PartitionSpec as P

ROUNDS = 2

weight_decay = 0.02

PLANE = 4
NT = (((1,), (1,)), ((), ()))
NN = (((1,), (0,)), ((), ()))
VMEM_LIMIT = 24 * 1024 * 1024


def dot(a, b, dims):
    return lax.dot_general(a, b, dims, preferred_element_type=jnp.float32)


def split3(x):
    hi = x.astype(jnp.bfloat16)
    rest = x - hi.astype(jnp.float32)
    mid = rest.astype(jnp.bfloat16)
    lo = (rest - mid.astype(jnp.float32)).astype(jnp.bfloat16)
    return hi, mid, lo


def low_half(rows):
    return lax.broadcasted_iota(jnp.int32, (rows, 128), 1) < 64


def double(x, low):
    turned = pltpu.roll(x, 64, 1)
    return jnp.where(low, x, turned), jnp.where(low, turned, x)


def load_kernel(geno, samples, geno_out, samples_out, sems):
    copies = [
        pltpu.make_async_copy(samples, samples_out, sems.at[0]),
        pltpu.make_async_copy(geno, geno_out, sems.at[1]),
    ]
    for copy in copies:
        copy.start()
    for copy in copies:
        copy.wait()


def table_kernel(planes, per_owner, own_blocks, pos_ref, cov, table):
    for mate in range(PLANE):
        batch = lax.bitwise_xor(pos_ref[0], mate)
        for turn in range(planes):
            owner = lax.bitwise_xor(pos_ref[0], turn * PLANE)
            for p in range(per_owner):
                table[mate * planes + turn, p] = cov[batch, owner * per_owner + p] - owner * own_blocks


def steps_kernel(scale, own_blocks, pos_ref, cov, steps):
    def step_of(block):
        seen = (cov[...] == pos_ref[0] * own_blocks + block).astype(jnp.float32)
        return scale / jnp.sum(jnp.sum(seen, axis=1, keepdims=True), axis=0, keepdims=True)

    low = low_half(steps.shape[0])
    for j in range(own_blocks // 2):
        steps[:, 128 * j:128 * (j + 1)] = jnp.where(low, step_of(2 * j), step_of(2 * j + 1))


def pick_kernel(planes, turns, per_owner, own_blocks, table, *refs):
    held, packets, blocks = refs[:len(turns)], refs[len(turns):-1], refs[-1]
    low = low_half(held[0].shape[0])
    for i in range(len(turns)):
        for j in range(own_blocks // 2):
            x = held[i][:, 128 * j:128 * (j + 1)].astype(jnp.float32)
            blocks[i, 2 * j], blocks[i, 2 * j + 1] = double(x, low)
    for mate in range(PLANE):
        for i, turn in enumerate(turns):
            for q in range(per_owner // 2):
                first = table[mate * planes + turn, 2 * q]
                second = table[mate * planes + turn, 2 * q + 1]
                pair = jnp.where(low, blocks[i, first], blocks[i, second])
                packets[mate][i, :, 128 * q:128 * (q + 1)] = pair.astype(jnp.bfloat16)


def plane_sum_kernel(planes, turns, per_owner, own_blocks, table, *refs):
    terms, sums, total = refs[:PLANE], refs[PLANE:-1], refs[-1]
    low = low_half(terms[0].shape[1])
    total[...] = jnp.zeros_like(total)
    for i, turn in enumerate(turns):
        for mate in range(PLANE):
            for q in range(per_owner // 2):
                first = table[mate * planes + turn, 2 * q]
                second = table[mate * planes + turn, 2 * q + 1]
                pair = terms[mate][i, :, 128 * q:128 * (q + 1)].astype(jnp.float32)
                total[i, first] += jnp.where(low, pair, 0.0)
                total[i, second] += jnp.where(low, 0.0, pair)
    for i in range(len(turns)):
        for j in range(own_blocks // 2):
            first, second = total[i, 2 * j], total[i, 2 * j + 1]
            both = jnp.where(low, first, second) + pltpu.roll(jnp.where(low, second, first), 64, 1)
            sums[i][:, 128 * j:128 * (j + 1)] = both.astype(sums[i].dtype)


def columns_of(pos, turn, mate, width):
    owner = lax.bitwise_xor(pos, turn * PLANE + mate)
    return pl.ds(pl.multiple_of(owner * width, width), width)


def product_kernel(turns, mates, first, rows, pos_ref, geno, *refs):
    packets, before, (gradient, gram) = refs[:len(mates)], refs[len(mates):-2], refs[-2:]
    pos = pos_ref[0]
    width = packets[0].shape[2]
    places = [(i, turn, m, mate) for m, mate in enumerate(mates) for i, turn in enumerate(turns)]
    total = None if first else before[1][...]
    for i, turn, m, mate in places:
        term = dot(packets[m][i], packets[m][i], NT)
        total = term if total is None else total + term
    gram[...] = total
    for r in range(geno.shape[0] // rows):
        here = slice(r * rows, (r + 1) * rows)
        total = None if first else before[0][:, here]
        for i, turn, m, mate in places:
            term = dot(packets[m][i], geno[here, columns_of(pos, turn, mate, width)], NT)
            total = term if total is None else total + term
        gradient[:, here] = total


def sample_kernel(sample_step, samples, gradient, gram, new_samples, new_bf16, new_gram):
    old = samples[...]
    old_bf16 = old.astype(jnp.bfloat16)
    total = gradient[...]
    for part in split3(gram[...]):
        total -= dot(part, old_bf16, NN)
    new = (1.0 - weight_decay) * old + sample_step * total
    new_samples[...] = new
    rounded = new.astype(jnp.bfloat16)
    new_bf16[...] = rounded
    new_gram[...] = dot(rounded, rounded, NT)


def term_kernel(turns, mate, pos_ref, geno, samples, gram, packet, terms):
    pos = pos_ref[0]
    width = packet.shape[2]
    parts = split3(gram[...])
    for i, turn in enumerate(turns):
        term = dot(samples[...], geno[:, columns_of(pos, turn, mate, width)], NN)
        for part in parts:
            term -= dot(part, packet[i], NN)
        terms[i] = term.astype(jnp.bfloat16)


def on_device(genotypes, sample_factors, snp_factors, coverage):
    devices = lax.axis_size("rows")
    planes = devices // PLANE
    position = lax.axis_index("rows").astype(jnp.int32)
    samples_here, snps_here = genotypes.shape
    rank = sample_factors.shape[1]
    covered = coverage.shape[1]
    tile_size = snps_here // covered
    per_owner = covered // devices
    own_snps = snp_factors.shape[0]
    own_blocks = own_snps // tile_size
    width = per_owner * tile_size
    assert tile_size == 64 and per_owner % 2 == 0 and own_blocks % 2 == 0
    assert devices % PLANE == 0 and planes % 2 == 0 and planes & (planes - 1) == 0

    sample_step = 0.5 * math.sqrt(rank) / (covered * tile_size)

    smem = pl.BlockSpec(memory_space=pltpu.SMEM)
    vmem = pl.BlockSpec(memory_space=pltpu.VMEM)
    hbm = pl.BlockSpec(memory_space=pltpu.HBM)
    params = pltpu.CompilerParams(vmem_limit_bytes=VMEM_LIMIT)
    pos = position.reshape(1)
    half = planes // 2
    near, far = tuple(range(half)), tuple(range(half, planes))
    packet = jax.ShapeDtypeStruct((half, rank, width), jnp.bfloat16)
    dense_blocks = pltpu.VMEM((half, own_blocks, rank, 128), jnp.float32)
    by_samples = jax.ShapeDtypeStruct((rank, samples_here), jnp.float32)
    square = jax.ShapeDtypeStruct((rank, rank), jnp.float32)
    sizes = (planes, per_owner, own_blocks)

    def cost(flops, bytes_accessed):
        return pl.CostEstimate(flops=flops, bytes_accessed=bytes_accessed, transcendentals=0)

    table = pl.pallas_call(
        functools.partial(table_kernel, *sizes),
        out_shape=jax.ShapeDtypeStruct((PLANE * planes, per_owner), jnp.int32),
        in_specs=[smem, smem],
        out_specs=smem,
        compiler_params=params,
        name="block_table",
    )(pos, coverage)
    geno, samples = pl.pallas_call(
        load_kernel,
        out_shape=(
            pltpu.VMEM((samples_here, snps_here), jnp.bfloat16),
            pltpu.VMEM((rank, samples_here), jnp.float32),
        ),
        in_specs=[hbm, hbm],
        out_specs=(vmem, vmem),
        scratch_shapes=[pltpu.SemaphoreType.DMA((2,))],
        compiler_params=pltpu.CompilerParams(
            vmem_limit_bytes=58 * 1024 * 1024 - 2 * samples_here * snps_here
        ),
        cost_estimate=cost(0, 2 * samples_here * snps_here),
        name="load_batch",
    )(genotypes, sample_factors.T)

    snp_step = pl.pallas_call(
        functools.partial(steps_kernel, 0.5 * math.sqrt(rank) / samples_here, own_blocks),
        out_shape=jax.ShapeDtypeStruct((rank, own_snps), jnp.float32),
        in_specs=[smem, vmem],
        out_specs=vmem,
        compiler_params=params,
        name="snp_steps",
    )(pos, coverage)
    small = cost(0, 2 * 1024 * 1024)

    def pick(turns, held):
        return pl.pallas_call(
            functools.partial(pick_kernel, planes, turns, per_owner, own_blocks),
            out_shape=(packet,) * PLANE,
            in_specs=[smem] + [vmem] * half,
            out_specs=(vmem,) * PLANE,
            scratch_shapes=[dense_blocks],
            compiler_params=params,
            cost_estimate=small,
            name="pick_blocks",
        )(table, *[held[turn] for turn in turns])

    def plane_sum(turns, terms):
        sums = pl.pallas_call(
            functools.partial(plane_sum_kernel, planes, turns, per_owner, own_blocks),
            out_shape=tuple(
                jax.ShapeDtypeStruct((rank, own_snps), jnp.bfloat16 if turn % 2 else jnp.float32)
                for turn in turns
            ),
            in_specs=[smem] + [vmem] * PLANE,
            out_specs=(vmem,) * half,
            scratch_shapes=[dense_blocks],
            compiler_params=params,
            cost_estimate=small,
            name="plane_sum",
        )(table, *terms)
        return dict(zip(turns, sums))

    def product(turns, mates, panels, before):
        share = len(turns) * len(mates) * samples_here * snps_here // devices
        return pl.pallas_call(
            functools.partial(product_kernel, turns, mates, not before, 256),
            out_shape=(by_samples, square),
            in_specs=[smem] + [vmem] * (1 + len(mates) + len(before)),
            out_specs=(vmem, vmem),
            compiler_params=params,
            cost_estimate=cost(8 * rank * share, 2 * share),
            name="panel_product",
        )(pos, geno, *[panels[turns][mate] for mate in mates], *before)

    def sample_update(samples, gradient, gram):
        return pl.pallas_call(
            functools.partial(sample_kernel, sample_step),
            out_shape=(by_samples, jax.ShapeDtypeStruct((rank, samples_here), jnp.bfloat16), square),
            in_specs=[vmem] * 3,
            out_specs=(vmem,) * 3,
            compiler_params=params,
            name="sample_update",
        )(samples, gradient, gram)

    def terms_for(turns, mate, samples_bf16, gram, panels):
        share = len(turns) * samples_here * snps_here // devices
        return pl.pallas_call(
            functools.partial(term_kernel, turns, mate),
            out_shape=packet,
            in_specs=[smem] + [vmem] * 4,
            out_specs=vmem,
            compiler_params=params,
            cost_estimate=cost(8 * rank * share, 2 * share),
            name="mate_terms",
        )(pos, geno, samples_bf16, gram, panels[turns][mate])

    def swap(x, turn):
        return lax.ppermute(x, "rows", [(r, r ^ turn) for r in range(devices)])

    def to_mate(x, mate):
        return swap(x, mate) if mate else x

    snps = snp_factors.T
    for iteration in range(ROUNDS):
        held = {0: snps.astype(jnp.bfloat16)}
        for turn in sorted(range(1, planes), key=lambda turn: (turn & (turn - 1), -turn)):
            bit = turn & -turn
            held[turn] = swap(held[turn ^ bit], bit * PLANE)
        panels = {}
        for turns in (near, far):
            packets = pick(turns, held)
            panels[turns] = [to_mate(packets[mate], mate) for mate in range(PLANE)]
        partial = ()
        for turns, mates in (
            (near, (0,)), (far, (0,)), (near, (1,)), (near, (2, 3)), (far, (1,)), (far, (2,)), (far, (3,))
        ):
            partial = product(turns, mates, panels, partial)
        samples, samples_bf16, sample_gram = sample_update(samples, *partial)
        sums = {}
        for turns in (far, near):
            terms = {}
            for mate in (2, 3, 1, 0):
                terms[mate] = to_mate(terms_for(turns, mate, samples_bf16, sample_gram, panels), mate)
            sums.update(plane_sum(turns, [terms[mate] for mate in range(PLANE)]))
        for turn in range(planes - 1, 0, -1):
            bit = turn & -turn
            arrived = swap(sums[turn].astype(jnp.bfloat16), bit * PLANE)
            sums[turn ^ bit] = sums[turn ^ bit] + arrived.astype(jnp.float32)
        snps = (1.0 - weight_decay) * snps + snp_step * sums[0]
    return (samples.T, snps.T)


def solution(mesh):
    placed = (
        P(("groups", "rows"), None),
        P(("groups", "rows"), None),
        P(("groups", "rows"), None),
        P("groups", None),
    )
    return jax.shard_map(
        on_device,
        mesh=mesh,
        in_specs=placed,
        out_specs=(P(("groups", "rows"), None), P(("groups", "rows"), None)),
        check_vma=False,
    )
```

time: 87.7 us -> 94 us (1.072)
  starting transfers between devices: 29.4 us -> 35.8 us
  Pallas kernels: 21.8 us -> 26.9 us
  local copies, waits for them, and re-layouts: 5.1 us -> 0.71 us
    ppermute x24 -> x36, starting transfers between devices: 29.4 us -> 35.8 us  [swap(): return lax.ppermute(x, 'rows', [(r, r ^ turn) for r in range(devices)])]
    pallas_call x18 -> x39, Pallas kernels: 15.4 us -> 20.5 us  [the longest x14 7.18 us: product(): pl.pallas_call(functools.partial(product_kernel, turns, mates, not before...]
    unnamed x13 -> x6, local copies, waits for them, and re-layouts: 4.18 us -> 0.71 us
    ppermute x24 -> x36, waiting for transfers between devices: 28.4 us -> 27.5 us  [swap(): return lax.ppermute(x, 'rows', [(r, r ^ turn) for r in range(devices)])]
  transfers between devices with their start and end apart: 24 -> 36, of which waited for: 14 -> 13; matrix products, arithmetic and copies ran while one was open for 1% -> 0% of each run, Pallas kernels for 14% -> 25%
where the time goes in v4:
time: 94 us; the launch traced here: 93.8 us
  starting transfers between devices  35.8 us (38%)
  waiting for transfers between devices  27.5 us (29%)
  Pallas kernels  26.9 us (29%)
  other arithmetic  1.77 us (2%)
  between operations  1.06 us (1%)
    ppermute x36, starting transfers between devices, swap(): return lax.ppermute(x, 'rows', [(r, r ^ turn) for r in range(devices)])  35.8 us
    ppermute x36, waiting for transfers between devices, swap(): return lax.ppermute(x, 'rows', [(r, r ^ turn) for r in range(devices)])  27.5 us
    pallas_call x14, Pallas kernels, product(): pl.pallas_call(functools.partial(product_kernel, turns, mates, not before...  7.18 us
    pallas_call x16, Pallas kernels, terms_for(): pl.pallas_call(functools.partial(term_kernel, turns, mate), out_shape=pac...  5.86 us
    pallas_call x4, Pallas kernels, plane_sum(): pl.pallas_call(functools.partial(plane_sum_kernel, planes, turns, per_own...  4.03 us
    pallas_call x1, Pallas kernels, on_device(): pl.pallas_call(load_kernel, out_shape=(pltpu.VMEM((samples_here, snps_her...  3.5 us
    pallas_call x4, Pallas kernels, pick(): pl.pallas_call(functools.partial(pick_kernel, planes, turns, per_owner, o...  3.34 us
  transfers between devices with their start and end apart: 36, of which 13 were waited for; matrix products, arithmetic and copies ran while one was open for 0% of the time, Pallas kernels for 25%

profile of v4, /device:TPU:0, one launch (start us, length us, event | category | flops | bytes accessed | tf_op | source)
XLA Modules:
  0.0 93.8 jit_solution(12483587186049909496)
XLA Ops:
  1.6 4.1 %collective-permute-start = (bf16[64,640]{1,0:T(8,128)(2,1)S(1)}, bf16[64,640]{1,0:T(8,128)(2,1)S(1)}, u32[]{:S(2)}, u32[]{:S(2)}) collective-permute-start(bf16[64,640]{1,0:T(8,128)(2,1)S(1)} %convert_bitcast_fusion.refs_0_), channel_id=1, source_target_pairs={{0,8},{1,9},{2,10},{3,11},{4,12},{5,13},{6,14},{7,15},{8,0},{9,1},... | collective-permute-start | bytes 245768 | tf_op jit(solution)/shard_map/ppermute | solution.py:285
  5.7 1.6 %collective-permute-start.5 = (bf16[64,640]{1,0:T(8,128)(2,1)S(1)}, bf16[64,640]{1,0:T(8,128)(2,1)S(1)}, u32[]{:S(2)}, u32[]{:S(2)}) collective-permute-start(bf16[64,640]{1,0:T(8,128)(2,1)S(1)} %convert_bitcast_fusion.refs_0_), channel_id=1, source_target_pairs={{0,4},{1,5},{2,6},{3,7},{4,0},{5,1},{6,2},{7,3},{8,12},{9,13},{10,... | collective-permute-start | bytes 245768 | tf_op jit(solution)/shard_map/ppermute | solution.py:285
  7.2 2.2 %collective-permute-done.refs_0_ = bf16[64,640]{1,0:T(8,128)(2,1)S(1)} collective-permute-done((bf16[64,640]{1,0:T(8,128)(2,1)S(1)}, bf16[64,640]{1,0:T(8,128)(2,1)S(1)}, u32[]{:S(2)}, u32[]{:S(2)}) %collective-permute-start) | collective-permute-done | bytes 81952 | tf_op jit(solution)/shard_map/ppermute | solution.py:285
  9.4 1.2 %collective-permute-start.1 = (bf16[64,640]{1,0:T(8,128)(2,1)S(1)}, bf16[64,640]{1,0:T(8,128)(2,1)S(1)}, u32[]{:S(2)}, u32[]{:S(2)}) collective-permute-start(bf16[64,640]{1,0:T(8,128)(2,1)S(1)} %collective-permute-done.refs_0_), channel_id=1, source_target_pairs={{0,4},{1,5},{2,6},{3,7},{4,0},{5,1},{6,2},{7,3},{8,12},{9,13},{10,... | collective-permute-start | bytes 245768 | tf_op jit(solution)/shard_map/ppermute | solution.py:285
  11.3 1.5 %block_table.1.table = s32[16,4]{1,0:T(8,128)S(1)} custom-call(s32[1]{0:T(128)} %bitcast.1.pos_ref, s32[16,64]{1,0:T(8,128)S(1)} %copy-done), custom_call_target="tpu_custom_call" | custom-call | tf_op jit(solution)/shard_map/block_table/pallas_call | solution.py:188
  13.8 3.5 %load_batch.1 = (bf16[1024,4096]{1,0:T(8,128)(2,1)S(1)}, f32[64,1024]{1,0:T(8,128)S(1)}) custom-call(bf16[1024,4096]{1,0:T(8,128)(2,1)} %geno.1, f32[64,1024]{1,0:T(8,128)} %bitcast.13), custom_call_target="tpu_custom_call" | custom-call | bytes 8388608 | tf_op jit(solution)/shard_map/load_batch/pallas_call | solution.py:196
  17.3 1.6 %collective-permute-start.6 = (bf16[2,64,256]{2,1,0:T(8,128)(2,1)S(1)}, bf16[2,64,256]{2,1,0:T(8,128)(2,1)S(1)}, u32[]{:S(2)}, u32[]{:S(2)}) collective-permute-start(bf16[2,64,256]{2,1,0:T(8,128)(2,1)S(1)} %get-tuple-element.67), channel_id=1, source_target_pairs={{0,2},{1,3},{2,0},{3,1},{4,6},{5,7},{6,4},{7,5},{8,10},{9,11},{10,... | collective-permute-start | bytes 196616 | tf_op jit(solution)/shard_map/ppermute | solution.py:285
  20.5 1.5 %collective-permute-start.2 = (bf16[2,64,256]{2,1,0:T(8,128)(2,1)S(1)}, bf16[2,64,256]{2,1,0:T(8,128)(2,1)S(1)}, u32[]{:S(2)}, u32[]{:S(2)}) collective-permute-start(bf16[2,64,256]{2,1,0:T(8,128)(2,1)S(1)} %get-tuple-element.64), channel_id=1, source_target_pairs={{0,3},{1,2},{2,1},{3,0},{4,7},{5,6},{6,5},{7,4},{8,11},{9,10},{10,... | collective-permute-start | bytes 196616 | tf_op jit(solution)/shard_map/ppermute | solution.py:285
  24.9 1.5 %collective-permute-done.3.refs_0_.packet = bf16[2,64,256]{2,1,0:T(8,128)(2,1)S(1)} collective-permute-done((bf16[2,64,256]{2,1,0:T(8,128)(2,1)S(1)}, bf16[2,64,256]{2,1,0:T(8,128)(2,1)S(1)}, u32[]{:S(2)}, u32[]{:S(2)}) %collective-permute-start.3) | collective-permute-done | bytes 65568 | tf_op jit(solution)/shard_map/ppermute | solution.py:285
  28.6 1.6 %collective-permute-start.13 = (bf16[2,64,256]{2,1,0:T(8,128)(2,1)S(1)}, bf16[2,64,256]{2,1,0:T(8,128)(2,1)S(1)}, u32[]{:S(2)}, u32[]{:S(2)}) collective-permute-start(bf16[2,64,256]{2,1,0:T(8,128)(2,1)S(1)} %mate_terms.22), channel_id=1, source_target_pairs={{0,2},{1,3},{2,0},{3,1},{4,6},{5,7},{6,4},{7,5},{8,10},{9,11},{10,... | collective-permute-start | bytes 196616 | tf_op jit(solution)/shard_map/ppermute | solution.py:285
  32.0 1.6 %collective-permute-start.10 = (bf16[2,64,256]{2,1,0:T(8,128)(2,1)S(1)}, bf16[2,64,256]{2,1,0:T(8,128)(2,1)S(1)}, u32[]{:S(2)}, u32[]{:S(2)}) collective-permute-start(bf16[2,64,256]{2,1,0:T(8,128)(2,1)S(1)} %mate_terms.18), channel_id=1, source_target_pairs={{0,2},{1,3},{2,0},{3,1},{4,6},{5,7},{6,4},{7,5},{8,10},{9,11},{10,... | collective-permute-start | bytes 196616 | tf_op jit(solution)/shard_map/ppermute | solution.py:285
  34.7 1.0 %plane_sum.5 = (f32[64,640]{1,0:T(8,128)S(1)}, bf16[64,640]{1,0:T(8,128)(2,1)S(1)}) custom-call(s32[16,4]{1,0:T(8,128)S(1)} %block_table.1.table, bf16[2,64,256]{2,1,0:T(8,128)(2,1)S(1)} %mate_terms.20.refs_0_, bf16[2,64,256]{2,1,0:T(8,128)(2,1)S(1)} %collective-permute-done.12.refs_1_, bf16[2,64,256]{2,1,0:T(8,128)(2,1)S(1)} %collective-permute-done.13.refs_2_, ...), custom_call_target="tpu_custom_call" | custom-call | bytes 2097152 | tf_op jit(solution)/shard_map/plane_sum/pallas_call | solution.py:235
  35.7 1.3 %collective-permute-start.15 = (bf16[64,640]{1,0:T(8,128)(2,1)S(1)}, bf16[64,640]{1,0:T(8,128)(2,1)S(1)}, u32[]{:S(2)}, u32[]{:S(2)}) collective-permute-start(bf16[64,640]{1,0:T(8,128)(2,1)S(1)} %get-tuple-element.91), channel_id=1, source_target_pairs={{0,4},{1,5},{2,6},{3,7},{4,0},{5,1},{6,2},{7,3},{8,12},{9,13},{10,... | collective-permute-start | bytes 245768 | tf_op jit(solution)/shard_map/ppermute | solution.py:285
  38.3 3.3 %collective-permute-done.11.refs_3_ = bf16[2,64,256]{2,1,0:T(8,128)(2,1)S(1)} collective-permute-done((bf16[2,64,256]{2,1,0:T(8,128)(2,1)S(1)}, bf16[2,64,256]{2,1,0:T(8,128)(2,1)S(1)}, u32[]{:S(2)}, u32[]{:S(2)}) %collective-permute-start.11) | collective-permute-done | bytes 65568 | tf_op jit(solution)/shard_map/ppermute | solution.py:285
  41.6 1.0 %plane_sum.4 = (f32[64,640]{1,0:T(8,128)S(1)}, bf16[64,640]{1,0:T(8,128)(2,1)S(1)}) custom-call(s32[16,4]{1,0:T(8,128)S(1)} %block_table.1.table, bf16[2,64,256]{2,1,0:T(8,128)(2,1)S(1)} %mate_terms.16.refs_0_, bf16[2,64,256]{2,1,0:T(8,128)(2,1)S(1)} %collective-permute-done.9.refs_1_, bf16[2,64,256]{2,1,0:T(8,128)(2,1)S(1)} %collective-permute-done.10.refs_2_, ...), custom_call_target="tpu_custom_call" | custom-call | bytes 2097152 | tf_op jit(solution)/shard_map/plane_sum/pallas_call | solution.py:235
  43.6 3.4 %collective-permute-start.16 = (bf16[64,640]{1,0:T(8,128)(2,1)S(1)}, bf16[64,640]{1,0:T(8,128)(2,1)S(1)}, u32[]{:S(2)}, u32[]{:S(2)}) collective-permute-start(bf16[64,640]{1,0:T(8,128)(2,1)S(1)} %add_convert_fusion.1), channel_id=1, source_target_pairs={{0,8},{1,9},{2,10},{3,11},{4,12},{5,13},{6,14},{7,15},{8,0},{9,1},... | collective-permute-start | bytes 245768 | tf_op jit(solution)/shard_map/ppermute | solution.py:285
  47.1 4.1 %collective-permute-done.16 = bf16[64,640]{1,0:T(8,128)(2,1)S(1)} collective-permute-done((bf16[64,640]{1,0:T(8,128)(2,1)S(1)}, bf16[64,640]{1,0:T(8,128)(2,1)S(1)}, u32[]{:S(2)}, u32[]{:S(2)}) %collective-permute-start.16) | collective-permute-done | bytes 81952 | tf_op jit(solution)/shard_map/ppermute | solution.py:285
  51.3 1.2 %collective-permute-start.18 = (bf16[64,640]{1,0:T(8,128)(2,1)S(1)}, bf16[64,640]{1,0:T(8,128)(2,1)S(1)}, u32[]{:S(2)}, u32[]{:S(2)}) collective-permute-start(bf16[64,640]{1,0:T(8,128)(2,1)S(1)} %fusion.refs_0_), channel_id=1, source_target_pairs={{0,8},{1,9},{2,10},{3,11},{4,12},{5,13},{6,14},{7,15},{8,0},{9,1},... | collective-permute-start | bytes 245768 | tf_op jit(solution)/shard_map/ppermute | solution.py:285
  52.5 1.8 %collective-permute-start.23 = (bf16[64,640]{1,0:T(8,128)(2,1)S(1)}, bf16[64,640]{1,0:T(8,128)(2,1)S(1)}, u32[]{:S(2)}, u32[]{:S(2)}) collective-permute-start(bf16[64,640]{1,0:T(8,128)(2,1)S(1)} %fusion.refs_0_), channel_id=1, source_target_pairs={{0,4},{1,5},{2,6},{3,7},{4,0},{5,1},{6,2},{7,3},{8,12},{9,13},{10,... | collective-permute-start | bytes 245768 | tf_op jit(solution)/shard_map/ppermute | solution.py:285
  54.3 3.2 %collective-permute-done.18.refs_0_ = bf16[64,640]{1,0:T(8,128)(2,1)S(1)} collective-permute-done((bf16[64,640]{1,0:T(8,128)(2,1)S(1)}, bf16[64,640]{1,0:T(8,128)(2,1)S(1)}, u32[]{:S(2)}, u32[]{:S(2)}) %collective-permute-start.18) | collective-permute-done | bytes 81952 | tf_op jit(solution)/shard_map/ppermute | solution.py:285
  59.4 1.0 %collective-permute-start.24 = (bf16[2,64,256]{2,1,0:T(8,128)(2,1)S(1)}, bf16[2,64,256]{2,1,0:T(8,128)(2,1)S(1)}, u32[]{:S(2)}, u32[]{:S(2)}) collective-permute-start(bf16[2,64,256]{2,1,0:T(8,128)(2,1)S(1)} %get-tuple-element.96), channel_id=1, source_target_pairs={{0,2},{1,3},{2,0},{3,1},{4,6},{5,7},{6,4},{7,5},{8,10},{9,11},{10,... | collective-permute-start | bytes 196616 | tf_op jit(solution)/shard_map/ppermute | solution.py:285
  63.6 1.1 %collective-permute-start.21 = (bf16[2,64,256]{2,1,0:T(8,128)(2,1)S(1)}, bf16[2,64,256]{2,1,0:T(8,128)(2,1)S(1)}, u32[]{:S(2)}, u32[]{:S(2)}) collective-permute-start(bf16[2,64,256]{2,1,0:T(8,128)(2,1)S(1)} %get-tuple-element.94), channel_id=1, source_target_pairs={{0,2},{1,3},{2,0},{3,1},{4,6},{5,7},{6,4},{7,5},{8,10},{9,11},{10,... | collective-permute-start | bytes 196616 | tf_op jit(solution)/shard_map/ppermute | solution.py:285
  67.1 1.6 %collective-permute-done.21.refs_0_.packet = bf16[2,64,256]{2,1,0:T(8,128)(2,1)S(1)} collective-permute-done((bf16[2,64,256]{2,1,0:T(8,128)(2,1)S(1)}, bf16[2,64,256]{2,1,0:T(8,128)(2,1)S(1)}, u32[]{:S(2)}, u32[]{:S(2)}) %collective-permute-start.21) | collective-permute-done | bytes 65568 | tf_op jit(solution)/shard_map/ppermute | solution.py:285
  71.5 1.0 %collective-permute-start.31 = (bf16[2,64,256]{2,1,0:T(8,128)(2,1)S(1)}, bf16[2,64,256]{2,1,0:T(8,128)(2,1)S(1)}, u32[]{:S(2)}, u32[]{:S(2)}) collective-permute-start(bf16[2,64,256]{2,1,0:T(8,128)(2,1)S(1)} %mate_terms.30), channel_id=1, source_target_pairs={{0,2},{1,3},{2,0},{3,1},{4,6},{5,7},{6,4},{7,5},{8,10},{9,11},{10,... | collective-permute-start | bytes 196616 | tf_op jit(solution)/shard_map/ppermute | solution.py:285
  74.9 1.0 %collective-permute-start.28 = (bf16[2,64,256]{2,1,0:T(8,128)(2,1)S(1)}, bf16[2,64,256]{2,1,0:T(8,128)(2,1)S(1)}, u32[]{:S(2)}, u32[]{:S(2)}) collective-permute-start(bf16[2,64,256]{2,1,0:T(8,128)(2,1)S(1)} %mate_terms.26), channel_id=1, source_target_pairs={{0,2},{1,3},{2,0},{3,1},{4,6},{5,7},{6,4},{7,5},{8,10},{9,11},{10,... | collective-permute-start | bytes 196616 | tf_op jit(solution)/shard_map/ppermute | solution.py:285
  77.1 1.0 %plane_sum.7 = (f32[64,640]{1,0:T(8,128)S(1)}, bf16[64,640]{1,0:T(8,128)(2,1)S(1)}) custom-call(s32[16,4]{1,0:T(8,128)S(1)} %block_table.1.table, bf16[2,64,256]{2,1,0:T(8,128)(2,1)S(1)} %mate_terms.28.refs_0_, bf16[2,64,256]{2,1,0:T(8,128)(2,1)S(1)} %collective-permute-done.30.refs_1_, bf16[2,64,256]{2,1,0:T(8,128)(2,1)S(1)} %collective-permute-done.31.refs_2_, ...), custom_call_target="tpu_custom_call" | custom-call | bytes 2097152 | tf_op jit(solution)/shard_map/plane_sum/pallas_call | solution.py:235
  80.3 3.6 %collective-permute-done.29.refs_3_ = bf16[2,64,256]{2,1,0:T(8,128)(2,1)S(1)} collective-permute-done((bf16[2,64,256]{2,1,0:T(8,128)(2,1)S(1)}, bf16[2,64,256]{2,1,0:T(8,128)(2,1)S(1)}, u32[]{:S(2)}, u32[]{:S(2)}) %collective-permute-start.29) | collective-permute-done | bytes 65568 | tf_op jit(solution)/shard_map/ppermute | solution.py:285
  83.9 1.0 %plane_sum.6 = (f32[64,640]{1,0:T(8,128)S(1)}, bf16[64,640]{1,0:T(8,128)(2,1)S(1)}) custom-call(s32[16,4]{1,0:T(8,128)S(1)} %block_table.1.table, bf16[2,64,256]{2,1,0:T(8,128)(2,1)S(1)} %mate_terms.24.refs_0_, bf16[2,64,256]{2,1,0:T(8,128)(2,1)S(1)} %collective-permute-done.27.refs_1_, bf16[2,64,256]{2,1,0:T(8,128)(2,1)S(1)} %collective-permute-done.28.refs_2_, ...), custom_call_target="tpu_custom_call" | custom-call | bytes 2097152 | tf_op jit(solution)/shard_map/plane_sum/pallas_call | solution.py:235
  84.9 1.2 %collective-permute-start.35 = (bf16[64,640]{1,0:T(8,128)(2,1)S(1)}, bf16[64,640]{1,0:T(8,128)(2,1)S(1)}, u32[]{:S(2)}, u32[]{:S(2)}) collective-permute-start(bf16[64,640]{1,0:T(8,128)(2,1)S(1)} %get-tuple-element.121), channel_id=1, source_target_pairs={{0,4},{1,5},{2,6},{3,7},{4,0},{5,1},{6,2},{7,3},{8,12},{9,13},{10,... | collective-permute-start | bytes 245768 | tf_op jit(solution)/shard_map/ppermute | solution.py:285
  86.1 1.6 %collective-permute-start.34 = (bf16[64,640]{1,0:T(8,128)(2,1)S(1)}, bf16[64,640]{1,0:T(8,128)(2,1)S(1)}, u32[]{:S(2)}, u32[]{:S(2)}) collective-permute-start(bf16[64,640]{1,0:T(8,128)(2,1)S(1)} %add_convert_fusion), channel_id=1, source_target_pairs={{0,8},{1,9},{2,10},{3,11},{4,12},{5,13},{6,14},{7,15},{8,0},{9,1},... | collective-permute-start | bytes 245768 | tf_op jit(solution)/shard_map/ppermute | solution.py:285
  87.7 1.7 %collective-permute-done.35 = bf16[64,640]{1,0:T(8,128)(2,1)S(1)} collective-permute-done((bf16[64,640]{1,0:T(8,128)(2,1)S(1)}, bf16[64,640]{1,0:T(8,128)(2,1)S(1)}, u32[]{:S(2)}, u32[]{:S(2)}) %collective-permute-start.35) | collective-permute-done | bytes 81952 | tf_op jit(solution)/shard_map/ppermute | solution.py:285
  89.4 3.6 %collective-permute-done.34 = bf16[64,640]{1,0:T(8,128)(2,1)S(1)} collective-permute-done((bf16[64,640]{1,0:T(8,128)(2,1)S(1)}, bf16[64,640]{1,0:T(8,128)(2,1)S(1)}, u32[]{:S(2)}, u32[]{:S(2)}) %collective-permute-start.34) | collective-permute-done | bytes 81952 | tf_op jit(solution)/shard_map/ppermute | solution.py:285
  (94 shorter events, 31.1 us)
Async XLA Ops:
  1.6 7.8 %collective-permute-start = (bf16[64,640]{1,0:T(8,128)(2,1)S(1)}, bf16[64,640]{1,0:T(8,128)(2,1)S(1)}, u32[]{:S(2)}, u32[]{:S(2)}) collective-permute-start(bf16[64,640]{1,0:T(8,128)(2,1)S(1)} %convert_bitcast_fusion.refs_0_), channel_id=1, source_target_pairs={{0,8},{1,9},{2,10},{3,11},{4,12},{5,13},{6,14},{7,15},{8,0},{9,1},... | collective-permute-start | bytes 245768 | tf_op jit(solution)/shard_map/ppermute | solution.py:285
  5.7 7.2 %collective-permute-start.5 = (bf16[64,640]{1,0:T(8,128)(2,1)S(1)}, bf16[64,640]{1,0:T(8,128)(2,1)S(1)}, u32[]{:S(2)}, u32[]{:S(2)}) collective-permute-start(bf16[64,640]{1,0:T(8,128)(2,1)S(1)} %convert_bitcast_fusion.refs_0_), channel_id=1, source_target_pairs={{0,4},{1,5},{2,6},{3,7},{4,0},{5,1},{6,2},{7,3},{8,12},{9,13},{10,... | collective-permute-start | bytes 245768 | tf_op jit(solution)/shard_map/ppermute | solution.py:285
  9.4 10.3 %collective-permute-start.1 = (bf16[64,640]{1,0:T(8,128)(2,1)S(1)}, bf16[64,640]{1,0:T(8,128)(2,1)S(1)}, u32[]{:S(2)}, u32[]{:S(2)}) collective-permute-start(bf16[64,640]{1,0:T(8,128)(2,1)S(1)} %collective-permute-done.refs_0_), channel_id=1, source_target_pairs={{0,4},{1,5},{2,6},{3,7},{4,0},{5,1},{6,2},{7,3},{8,12},{9,13},{10,... | collective-permute-start | bytes 245768 | tf_op jit(solution)/shard_map/ppermute | solution.py:285
  13.7 9.3 %collective-permute-start.8 = (bf16[2,64,256]{2,1,0:T(8,128)(2,1)S(1)}, bf16[2,64,256]{2,1,0:T(8,128)(2,1)S(1)}, u32[]{:S(2)}, u32[]{:S(2)}) collective-permute-start(bf16[2,64,256]{2,1,0:T(8,128)(2,1)S(1)} %get-tuple-element.69), channel_id=1, source_target_pairs={{0,1},{1,0},{2,3},{3,2},{4,5},{5,4},{6,7},{7,6},{8,9},{9,8},{10,11... | collective-permute-start | bytes 196616 | tf_op jit(solution)/shard_map/ppermute | solution.py:285
  17.3 6.3 %collective-permute-start.6 = (bf16[2,64,256]{2,1,0:T(8,128)(2,1)S(1)}, bf16[2,64,256]{2,1,0:T(8,128)(2,1)S(1)}, u32[]{:S(2)}, u32[]{:S(2)}) collective-permute-start(bf16[2,64,256]{2,1,0:T(8,128)(2,1)S(1)} %get-tuple-element.67), channel_id=1, source_target_pairs={{0,2},{1,3},{2,0},{3,1},{4,6},{5,7},{6,4},{7,5},{8,10},{9,11},{10,... | collective-permute-start | bytes 196616 | tf_op jit(solution)/shard_map/ppermute | solution.py:285
  18.9 4.7 %collective-permute-start.7 = (bf16[2,64,256]{2,1,0:T(8,128)(2,1)S(1)}, bf16[2,64,256]{2,1,0:T(8,128)(2,1)S(1)}, u32[]{:S(2)}, u32[]{:S(2)}) collective-permute-start(bf16[2,64,256]{2,1,0:T(8,128)(2,1)S(1)} %get-tuple-element.68), channel_id=1, source_target_pairs={{0,3},{1,2},{2,1},{3,0},{4,7},{5,6},{6,5},{7,4},{8,11},{9,10},{10,... | collective-permute-start | bytes 196616 | tf_op jit(solution)/shard_map/ppermute | solution.py:285
  20.5 6.3 %collective-permute-start.2 = (bf16[2,64,256]{2,1,0:T(8,128)(2,1)S(1)}, bf16[2,64,256]{2,1,0:T(8,128)(2,1)S(1)}, u32[]{:S(2)}, u32[]{:S(2)}) collective-permute-start(bf16[2,64,256]{2,1,0:T(8,128)(2,1)S(1)} %get-tuple-element.64), channel_id=1, source_target_pairs={{0,3},{1,2},{2,1},{3,0},{4,7},{5,6},{6,5},{7,4},{8,11},{9,10},{10,... | collective-permute-start | bytes 196616 | tf_op jit(solution)/shard_map/ppermute | solution.py:285
  22.0 4.4 %collective-permute-start.3 = (bf16[2,64,256]{2,1,0:T(8,128)(2,1)S(1)}, bf16[2,64,256]{2,1,0:T(8,128)(2,1)S(1)}, u32[]{:S(2)}, u32[]{:S(2)}) collective-permute-start(bf16[2,64,256]{2,1,0:T(8,128)(2,1)S(1)} %get-tuple-element.65), channel_id=1, source_target_pairs={{0,2},{1,3},{2,0},{3,1},{4,6},{5,7},{6,4},{7,5},{8,10},{9,11},{10,... | collective-permute-start | bytes 196616 | tf_op jit(solution)/shard_map/ppermute | solution.py:285
  28.1 5.8 %collective-permute-start.12 = (bf16[2,64,256]{2,1,0:T(8,128)(2,1)S(1)}, bf16[2,64,256]{2,1,0:T(8,128)(2,1)S(1)}, u32[]{:S(2)}, u32[]{:S(2)}) collective-permute-start(bf16[2,64,256]{2,1,0:T(8,128)(2,1)S(1)} %mate_terms.21), channel_id=1, source_target_pairs={{0,1},{1,0},{2,3},{3,2},{4,5},{5,4},{6,7},{7,6},{8,9},{9,8},{10,11... | collective-permute-start | bytes 196616 | tf_op jit(solution)/shard_map/ppermute | solution.py:285
  28.6 5.4 %collective-permute-start.13 = (bf16[2,64,256]{2,1,0:T(8,128)(2,1)S(1)}, bf16[2,64,256]{2,1,0:T(8,128)(2,1)S(1)}, u32[]{:S(2)}, u32[]{:S(2)}) collective-permute-start(bf16[2,64,256]{2,1,0:T(8,128)(2,1)S(1)} %mate_terms.22), channel_id=1, source_target_pairs={{0,2},{1,3},{2,0},{3,1},{4,6},{5,7},{6,4},{7,5},{8,10},{9,11},{10,... | collective-permute-start | bytes 196616 | tf_op jit(solution)/shard_map/ppermute | solution.py:285
  31.3 7.0 %collective-permute-start.9 = (bf16[2,64,256]{2,1,0:T(8,128)(2,1)S(1)}, bf16[2,64,256]{2,1,0:T(8,128)(2,1)S(1)}, u32[]{:S(2)}, u32[]{:S(2)}) collective-permute-start(bf16[2,64,256]{2,1,0:T(8,128)(2,1)S(1)} %mate_terms.17), channel_id=1, source_target_pairs={{0,1},{1,0},{2,3},{3,2},{4,5},{5,4},{6,7},{7,6},{8,9},{9,8},{10,11... | collective-permute-start | bytes 196616 | tf_op jit(solution)/shard_map/ppermute | solution.py:285
  32.0 6.3 %collective-permute-start.10 = (bf16[2,64,256]{2,1,0:T(8,128)(2,1)S(1)}, bf16[2,64,256]{2,1,0:T(8,128)(2,1)S(1)}, u32[]{:S(2)}, u32[]{:S(2)}) collective-permute-start(bf16[2,64,256]{2,1,0:T(8,128)(2,1)S(1)} %mate_terms.18), channel_id=1, source_target_pairs={{0,2},{1,3},{2,0},{3,1},{4,6},{5,7},{6,4},{7,5},{8,10},{9,11},{10,... | collective-permute-start | bytes 196616 | tf_op jit(solution)/shard_map/ppermute | solution.py:285
  35.7 7.9 %collective-permute-start.15 = (bf16[64,640]{1,0:T(8,128)(2,1)S(1)}, bf16[64,640]{1,0:T(8,128)(2,1)S(1)}, u32[]{:S(2)}, u32[]{:S(2)}) collective-permute-start(bf16[64,640]{1,0:T(8,128)(2,1)S(1)} %get-tuple-element.91), channel_id=1, source_target_pairs={{0,4},{1,5},{2,6},{3,7},{4,0},{5,1},{6,2},{7,3},{8,12},{9,13},{10,... | collective-permute-start | bytes 245768 | tf_op jit(solution)/shard_map/ppermute | solution.py:285
  42.6 4.6 %collective-permute-start.17 = (bf16[64,640]{1,0:T(8,128)(2,1)S(1)}, bf16[64,640]{1,0:T(8,128)(2,1)S(1)}, u32[]{:S(2)}, u32[]{:S(2)}) collective-permute-start(bf16[64,640]{1,0:T(8,128)(2,1)S(1)} %get-tuple-element.92), channel_id=1, source_target_pairs={{0,4},{1,5},{2,6},{3,7},{4,0},{5,1},{6,2},{7,3},{8,12},{9,13},{10,... | collective-permute-start | bytes 245768 | tf_op jit(solution)/shard_map/ppermute | solution.py:285
  43.6 7.6 %collective-permute-start.16 = (bf16[64,640]{1,0:T(8,128)(2,1)S(1)}, bf16[64,640]{1,0:T(8,128)(2,1)S(1)}, u32[]{:S(2)}, u32[]{:S(2)}) collective-permute-start(bf16[64,640]{1,0:T(8,128)(2,1)S(1)} %add_convert_fusion.1), channel_id=1, source_target_pairs={{0,8},{1,9},{2,10},{3,11},{4,12},{5,13},{6,14},{7,15},{8,0},{9,1},... | collective-permute-start | bytes 245768 | tf_op jit(solution)/shard_map/ppermute | solution.py:285
  51.3 6.3 %collective-permute-start.18 = (bf16[64,640]{1,0:T(8,128)(2,1)S(1)}, bf16[64,640]{1,0:T(8,128)(2,1)S(1)}, u32[]{:S(2)}, u32[]{:S(2)}) collective-permute-start(bf16[64,640]{1,0:T(8,128)(2,1)S(1)} %fusion.refs_0_), channel_id=1, source_target_pairs={{0,8},{1,9},{2,10},{3,11},{4,12},{5,13},{6,14},{7,15},{8,0},{9,1},... | collective-permute-start | bytes 245768 | tf_op jit(solution)/shard_map/ppermute | solution.py:285
  52.5 6.0 %collective-permute-start.23 = (bf16[64,640]{1,0:T(8,128)(2,1)S(1)}, bf16[64,640]{1,0:T(8,128)(2,1)S(1)}, u32[]{:S(2)}, u32[]{:S(2)}) collective-permute-start(bf16[64,640]{1,0:T(8,128)(2,1)S(1)} %fusion.refs_0_), channel_id=1, source_target_pairs={{0,4},{1,5},{2,6},{3,7},{4,0},{5,1},{6,2},{7,3},{8,12},{9,13},{10,... | collective-permute-start | bytes 245768 | tf_op jit(solution)/shard_map/ppermute | solution.py:285
  57.6 4.4 %collective-permute-start.19 = (bf16[64,640]{1,0:T(8,128)(2,1)S(1)}, bf16[64,640]{1,0:T(8,128)(2,1)S(1)}, u32[]{:S(2)}, u32[]{:S(2)}) collective-permute-start(bf16[64,640]{1,0:T(8,128)(2,1)S(1)} %collective-permute-done.18.refs_0_), channel_id=1, source_target_pairs={{0,4},{1,5},{2,6},{3,7},{4,0},{5,1},{6,2},{7,3},{8,12},{9,13},{10,... | collective-permute-start | bytes 245768 | tf_op jit(solution)/shard_map/ppermute | solution.py:285
  59.4 5.8 %collective-permute-start.26 = (bf16[2,64,256]{2,1,0:T(8,128)(2,1)S(1)}, bf16[2,64,256]{2,1,0:T(8,128)(2,1)S(1)}, u32[]{:S(2)}, u32[]{:S(2)}) collective-permute-start(bf16[2,64,256]{2,1,0:T(8,128)(2,1)S(1)} %get-tuple-element.98), channel_id=1, source_target_pairs={{0,1},{1,0},{2,3},{3,2},{4,5},{5,4},{6,7},{7,6},{8,9},{9,8},{10,11... | collective-permute-start | bytes 196616 | tf_op jit(solution)/shard_map/ppermute | solution.py:285
  59.4 6.3 %collective-permute-start.24 = (bf16[2,64,256]{2,1,0:T(8,128)(2,1)S(1)}, bf16[2,64,256]{2,1,0:T(8,128)(2,1)S(1)}, u32[]{:S(2)}, u32[]{:S(2)}) collective-permute-start(bf16[2,64,256]{2,1,0:T(8,128)(2,1)S(1)} %get-tuple-element.96), channel_id=1, source_target_pairs={{0,2},{1,3},{2,0},{3,1},{4,6},{5,7},{6,4},{7,5},{8,10},{9,11},{10,... | collective-permute-start | bytes 196616 | tf_op jit(solution)/shard_map/ppermute | solution.py:285
  60.5 5.3 %collective-permute-start.25 = (bf16[2,64,256]{2,1,0:T(8,128)(2,1)S(1)}, bf16[2,64,256]{2,1,0:T(8,128)(2,1)S(1)}, u32[]{:S(2)}, u32[]{:S(2)}) collective-permute-start(bf16[2,64,256]{2,1,0:T(8,128)(2,1)S(1)} %get-tuple-element.97), channel_id=1, source_target_pairs={{0,3},{1,2},{2,1},{3,0},{4,7},{5,6},{6,5},{7,4},{8,11},{9,10},{10,... | collective-permute-start | bytes 196616 | tf_op jit(solution)/shard_map/ppermute | solution.py:285
  62.8 6.3 %collective-permute-start.20 = (bf16[2,64,256]{2,1,0:T(8,128)(2,1)S(1)}, bf16[2,64,256]{2,1,0:T(8,128)(2,1)S(1)}, u32[]{:S(2)}, u32[]{:S(2)}) collective-permute-start(bf16[2,64,256]{2,1,0:T(8,128)(2,1)S(1)} %get-tuple-element.93), channel_id=1, source_target_pairs={{0,3},{1,2},{2,1},{3,0},{4,7},{5,6},{6,5},{7,4},{8,11},{9,10},{10,... | collective-permute-start | bytes 196616 | tf_op jit(solution)/shard_map/ppermute | solution.py:285
  63.6 5.1 %collective-permute-start.21 = (bf16[2,64,256]{2,1,0:T(8,128)(2,1)S(1)}, bf16[2,64,256]{2,1,0:T(8,128)(2,1)S(1)}, u32[]{:S(2)}, u32[]{:S(2)}) collective-permute-start(bf16[2,64,256]{2,1,0:T(8,128)(2,1)S(1)} %get-tuple-element.94), channel_id=1, source_target_pairs={{0,2},{1,3},{2,0},{3,1},{4,6},{5,7},{6,4},{7,5},{8,10},{9,11},{10,... | collective-permute-start | bytes 196616 | tf_op jit(solution)/shard_map/ppermute | solution.py:285
  71.0 5.3 %collective-permute-start.30 = (bf16[2,64,256]{2,1,0:T(8,128)(2,1)S(1)}, bf16[2,64,256]{2,1,0:T(8,128)(2,1)S(1)}, u32[]{:S(2)}, u32[]{:S(2)}) collective-permute-start(bf16[2,64,256]{2,1,0:T(8,128)(2,1)S(1)} %mate_terms.29), channel_id=1, source_target_pairs={{0,1},{1,0},{2,3},{3,2},{4,5},{5,4},{6,7},{7,6},{8,9},{9,8},{10,11... | collective-permute-start | bytes 196616 | tf_op jit(solution)/shard_map/ppermute | solution.py:285
  71.5 4.9 %collective-permute-start.31 = (bf16[2,64,256]{2,1,0:T(8,128)(2,1)S(1)}, bf16[2,64,256]{2,1,0:T(8,128)(2,1)S(1)}, u32[]{:S(2)}, u32[]{:S(2)}) collective-permute-start(bf16[2,64,256]{2,1,0:T(8,128)(2,1)S(1)} %mate_terms.30), channel_id=1, source_target_pairs={{0,2},{1,3},{2,0},{3,1},{4,6},{5,7},{6,4},{7,5},{8,10},{9,11},{10,... | collective-permute-start | bytes 196616 | tf_op jit(solution)/shard_map/ppermute | solution.py:285
  72.9 4.3 %collective-permute-start.32 = (bf16[2,64,256]{2,1,0:T(8,128)(2,1)S(1)}, bf16[2,64,256]{2,1,0:T(8,128)(2,1)S(1)}, u32[]{:S(2)}, u32[]{:S(2)}) collective-permute-start(bf16[2,64,256]{2,1,0:T(8,128)(2,1)S(1)} %mate_terms.31), channel_id=1, source_target_pairs={{0,3},{1,2},{2,1},{3,0},{4,7},{5,6},{6,5},{7,4},{8,11},{9,10},{10,... | collective-permute-start | bytes 196616 | tf_op jit(solution)/shard_map/ppermute | solution.py:285
  74.2 6.1 %collective-permute-start.27 = (bf16[2,64,256]{2,1,0:T(8,128)(2,1)S(1)}, bf16[2,64,256]{2,1,0:T(8,128)(2,1)S(1)}, u32[]{:S(2)}, u32[]{:S(2)}) collective-permute-start(bf16[2,64,256]{2,1,0:T(8,128)(2,1)S(1)} %mate_terms.25), channel_id=1, source_target_pairs={{0,1},{1,0},{2,3},{3,2},{4,5},{5,4},{6,7},{7,6},{8,9},{9,8},{10,11... | collective-permute-start | bytes 196616 | tf_op jit(solution)/shard_map/ppermute | solution.py:285
  74.9 5.4 %collective-permute-start.28 = (bf16[2,64,256]{2,1,0:T(8,128)(2,1)S(1)}, bf16[2,64,256]{2,1,0:T(8,128)(2,1)S(1)}, u32[]{:S(2)}, u32[]{:S(2)}) collective-permute-start(bf16[2,64,256]{2,1,0:T(8,128)(2,1)S(1)} %mate_terms.26), channel_id=1, source_target_pairs={{0,2},{1,3},{2,0},{3,1},{4,6},{5,7},{6,4},{7,5},{8,10},{9,11},{10,... | collective-permute-start | bytes 196616 | tf_op jit(solution)/shard_map/ppermute | solution.py:285
  78.1 8.0 %collective-permute-start.33 = (bf16[64,640]{1,0:T(8,128)(2,1)S(1)}, bf16[64,640]{1,0:T(8,128)(2,1)S(1)}, u32[]{:S(2)}, u32[]{:S(2)}) collective-permute-start(bf16[64,640]{1,0:T(8,128)(2,1)S(1)} %get-tuple-element.120), channel_id=1, source_target_pairs={{0,4},{1,5},{2,6},{3,7},{4,0},{5,1},{6,2},{7,3},{8,12},{9,13},{10,... | collective-permute-start | bytes 245768 | tf_op jit(solution)/shard_map/ppermute | solution.py:285
  79.4 4.4 %collective-permute-start.29 = (bf16[2,64,256]{2,1,0:T(8,128)(2,1)S(1)}, bf16[2,64,256]{2,1,0:T(8,128)(2,1)S(1)}, u32[]{:S(2)}, u32[]{:S(2)}) collective-permute-start(bf16[2,64,256]{2,1,0:T(8,128)(2,1)S(1)} %mate_terms.27), channel_id=1, source_target_pairs={{0,3},{1,2},{2,1},{3,0},{4,7},{5,6},{6,5},{7,4},{8,11},{9,10},{10,... | collective-permute-start | bytes 196616 | tf_op jit(solution)/shard_map/ppermute | solution.py:285
  84.9 4.5 %collective-permute-start.35 = (bf16[64,640]{1,0:T(8,128)(2,1)S(1)}, bf16[64,640]{1,0:T(8,128)(2,1)S(1)}, u32[]{:S(2)}, u32[]{:S(2)}) collective-permute-start(bf16[64,640]{1,0:T(8,128)(2,1)S(1)} %get-tuple-element.121), channel_id=1, source_target_pairs={{0,4},{1,5},{2,6},{3,7},{4,0},{5,1},{6,2},{7,3},{8,12},{9,13},{10,... | collective-permute-start | bytes 245768 | tf_op jit(solution)/shard_map/ppermute | solution.py:285
  86.1 6.9 %collective-permute-start.34 = (bf16[64,640]{1,0:T(8,128)(2,1)S(1)}, bf16[64,640]{1,0:T(8,128)(2,1)S(1)}, u32[]{:S(2)}, u32[]{:S(2)}) collective-permute-start(bf16[64,640]{1,0:T(8,128)(2,1)S(1)} %add_convert_fusion), channel_id=1, source_target_pairs={{0,8},{1,9},{2,10},{3,11},{4,12},{5,13},{6,14},{7,15},{8,0},{9,1},... | collective-permute-start | bytes 245768 | tf_op jit(solution)/shard_map/ppermute | solution.py:285
  (7 other events, 38.7 us)

commit v5 on v4

--- a/solution.py
+++ b/solution.py
@@ -39,24 +39,23 @@
     return jnp.where(low, x, turned), jnp.where(low, turned, x)
 
 
-def load_kernel(geno, samples, geno_out, samples_out, sems):
+def load_kernel(planes, per_owner, own_blocks, pos_ref, cov, geno, samples, geno_out, samples_out, table, listed, sems):
     copies = [
-        pltpu.make_async_copy(samples, samples_out, sems.at[0]),
-        pltpu.make_async_copy(geno, geno_out, sems.at[1]),
+        pltpu.make_async_copy(cov, listed, sems.at[0]),
+        pltpu.make_async_copy(samples, samples_out, sems.at[1]),
+        pltpu.make_async_copy(geno, geno_out, sems.at[2]),
     ]
     for copy in copies:
         copy.start()
-    for copy in copies:
-        copy.wait()
-
-
-def table_kernel(planes, per_owner, own_blocks, pos_ref, cov, table):
+    copies[0].wait()
     for mate in range(PLANE):
         batch = lax.bitwise_xor(pos_ref[0], mate)
         for turn in range(planes):
             owner = lax.bitwise_xor(pos_ref[0], turn * PLANE)
             for p in range(per_owner):
-                table[mate * planes + turn, p] = cov[batch, owner * per_owner + p] - owner * own_blocks
+                table[mate * planes + turn, p] = listed[batch, owner * per_owner + p] - owner * own_blocks
+    for copy in copies[1:]:
+        copy.wait()
 
 
 def steps_kernel(scale, own_blocks, pos_ref, cov, steps):
@@ -86,7 +85,7 @@
 
 
 def plane_sum_kernel(planes, turns, per_owner, own_blocks, table, *refs):
-    terms, sums, total = refs[:PLANE], refs[PLANE:-1], refs[-1]
+    terms, sums, total = refs[:PLANE], refs[-1 - len(turns):-1], refs[-1]
     low = low_half(terms[0].shape[1])
     total[...] = jnp.zeros_like(total)
     for i, turn in enumerate(turns):
@@ -172,6 +171,7 @@
     smem = pl.BlockSpec(memory_space=pltpu.SMEM)
     vmem = pl.BlockSpec(memory_space=pltpu.VMEM)
     hbm = pl.BlockSpec(memory_space=pltpu.HBM)
+    anywhere = pl.BlockSpec(memory_space=pl.ANY)
     params = pltpu.CompilerParams(vmem_limit_bytes=VMEM_LIMIT)
     pos = position.reshape(1)
     half = planes // 2
@@ -180,34 +180,26 @@
     dense_blocks = pltpu.VMEM((half, own_blocks, rank, 128), jnp.float32)
     by_samples = jax.ShapeDtypeStruct((rank, samples_here), jnp.float32)
     square = jax.ShapeDtypeStruct((rank, rank), jnp.float32)
-    sizes = (planes, per_owner, own_blocks)
 
     def cost(flops, bytes_accessed):
         return pl.CostEstimate(flops=flops, bytes_accessed=bytes_accessed, transcendentals=0)
 
-    table = pl.pallas_call(
-        functools.partial(table_kernel, *sizes),
-        out_shape=jax.ShapeDtypeStruct((PLANE * planes, per_owner), jnp.int32),
-        in_specs=[smem, smem],
-        out_specs=smem,
-        compiler_params=params,
-        name="block_table",
-    )(pos, coverage)
-    geno, samples = pl.pallas_call(
-        load_kernel,
+    geno, samples, table = pl.pallas_call(
+        functools.partial(load_kernel, planes, per_owner, own_blocks),
         out_shape=(
             pltpu.VMEM((samples_here, snps_here), jnp.bfloat16),
             pltpu.VMEM((rank, samples_here), jnp.float32),
+            pltpu.SMEM((PLANE * planes, per_owner), jnp.int32),
         ),
-        in_specs=[hbm, hbm],
-        out_specs=(vmem, vmem),
-        scratch_shapes=[pltpu.SemaphoreType.DMA((2,))],
+        in_specs=[smem, hbm, hbm, hbm],
+        out_specs=(vmem, vmem, smem),
+        scratch_shapes=[pltpu.SMEM(coverage.shape, jnp.int32), pltpu.SemaphoreType.DMA((3,))],
         compiler_params=pltpu.CompilerParams(
             vmem_limit_bytes=58 * 1024 * 1024 - 2 * samples_here * snps_here
         ),
         cost_estimate=cost(0, 2 * samples_here * snps_here),
         name="load_batch",
-    )(genotypes, sample_factors.T)
+    )(pos, coverage, genotypes, sample_factors.T)
 
     snp_step = pl.pallas_call(
         functools.partial(steps_kernel, 0.5 * math.sqrt(rank) / samples_here, own_blocks),
@@ -231,20 +223,20 @@
             name="pick_blocks",
         )(table, *[held[turn] for turn in turns])
 
-    def plane_sum(turns, terms):
+    def plane_sum(turns, terms, after):
         sums = pl.pallas_call(
             functools.partial(plane_sum_kernel, planes, turns, per_owner, own_blocks),
             out_shape=tuple(
                 jax.ShapeDtypeStruct((rank, own_snps), jnp.bfloat16 if turn % 2 else jnp.float32)
                 for turn in turns
             ),
-            in_specs=[smem] + [vmem] * PLANE,
+            in_specs=[smem] + [vmem] * PLANE + [anywhere] * len(after),
             out_specs=(vmem,) * half,
             scratch_shapes=[dense_blocks],
             compiler_params=params,
             cost_estimate=small,
             name="plane_sum",
-        )(table, *terms)
+        )(table, *terms, *after)
         return dict(zip(turns, sums))
 
     def product(turns, mates, panels, before):
@@ -292,7 +284,10 @@
         held = {0: snps.astype(jnp.bfloat16)}
         for turn in sorted(range(1, planes), key=lambda turn: (turn & (turn - 1), -turn)):
             bit = turn & -turn
-            held[turn] = swap(held[turn ^ bit], bit * PLANE)
+            source = held[turn ^ bit]
+            if iteration == 0 and turn != bit:
+                source, _ = lax.optimization_barrier((source, samples))
+            held[turn] = swap(source, bit * PLANE)
         panels = {}
         for turns in (near, far):
             packets = pick(turns, held)
@@ -303,12 +298,13 @@
         ):
             partial = product(turns, mates, panels, partial)
         samples, samples_bf16, sample_gram = sample_update(samples, *partial)
-        sums = {}
+        terms, sent = {}, {}
         for turns in (far, near):
-            terms = {}
             for mate in (2, 3, 1, 0):
-                terms[mate] = to_mate(terms_for(turns, mate, samples_bf16, sample_gram, panels), mate)
-            sums.update(plane_sum(turns, [terms[mate] for mate in range(PLANE)]))
+                terms[turns, mate] = terms_for(turns, mate, samples_bf16, sample_gram, panels)
+                sent[turns, mate] = to_mate(terms[turns, mate], mate)
+        sums = plane_sum(far, [sent[far, mate] for mate in range(PLANE)], [terms[near, mate] for mate in range(PLANE)])
+        sums.update(plane_sum(near, [sent[near, mate] for mate in range(PLANE)], []))
         for turn in range(planes - 1, 0, -1):
             bit = turn & -turn
             arrived = swap(sums[turn].astype(jnp.bfloat16), bit * PLANE)

time: 94 us -> 87.2 us (0.928)
  Pallas kernels: 26.9 us -> 20.2 us
  waiting for transfers between devices: 27.5 us -> 30.7 us
  starting transfers between devices: 35.8 us -> 33.3 us
    ppermute x36, waiting for transfers between devices: 27.5 us -> 30.7 us  [swap(): return lax.ppermute(x, 'rows', [(r, r ^ turn) for r in range(devices)])]
    pallas_call x4, Pallas kernels: 3.34 us -> 0.67 us  [pick(): pl.pallas_call(functools.partial(pick_kernel, planes, turns, per_owner, o...]
    pallas_call x4, Pallas kernels: 4.03 us -> 1.49 us  [plane_sum(): pl.pallas_call(functools.partial(plane_sum_kernel, planes, turns, per_own...]
    ppermute x36, starting transfers between devices: 35.8 us -> 33.3 us  [swap(): return lax.ppermute(x, 'rows', [(r, r ^ turn) for r in range(devices)])]
    pallas_call x2 -> x1, Pallas kernels: 5.03 us -> 3.51 us  [on_device(): pl.pallas_call(functools.partial(load_kernel, planes, per_owner, own_bloc...]
  transfers between devices with their start and end apart: 36 -> 36, of which waited for: 13 -> 17; matrix products, arithmetic and copies ran while one was open for 0% -> 0% of each run, Pallas kernels for 25% -> 17%
where the time goes in v5:
time: 87.2 us; the launch traced here: 87 us
  starting transfers between devices  33.3 us (38%)
  waiting for transfers between devices  30.7 us (35%)
  Pallas kernels  20.2 us (23%)
  other arithmetic  1.77 us (2%)
  between operations  0.99 us (1%)
    ppermute x36, starting transfers between devices, swap(): return lax.ppermute(x, 'rows', [(r, r ^ turn) for r in range(devices)])  33.3 us
    ppermute x36, waiting for transfers between devices, swap(): return lax.ppermute(x, 'rows', [(r, r ^ turn) for r in range(devices)])  30.7 us
    pallas_call x14, Pallas kernels, product(): pl.pallas_call(functools.partial(product_kernel, turns, mates, not before...  7.16 us
    pallas_call x16, Pallas kernels, terms_for(): pl.pallas_call(functools.partial(term_kernel, turns, mate), out_shape=pac...  5.89 us
    pallas_call x1, Pallas kernels, on_device(): pl.pallas_call(functools.partial(load_kernel, planes, per_owner, own_bloc...  3.51 us
  transfers between devices with their start and end apart: 36, of which 17 were waited for; matrix products, arithmetic and copies ran while one was open for 0% of the time, Pallas kernels for 17%

profile of v5, /device:TPU:0, one launch (start us, length us, event | category | flops | bytes accessed | tf_op | source)
XLA Modules:
  0.0 87.0 jit_solution(1232144976003570556)
XLA Ops:
  0.6 0.9 %convert_bitcast_fusion.refs_0_ = bf16[64,640]{1,0:T(8,128)(2,1)S(1)} fusion(f32[640,64]{0,1:T(8,128)} %param.6), kind=kLoop, calls=%fused_computation.4 | loop fusion | flops 40960 | bytes 245760 | tf_op jit(solution)/shard_map/convert_element_type | solution.py:284
  1.6 4.1 %collective-permute-start = (bf16[64,640]{1,0:T(8,128)(2,1)S(1)}, bf16[64,640]{1,0:T(8,128)(2,1)S(1)}, u32[]{:S(2)}, u32[]{:S(2)}) collective-permute-start(bf16[64,640]{1,0:T(8,128)(2,1)S(1)} %convert_bitcast_fusion.refs_0_), channel_id=1, source_target_pairs={{0,8},{1,9},{2,10},{3,11},{4,12},{5,13},{6,14},{7,15},{8,0},{9,1},... | collective-permute-start | bytes 245768 | tf_op jit(solution)/shard_map/ppermute | solution.py:277
  5.7 1.6 %collective-permute-start.5 = (bf16[64,640]{1,0:T(8,128)(2,1)S(1)}, bf16[64,640]{1,0:T(8,128)(2,1)S(1)}, u32[]{:S(2)}, u32[]{:S(2)}) collective-permute-start(bf16[64,640]{1,0:T(8,128)(2,1)S(1)} %convert_bitcast_fusion.refs_0_), channel_id=1, source_target_pairs={{0,4},{1,5},{2,6},{3,7},{4,0},{5,1},{6,2},{7,3},{8,12},{9,13},{10,... | collective-permute-start | bytes 245768 | tf_op jit(solution)/shard_map/ppermute | solution.py:277
  7.2 3.5 %load_batch.1 = (bf16[1024,4096]{1,0:T(8,128)(2,1)S(1)}, f32[64,1024]{1,0:T(8,128)S(1)}, s32[16,4]{1,0:T(8,128)S(4)}) custom-call(s32[1]{0:T(128)} %bitcast.pos_ref, s32[16,64]{1,0:T(8,128)} %cov.3, bf16[1024,4096]{1,0:T(8,128)(2,1)} %geno.1, f32[64,1024]{1,0:T(8,128)} %bitcast.13), custom_call_target="tpu_custom_call" | custom-call | bytes 8388608 | tf_op jit(solution)/shard_map/load_batch/pallas_call | solution.py:187
  11.5 1.6 %collective-permute-start.6 = (bf16[2,64,256]{2,1,0:T(8,128)(2,1)S(1)}, bf16[2,64,256]{2,1,0:T(8,128)(2,1)S(1)}, u32[]{:S(2)}, u32[]{:S(2)}) collective-permute-start(bf16[2,64,256]{2,1,0:T(8,128)(2,1)S(1)} %get-tuple-element.71), channel_id=1, source_target_pairs={{0,2},{1,3},{2,0},{3,1},{4,6},{5,7},{6,4},{7,5},{8,10},{9,11},{10,... | collective-permute-start | bytes 196616 | tf_op jit(solution)/shard_map/ppermute | solution.py:277
  13.9 1.4 %collective-permute-done.1.refs_1_ = bf16[64,640]{1,0:T(8,128)(2,1)S(1)} collective-permute-done((bf16[64,640]{1,0:T(8,128)(2,1)S(1)}, bf16[64,640]{1,0:T(8,128)(2,1)S(1)}, u32[]{:S(2)}, u32[]{:S(2)}) %collective-permute-start.1) | collective-permute-done | bytes 81952 | tf_op jit(solution)/shard_map/ppermute | solution.py:277
  15.6 1.5 %collective-permute-start.3 = (bf16[2,64,256]{2,1,0:T(8,128)(2,1)S(1)}, bf16[2,64,256]{2,1,0:T(8,128)(2,1)S(1)}, u32[]{:S(2)}, u32[]{:S(2)}) collective-permute-start(bf16[2,64,256]{2,1,0:T(8,128)(2,1)S(1)} %get-tuple-element.69), channel_id=1, source_target_pairs={{0,2},{1,3},{2,0},{3,1},{4,6},{5,7},{6,4},{7,5},{8,10},{9,11},{10,... | collective-permute-start | bytes 196616 | tf_op jit(solution)/shard_map/ppermute | solution.py:277
  19.7 1.6 %collective-permute-done.3.refs_0_.packet = bf16[2,64,256]{2,1,0:T(8,128)(2,1)S(1)} collective-permute-done((bf16[2,64,256]{2,1,0:T(8,128)(2,1)S(1)}, bf16[2,64,256]{2,1,0:T(8,128)(2,1)S(1)}, u32[]{:S(2)}, u32[]{:S(2)}) %collective-permute-start.3) | collective-permute-done | bytes 65568 | tf_op jit(solution)/shard_map/ppermute | solution.py:277
  25.5 1.1 %collective-permute-start.14 = (bf16[2,64,256]{2,1,0:T(8,128)(2,1)S(1)}, bf16[2,64,256]{2,1,0:T(8,128)(2,1)S(1)}, u32[]{:S(2)}, u32[]{:S(2)}) collective-permute-start(bf16[2,64,256]{2,1,0:T(8,128)(2,1)S(1)} %mate_terms.23), channel_id=1, source_target_pairs={{0,3},{1,2},{2,1},{3,0},{4,7},{5,6},{6,5},{7,4},{8,11},{9,10},{10,... | collective-permute-start | bytes 196616 | tf_op jit(solution)/shard_map/ppermute | solution.py:277
  27.7 1.4 %collective-permute-done.13.refs_2_ = bf16[2,64,256]{2,1,0:T(8,128)(2,1)S(1)} collective-permute-done((bf16[2,64,256]{2,1,0:T(8,128)(2,1)S(1)}, bf16[2,64,256]{2,1,0:T(8,128)(2,1)S(1)}, u32[]{:S(2)}, u32[]{:S(2)}) %collective-permute-start.13) | collective-permute-done | bytes 65568 | tf_op jit(solution)/shard_map/ppermute | solution.py:277
  30.3 1.0 %collective-permute-start.15 = (bf16[64,640]{1,0:T(8,128)(2,1)S(1)}, bf16[64,640]{1,0:T(8,128)(2,1)S(1)}, u32[]{:S(2)}, u32[]{:S(2)}) collective-permute-start(bf16[64,640]{1,0:T(8,128)(2,1)S(1)} %get-tuple-element.95), channel_id=1, source_target_pairs={{0,4},{1,5},{2,6},{3,7},{4,0},{5,1},{6,2},{7,3},{8,12},{9,13},{10,... | collective-permute-start | bytes 245768 | tf_op jit(solution)/shard_map/ppermute | solution.py:277
  31.3 1.0 %collective-permute-start.10 = (bf16[2,64,256]{2,1,0:T(8,128)(2,1)S(1)}, bf16[2,64,256]{2,1,0:T(8,128)(2,1)S(1)}, u32[]{:S(2)}, u32[]{:S(2)}) collective-permute-start(bf16[2,64,256]{2,1,0:T(8,128)(2,1)S(1)} %mate_terms.18.refs_6_), channel_id=1, source_target_pairs={{0,2},{1,3},{2,0},{3,1},{4,6},{5,7},{6,4},{7,5},{8,10},{9,11},{10,... | collective-permute-start | bytes 196616 | tf_op jit(solution)/shard_map/ppermute | solution.py:277
  33.2 3.0 %collective-permute-done.10.refs_2_ = bf16[2,64,256]{2,1,0:T(8,128)(2,1)S(1)} collective-permute-done((bf16[2,64,256]{2,1,0:T(8,128)(2,1)S(1)}, bf16[2,64,256]{2,1,0:T(8,128)(2,1)S(1)}, u32[]{:S(2)}, u32[]{:S(2)}) %collective-permute-start.10) | collective-permute-done | bytes 65568 | tf_op jit(solution)/shard_map/ppermute | solution.py:277
  37.2 1.1 %collective-permute-start.17 = (bf16[64,640]{1,0:T(8,128)(2,1)S(1)}, bf16[64,640]{1,0:T(8,128)(2,1)S(1)}, u32[]{:S(2)}, u32[]{:S(2)}) collective-permute-start(bf16[64,640]{1,0:T(8,128)(2,1)S(1)} %get-tuple-element.96), channel_id=1, source_target_pairs={{0,4},{1,5},{2,6},{3,7},{4,0},{5,1},{6,2},{7,3},{8,12},{9,13},{10,... | collective-permute-start | bytes 245768 | tf_op jit(solution)/shard_map/ppermute | solution.py:277
  38.4 2.1 %collective-permute-start.16 = (bf16[64,640]{1,0:T(8,128)(2,1)S(1)}, bf16[64,640]{1,0:T(8,128)(2,1)S(1)}, u32[]{:S(2)}, u32[]{:S(2)}) collective-permute-start(bf16[64,640]{1,0:T(8,128)(2,1)S(1)} %add_convert_fusion.1), channel_id=1, source_target_pairs={{0,8},{1,9},{2,10},{3,11},{4,12},{5,13},{6,14},{7,15},{8,0},{9,1},... | collective-permute-start | bytes 245768 | tf_op jit(solution)/shard_map/ppermute | solution.py:277
  40.6 1.2 %collective-permute-done.17 = bf16[64,640]{1,0:T(8,128)(2,1)S(1)} collective-permute-done((bf16[64,640]{1,0:T(8,128)(2,1)S(1)}, bf16[64,640]{1,0:T(8,128)(2,1)S(1)}, u32[]{:S(2)}, u32[]{:S(2)}) %collective-permute-start.17) | collective-permute-done | bytes 81952 | tf_op jit(solution)/shard_map/ppermute | solution.py:277
  41.8 3.6 %collective-permute-done.16 = bf16[64,640]{1,0:T(8,128)(2,1)S(1)} collective-permute-done((bf16[64,640]{1,0:T(8,128)(2,1)S(1)}, bf16[64,640]{1,0:T(8,128)(2,1)S(1)}, u32[]{:S(2)}, u32[]{:S(2)}) %collective-permute-start.16) | collective-permute-done | bytes 81952 | tf_op jit(solution)/shard_map/ppermute | solution.py:277
  46.0 2.6 %collective-permute-start.23 = (bf16[64,640]{1,0:T(8,128)(2,1)S(1)}, bf16[64,640]{1,0:T(8,128)(2,1)S(1)}, u32[]{:S(2)}, u32[]{:S(2)}) collective-permute-start(bf16[64,640]{1,0:T(8,128)(2,1)S(1)} %fusion.refs_0_), channel_id=1, source_target_pairs={{0,4},{1,5},{2,6},{3,7},{4,0},{5,1},{6,2},{7,3},{8,12},{9,13},{10,... | collective-permute-start | bytes 245768 | tf_op jit(solution)/shard_map/ppermute | solution.py:277
  48.6 3.2 %collective-permute-done.18.refs_0_ = bf16[64,640]{1,0:T(8,128)(2,1)S(1)} collective-permute-done((bf16[64,640]{1,0:T(8,128)(2,1)S(1)}, bf16[64,640]{1,0:T(8,128)(2,1)S(1)}, u32[]{:S(2)}, u32[]{:S(2)}) %collective-permute-start.18) | collective-permute-done | bytes 81952 | tf_op jit(solution)/shard_map/ppermute | solution.py:277
  52.1 1.1 %collective-permute-start.24 = (bf16[2,64,256]{2,1,0:T(8,128)(2,1)S(1)}, bf16[2,64,256]{2,1,0:T(8,128)(2,1)S(1)}, u32[]{:S(2)}, u32[]{:S(2)}) collective-permute-start(bf16[2,64,256]{2,1,0:T(8,128)(2,1)S(1)} %get-tuple-element.100), channel_id=1, source_target_pairs={{0,2},{1,3},{2,0},{3,1},{4,6},{5,7},{6,4},{7,5},{8,10},{9,11},{10,... | collective-permute-start | bytes 196616 | tf_op jit(solution)/shard_map/ppermute | solution.py:277
  54.4 1.9 %collective-permute-done.19.refs_1_ = bf16[64,640]{1,0:T(8,128)(2,1)S(1)} collective-permute-done((bf16[64,640]{1,0:T(8,128)(2,1)S(1)}, bf16[64,640]{1,0:T(8,128)(2,1)S(1)}, u32[]{:S(2)}, u32[]{:S(2)}) %collective-permute-start.19) | collective-permute-done | bytes 81952 | tf_op jit(solution)/shard_map/ppermute | solution.py:277
  56.5 1.0 %collective-permute-start.21 = (bf16[2,64,256]{2,1,0:T(8,128)(2,1)S(1)}, bf16[2,64,256]{2,1,0:T(8,128)(2,1)S(1)}, u32[]{:S(2)}, u32[]{:S(2)}) collective-permute-start(bf16[2,64,256]{2,1,0:T(8,128)(2,1)S(1)} %get-tuple-element.98), channel_id=1, source_target_pairs={{0,2},{1,3},{2,0},{3,1},{4,6},{5,7},{6,4},{7,5},{8,10},{9,11},{10,... | collective-permute-start | bytes 196616 | tf_op jit(solution)/shard_map/ppermute | solution.py:277
  62.5 1.0 %sample_update.3 = (f32[64,1024]{1,0:T(8,128)}, bf16[64,1024]{1,0:T(8,128)(2,1)S(1)}, f32[64,64]{1,0:T(8,128)S(1)}) custom-call(f32[64,1024]{1,0:T(8,128)S(1)} %get-tuple-element.90.samples, f32[64,1024]{1,0:T(8,128)S(1)} %get-tuple-element.117.gradient, f32[64,64]{1,0:T(8,128)S(1)} %get-tuple-element.118.gram), custom_call_target="tpu_custom_call" | custom-call | tf_op jit(solution)/shard_map/sample_update/pallas_call | solution.py:255
  65.1 1.1 %collective-permute-start.31 = (bf16[2,64,256]{2,1,0:T(8,128)(2,1)S(1)}, bf16[2,64,256]{2,1,0:T(8,128)(2,1)S(1)}, u32[]{:S(2)}, u32[]{:S(2)}) collective-permute-start(bf16[2,64,256]{2,1,0:T(8,128)(2,1)S(1)} %mate_terms.30), channel_id=1, source_target_pairs={{0,2},{1,3},{2,0},{3,1},{4,6},{5,7},{6,4},{7,5},{8,10},{9,11},{10,... | collective-permute-start | bytes 196616 | tf_op jit(solution)/shard_map/ppermute | solution.py:277
  68.5 1.1 %collective-permute-done.31.refs_2_ = bf16[2,64,256]{2,1,0:T(8,128)(2,1)S(1)} collective-permute-done((bf16[2,64,256]{2,1,0:T(8,128)(2,1)S(1)}, bf16[2,64,256]{2,1,0:T(8,128)(2,1)S(1)}, u32[]{:S(2)}, u32[]{:S(2)}) %collective-permute-start.31) | collective-permute-done | bytes 65568 | tf_op jit(solution)/shard_map/ppermute | solution.py:277
  69.6 1.2 %collective-permute-done.32.refs_3_ = bf16[2,64,256]{2,1,0:T(8,128)(2,1)S(1)} collective-permute-done((bf16[2,64,256]{2,1,0:T(8,128)(2,1)S(1)}, bf16[2,64,256]{2,1,0:T(8,128)(2,1)S(1)}, u32[]{:S(2)}, u32[]{:S(2)}) %collective-permute-start.32) | collective-permute-done | bytes 65568 | tf_op jit(solution)/shard_map/ppermute | solution.py:277
  71.1 1.3 %collective-permute-start.33 = (bf16[64,640]{1,0:T(8,128)(2,1)S(1)}, bf16[64,640]{1,0:T(8,128)(2,1)S(1)}, u32[]{:S(2)}, u32[]{:S(2)}) collective-permute-start(bf16[64,640]{1,0:T(8,128)(2,1)S(1)} %get-tuple-element.124), channel_id=1, source_target_pairs={{0,4},{1,5},{2,6},{3,7},{4,0},{5,1},{6,2},{7,3},{8,12},{9,13},{10,... | collective-permute-start | bytes 245768 | tf_op jit(solution)/shard_map/ppermute | solution.py:277
  72.4 1.0 %collective-permute-start.28 = (bf16[2,64,256]{2,1,0:T(8,128)(2,1)S(1)}, bf16[2,64,256]{2,1,0:T(8,128)(2,1)S(1)}, u32[]{:S(2)}, u32[]{:S(2)}) collective-permute-start(bf16[2,64,256]{2,1,0:T(8,128)(2,1)S(1)} %mate_terms.26.refs_6_), channel_id=1, source_target_pairs={{0,2},{1,3},{2,0},{3,1},{4,6},{5,7},{6,4},{7,5},{8,10},{9,11},{10,... | collective-permute-start | bytes 196616 | tf_op jit(solution)/shard_map/ppermute | solution.py:277
  74.3 3.0 %collective-permute-done.28.refs_2_ = bf16[2,64,256]{2,1,0:T(8,128)(2,1)S(1)} collective-permute-done((bf16[2,64,256]{2,1,0:T(8,128)(2,1)S(1)}, bf16[2,64,256]{2,1,0:T(8,128)(2,1)S(1)}, u32[]{:S(2)}, u32[]{:S(2)}) %collective-permute-start.28) | collective-permute-done | bytes 65568 | tf_op jit(solution)/shard_map/ppermute | solution.py:277
  79.2 1.9 %collective-permute-start.34 = (bf16[64,640]{1,0:T(8,128)(2,1)S(1)}, bf16[64,640]{1,0:T(8,128)(2,1)S(1)}, u32[]{:S(2)}, u32[]{:S(2)}) collective-permute-start(bf16[64,640]{1,0:T(8,128)(2,1)S(1)} %add_convert_fusion), channel_id=1, source_target_pairs={{0,8},{1,9},{2,10},{3,11},{4,12},{5,13},{6,14},{7,15},{8,0},{9,1},... | collective-permute-start | bytes 245768 | tf_op jit(solution)/shard_map/ppermute | solution.py:277
  81.1 2.7 %collective-permute-done.35 = bf16[64,640]{1,0:T(8,128)(2,1)S(1)} collective-permute-done((bf16[64,640]{1,0:T(8,128)(2,1)S(1)}, bf16[64,640]{1,0:T(8,128)(2,1)S(1)}, u32[]{:S(2)}, u32[]{:S(2)}) %collective-permute-start.35) | collective-permute-done | bytes 81952 | tf_op jit(solution)/shard_map/ppermute | solution.py:277
  83.8 2.4 %collective-permute-done.34 = bf16[64,640]{1,0:T(8,128)(2,1)S(1)} collective-permute-done((bf16[64,640]{1,0:T(8,128)(2,1)S(1)}, bf16[64,640]{1,0:T(8,128)(2,1)S(1)}, u32[]{:S(2)}, u32[]{:S(2)}) %collective-permute-start.34) | collective-permute-done | bytes 81952 | tf_op jit(solution)/shard_map/ppermute | solution.py:277
  (91 shorter events, 27.6 us)
Async XLA Ops:
  1.6 9.2 %collective-permute-start = (bf16[64,640]{1,0:T(8,128)(2,1)S(1)}, bf16[64,640]{1,0:T(8,128)(2,1)S(1)}, u32[]{:S(2)}, u32[]{:S(2)}) collective-permute-start(bf16[64,640]{1,0:T(8,128)(2,1)S(1)} %convert_bitcast_fusion.refs_0_), channel_id=1, source_target_pairs={{0,8},{1,9},{2,10},{3,11},{4,12},{5,13},{6,14},{7,15},{8,0},{9,1},... | collective-permute-start | bytes 245768 | tf_op jit(solution)/shard_map/ppermute | solution.py:277
  5.7 5.6 %collective-permute-start.5 = (bf16[64,640]{1,0:T(8,128)(2,1)S(1)}, bf16[64,640]{1,0:T(8,128)(2,1)S(1)}, u32[]{:S(2)}, u32[]{:S(2)}) collective-permute-start(bf16[64,640]{1,0:T(8,128)(2,1)S(1)} %convert_bitcast_fusion.refs_0_), channel_id=1, source_target_pairs={{0,4},{1,5},{2,6},{3,7},{4,0},{5,1},{6,2},{7,3},{8,12},{9,13},{10,... | collective-permute-start | bytes 245768 | tf_op jit(solution)/shard_map/ppermute | solution.py:277
  10.8 4.5 %collective-permute-start.1 = (bf16[64,640]{1,0:T(8,128)(2,1)S(1)}, bf16[64,640]{1,0:T(8,128)(2,1)S(1)}, u32[]{:S(2)}, u32[]{:S(2)}) collective-permute-start(bf16[64,640]{1,0:T(8,128)(2,1)S(1)} %collective-permute-done.refs_0_), channel_id=1, source_target_pairs={{0,4},{1,5},{2,6},{3,7},{4,0},{5,1},{6,2},{7,3},{8,12},{9,13},{10,... | collective-permute-start | bytes 245768 | tf_op jit(solution)/shard_map/ppermute | solution.py:277
  11.5 6.1 %collective-permute-start.8 = (bf16[2,64,256]{2,1,0:T(8,128)(2,1)S(1)}, bf16[2,64,256]{2,1,0:T(8,128)(2,1)S(1)}, u32[]{:S(2)}, u32[]{:S(2)}) collective-permute-start(bf16[2,64,256]{2,1,0:T(8,128)(2,1)S(1)} %get-tuple-element.73), channel_id=1, source_target_pairs={{0,1},{1,0},{2,3},{3,2},{4,5},{5,4},{6,7},{7,6},{8,9},{9,8},{10,11... | collective-permute-start | bytes 196616 | tf_op jit(solution)/shard_map/ppermute | solution.py:277
  11.5 6.8 %collective-permute-start.6 = (bf16[2,64,256]{2,1,0:T(8,128)(2,1)S(1)}, bf16[2,64,256]{2,1,0:T(8,128)(2,1)S(1)}, u32[]{:S(2)}, u32[]{:S(2)}) collective-permute-start(bf16[2,64,256]{2,1,0:T(8,128)(2,1)S(1)} %get-tuple-element.71), channel_id=1, source_target_pairs={{0,2},{1,3},{2,0},{3,1},{4,6},{5,7},{6,4},{7,5},{8,10},{9,11},{10,... | collective-permute-start | bytes 196616 | tf_op jit(solution)/shard_map/ppermute | solution.py:277
  13.1 5.3 %collective-permute-start.7 = (bf16[2,64,256]{2,1,0:T(8,128)(2,1)S(1)}, bf16[2,64,256]{2,1,0:T(8,128)(2,1)S(1)}, u32[]{:S(2)}, u32[]{:S(2)}) collective-permute-start(bf16[2,64,256]{2,1,0:T(8,128)(2,1)S(1)} %get-tuple-element.72), channel_id=1, source_target_pairs={{0,3},{1,2},{2,1},{3,0},{4,7},{5,6},{6,5},{7,4},{8,11},{9,10},{10,... | collective-permute-start | bytes 196616 | tf_op jit(solution)/shard_map/ppermute | solution.py:277
  15.4 6.3 %collective-permute-start.2 = (bf16[2,64,256]{2,1,0:T(8,128)(2,1)S(1)}, bf16[2,64,256]{2,1,0:T(8,128)(2,1)S(1)}, u32[]{:S(2)}, u32[]{:S(2)}) collective-permute-start(bf16[2,64,256]{2,1,0:T(8,128)(2,1)S(1)} %get-tuple-element.68), channel_id=1, source_target_pairs={{0,3},{1,2},{2,1},{3,0},{4,7},{5,6},{6,5},{7,4},{8,11},{9,10},{10,... | collective-permute-start | bytes 196616 | tf_op jit(solution)/shard_map/ppermute | solution.py:277
  15.6 5.7 %collective-permute-start.3 = (bf16[2,64,256]{2,1,0:T(8,128)(2,1)S(1)}, bf16[2,64,256]{2,1,0:T(8,128)(2,1)S(1)}, u32[]{:S(2)}, u32[]{:S(2)}) collective-permute-start(bf16[2,64,256]{2,1,0:T(8,128)(2,1)S(1)} %get-tuple-element.69), channel_id=1, source_target_pairs={{0,2},{1,3},{2,0},{3,1},{4,6},{5,7},{6,4},{7,5},{8,10},{9,11},{10,... | collective-permute-start | bytes 196616 | tf_op jit(solution)/shard_map/ppermute | solution.py:277
  23.8 3.9 %collective-permute-start.12 = (bf16[2,64,256]{2,1,0:T(8,128)(2,1)S(1)}, bf16[2,64,256]{2,1,0:T(8,128)(2,1)S(1)}, u32[]{:S(2)}, u32[]{:S(2)}) collective-permute-start(bf16[2,64,256]{2,1,0:T(8,128)(2,1)S(1)} %mate_terms.21), channel_id=1, source_target_pairs={{0,1},{1,0},{2,3},{3,2},{4,5},{5,4},{6,7},{7,6},{8,9},{9,8},{10,11... | collective-permute-start | bytes 196616 | tf_op jit(solution)/shard_map/ppermute | solution.py:277
  24.3 4.8 %collective-permute-start.13 = (bf16[2,64,256]{2,1,0:T(8,128)(2,1)S(1)}, bf16[2,64,256]{2,1,0:T(8,128)(2,1)S(1)}, u32[]{:S(2)}, u32[]{:S(2)}) collective-permute-start(bf16[2,64,256]{2,1,0:T(8,128)(2,1)S(1)} %mate_terms.22), channel_id=1, source_target_pairs={{0,2},{1,3},{2,0},{3,1},{4,6},{5,7},{6,4},{7,5},{8,10},{9,11},{10,... | collective-permute-start | bytes 196616 | tf_op jit(solution)/shard_map/ppermute | solution.py:277
  25.5 4.4 %collective-permute-start.14 = (bf16[2,64,256]{2,1,0:T(8,128)(2,1)S(1)}, bf16[2,64,256]{2,1,0:T(8,128)(2,1)S(1)}, u32[]{:S(2)}, u32[]{:S(2)}) collective-permute-start(bf16[2,64,256]{2,1,0:T(8,128)(2,1)S(1)} %mate_terms.23), channel_id=1, source_target_pairs={{0,3},{1,2},{2,1},{3,0},{4,7},{5,6},{6,5},{7,4},{8,11},{9,10},{10,... | collective-permute-start | bytes 196616 | tf_op jit(solution)/shard_map/ppermute | solution.py:277
  30.3 8.1 %collective-permute-start.15 = (bf16[64,640]{1,0:T(8,128)(2,1)S(1)}, bf16[64,640]{1,0:T(8,128)(2,1)S(1)}, u32[]{:S(2)}, u32[]{:S(2)}) collective-permute-start(bf16[64,640]{1,0:T(8,128)(2,1)S(1)} %get-tuple-element.95), channel_id=1, source_target_pairs={{0,4},{1,5},{2,6},{3,7},{4,0},{5,1},{6,2},{7,3},{8,12},{9,13},{10,... | collective-permute-start | bytes 245768 | tf_op jit(solution)/shard_map/ppermute | solution.py:277
  31.3 4.9 %collective-permute-start.10 = (bf16[2,64,256]{2,1,0:T(8,128)(2,1)S(1)}, bf16[2,64,256]{2,1,0:T(8,128)(2,1)S(1)}, u32[]{:S(2)}, u32[]{:S(2)}) collective-permute-start(bf16[2,64,256]{2,1,0:T(8,128)(2,1)S(1)} %mate_terms.18.refs_6_), channel_id=1, source_target_pairs={{0,2},{1,3},{2,0},{3,1},{4,6},{5,7},{6,4},{7,5},{8,10},{9,11},{10,... | collective-permute-start | bytes 196616 | tf_op jit(solution)/shard_map/ppermute | solution.py:277
  32.3 4.5 %collective-permute-start.11 = (bf16[2,64,256]{2,1,0:T(8,128)(2,1)S(1)}, bf16[2,64,256]{2,1,0:T(8,128)(2,1)S(1)}, u32[]{:S(2)}, u32[]{:S(2)}) collective-permute-start(bf16[2,64,256]{2,1,0:T(8,128)(2,1)S(1)} %mate_terms.19.refs_7_), channel_id=1, source_target_pairs={{0,3},{1,2},{2,1},{3,0},{4,7},{5,6},{6,5},{7,4},{8,11},{9,10},{10,... | collective-permute-start | bytes 196616 | tf_op jit(solution)/shard_map/ppermute | solution.py:277
  37.2 4.6 %collective-permute-start.17 = (bf16[64,640]{1,0:T(8,128)(2,1)S(1)}, bf16[64,640]{1,0:T(8,128)(2,1)S(1)}, u32[]{:S(2)}, u32[]{:S(2)}) collective-permute-start(bf16[64,640]{1,0:T(8,128)(2,1)S(1)} %get-tuple-element.96), channel_id=1, source_target_pairs={{0,4},{1,5},{2,6},{3,7},{4,0},{5,1},{6,2},{7,3},{8,12},{9,13},{10,... | collective-permute-start | bytes 245768 | tf_op jit(solution)/shard_map/ppermute | solution.py:277
  38.4 7.1 %collective-permute-start.16 = (bf16[64,640]{1,0:T(8,128)(2,1)S(1)}, bf16[64,640]{1,0:T(8,128)(2,1)S(1)}, u32[]{:S(2)}, u32[]{:S(2)}) collective-permute-start(bf16[64,640]{1,0:T(8,128)(2,1)S(1)} %add_convert_fusion.1), channel_id=1, source_target_pairs={{0,8},{1,9},{2,10},{3,11},{4,12},{5,13},{6,14},{7,15},{8,0},{9,1},... | collective-permute-start | bytes 245768 | tf_op jit(solution)/shard_map/ppermute | solution.py:277
  45.5 6.3 %collective-permute-start.18 = (bf16[64,640]{1,0:T(8,128)(2,1)S(1)}, bf16[64,640]{1,0:T(8,128)(2,1)S(1)}, u32[]{:S(2)}, u32[]{:S(2)}) collective-permute-start(bf16[64,640]{1,0:T(8,128)(2,1)S(1)} %fusion.refs_0_), channel_id=1, source_target_pairs={{0,8},{1,9},{2,10},{3,11},{4,12},{5,13},{6,14},{7,15},{8,0},{9,1},... | collective-permute-start | bytes 245768 | tf_op jit(solution)/shard_map/ppermute | solution.py:277
  46.0 5.9 %collective-permute-start.23 = (bf16[64,640]{1,0:T(8,128)(2,1)S(1)}, bf16[64,640]{1,0:T(8,128)(2,1)S(1)}, u32[]{:S(2)}, u32[]{:S(2)}) collective-permute-start(bf16[64,640]{1,0:T(8,128)(2,1)S(1)} %fusion.refs_0_), channel_id=1, source_target_pairs={{0,4},{1,5},{2,6},{3,7},{4,0},{5,1},{6,2},{7,3},{8,12},{9,13},{10,... | collective-permute-start | bytes 245768 | tf_op jit(solution)/shard_map/ppermute | solution.py:277
  51.8 4.4 %collective-permute-start.19 = (bf16[64,640]{1,0:T(8,128)(2,1)S(1)}, bf16[64,640]{1,0:T(8,128)(2,1)S(1)}, u32[]{:S(2)}, u32[]{:S(2)}) collective-permute-start(bf16[64,640]{1,0:T(8,128)(2,1)S(1)} %collective-permute-done.18.refs_0_), channel_id=1, source_target_pairs={{0,4},{1,5},{2,6},{3,7},{4,0},{5,1},{6,2},{7,3},{8,12},{9,13},{10,... | collective-permute-start | bytes 245768 | tf_op jit(solution)/shard_map/ppermute | solution.py:277
  52.0 6.0 %collective-permute-start.26 = (bf16[2,64,256]{2,1,0:T(8,128)(2,1)S(1)}, bf16[2,64,256]{2,1,0:T(8,128)(2,1)S(1)}, u32[]{:S(2)}, u32[]{:S(2)}) collective-permute-start(bf16[2,64,256]{2,1,0:T(8,128)(2,1)S(1)} %get-tuple-element.102), channel_id=1, source_target_pairs={{0,1},{1,0},{2,3},{3,2},{4,5},{5,4},{6,7},{7,6},{8,9},{9,8},{10,11... | collective-permute-start | bytes 196616 | tf_op jit(solution)/shard_map/ppermute | solution.py:277
  52.1 7.3 %collective-permute-start.24 = (bf16[2,64,256]{2,1,0:T(8,128)(2,1)S(1)}, bf16[2,64,256]{2,1,0:T(8,128)(2,1)S(1)}, u32[]{:S(2)}, u32[]{:S(2)}) collective-permute-start(bf16[2,64,256]{2,1,0:T(8,128)(2,1)S(1)} %get-tuple-element.100), channel_id=1, source_target_pairs={{0,2},{1,3},{2,0},{3,1},{4,6},{5,7},{6,4},{7,5},{8,10},{9,11},{10,... | collective-permute-start | bytes 196616 | tf_op jit(solution)/shard_map/ppermute | solution.py:277
  53.2 6.2 %collective-permute-start.25 = (bf16[2,64,256]{2,1,0:T(8,128)(2,1)S(1)}, bf16[2,64,256]{2,1,0:T(8,128)(2,1)S(1)}, u32[]{:S(2)}, u32[]{:S(2)}) collective-permute-start(bf16[2,64,256]{2,1,0:T(8,128)(2,1)S(1)} %get-tuple-element.101), channel_id=1, source_target_pairs={{0,3},{1,2},{2,1},{3,0},{4,7},{5,6},{6,5},{7,4},{8,11},{9,10},{10,... | collective-permute-start | bytes 196616 | tf_op jit(solution)/shard_map/ppermute | solution.py:277
  56.5 5.5 %collective-permute-start.20 = (bf16[2,64,256]{2,1,0:T(8,128)(2,1)S(1)}, bf16[2,64,256]{2,1,0:T(8,128)(2,1)S(1)}, u32[]{:S(2)}, u32[]{:S(2)}) collective-permute-start(bf16[2,64,256]{2,1,0:T(8,128)(2,1)S(1)} %get-tuple-element.97), channel_id=1, source_target_pairs={{0,3},{1,2},{2,1},{3,0},{4,7},{5,6},{6,5},{7,4},{8,11},{9,10},{10,... | collective-permute-start | bytes 196616 | tf_op jit(solution)/shard_map/ppermute | solution.py:277
  56.5 5.0 %collective-permute-start.21 = (bf16[2,64,256]{2,1,0:T(8,128)(2,1)S(1)}, bf16[2,64,256]{2,1,0:T(8,128)(2,1)S(1)}, u32[]{:S(2)}, u32[]{:S(2)}) collective-permute-start(bf16[2,64,256]{2,1,0:T(8,128)(2,1)S(1)} %get-tuple-element.98), channel_id=1, source_target_pairs={{0,2},{1,3},{2,0},{3,1},{4,6},{5,7},{6,4},{7,5},{8,10},{9,11},{10,... | collective-permute-start | bytes 196616 | tf_op jit(solution)/shard_map/ppermute | solution.py:277
  64.6 3.9 %collective-permute-start.30 = (bf16[2,64,256]{2,1,0:T(8,128)(2,1)S(1)}, bf16[2,64,256]{2,1,0:T(8,128)(2,1)S(1)}, u32[]{:S(2)}, u32[]{:S(2)}) collective-permute-start(bf16[2,64,256]{2,1,0:T(8,128)(2,1)S(1)} %mate_terms.29), channel_id=1, source_target_pairs={{0,1},{1,0},{2,3},{3,2},{4,5},{5,4},{6,7},{7,6},{8,9},{9,8},{10,11... | collective-permute-start | bytes 196616 | tf_op jit(solution)/shard_map/ppermute | solution.py:277
  65.1 4.4 %collective-permute-start.31 = (bf16[2,64,256]{2,1,0:T(8,128)(2,1)S(1)}, bf16[2,64,256]{2,1,0:T(8,128)(2,1)S(1)}, u32[]{:S(2)}, u32[]{:S(2)}) collective-permute-start(bf16[2,64,256]{2,1,0:T(8,128)(2,1)S(1)} %mate_terms.30), channel_id=1, source_target_pairs={{0,2},{1,3},{2,0},{3,1},{4,6},{5,7},{6,4},{7,5},{8,10},{9,11},{10,... | collective-permute-start | bytes 196616 | tf_op jit(solution)/shard_map/ppermute | solution.py:277
  66.6 4.1 %collective-permute-start.32 = (bf16[2,64,256]{2,1,0:T(8,128)(2,1)S(1)}, bf16[2,64,256]{2,1,0:T(8,128)(2,1)S(1)}, u32[]{:S(2)}, u32[]{:S(2)}) collective-permute-start(bf16[2,64,256]{2,1,0:T(8,128)(2,1)S(1)} %mate_terms.31), channel_id=1, source_target_pairs={{0,3},{1,2},{2,1},{3,0},{4,7},{5,6},{6,5},{7,4},{8,11},{9,10},{10,... | collective-permute-start | bytes 196616 | tf_op jit(solution)/shard_map/ppermute | solution.py:277
  71.1 8.1 %collective-permute-start.33 = (bf16[64,640]{1,0:T(8,128)(2,1)S(1)}, bf16[64,640]{1,0:T(8,128)(2,1)S(1)}, u32[]{:S(2)}, u32[]{:S(2)}) collective-permute-start(bf16[64,640]{1,0:T(8,128)(2,1)S(1)} %get-tuple-element.124), channel_id=1, source_target_pairs={{0,4},{1,5},{2,6},{3,7},{4,0},{5,1},{6,2},{7,3},{8,12},{9,13},{10,... | collective-permute-start | bytes 245768 | tf_op jit(solution)/shard_map/ppermute | solution.py:277
  72.4 4.9 %collective-permute-start.28 = (bf16[2,64,256]{2,1,0:T(8,128)(2,1)S(1)}, bf16[2,64,256]{2,1,0:T(8,128)(2,1)S(1)}, u32[]{:S(2)}, u32[]{:S(2)}) collective-permute-start(bf16[2,64,256]{2,1,0:T(8,128)(2,1)S(1)} %mate_terms.26.refs_6_), channel_id=1, source_target_pairs={{0,2},{1,3},{2,0},{3,1},{4,6},{5,7},{6,4},{7,5},{8,10},{9,11},{10,... | collective-permute-start | bytes 196616 | tf_op jit(solution)/shard_map/ppermute | solution.py:277
  73.4 4.5 %collective-permute-start.29 = (bf16[2,64,256]{2,1,0:T(8,128)(2,1)S(1)}, bf16[2,64,256]{2,1,0:T(8,128)(2,1)S(1)}, u32[]{:S(2)}, u32[]{:S(2)}) collective-permute-start(bf16[2,64,256]{2,1,0:T(8,128)(2,1)S(1)} %mate_terms.27.refs_7_), channel_id=1, source_target_pairs={{0,3},{1,2},{2,1},{3,0},{4,7},{5,6},{6,5},{7,4},{8,11},{9,10},{10,... | collective-permute-start | bytes 196616 | tf_op jit(solution)/shard_map/ppermute | solution.py:277
  78.3 5.5 %collective-permute-start.35 = (bf16[64,640]{1,0:T(8,128)(2,1)S(1)}, bf16[64,640]{1,0:T(8,128)(2,1)S(1)}, u32[]{:S(2)}, u32[]{:S(2)}) collective-permute-start(bf16[64,640]{1,0:T(8,128)(2,1)S(1)} %get-tuple-element.125), channel_id=1, source_target_pairs={{0,4},{1,5},{2,6},{3,7},{4,0},{5,1},{6,2},{7,3},{8,12},{9,13},{10,... | collective-permute-start | bytes 245768 | tf_op jit(solution)/shard_map/ppermute | solution.py:277
  79.2 7.0 %collective-permute-start.34 = (bf16[64,640]{1,0:T(8,128)(2,1)S(1)}, bf16[64,640]{1,0:T(8,128)(2,1)S(1)}, u32[]{:S(2)}, u32[]{:S(2)}) collective-permute-start(bf16[64,640]{1,0:T(8,128)(2,1)S(1)} %add_convert_fusion), channel_id=1, source_target_pairs={{0,8},{1,9},{2,10},{3,11},{4,12},{5,13},{6,14},{7,15},{8,0},{9,1},... | collective-permute-start | bytes 245768 | tf_op jit(solution)/shard_map/ppermute | solution.py:277
  (6 other events, 39.6 us)

commit v6 on v5

--- a/solution.py
+++ b/solution.py
@@ -84,23 +84,23 @@
                 packets[mate][i, :, 128 * q:128 * (q + 1)] = pair.astype(jnp.bfloat16)
 
 
-def plane_sum_kernel(planes, turns, per_owner, own_blocks, table, *refs):
-    terms, sums, total = refs[:PLANE], refs[-1 - len(turns):-1], refs[-1]
+def plane_sum_kernel(planes, per_owner, own_blocks, table, *refs):
+    terms, sums, total = refs[:PLANE], refs[-1 - planes:-1], refs[-1]
     low = low_half(terms[0].shape[1])
     total[...] = jnp.zeros_like(total)
-    for i, turn in enumerate(turns):
+    for turn in range(planes):
         for mate in range(PLANE):
             for q in range(per_owner // 2):
                 first = table[mate * planes + turn, 2 * q]
                 second = table[mate * planes + turn, 2 * q + 1]
-                pair = terms[mate][i, :, 128 * q:128 * (q + 1)].astype(jnp.float32)
-                total[i, first] += jnp.where(low, pair, 0.0)
-                total[i, second] += jnp.where(low, 0.0, pair)
-    for i in range(len(turns)):
+                pair = terms[mate][turn, :, 128 * q:128 * (q + 1)].astype(jnp.float32)
+                total[turn, first] += jnp.where(low, pair, 0.0)
+                total[turn, second] += jnp.where(low, 0.0, pair)
+    for turn in range(planes):
         for j in range(own_blocks // 2):
-            first, second = total[i, 2 * j], total[i, 2 * j + 1]
+            first, second = total[turn, 2 * j], total[turn, 2 * j + 1]
             both = jnp.where(low, first, second) + pltpu.roll(jnp.where(low, second, first), 64, 1)
-            sums[i][:, 128 * j:128 * (j + 1)] = both.astype(sums[i].dtype)
+            sums[turn][:, 128 * j:128 * (j + 1)] = both.astype(sums[turn].dtype)
 
 
 def columns_of(pos, turn, mate, width):
@@ -127,28 +127,34 @@
         gradient[:, here] = total
 
 
-def sample_kernel(sample_step, samples, gradient, gram, new_samples, new_bf16, new_gram):
+def sample_kernel(sample_step, samples, gradient, gram, *outs):
     old = samples[...]
     old_bf16 = old.astype(jnp.bfloat16)
     total = gradient[...]
     for part in split3(gram[...]):
         total -= dot(part, old_bf16, NN)
     new = (1.0 - weight_decay) * old + sample_step * total
-    new_samples[...] = new
+    *full, last = outs
     rounded = new.astype(jnp.bfloat16)
-    new_bf16[...] = rounded
-    new_gram[...] = dot(rounded, rounded, NT)
-
-
-def term_kernel(turns, mate, pos_ref, geno, samples, gram, packet, terms):
+    for out in full:
+        out[...] = new if out.dtype == jnp.float32 else rounded
+    if last.shape[0] == last.shape[1]:
+        last[...] = dot(rounded, rounded, NT)
+    else:
+        last[...] = jnp.zeros_like(last)
+
+
+def term_kernel(groups, mate, pos_ref, geno, samples, gram, *refs):
+    packets, terms = refs[:len(groups)], refs[-1]
     pos = pos_ref[0]
-    width = packet.shape[2]
+    width = terms.shape[2]
     parts = split3(gram[...])
-    for i, turn in enumerate(turns):
-        term = dot(samples[...], geno[:, columns_of(pos, turn, mate, width)], NN)
-        for part in parts:
-            term -= dot(part, packet[i], NN)
-        terms[i] = term.astype(jnp.bfloat16)
+    for turns, packet in zip(groups, packets):
+        for i, turn in enumerate(turns):
+            term = dot(samples[...], geno[:, columns_of(pos, turn, mate, width)], NN)
+            for part in parts:
+                term -= dot(part, packet[i], NN)
+            terms[turn] = term.astype(jnp.bfloat16)
 
 
 def on_device(genotypes, sample_factors, snp_factors, coverage):
@@ -175,7 +181,7 @@
     params = pltpu.CompilerParams(vmem_limit_bytes=VMEM_LIMIT)
     pos = position.reshape(1)
     half = planes // 2
-    near, far = tuple(range(half)), tuple(range(half, planes))
+    near, far = groups = tuple(range(half)), tuple(range(half, planes))
     packet = jax.ShapeDtypeStruct((half, rank, width), jnp.bfloat16)
     dense_blocks = pltpu.VMEM((half, own_blocks, rank, 128), jnp.float32)
     by_samples = jax.ShapeDtypeStruct((rank, samples_here), jnp.float32)
@@ -223,21 +229,21 @@
             name="pick_blocks",
         )(table, *[held[turn] for turn in turns])
 
-    def plane_sum(turns, terms, after):
+    def plane_sum(terms, after):
         sums = pl.pallas_call(
-            functools.partial(plane_sum_kernel, planes, turns, per_owner, own_blocks),
+            functools.partial(plane_sum_kernel, planes, per_owner, own_blocks),
             out_shape=tuple(
                 jax.ShapeDtypeStruct((rank, own_snps), jnp.bfloat16 if turn % 2 else jnp.float32)
-                for turn in turns
+                for turn in range(planes)
             ),
             in_specs=[smem] + [vmem] * PLANE + [anywhere] * len(after),
-            out_specs=(vmem,) * half,
-            scratch_shapes=[dense_blocks],
+            out_specs=(vmem,) * planes,
+            scratch_shapes=[pltpu.VMEM((planes, own_blocks, rank, 128), jnp.float32)],
             compiler_params=params,
             cost_estimate=small,
             name="plane_sum",
         )(table, *terms, *after)
-        return dict(zip(turns, sums))
+        return list(sums)
 
     def product(turns, mates, panels, before):
         share = len(turns) * len(mates) * samples_here * snps_here // devices
@@ -251,27 +257,28 @@
             name="panel_product",
         )(pos, geno, *[panels[turns][mate] for mate in mates], *before)
 
-    def sample_update(samples, gradient, gram):
+    def sample_update(samples, gradient, gram, outs):
         return pl.pallas_call(
             functools.partial(sample_kernel, sample_step),
-            out_shape=(by_samples, jax.ShapeDtypeStruct((rank, samples_here), jnp.bfloat16), square),
+            out_shape=outs,
             in_specs=[vmem] * 3,
-            out_specs=(vmem,) * 3,
-            compiler_params=params,
+            out_specs=(vmem,) * len(outs),
+            compiler_params=params,
+            cost_estimate=small,
             name="sample_update",
         )(samples, gradient, gram)
 
-    def terms_for(turns, mate, samples_bf16, gram, panels):
-        share = len(turns) * samples_here * snps_here // devices
+    def terms_for(mate, samples_bf16, gram, panels, after):
+        share = samples_here * snps_here // PLANE
         return pl.pallas_call(
-            functools.partial(term_kernel, turns, mate),
-            out_shape=packet,
-            in_specs=[smem] + [vmem] * 4,
+            functools.partial(term_kernel, groups, mate),
+            out_shape=jax.ShapeDtypeStruct((planes, rank, width), jnp.bfloat16),
+            in_specs=[smem] + [vmem] * (3 + len(groups)) + [anywhere] * len(after),
             out_specs=vmem,
             compiler_params=params,
             cost_estimate=cost(8 * rank * share, 2 * share),
             name="mate_terms",
-        )(pos, geno, samples_bf16, gram, panels[turns][mate])
+        )(pos, geno, samples_bf16, gram, *[panels[turns][mate] for turns in groups], *after)
 
     def swap(x, turn):
         return lax.ppermute(x, "rows", [(r, r ^ turn) for r in range(devices)])
@@ -297,14 +304,18 @@
             (near, (0,)), (far, (0,)), (near, (1,)), (near, (2, 3)), (far, (1,)), (far, (2,)), (far, (3,))
         ):
             partial = product(turns, mates, panels, partial)
-        samples, samples_bf16, sample_gram = sample_update(samples, *partial)
-        terms, sent = {}, {}
-        for turns in (far, near):
-            for mate in (2, 3, 1, 0):
-                terms[turns, mate] = terms_for(turns, mate, samples_bf16, sample_gram, panels)
-                sent[turns, mate] = to_mate(terms[turns, mate], mate)
-        sums = plane_sum(far, [sent[far, mate] for mate in range(PLANE)], [terms[near, mate] for mate in range(PLANE)])
-        sums.update(plane_sum(near, [sent[near, mate] for mate in range(PLANE)], []))
+        rounded = (jax.ShapeDtypeStruct((rank, samples_here), jnp.bfloat16), square)
+        if iteration < ROUNDS - 1:
+            samples, *current = sample_update(samples, *partial, (by_samples,) + rounded)
+            after = []
+        else:
+            current = sample_update(samples, *partial, rounded)
+            samples, token = sample_update(
+                samples, *partial, (by_samples, jax.ShapeDtypeStruct((8, 128), jnp.float32))
+            )
+            after = [token]
+        terms = {mate: terms_for(mate, *current, panels, []) for mate in (2, 3, 1, 0)}
+        sums = plane_sum([to_mate(terms[mate], mate) for mate in range(PLANE)], after)
         for turn in range(planes - 1, 0, -1):
             bit = turn & -turn
             arrived = swap(sums[turn].astype(jnp.bfloat16), bit * PLANE)

time: 87.2 us -> 83.6 us (0.959)
  waiting for transfers between devices: 30.7 us -> 29.2 us
  starting transfers between devices: 33.3 us -> 32 us
    ppermute x36 -> x30, waiting for transfers between devices: 30.7 us -> 29.2 us  [swap(): return lax.ppermute(x, 'rows', [(r, r ^ turn) for r in range(devices)])]
    ppermute x36 -> x30, starting transfers between devices: 33.3 us -> 32 us  [swap(): return lax.ppermute(x, 'rows', [(r, r ^ turn) for r in range(devices)])]
    pallas_call x22 -> x13, Pallas kernels: 8.77 us -> 7.98 us  [the longest x8 4.9 us: terms_for(): pl.pallas_call(functools.partial(term_kernel, groups, mate), out_shape=ja...]
  transfers between devices with their start and end apart: 36 -> 30, of which waited for: 17 -> 15; matrix products, arithmetic and copies ran while one was open for 0% -> 0% of each run, Pallas kernels for 17% -> 18%
where the time goes in v6:
time: 83.6 us; the launch traced here: 83.4 us
  starting transfers between devices  32 us (38%)
  waiting for transfers between devices  29.2 us (35%)
  Pallas kernels  19.4 us (23%)
  other arithmetic  1.75 us (2%)
  between operations  0.97 us (1%)
    ppermute x30, starting transfers between devices, swap(): return lax.ppermute(x, 'rows', [(r, r ^ turn) for r in range(devices)])  32 us
    ppermute x30, waiting for transfers between devices, swap(): return lax.ppermute(x, 'rows', [(r, r ^ turn) for r in range(devices)])  29.2 us
    pallas_call x14, Pallas kernels, product(): pl.pallas_call(functools.partial(product_kernel, turns, mates, not before...  7.14 us
    pallas_call x8, Pallas kernels, terms_for(): pl.pallas_call(functools.partial(term_kernel, groups, mate), out_shape=ja...  4.9 us
    pallas_call x1, Pallas kernels, on_device(): pl.pallas_call(functools.partial(load_kernel, planes, per_owner, own_bloc...  3.51 us
    pallas_call x3, Pallas kernels, sample_update(): pl.pallas_call(functools.partial(sample_kernel, sample_step), out_shape=o...  1.78 us
  transfers between devices with their start and end apart: 30, of which 15 were waited for; matrix products, arithmetic and copies ran while one was open for 0% of the time, Pallas kernels for 18%

profile of v6, /device:TPU:0, one launch (start us, length us, event | category | flops | bytes accessed | tf_op | source)
XLA Modules:
  0.0 83.4 jit_solution(5513178734472098049)
XLA Ops:
  0.6 0.9 %convert_bitcast_fusion.refs_0_ = bf16[64,640]{1,0:T(8,128)(2,1)S(1)} fusion(f32[640,64]{0,1:T(8,128)} %param.6), kind=kLoop, calls=%fused_computation.4 | loop fusion | flops 40960 | bytes 245760 | tf_op jit(solution)/shard_map/convert_element_type | solution.py:291
  1.6 4.1 %collective-permute-start = (bf16[64,640]{1,0:T(8,128)(2,1)S(1)}, bf16[64,640]{1,0:T(8,128)(2,1)S(1)}, u32[]{:S(2)}, u32[]{:S(2)}) collective-permute-start(bf16[64,640]{1,0:T(8,128)(2,1)S(1)} %convert_bitcast_fusion.refs_0_), channel_id=1, source_target_pairs={{0,8},{1,9},{2,10},{3,11},{4,12},{5,13},{6,14},{7,15},{8,0},{9,1},... | collective-permute-start | bytes 245768 | tf_op jit(solution)/shard_map/ppermute | solution.py:284
  5.7 1.6 %collective-permute-start.5 = (bf16[64,640]{1,0:T(8,128)(2,1)S(1)}, bf16[64,640]{1,0:T(8,128)(2,1)S(1)}, u32[]{:S(2)}, u32[]{:S(2)}) collective-permute-start(bf16[64,640]{1,0:T(8,128)(2,1)S(1)} %convert_bitcast_fusion.refs_0_), channel_id=1, source_target_pairs={{0,4},{1,5},{2,6},{3,7},{4,0},{5,1},{6,2},{7,3},{8,12},{9,13},{10,... | collective-permute-start | bytes 245768 | tf_op jit(solution)/shard_map/ppermute | solution.py:284
  7.2 3.5 %load_batch.1 = (bf16[1024,4096]{1,0:T(8,128)(2,1)S(1)}, f32[64,1024]{1,0:T(8,128)S(1)}, s32[16,4]{1,0:T(8,128)S(4)}) custom-call(s32[1]{0:T(128)} %bitcast.pos_ref, s32[16,64]{1,0:T(8,128)} %cov.3, bf16[1024,4096]{1,0:T(8,128)(2,1)} %geno.1, f32[64,1024]{1,0:T(8,128)} %bitcast.13), custom_call_target="tpu_custom_call" | custom-call | bytes 8388608 | tf_op jit(solution)/shard_map/load_batch/pallas_call | solution.py:193
  11.5 1.6 %collective-permute-start.6 = (bf16[2,64,256]{2,1,0:T(8,128)(2,1)S(1)}, bf16[2,64,256]{2,1,0:T(8,128)(2,1)S(1)}, u32[]{:S(2)}, u32[]{:S(2)}) collective-permute-start(bf16[2,64,256]{2,1,0:T(8,128)(2,1)S(1)} %get-tuple-element.72), channel_id=1, source_target_pairs={{0,2},{1,3},{2,0},{3,1},{4,6},{5,7},{6,4},{7,5},{8,10},{9,11},{10,... | collective-permute-start | bytes 196616 | tf_op jit(solution)/shard_map/ppermute | solution.py:284
  13.9 1.4 %collective-permute-done.1.refs_1_ = bf16[64,640]{1,0:T(8,128)(2,1)S(1)} collective-permute-done((bf16[64,640]{1,0:T(8,128)(2,1)S(1)}, bf16[64,640]{1,0:T(8,128)(2,1)S(1)}, u32[]{:S(2)}, u32[]{:S(2)}) %collective-permute-start.1) | collective-permute-done | bytes 81952 | tf_op jit(solution)/shard_map/ppermute | solution.py:284
  15.5 1.6 %collective-permute-start.3 = (bf16[2,64,256]{2,1,0:T(8,128)(2,1)S(1)}, bf16[2,64,256]{2,1,0:T(8,128)(2,1)S(1)}, u32[]{:S(2)}, u32[]{:S(2)}) collective-permute-start(bf16[2,64,256]{2,1,0:T(8,128)(2,1)S(1)} %get-tuple-element.70), channel_id=1, source_target_pairs={{0,2},{1,3},{2,0},{3,1},{4,6},{5,7},{6,4},{7,5},{8,10},{9,11},{10,... | collective-permute-start | bytes 196616 | tf_op jit(solution)/shard_map/ppermute | solution.py:284
  18.4 0.8 panel_product.17
  20.5 1.3 %collective-permute-done.2.refs_0_.refs_1_ = bf16[2,64,256]{2,1,0:T(8,128)(2,1)S(1)} collective-permute-done((bf16[2,64,256]{2,1,0:T(8,128)(2,1)S(1)}, bf16[2,64,256]{2,1,0:T(8,128)(2,1)S(1)}, u32[]{:S(2)}, u32[]{:S(2)}) %collective-permute-start.2) | collective-permute-done | bytes 65568 | tf_op jit(solution)/shard_map/ppermute | solution.py:284
  24.6 1.2 %collective-permute-start.10 = (bf16[4,64,256]{2,1,0:T(8,128)(2,1)S(1)}, bf16[4,64,256]{2,1,0:T(8,128)(2,1)S(1)}, u32[]{:S(2)}, u32[]{:S(2)}) collective-permute-start(bf16[4,64,256]{2,1,0:T(8,128)(2,1)S(1)} %mate_terms.10), channel_id=1, source_target_pairs={{0,2},{1,3},{2,0},{3,1},{4,6},{5,7},{6,4},{7,5},{8,10},{9,11},{10,... | collective-permute-start | bytes 393224 | tf_op jit(solution)/shard_map/ppermute | solution.py:284
  27.2 1.6 %collective-permute-done.11.refs_3_ = bf16[4,64,256]{2,1,0:T(8,128)(2,1)S(1)} collective-permute-done((bf16[4,64,256]{2,1,0:T(8,128)(2,1)S(1)}, bf16[4,64,256]{2,1,0:T(8,128)(2,1)S(1)}, u32[]{:S(2)}, u32[]{:S(2)}) %collective-permute-start.11) | collective-permute-done | bytes 131104 | tf_op jit(solution)/shard_map/ppermute | solution.py:284
  28.9 3.1 %collective-permute-done.10.refs_2_ = bf16[4,64,256]{2,1,0:T(8,128)(2,1)S(1)} collective-permute-done((bf16[4,64,256]{2,1,0:T(8,128)(2,1)S(1)}, bf16[4,64,256]{2,1,0:T(8,128)(2,1)S(1)}, u32[]{:S(2)}, u32[]{:S(2)}) %collective-permute-start.10) | collective-permute-done | bytes 131104 | tf_op jit(solution)/shard_map/ppermute | solution.py:284
  33.2 1.6 %collective-permute-start.14 = (bf16[64,640]{1,0:T(8,128)(2,1)S(1)}, bf16[64,640]{1,0:T(8,128)(2,1)S(1)}, u32[]{:S(2)}, u32[]{:S(2)}) collective-permute-start(bf16[64,640]{1,0:T(8,128)(2,1)S(1)} %get-tuple-element.97), channel_id=1, source_target_pairs={{0,4},{1,5},{2,6},{3,7},{4,0},{5,1},{6,2},{7,3},{8,12},{9,13},{10,... | collective-permute-start | bytes 245768 | tf_op jit(solution)/shard_map/ppermute | solution.py:284
  34.7 3.0 %collective-permute-done.12 = bf16[64,640]{1,0:T(8,128)(2,1)S(1)} collective-permute-done((bf16[64,640]{1,0:T(8,128)(2,1)S(1)}, bf16[64,640]{1,0:T(8,128)(2,1)S(1)}, u32[]{:S(2)}, u32[]{:S(2)}) %collective-permute-start.12) | collective-permute-done | bytes 81952 | tf_op jit(solution)/shard_map/ppermute | solution.py:284
  37.8 1.9 %collective-permute-start.13 = (bf16[64,640]{1,0:T(8,128)(2,1)S(1)}, bf16[64,640]{1,0:T(8,128)(2,1)S(1)}, u32[]{:S(2)}, u32[]{:S(2)}) collective-permute-start(bf16[64,640]{1,0:T(8,128)(2,1)S(1)} %add_convert_fusion.1), channel_id=1, source_target_pairs={{0,8},{1,9},{2,10},{3,11},{4,12},{5,13},{6,14},{7,15},{8,0},{9,1},... | collective-permute-start | bytes 245768 | tf_op jit(solution)/shard_map/ppermute | solution.py:284
  39.8 4.2 %collective-permute-done.13 = bf16[64,640]{1,0:T(8,128)(2,1)S(1)} collective-permute-done((bf16[64,640]{1,0:T(8,128)(2,1)S(1)}, bf16[64,640]{1,0:T(8,128)(2,1)S(1)}, u32[]{:S(2)}, u32[]{:S(2)}) %collective-permute-start.13) | collective-permute-done | bytes 81952 | tf_op jit(solution)/shard_map/ppermute | solution.py:284
  44.1 1.1 %collective-permute-start.15 = (bf16[64,640]{1,0:T(8,128)(2,1)S(1)}, bf16[64,640]{1,0:T(8,128)(2,1)S(1)}, u32[]{:S(2)}, u32[]{:S(2)}) collective-permute-start(bf16[64,640]{1,0:T(8,128)(2,1)S(1)} %fusion.refs_0_), channel_id=1, source_target_pairs={{0,8},{1,9},{2,10},{3,11},{4,12},{5,13},{6,14},{7,15},{8,0},{9,1},... | collective-permute-start | bytes 245768 | tf_op jit(solution)/shard_map/ppermute | solution.py:284
  45.2 2.8 %collective-permute-start.20 = (bf16[64,640]{1,0:T(8,128)(2,1)S(1)}, bf16[64,640]{1,0:T(8,128)(2,1)S(1)}, u32[]{:S(2)}, u32[]{:S(2)}) collective-permute-start(bf16[64,640]{1,0:T(8,128)(2,1)S(1)} %fusion.refs_0_), channel_id=1, source_target_pairs={{0,4},{1,5},{2,6},{3,7},{4,0},{5,1},{6,2},{7,3},{8,12},{9,13},{10,... | collective-permute-start | bytes 245768 | tf_op jit(solution)/shard_map/ppermute | solution.py:284
  48.1 1.9 %collective-permute-done.15.refs_0_ = bf16[64,640]{1,0:T(8,128)(2,1)S(1)} collective-permute-done((bf16[64,640]{1,0:T(8,128)(2,1)S(1)}, bf16[64,640]{1,0:T(8,128)(2,1)S(1)}, u32[]{:S(2)}, u32[]{:S(2)}) %collective-permute-start.15) | collective-permute-done | bytes 81952 | tf_op jit(solution)/shard_map/ppermute | solution.py:284
  50.0 1.2 %collective-permute-start.16 = (bf16[64,640]{1,0:T(8,128)(2,1)S(1)}, bf16[64,640]{1,0:T(8,128)(2,1)S(1)}, u32[]{:S(2)}, u32[]{:S(2)}) collective-permute-start(bf16[64,640]{1,0:T(8,128)(2,1)S(1)} %collective-permute-done.15.refs_0_), channel_id=1, source_target_pairs={{0,4},{1,5},{2,6},{3,7},{4,0},{5,1},{6,2},{7,3},{8,12},{9,13},{10,... | collective-permute-start | bytes 245768 | tf_op jit(solution)/shard_map/ppermute | solution.py:284
  51.5 0.9 %collective-permute-start.21 = (bf16[2,64,256]{2,1,0:T(8,128)(2,1)S(1)}, bf16[2,64,256]{2,1,0:T(8,128)(2,1)S(1)}, u32[]{:S(2)}, u32[]{:S(2)}) collective-permute-start(bf16[2,64,256]{2,1,0:T(8,128)(2,1)S(1)} %get-tuple-element.101), channel_id=1, source_target_pairs={{0,2},{1,3},{2,0},{3,1},{4,6},{5,7},{6,4},{7,5},{8,10},{9,11},{10,... | collective-permute-start | bytes 196616 | tf_op jit(solution)/shard_map/ppermute | solution.py:284
  52.4 0.9 %collective-permute-start.22 = (bf16[2,64,256]{2,1,0:T(8,128)(2,1)S(1)}, bf16[2,64,256]{2,1,0:T(8,128)(2,1)S(1)}, u32[]{:S(2)}, u32[]{:S(2)}) collective-permute-start(bf16[2,64,256]{2,1,0:T(8,128)(2,1)S(1)} %get-tuple-element.102), channel_id=1, source_target_pairs={{0,3},{1,2},{2,1},{3,0},{4,7},{5,6},{6,5},{7,4},{8,11},{9,10},{10,... | collective-permute-start | bytes 196616 | tf_op jit(solution)/shard_map/ppermute | solution.py:284
  55.8 1.3 %collective-permute-start.17 = (bf16[2,64,256]{2,1,0:T(8,128)(2,1)S(1)}, bf16[2,64,256]{2,1,0:T(8,128)(2,1)S(1)}, u32[]{:S(2)}, u32[]{:S(2)}) collective-permute-start(bf16[2,64,256]{2,1,0:T(8,128)(2,1)S(1)} %get-tuple-element.98), channel_id=1, source_target_pairs={{0,3},{1,2},{2,1},{3,0},{4,7},{5,6},{6,5},{7,4},{8,11},{9,10},{10,... | collective-permute-start | bytes 196616 | tf_op jit(solution)/shard_map/ppermute | solution.py:284
  57.6 0.8 panel_product.24
  61.8 1.0 %collective-permute-start.26 = (bf16[4,64,256]{2,1,0:T(8,128)(2,1)S(1)}, bf16[4,64,256]{2,1,0:T(8,128)(2,1)S(1)}, u32[]{:S(2)}, u32[]{:S(2)}) collective-permute-start(bf16[4,64,256]{2,1,0:T(8,128)(2,1)S(1)} %mate_terms.15), channel_id=1, source_target_pairs={{0,3},{1,2},{2,1},{3,0},{4,7},{5,6},{6,5},{7,4},{8,11},{9,10},{10,... | collective-permute-start | bytes 393224 | tf_op jit(solution)/shard_map/ppermute | solution.py:284
  63.3 1.0 %collective-permute-start.25 = (bf16[4,64,256]{2,1,0:T(8,128)(2,1)S(1)}, bf16[4,64,256]{2,1,0:T(8,128)(2,1)S(1)}, u32[]{:S(2)}, u32[]{:S(2)}) collective-permute-start(bf16[4,64,256]{2,1,0:T(8,128)(2,1)S(1)} %mate_terms.14), channel_id=1, source_target_pairs={{0,2},{1,3},{2,0},{3,1},{4,6},{5,7},{6,4},{7,5},{8,10},{9,11},{10,... | collective-permute-start | bytes 393224 | tf_op jit(solution)/shard_map/ppermute | solution.py:284
  65.0 1.0 %sample_update.4 = (f32[64,1024]{1,0:T(8,128)}, f32[8,128]{1,0:T(8,128)S(1)}) custom-call(f32[64,1024]{1,0:T(8,128)S(1)} %get-tuple-element.91.samples, f32[64,1024]{1,0:T(8,128)S(1)} %get-tuple-element.118.gradient, f32[64,64]{1,0:T(8,128)S(1)} %get-tuple-element.119.gram), custom_call_target="tpu_custom_call" | custom-call | bytes 2097152 | tf_op jit(solution)/shard_map/sample_update/pallas_call | solution.py:261
  67.4 3.1 %collective-permute-done.25.refs_2_ = bf16[4,64,256]{2,1,0:T(8,128)(2,1)S(1)} collective-permute-done((bf16[4,64,256]{2,1,0:T(8,128)(2,1)S(1)}, bf16[4,64,256]{2,1,0:T(8,128)(2,1)S(1)}, u32[]{:S(2)}, u32[]{:S(2)}) %collective-permute-start.25) | collective-permute-done | bytes 131104 | tf_op jit(solution)/shard_map/ppermute | solution.py:284
  71.1 1.4 %collective-permute-start.27 = (bf16[64,640]{1,0:T(8,128)(2,1)S(1)}, bf16[64,640]{1,0:T(8,128)(2,1)S(1)}, u32[]{:S(2)}, u32[]{:S(2)}) collective-permute-start(bf16[64,640]{1,0:T(8,128)(2,1)S(1)} %get-tuple-element.126), channel_id=1, source_target_pairs={{0,4},{1,5},{2,6},{3,7},{4,0},{5,1},{6,2},{7,3},{8,12},{9,13},{10,... | collective-permute-start | bytes 245768 | tf_op jit(solution)/shard_map/ppermute | solution.py:284
  73.2 3.1 %collective-permute-done.27 = bf16[64,640]{1,0:T(8,128)(2,1)S(1)} collective-permute-done((bf16[64,640]{1,0:T(8,128)(2,1)S(1)}, bf16[64,640]{1,0:T(8,128)(2,1)S(1)}, u32[]{:S(2)}, u32[]{:S(2)}) %collective-permute-start.27) | collective-permute-done | bytes 81952 | tf_op jit(solution)/shard_map/ppermute | solution.py:284
  76.3 2.5 %collective-permute-start.28 = (bf16[64,640]{1,0:T(8,128)(2,1)S(1)}, bf16[64,640]{1,0:T(8,128)(2,1)S(1)}, u32[]{:S(2)}, u32[]{:S(2)}) collective-permute-start(bf16[64,640]{1,0:T(8,128)(2,1)S(1)} %add_convert_fusion), channel_id=1, source_target_pairs={{0,8},{1,9},{2,10},{3,11},{4,12},{5,13},{6,14},{7,15},{8,0},{9,1},... | collective-permute-start | bytes 245768 | tf_op jit(solution)/shard_map/ppermute | solution.py:284
  78.9 3.8 %collective-permute-done.28 = bf16[64,640]{1,0:T(8,128)(2,1)S(1)} collective-permute-done((bf16[64,640]{1,0:T(8,128)(2,1)S(1)}, bf16[64,640]{1,0:T(8,128)(2,1)S(1)}, u32[]{:S(2)}, u32[]{:S(2)}) %collective-permute-start.28) | collective-permute-done | bytes 81952 | tf_op jit(solution)/shard_map/ppermute | solution.py:284
  (70 shorter events, 21.1 us)
Async XLA Ops:
  1.6 9.2 %collective-permute-start = (bf16[64,640]{1,0:T(8,128)(2,1)S(1)}, bf16[64,640]{1,0:T(8,128)(2,1)S(1)}, u32[]{:S(2)}, u32[]{:S(2)}) collective-permute-start(bf16[64,640]{1,0:T(8,128)(2,1)S(1)} %convert_bitcast_fusion.refs_0_), channel_id=1, source_target_pairs={{0,8},{1,9},{2,10},{3,11},{4,12},{5,13},{6,14},{7,15},{8,0},{9,1},... | collective-permute-start | bytes 245768 | tf_op jit(solution)/shard_map/ppermute | solution.py:284
  5.7 5.6 %collective-permute-start.5 = (bf16[64,640]{1,0:T(8,128)(2,1)S(1)}, bf16[64,640]{1,0:T(8,128)(2,1)S(1)}, u32[]{:S(2)}, u32[]{:S(2)}) collective-permute-start(bf16[64,640]{1,0:T(8,128)(2,1)S(1)} %convert_bitcast_fusion.refs_0_), channel_id=1, source_target_pairs={{0,4},{1,5},{2,6},{3,7},{4,0},{5,1},{6,2},{7,3},{8,12},{9,13},{10,... | collective-permute-start | bytes 245768 | tf_op jit(solution)/shard_map/ppermute | solution.py:284
  10.8 4.5 %collective-permute-start.1 = (bf16[64,640]{1,0:T(8,128)(2,1)S(1)}, bf16[64,640]{1,0:T(8,128)(2,1)S(1)}, u32[]{:S(2)}, u32[]{:S(2)}) collective-permute-start(bf16[64,640]{1,0:T(8,128)(2,1)S(1)} %collective-permute-done.refs_0_), channel_id=1, source_target_pairs={{0,4},{1,5},{2,6},{3,7},{4,0},{5,1},{6,2},{7,3},{8,12},{9,13},{10,... | collective-permute-start | bytes 245768 | tf_op jit(solution)/shard_map/ppermute | solution.py:284
  11.5 6.1 %collective-permute-start.8 = (bf16[2,64,256]{2,1,0:T(8,128)(2,1)S(1)}, bf16[2,64,256]{2,1,0:T(8,128)(2,1)S(1)}, u32[]{:S(2)}, u32[]{:S(2)}) collective-permute-start(bf16[2,64,256]{2,1,0:T(8,128)(2,1)S(1)} %get-tuple-element.74), channel_id=1, source_target_pairs={{0,1},{1,0},{2,3},{3,2},{4,5},{5,4},{6,7},{7,6},{8,9},{9,8},{10,11... | collective-permute-start | bytes 196616 | tf_op jit(solution)/shard_map/ppermute | solution.py:284
  11.5 6.9 %collective-permute-start.6 = (bf16[2,64,256]{2,1,0:T(8,128)(2,1)S(1)}, bf16[2,64,256]{2,1,0:T(8,128)(2,1)S(1)}, u32[]{:S(2)}, u32[]{:S(2)}) collective-permute-start(bf16[2,64,256]{2,1,0:T(8,128)(2,1)S(1)} %get-tuple-element.72), channel_id=1, source_target_pairs={{0,2},{1,3},{2,0},{3,1},{4,6},{5,7},{6,4},{7,5},{8,10},{9,11},{10,... | collective-permute-start | bytes 196616 | tf_op jit(solution)/shard_map/ppermute | solution.py:284
  13.1 5.3 %collective-permute-start.7 = (bf16[2,64,256]{2,1,0:T(8,128)(2,1)S(1)}, bf16[2,64,256]{2,1,0:T(8,128)(2,1)S(1)}, u32[]{:S(2)}, u32[]{:S(2)}) collective-permute-start(bf16[2,64,256]{2,1,0:T(8,128)(2,1)S(1)} %get-tuple-element.73), channel_id=1, source_target_pairs={{0,3},{1,2},{2,1},{3,0},{4,7},{5,6},{6,5},{7,4},{8,11},{9,10},{10,... | collective-permute-start | bytes 196616 | tf_op jit(solution)/shard_map/ppermute | solution.py:284
  15.4 3.8 %collective-permute-start.4 = (bf16[2,64,256]{2,1,0:T(8,128)(2,1)S(1)}, bf16[2,64,256]{2,1,0:T(8,128)(2,1)S(1)}, u32[]{:S(2)}, u32[]{:S(2)}) collective-permute-start(bf16[2,64,256]{2,1,0:T(8,128)(2,1)S(1)} %get-tuple-element.71), channel_id=1, source_target_pairs={{0,1},{1,0},{2,3},{3,2},{4,5},{5,4},{6,7},{7,6},{8,9},{9,8},{10,11... | collective-permute-start | bytes 196616 | tf_op jit(solution)/shard_map/ppermute | solution.py:284
  15.5 4.5 %collective-permute-start.3 = (bf16[2,64,256]{2,1,0:T(8,128)(2,1)S(1)}, bf16[2,64,256]{2,1,0:T(8,128)(2,1)S(1)}, u32[]{:S(2)}, u32[]{:S(2)}) collective-permute-start(bf16[2,64,256]{2,1,0:T(8,128)(2,1)S(1)} %get-tuple-element.70), channel_id=1, source_target_pairs={{0,2},{1,3},{2,0},{3,1},{4,6},{5,7},{6,4},{7,5},{8,10},{9,11},{10,... | collective-permute-start | bytes 196616 | tf_op jit(solution)/shard_map/ppermute | solution.py:284
  17.6 4.2 %collective-permute-start.2 = (bf16[2,64,256]{2,1,0:T(8,128)(2,1)S(1)}, bf16[2,64,256]{2,1,0:T(8,128)(2,1)S(1)}, u32[]{:S(2)}, u32[]{:S(2)}) collective-permute-start(bf16[2,64,256]{2,1,0:T(8,128)(2,1)S(1)} %get-tuple-element.69), channel_id=1, source_target_pairs={{0,3},{1,2},{2,1},{3,0},{4,7},{5,6},{6,5},{7,4},{8,11},{9,10},{10,... | collective-permute-start | bytes 196616 | tf_op jit(solution)/shard_map/ppermute | solution.py:284
  23.3 5.6 %collective-permute-start.11 = (bf16[4,64,256]{2,1,0:T(8,128)(2,1)S(1)}, bf16[4,64,256]{2,1,0:T(8,128)(2,1)S(1)}, u32[]{:S(2)}, u32[]{:S(2)}) collective-permute-start(bf16[4,64,256]{2,1,0:T(8,128)(2,1)S(1)} %mate_terms.11), channel_id=1, source_target_pairs={{0,3},{1,2},{2,1},{3,0},{4,7},{5,6},{6,5},{7,4},{8,11},{9,10},{10,... | collective-permute-start | bytes 393224 | tf_op jit(solution)/shard_map/ppermute | solution.py:284
  24.6 15.1 %copy-start = (s32[16,64]{1,0:T(8,128)S(1)}, s32[16,64]{1,0:T(8,128)}, u32[]{:S(2)}) copy-start(s32[16,64]{1,0:T(8,128)} %cov.3) | copy-start | bytes 12292
  24.6 19.5 %copy-start.1 = (f32[640,64]{0,1:T(8,128)S(1)}, f32[640,64]{0,1:T(8,128)}, u32[]{:S(2)}) copy-start(f32[640,64]{0,1:T(8,128)} %param.6) | copy-start | bytes 491524
  24.6 7.4 %collective-permute-start.10 = (bf16[4,64,256]{2,1,0:T(8,128)(2,1)S(1)}, bf16[4,64,256]{2,1,0:T(8,128)(2,1)S(1)}, u32[]{:S(2)}, u32[]{:S(2)}) collective-permute-start(bf16[4,64,256]{2,1,0:T(8,128)(2,1)S(1)} %mate_terms.10), channel_id=1, source_target_pairs={{0,2},{1,3},{2,0},{3,1},{4,6},{5,7},{6,4},{7,5},{8,10},{9,11},{10,... | collective-permute-start | bytes 393224 | tf_op jit(solution)/shard_map/ppermute | solution.py:284
  26.4 5.6 %collective-permute-start.9 = (bf16[4,64,256]{2,1,0:T(8,128)(2,1)S(1)}, bf16[4,64,256]{2,1,0:T(8,128)(2,1)S(1)}, u32[]{:S(2)}, u32[]{:S(2)}) collective-permute-start(bf16[4,64,256]{2,1,0:T(8,128)(2,1)S(1)} %mate_terms.9), channel_id=1, source_target_pairs={{0,1},{1,0},{2,3},{3,2},{4,5},{5,4},{6,7},{7,6},{8,9},{9,8},{10,11... | collective-permute-start | bytes 393224 | tf_op jit(solution)/shard_map/ppermute | solution.py:284
  32.6 5.1 %collective-permute-start.12 = (bf16[64,640]{1,0:T(8,128)(2,1)S(1)}, bf16[64,640]{1,0:T(8,128)(2,1)S(1)}, u32[]{:S(2)}, u32[]{:S(2)}) collective-permute-start(bf16[64,640]{1,0:T(8,128)(2,1)S(1)} %get-tuple-element.96), channel_id=1, source_target_pairs={{0,4},{1,5},{2,6},{3,7},{4,0},{5,1},{6,2},{7,3},{8,12},{9,13},{10,... | collective-permute-start | bytes 245768 | tf_op jit(solution)/shard_map/ppermute | solution.py:284
  33.2 6.6 %collective-permute-start.14 = (bf16[64,640]{1,0:T(8,128)(2,1)S(1)}, bf16[64,640]{1,0:T(8,128)(2,1)S(1)}, u32[]{:S(2)}, u32[]{:S(2)}) collective-permute-start(bf16[64,640]{1,0:T(8,128)(2,1)S(1)} %get-tuple-element.97), channel_id=1, source_target_pairs={{0,4},{1,5},{2,6},{3,7},{4,0},{5,1},{6,2},{7,3},{8,12},{9,13},{10,... | collective-permute-start | bytes 245768 | tf_op jit(solution)/shard_map/ppermute | solution.py:284
  37.8 6.3 %collective-permute-start.13 = (bf16[64,640]{1,0:T(8,128)(2,1)S(1)}, bf16[64,640]{1,0:T(8,128)(2,1)S(1)}, u32[]{:S(2)}, u32[]{:S(2)}) collective-permute-start(bf16[64,640]{1,0:T(8,128)(2,1)S(1)} %add_convert_fusion.1), channel_id=1, source_target_pairs={{0,8},{1,9},{2,10},{3,11},{4,12},{5,13},{6,14},{7,15},{8,0},{9,1},... | collective-permute-start | bytes 245768 | tf_op jit(solution)/shard_map/ppermute | solution.py:284
  44.1 5.9 %collective-permute-start.15 = (bf16[64,640]{1,0:T(8,128)(2,1)S(1)}, bf16[64,640]{1,0:T(8,128)(2,1)S(1)}, u32[]{:S(2)}, u32[]{:S(2)}) collective-permute-start(bf16[64,640]{1,0:T(8,128)(2,1)S(1)} %fusion.refs_0_), channel_id=1, source_target_pairs={{0,8},{1,9},{2,10},{3,11},{4,12},{5,13},{6,14},{7,15},{8,0},{9,1},... | collective-permute-start | bytes 245768 | tf_op jit(solution)/shard_map/ppermute | solution.py:284
  45.2 6.0 %collective-permute-start.20 = (bf16[64,640]{1,0:T(8,128)(2,1)S(1)}, bf16[64,640]{1,0:T(8,128)(2,1)S(1)}, u32[]{:S(2)}, u32[]{:S(2)}) collective-permute-start(bf16[64,640]{1,0:T(8,128)(2,1)S(1)} %fusion.refs_0_), channel_id=1, source_target_pairs={{0,4},{1,5},{2,6},{3,7},{4,0},{5,1},{6,2},{7,3},{8,12},{9,13},{10,... | collective-permute-start | bytes 245768 | tf_op jit(solution)/shard_map/ppermute | solution.py:284
  50.0 4.4 %collective-permute-start.16 = (bf16[64,640]{1,0:T(8,128)(2,1)S(1)}, bf16[64,640]{1,0:T(8,128)(2,1)S(1)}, u32[]{:S(2)}, u32[]{:S(2)}) collective-permute-start(bf16[64,640]{1,0:T(8,128)(2,1)S(1)} %collective-permute-done.15.refs_0_), channel_id=1, source_target_pairs={{0,4},{1,5},{2,6},{3,7},{4,0},{5,1},{6,2},{7,3},{8,12},{9,13},{10,... | collective-permute-start | bytes 245768 | tf_op jit(solution)/shard_map/ppermute | solution.py:284
  51.4 4.3 %collective-permute-start.23 = (bf16[2,64,256]{2,1,0:T(8,128)(2,1)S(1)}, bf16[2,64,256]{2,1,0:T(8,128)(2,1)S(1)}, u32[]{:S(2)}, u32[]{:S(2)}) collective-permute-start(bf16[2,64,256]{2,1,0:T(8,128)(2,1)S(1)} %get-tuple-element.103), channel_id=1, source_target_pairs={{0,1},{1,0},{2,3},{3,2},{4,5},{5,4},{6,7},{7,6},{8,9},{9,8},{10,11... | collective-permute-start | bytes 196616 | tf_op jit(solution)/shard_map/ppermute | solution.py:284
  51.5 6.0 %collective-permute-start.21 = (bf16[2,64,256]{2,1,0:T(8,128)(2,1)S(1)}, bf16[2,64,256]{2,1,0:T(8,128)(2,1)S(1)}, u32[]{:S(2)}, u32[]{:S(2)}) collective-permute-start(bf16[2,64,256]{2,1,0:T(8,128)(2,1)S(1)} %get-tuple-element.101), channel_id=1, source_target_pairs={{0,2},{1,3},{2,0},{3,1},{4,6},{5,7},{6,4},{7,5},{8,10},{9,11},{10,... | collective-permute-start | bytes 196616 | tf_op jit(solution)/shard_map/ppermute | solution.py:284
  52.4 5.1 %collective-permute-start.22 = (bf16[2,64,256]{2,1,0:T(8,128)(2,1)S(1)}, bf16[2,64,256]{2,1,0:T(8,128)(2,1)S(1)}, u32[]{:S(2)}, u32[]{:S(2)}) collective-permute-start(bf16[2,64,256]{2,1,0:T(8,128)(2,1)S(1)} %get-tuple-element.102), channel_id=1, source_target_pairs={{0,3},{1,2},{2,1},{3,0},{4,7},{5,6},{6,5},{7,4},{8,11},{9,10},{10,... | collective-permute-start | bytes 196616 | tf_op jit(solution)/shard_map/ppermute | solution.py:284
  54.6 3.8 %collective-permute-start.19 = (bf16[2,64,256]{2,1,0:T(8,128)(2,1)S(1)}, bf16[2,64,256]{2,1,0:T(8,128)(2,1)S(1)}, u32[]{:S(2)}, u32[]{:S(2)}) collective-permute-start(bf16[2,64,256]{2,1,0:T(8,128)(2,1)S(1)} %get-tuple-element.100), channel_id=1, source_target_pairs={{0,1},{1,0},{2,3},{3,2},{4,5},{5,4},{6,7},{7,6},{8,9},{9,8},{10,11... | collective-permute-start | bytes 196616 | tf_op jit(solution)/shard_map/ppermute | solution.py:284
  54.7 4.9 %collective-permute-start.18 = (bf16[2,64,256]{2,1,0:T(8,128)(2,1)S(1)}, bf16[2,64,256]{2,1,0:T(8,128)(2,1)S(1)}, u32[]{:S(2)}, u32[]{:S(2)}) collective-permute-start(bf16[2,64,256]{2,1,0:T(8,128)(2,1)S(1)} %get-tuple-element.99), channel_id=1, source_target_pairs={{0,2},{1,3},{2,0},{3,1},{4,6},{5,7},{6,4},{7,5},{8,10},{9,11},{10,... | collective-permute-start | bytes 196616 | tf_op jit(solution)/shard_map/ppermute | solution.py:284
  55.8 4.5 %collective-permute-start.17 = (bf16[2,64,256]{2,1,0:T(8,128)(2,1)S(1)}, bf16[2,64,256]{2,1,0:T(8,128)(2,1)S(1)}, u32[]{:S(2)}, u32[]{:S(2)}) collective-permute-start(bf16[2,64,256]{2,1,0:T(8,128)(2,1)S(1)} %get-tuple-element.98), channel_id=1, source_target_pairs={{0,3},{1,2},{2,1},{3,0},{4,7},{5,6},{6,5},{7,4},{8,11},{9,10},{10,... | collective-permute-start | bytes 196616 | tf_op jit(solution)/shard_map/ppermute | solution.py:284
  61.8 5.6 %collective-permute-start.26 = (bf16[4,64,256]{2,1,0:T(8,128)(2,1)S(1)}, bf16[4,64,256]{2,1,0:T(8,128)(2,1)S(1)}, u32[]{:S(2)}, u32[]{:S(2)}) collective-permute-start(bf16[4,64,256]{2,1,0:T(8,128)(2,1)S(1)} %mate_terms.15), channel_id=1, source_target_pairs={{0,3},{1,2},{2,1},{3,0},{4,7},{5,6},{6,5},{7,4},{8,11},{9,10},{10,... | collective-permute-start | bytes 393224 | tf_op jit(solution)/shard_map/ppermute | solution.py:284
  63.3 7.1 %collective-permute-start.25 = (bf16[4,64,256]{2,1,0:T(8,128)(2,1)S(1)}, bf16[4,64,256]{2,1,0:T(8,128)(2,1)S(1)}, u32[]{:S(2)}, u32[]{:S(2)}) collective-permute-start(bf16[4,64,256]{2,1,0:T(8,128)(2,1)S(1)} %mate_terms.14), channel_id=1, source_target_pairs={{0,2},{1,3},{2,0},{3,1},{4,6},{5,7},{6,4},{7,5},{8,10},{9,11},{10,... | collective-permute-start | bytes 393224 | tf_op jit(solution)/shard_map/ppermute | solution.py:284
  64.9 5.5 %collective-permute-start.24 = (bf16[4,64,256]{2,1,0:T(8,128)(2,1)S(1)}, bf16[4,64,256]{2,1,0:T(8,128)(2,1)S(1)}, u32[]{:S(2)}, u32[]{:S(2)}) collective-permute-start(bf16[4,64,256]{2,1,0:T(8,128)(2,1)S(1)} %mate_terms.13), channel_id=1, source_target_pairs={{0,1},{1,0},{2,3},{3,2},{4,5},{5,4},{6,7},{7,6},{8,9},{9,8},{10,11... | collective-permute-start | bytes 393224 | tf_op jit(solution)/shard_map/ppermute | solution.py:284
  71.1 5.2 %collective-permute-start.27 = (bf16[64,640]{1,0:T(8,128)(2,1)S(1)}, bf16[64,640]{1,0:T(8,128)(2,1)S(1)}, u32[]{:S(2)}, u32[]{:S(2)}) collective-permute-start(bf16[64,640]{1,0:T(8,128)(2,1)S(1)} %get-tuple-element.126), channel_id=1, source_target_pairs={{0,4},{1,5},{2,6},{3,7},{4,0},{5,1},{6,2},{7,3},{8,12},{9,13},{10,... | collective-permute-start | bytes 245768 | tf_op jit(solution)/shard_map/ppermute | solution.py:284
  72.5 6.4 %collective-permute-start.29 = (bf16[64,640]{1,0:T(8,128)(2,1)S(1)}, bf16[64,640]{1,0:T(8,128)(2,1)S(1)}, u32[]{:S(2)}, u32[]{:S(2)}) collective-permute-start(bf16[64,640]{1,0:T(8,128)(2,1)S(1)} %get-tuple-element.127), channel_id=1, source_target_pairs={{0,4},{1,5},{2,6},{3,7},{4,0},{5,1},{6,2},{7,3},{8,12},{9,13},{10,... | collective-permute-start | bytes 245768 | tf_op jit(solution)/shard_map/ppermute | solution.py:284
  76.3 6.3 %collective-permute-start.28 = (bf16[64,640]{1,0:T(8,128)(2,1)S(1)}, bf16[64,640]{1,0:T(8,128)(2,1)S(1)}, u32[]{:S(2)}, u32[]{:S(2)}) collective-permute-start(bf16[64,640]{1,0:T(8,128)(2,1)S(1)} %add_convert_fusion), channel_id=1, source_target_pairs={{0,8},{1,9},{2,10},{3,11},{4,12},{5,13},{6,14},{7,15},{8,0},{9,1},... | collective-permute-start | bytes 245768 | tf_op jit(solution)/shard_map/ppermute | solution.py:284

commit v7 on v6

--- a/solution.py
+++ b/solution.py
@@ -12,7 +12,7 @@
 
 weight_decay = 0.02
 
-PLANE = 4
+PLANE = 8
 NT = (((1,), (1,)), ((), ()))
 NN = (((1,), (0,)), ((), ()))
 VMEM_LIMIT = 24 * 1024 * 1024
@@ -68,20 +68,20 @@
         steps[:, 128 * j:128 * (j + 1)] = jnp.where(low, step_of(2 * j), step_of(2 * j + 1))
 
 
-def pick_kernel(planes, turns, per_owner, own_blocks, table, *refs):
-    held, packets, blocks = refs[:len(turns)], refs[len(turns):-1], refs[-1]
+def pick_kernel(planes, per_owner, own_blocks, table, *refs):
+    held, packets, blocks = refs[:planes], refs[planes:-1], refs[-1]
     low = low_half(held[0].shape[0])
-    for i in range(len(turns)):
+    for turn in range(planes):
         for j in range(own_blocks // 2):
-            x = held[i][:, 128 * j:128 * (j + 1)].astype(jnp.float32)
-            blocks[i, 2 * j], blocks[i, 2 * j + 1] = double(x, low)
+            x = held[turn][:, 128 * j:128 * (j + 1)].astype(jnp.float32)
+            blocks[turn, 2 * j], blocks[turn, 2 * j + 1] = double(x, low)
     for mate in range(PLANE):
-        for i, turn in enumerate(turns):
+        for turn in range(planes):
             for q in range(per_owner // 2):
                 first = table[mate * planes + turn, 2 * q]
                 second = table[mate * planes + turn, 2 * q + 1]
-                pair = jnp.where(low, blocks[i, first], blocks[i, second])
-                packets[mate][i, :, 128 * q:128 * (q + 1)] = pair.astype(jnp.bfloat16)
+                pair = jnp.where(low, blocks[turn, first], blocks[turn, second])
+                packets[mate][turn, :, 128 * q:128 * (q + 1)] = pair.astype(jnp.bfloat16)
 
 
 def plane_sum_kernel(planes, per_owner, own_blocks, table, *refs):
@@ -108,21 +108,20 @@
     return pl.ds(pl.multiple_of(owner * width, width), width)
 
 
-def product_kernel(turns, mates, first, rows, pos_ref, geno, *refs):
-    packets, before, (gradient, gram) = refs[:len(mates)], refs[len(mates):-2], refs[-2:]
+def product_kernel(mate, first, rows, pos_ref, geno, packet, *refs):
+    before, (gradient, gram) = refs[:-2], refs[-2:]
     pos = pos_ref[0]
-    width = packets[0].shape[2]
-    places = [(i, turn, m, mate) for m, mate in enumerate(mates) for i, turn in enumerate(turns)]
+    planes, width = packet.shape[0], packet.shape[2]
     total = None if first else before[1][...]
-    for i, turn, m, mate in places:
-        term = dot(packets[m][i], packets[m][i], NT)
+    for turn in range(planes):
+        term = dot(packet[turn], packet[turn], NT)
         total = term if total is None else total + term
     gram[...] = total
     for r in range(geno.shape[0] // rows):
         here = slice(r * rows, (r + 1) * rows)
         total = None if first else before[0][:, here]
-        for i, turn, m, mate in places:
-            term = dot(packets[m][i], geno[here, columns_of(pos, turn, mate, width)], NT)
+        for turn in range(planes):
+            term = dot(packet[turn], geno[here, columns_of(pos, turn, mate, width)], NT)
             total = term if total is None else total + term
         gradient[:, here] = total
 
@@ -144,17 +143,15 @@
         last[...] = jnp.zeros_like(last)
 
 
-def term_kernel(groups, mate, pos_ref, geno, samples, gram, *refs):
-    packets, terms = refs[:len(groups)], refs[-1]
+def term_kernel(mate, pos_ref, geno, samples, gram, packet, terms):
     pos = pos_ref[0]
-    width = terms.shape[2]
+    planes, width = packet.shape[0], packet.shape[2]
     parts = split3(gram[...])
-    for turns, packet in zip(groups, packets):
-        for i, turn in enumerate(turns):
-            term = dot(samples[...], geno[:, columns_of(pos, turn, mate, width)], NN)
-            for part in parts:
-                term -= dot(part, packet[i], NN)
-            terms[turn] = term.astype(jnp.bfloat16)
+    for turn in range(planes):
+        term = dot(samples[...], geno[:, columns_of(pos, turn, mate, width)], NN)
+        for part in parts:
+            term -= dot(part, packet[turn], NN)
+        terms[turn] = term.astype(jnp.bfloat16)
 
 
 def on_device(genotypes, sample_factors, snp_factors, coverage):
@@ -170,7 +167,7 @@
     own_blocks = own_snps // tile_size
     width = per_owner * tile_size
     assert tile_size == 64 and per_owner % 2 == 0 and own_blocks % 2 == 0
-    assert devices % PLANE == 0 and planes % 2 == 0 and planes & (planes - 1) == 0
+    assert devices % PLANE == 0 and planes & (planes - 1) == 0
 
     sample_step = 0.5 * math.sqrt(rank) / (covered * tile_size)
 
@@ -180,10 +177,8 @@
     anywhere = pl.BlockSpec(memory_space=pl.ANY)
     params = pltpu.CompilerParams(vmem_limit_bytes=VMEM_LIMIT)
     pos = position.reshape(1)
-    half = planes // 2
-    near, far = groups = tuple(range(half)), tuple(range(half, planes))
-    packet = jax.ShapeDtypeStruct((half, rank, width), jnp.bfloat16)
-    dense_blocks = pltpu.VMEM((half, own_blocks, rank, 128), jnp.float32)
+    packet = jax.ShapeDtypeStruct((planes, rank, width), jnp.bfloat16)
+    dense_blocks = pltpu.VMEM((planes, own_blocks, rank, 128), jnp.float32)
     by_samples = jax.ShapeDtypeStruct((rank, samples_here), jnp.float32)
     square = jax.ShapeDtypeStruct((rank, rank), jnp.float32)
 
@@ -217,17 +212,17 @@
     )(pos, coverage)
     small = cost(0, 2 * 1024 * 1024)
 
-    def pick(turns, held):
+    def pick(held):
         return pl.pallas_call(
-            functools.partial(pick_kernel, planes, turns, per_owner, own_blocks),
+            functools.partial(pick_kernel, planes, per_owner, own_blocks),
             out_shape=(packet,) * PLANE,
-            in_specs=[smem] + [vmem] * half,
+            in_specs=[smem] + [vmem] * planes,
             out_specs=(vmem,) * PLANE,
             scratch_shapes=[dense_blocks],
             compiler_params=params,
             cost_estimate=small,
             name="pick_blocks",
-        )(table, *[held[turn] for turn in turns])
+        )(table, *held)
 
     def plane_sum(terms, after):
         sums = pl.pallas_call(
@@ -238,24 +233,24 @@
             ),
             in_specs=[smem] + [vmem] * PLANE + [anywhere] * len(after),
             out_specs=(vmem,) * planes,
-            scratch_shapes=[pltpu.VMEM((planes, own_blocks, rank, 128), jnp.float32)],
+            scratch_shapes=[dense_blocks],
             compiler_params=params,
             cost_estimate=small,
             name="plane_sum",
         )(table, *terms, *after)
         return list(sums)
 
-    def product(turns, mates, panels, before):
-        share = len(turns) * len(mates) * samples_here * snps_here // devices
+    def product(mate, panel, before):
+        share = samples_here * snps_here // PLANE
         return pl.pallas_call(
-            functools.partial(product_kernel, turns, mates, not before, 256),
+            functools.partial(product_kernel, mate, not before, 256),
             out_shape=(by_samples, square),
-            in_specs=[smem] + [vmem] * (1 + len(mates) + len(before)),
+            in_specs=[smem] + [vmem] * (2 + len(before)),
             out_specs=(vmem, vmem),
             compiler_params=params,
             cost_estimate=cost(8 * rank * share, 2 * share),
             name="panel_product",
-        )(pos, geno, *[panels[turns][mate] for mate in mates], *before)
+        )(pos, geno, panel, *before)
 
     def sample_update(samples, gradient, gram, outs):
         return pl.pallas_call(
@@ -268,17 +263,17 @@
             name="sample_update",
         )(samples, gradient, gram)
 
-    def terms_for(mate, samples_bf16, gram, panels, after):
+    def terms_for(mate, samples_bf16, gram, panel):
         share = samples_here * snps_here // PLANE
         return pl.pallas_call(
-            functools.partial(term_kernel, groups, mate),
-            out_shape=jax.ShapeDtypeStruct((planes, rank, width), jnp.bfloat16),
-            in_specs=[smem] + [vmem] * (3 + len(groups)) + [anywhere] * len(after),
+            functools.partial(term_kernel, mate),
+            out_shape=packet,
+            in_specs=[smem] + [vmem] * 4,
             out_specs=vmem,
             compiler_params=params,
             cost_estimate=cost(8 * rank * share, 2 * share),
             name="mate_terms",
-        )(pos, geno, samples_bf16, gram, *[panels[turns][mate] for turns in groups], *after)
+        )(pos, geno, samples_bf16, gram, panel)
 
     def swap(x, turn):
         return lax.ppermute(x, "rows", [(r, r ^ turn) for r in range(devices)])
@@ -295,15 +290,11 @@
             if iteration == 0 and turn != bit:
                 source, _ = lax.optimization_barrier((source, samples))
             held[turn] = swap(source, bit * PLANE)
-        panels = {}
-        for turns in (near, far):
-            packets = pick(turns, held)
-            panels[turns] = [to_mate(packets[mate], mate) for mate in range(PLANE)]
+        packets = pick([held[turn] for turn in range(planes)])
+        panels = [to_mate(packets[mate], mate) for mate in range(PLANE)]
         partial = ()
-        for turns, mates in (
-            (near, (0,)), (far, (0,)), (near, (1,)), (near, (2, 3)), (far, (1,)), (far, (2,)), (far, (3,))
-        ):
-            partial = product(turns, mates, panels, partial)
+        for mate in (0, 7, 6, 5, 4, 3, 2, 1):
+            partial = product(mate, panels[mate], partial)
         rounded = (jax.ShapeDtypeStruct((rank, samples_here), jnp.bfloat16), square)
         if iteration < ROUNDS - 1:
             samples, *current = sample_update(samples, *partial, (by_samples,) + rounded)
@@ -314,8 +305,9 @@
                 samples, *partial, (by_samples, jax.ShapeDtypeStruct((8, 128), jnp.float32))
             )
             after = [token]
-        terms = {mate: terms_for(mate, *current, panels, []) for mate in (2, 3, 1, 0)}
-        sums = plane_sum([to_mate(terms[mate], mate) for mate in range(PLANE)], after)
+        sums = plane_sum(
+            [to_mate(terms_for(mate, *current, panels[mate]), mate) for mate in range(PLANE)], after
+        )
         for turn in range(planes - 1, 0, -1):
             bit = turn & -turn
             arrived = swap(sums[turn].astype(jnp.bfloat16), bit * PLANE)

time: 83.6 us -> 81.1 us (0.970)
  waiting for transfers between devices: 29.2 us -> 21.1 us
  starting transfers between devices: 32 us -> 36.9 us
    ppermute x30 -> x32, waiting for transfers between devices: 29.2 us -> 21.1 us  [swap(): return lax.ppermute(x, 'rows', [(r, r ^ turn) for r in range(devices)])]
    ppermute x30 -> x32, starting transfers between devices: 32 us -> 36.9 us  [swap(): return lax.ppermute(x, 'rows', [(r, r ^ turn) for r in range(devices)])]
    pallas_call x26 -> x34, Pallas kernels: 12.7 us -> 13.8 us  [the longest x16 7.43 us: product(): pl.pallas_call(functools.partial(product_kernel, mate, not before, 256),...]
  transfers between devices with their start and end apart: 30 -> 32, of which waited for: 15 -> 10; matrix products, arithmetic and copies ran while one was open for 0% -> 0% of each run, Pallas kernels for 18% -> 20%
where the time goes in v7:
time: 81.1 us; the launch traced here: 80.9 us
  starting transfers between devices  36.9 us (45%)
  waiting for transfers between devices  21.1 us (26%)
  Pallas kernels  20.2 us (25%)
  other arithmetic  1.7 us (2%)
  between operations  0.98 us (1%)
    ppermute x32, starting transfers between devices, swap(): return lax.ppermute(x, 'rows', [(r, r ^ turn) for r in range(devices)])  36.9 us
    ppermute x32, waiting for transfers between devices, swap(): return lax.ppermute(x, 'rows', [(r, r ^ turn) for r in range(devices)])  21.1 us
    pallas_call x16, Pallas kernels, product(): pl.pallas_call(functools.partial(product_kernel, mate, not before, 256),...  7.43 us
    pallas_call x16, Pallas kernels, terms_for(): pl.pallas_call(functools.partial(term_kernel, mate), out_shape=packet, in...  5.9 us
    pallas_call x1, Pallas kernels, on_device(): pl.pallas_call(functools.partial(load_kernel, planes, per_owner, own_bloc...  3.51 us
    pallas_call x3, Pallas kernels, sample_update(): pl.pallas_call(functools.partial(sample_kernel, sample_step), out_shape=o...  1.76 us
  transfers between devices with their start and end apart: 32, of which 10 were waited for; matrix products, arithmetic and copies ran while one was open for 0% of the time, Pallas kernels for 20%

profile of v7, /device:TPU:0, one launch (start us, length us, event | category | flops | bytes accessed | tf_op | source)
XLA Modules:
  0.0 80.9 jit_solution(128421903433678358)
XLA Ops:
  0.6 0.9 %convert_bitcast_fusion.refs_0_ = bf16[64,640]{1,0:T(8,128)(2,1)S(1)} fusion(f32[640,64]{0,1:T(8,128)} %param.6), kind=kLoop, calls=%fused_computation.2 | loop fusion | flops 40960 | bytes 245760 | tf_op jit(solution)/shard_map/convert_element_type | solution.py:286
  1.6 4.1 %collective-permute-start = (bf16[64,640]{1,0:T(8,128)(2,1)S(1)}, bf16[64,640]{1,0:T(8,128)(2,1)S(1)}, u32[]{:S(2)}, u32[]{:S(2)}) collective-permute-start(bf16[64,640]{1,0:T(8,128)(2,1)S(1)} %convert_bitcast_fusion.refs_0_), channel_id=1, source_target_pairs={{0,8},{1,9},{2,10},{3,11},{4,12},{5,13},{6,14},{7,15},{8,0},{9,1},... | collective-permute-start | bytes 245768 | tf_op jit(solution)/shard_map/ppermute | solution.py:279
  5.7 3.5 %load_batch.1 = (bf16[1024,4096]{1,0:T(8,128)(2,1)S(1)}, f32[64,1024]{1,0:T(8,128)S(1)}, s32[16,4]{1,0:T(8,128)S(4)}) custom-call(s32[1]{0:T(128)} %bitcast.pos_ref, s32[16,64]{1,0:T(8,128)} %cov.3, bf16[1024,4096]{1,0:T(8,128)(2,1)} %geno.1, f32[64,1024]{1,0:T(8,128)} %bitcast.13), custom_call_target="tpu_custom_call" | custom-call | bytes 8388608 | tf_op jit(solution)/shard_map/load_batch/pallas_call | solution.py:188
  9.2 0.7 collective-permute-done.refs_1_
  10.1 1.2 %collective-permute-start.7 = (bf16[2,64,256]{2,1,0:T(8,128)(2,1)S(1)}, bf16[2,64,256]{2,1,0:T(8,128)(2,1)S(1)}, u32[]{:S(2)}, u32[]{:S(2)}) collective-permute-start(bf16[2,64,256]{2,1,0:T(8,128)(2,1)S(1)} %get-tuple-element.73), channel_id=1, source_target_pairs={{0,7},{1,6},{2,5},{3,4},{4,3},{5,2},{6,1},{7,0},{8,15},{9,14},{10,... | collective-permute-start | bytes 196616 | tf_op jit(solution)/shard_map/ppermute | solution.py:279
  11.3 0.8 collective-permute-start.6
  12.1 1.3 %collective-permute-start.5 = (bf16[2,64,256]{2,1,0:T(8,128)(2,1)S(1)}, bf16[2,64,256]{2,1,0:T(8,128)(2,1)S(1)}, u32[]{:S(2)}, u32[]{:S(2)}) collective-permute-start(bf16[2,64,256]{2,1,0:T(8,128)(2,1)S(1)} %get-tuple-element.71), channel_id=1, source_target_pairs={{0,5},{1,4},{2,7},{3,6},{4,1},{5,0},{6,3},{7,2},{8,13},{9,12},{10,... | collective-permute-start | bytes 196616 | tf_op jit(solution)/shard_map/ppermute | solution.py:279
  13.4 1.1 %collective-permute-start.4 = (bf16[2,64,256]{2,1,0:T(8,128)(2,1)S(1)}, bf16[2,64,256]{2,1,0:T(8,128)(2,1)S(1)}, u32[]{:S(2)}, u32[]{:S(2)}) collective-permute-start(bf16[2,64,256]{2,1,0:T(8,128)(2,1)S(1)} %get-tuple-element.70), channel_id=1, source_target_pairs={{0,4},{1,5},{2,6},{3,7},{4,0},{5,1},{6,2},{7,3},{8,12},{9,13},{10,... | collective-permute-start | bytes 196616 | tf_op jit(solution)/shard_map/ppermute | solution.py:279
  15.2 1.6 %collective-permute-start.2 = (bf16[2,64,256]{2,1,0:T(8,128)(2,1)S(1)}, bf16[2,64,256]{2,1,0:T(8,128)(2,1)S(1)}, u32[]{:S(2)}, u32[]{:S(2)}) collective-permute-start(bf16[2,64,256]{2,1,0:T(8,128)(2,1)S(1)} %get-tuple-element.68), channel_id=1, source_target_pairs={{0,2},{1,3},{2,0},{3,1},{4,6},{5,7},{6,4},{7,5},{8,10},{9,11},{10,... | collective-permute-start | bytes 196616 | tf_op jit(solution)/shard_map/ppermute | solution.py:279
  18.5 0.6 collective-permute-done.4.packet
  21.8 1.5 %collective-permute-start.14 = (bf16[2,64,256]{2,1,0:T(8,128)(2,1)S(1)}, bf16[2,64,256]{2,1,0:T(8,128)(2,1)S(1)}, u32[]{:S(2)}, u32[]{:S(2)}) collective-permute-start(bf16[2,64,256]{2,1,0:T(8,128)(2,1)S(1)} %mate_terms.23), channel_id=1, source_target_pairs={{0,7},{1,6},{2,5},{3,4},{4,3},{5,2},{6,1},{7,0},{8,15},{9,14},{10,... | collective-permute-start | bytes 196616 | tf_op jit(solution)/shard_map/ppermute | solution.py:279
  23.7 1.4 %collective-permute-start.13 = (bf16[2,64,256]{2,1,0:T(8,128)(2,1)S(1)}, bf16[2,64,256]{2,1,0:T(8,128)(2,1)S(1)}, u32[]{:S(2)}, u32[]{:S(2)}) collective-permute-start(bf16[2,64,256]{2,1,0:T(8,128)(2,1)S(1)} %mate_terms.22), channel_id=1, source_target_pairs={{0,6},{1,7},{2,4},{3,5},{4,2},{5,3},{6,0},{7,1},{8,14},{9,15},{10,... | collective-permute-start | bytes 196616 | tf_op jit(solution)/shard_map/ppermute | solution.py:279
  25.4 1.2 %collective-permute-start.12 = (bf16[2,64,256]{2,1,0:T(8,128)(2,1)S(1)}, bf16[2,64,256]{2,1,0:T(8,128)(2,1)S(1)}, u32[]{:S(2)}, u32[]{:S(2)}) collective-permute-start(bf16[2,64,256]{2,1,0:T(8,128)(2,1)S(1)} %mate_terms.21), channel_id=1, source_target_pairs={{0,5},{1,4},{2,7},{3,6},{4,1},{5,0},{6,3},{7,2},{8,13},{9,12},{10,... | collective-permute-start | bytes 196616 | tf_op jit(solution)/shard_map/ppermute | solution.py:279
  27.9 0.8 %collective-permute-start.10 = (bf16[2,64,256]{2,1,0:T(8,128)(2,1)S(1)}, bf16[2,64,256]{2,1,0:T(8,128)(2,1)S(1)}, u32[]{:S(2)}, u32[]{:S(2)}) collective-permute-start(bf16[2,64,256]{2,1,0:T(8,128)(2,1)S(1)} %mate_terms.19), channel_id=1, source_target_pairs={{0,3},{1,2},{2,1},{3,0},{4,7},{5,6},{6,5},{7,4},{8,11},{9,10},{10,... | collective-permute-start | bytes 196616 | tf_op jit(solution)/shard_map/ppermute | solution.py:279
  29.6 1.1 %collective-permute-start.9 = (bf16[2,64,256]{2,1,0:T(8,128)(2,1)S(1)}, bf16[2,64,256]{2,1,0:T(8,128)(2,1)S(1)}, u32[]{:S(2)}, u32[]{:S(2)}) collective-permute-start(bf16[2,64,256]{2,1,0:T(8,128)(2,1)S(1)} %mate_terms.18), channel_id=1, source_target_pairs={{0,2},{1,3},{2,0},{3,1},{4,6},{5,7},{6,4},{7,5},{8,10},{9,11},{10,... | collective-permute-start | bytes 196616 | tf_op jit(solution)/shard_map/ppermute | solution.py:279
  32.1 2.2 %collective-permute-done.9.refs_2_ = bf16[2,64,256]{2,1,0:T(8,128)(2,1)S(1)} collective-permute-done((bf16[2,64,256]{2,1,0:T(8,128)(2,1)S(1)}, bf16[2,64,256]{2,1,0:T(8,128)(2,1)S(1)}, u32[]{:S(2)}, u32[]{:S(2)}) %collective-permute-start.9) | collective-permute-done | bytes 65568 | tf_op jit(solution)/shard_map/ppermute | solution.py:279
  34.8 3.3 %collective-permute-start.15 = (bf16[64,640]{1,0:T(8,128)(2,1)S(1)}, bf16[64,640]{1,0:T(8,128)(2,1)S(1)}, u32[]{:S(2)}, u32[]{:S(2)}) collective-permute-start(bf16[64,640]{1,0:T(8,128)(2,1)S(1)} %get-tuple-element.95), channel_id=1, source_target_pairs={{0,8},{1,9},{2,10},{3,11},{4,12},{5,13},{6,14},{7,15},{8,0},{9,1},... | collective-permute-start | bytes 245768 | tf_op jit(solution)/shard_map/ppermute | solution.py:279
  38.2 4.1 %collective-permute-done.15 = bf16[64,640]{1,0:T(8,128)(2,1)S(1)} collective-permute-done((bf16[64,640]{1,0:T(8,128)(2,1)S(1)}, bf16[64,640]{1,0:T(8,128)(2,1)S(1)}, u32[]{:S(2)}, u32[]{:S(2)}) %collective-permute-start.15) | collective-permute-done | bytes 81952 | tf_op jit(solution)/shard_map/ppermute | solution.py:279
  42.3 1.2 %collective-permute-start.16 = (bf16[64,640]{1,0:T(8,128)(2,1)S(1)}, bf16[64,640]{1,0:T(8,128)(2,1)S(1)}, u32[]{:S(2)}, u32[]{:S(2)}) collective-permute-start(bf16[64,640]{1,0:T(8,128)(2,1)S(1)} %fusion.refs_0_), channel_id=1, source_target_pairs={{0,8},{1,9},{2,10},{3,11},{4,12},{5,13},{6,14},{7,15},{8,0},{9,1},... | collective-permute-start | bytes 245768 | tf_op jit(solution)/shard_map/ppermute | solution.py:279
  43.5 5.4 %collective-permute-done.16.refs_1_ = bf16[64,640]{1,0:T(8,128)(2,1)S(1)} collective-permute-done((bf16[64,640]{1,0:T(8,128)(2,1)S(1)}, bf16[64,640]{1,0:T(8,128)(2,1)S(1)}, u32[]{:S(2)}, u32[]{:S(2)}) %collective-permute-start.16) | collective-permute-done | bytes 81952 | tf_op jit(solution)/shard_map/ppermute | solution.py:279
  49.4 2.0 %collective-permute-start.21 = (bf16[2,64,256]{2,1,0:T(8,128)(2,1)S(1)}, bf16[2,64,256]{2,1,0:T(8,128)(2,1)S(1)}, u32[]{:S(2)}, u32[]{:S(2)}) collective-permute-start(bf16[2,64,256]{2,1,0:T(8,128)(2,1)S(1)} %get-tuple-element.100), channel_id=1, source_target_pairs={{0,5},{1,4},{2,7},{3,6},{4,1},{5,0},{6,3},{7,2},{8,13},{9,12},{10,... | collective-permute-start | bytes 196616 | tf_op jit(solution)/shard_map/ppermute | solution.py:279
  51.4 2.2 %collective-permute-start.20 = (bf16[2,64,256]{2,1,0:T(8,128)(2,1)S(1)}, bf16[2,64,256]{2,1,0:T(8,128)(2,1)S(1)}, u32[]{:S(2)}, u32[]{:S(2)}) collective-permute-start(bf16[2,64,256]{2,1,0:T(8,128)(2,1)S(1)} %get-tuple-element.99), channel_id=1, source_target_pairs={{0,4},{1,5},{2,6},{3,7},{4,0},{5,1},{6,2},{7,3},{8,12},{9,13},{10,... | collective-permute-start | bytes 196616 | tf_op jit(solution)/shard_map/ppermute | solution.py:279
  54.0 0.9 %collective-permute-start.18 = (bf16[2,64,256]{2,1,0:T(8,128)(2,1)S(1)}, bf16[2,64,256]{2,1,0:T(8,128)(2,1)S(1)}, u32[]{:S(2)}, u32[]{:S(2)}) collective-permute-start(bf16[2,64,256]{2,1,0:T(8,128)(2,1)S(1)} %get-tuple-element.97), channel_id=1, source_target_pairs={{0,2},{1,3},{2,0},{3,1},{4,6},{5,7},{6,4},{7,5},{8,10},{9,11},{10,... | collective-permute-start | bytes 196616 | tf_op jit(solution)/shard_map/ppermute | solution.py:279
  55.5 1.0 %collective-permute-start.17 = (bf16[2,64,256]{2,1,0:T(8,128)(2,1)S(1)}, bf16[2,64,256]{2,1,0:T(8,128)(2,1)S(1)}, u32[]{:S(2)}, u32[]{:S(2)}) collective-permute-start(bf16[2,64,256]{2,1,0:T(8,128)(2,1)S(1)} %get-tuple-element.96), channel_id=1, source_target_pairs={{0,1},{1,0},{2,3},{3,2},{4,5},{5,4},{6,7},{7,6},{8,9},{9,8},{10,11... | collective-permute-start | bytes 196616 | tf_op jit(solution)/shard_map/ppermute | solution.py:279
  61.3 2.7 %collective-permute-start.29 = (bf16[2,64,256]{2,1,0:T(8,128)(2,1)S(1)}, bf16[2,64,256]{2,1,0:T(8,128)(2,1)S(1)}, u32[]{:S(2)}, u32[]{:S(2)}) collective-permute-start(bf16[2,64,256]{2,1,0:T(8,128)(2,1)S(1)} %mate_terms.30), channel_id=1, source_target_pairs={{0,6},{1,7},{2,4},{3,5},{4,2},{5,3},{6,0},{7,1},{8,14},{9,15},{10,... | collective-permute-start | bytes 196616 | tf_op jit(solution)/shard_map/ppermute | solution.py:279
  64.8 1.8 %collective-permute-start.27 = (bf16[2,64,256]{2,1,0:T(8,128)(2,1)S(1)}, bf16[2,64,256]{2,1,0:T(8,128)(2,1)S(1)}, u32[]{:S(2)}, u32[]{:S(2)}) collective-permute-start(bf16[2,64,256]{2,1,0:T(8,128)(2,1)S(1)} %mate_terms.28), channel_id=1, source_target_pairs={{0,4},{1,5},{2,6},{3,7},{4,0},{5,1},{6,2},{7,3},{8,12},{9,13},{10,... | collective-permute-start | bytes 196616 | tf_op jit(solution)/shard_map/ppermute | solution.py:279
  68.1 1.5 %collective-permute-start.25 = (bf16[2,64,256]{2,1,0:T(8,128)(2,1)S(1)}, bf16[2,64,256]{2,1,0:T(8,128)(2,1)S(1)}, u32[]{:S(2)}, u32[]{:S(2)}) collective-permute-start(bf16[2,64,256]{2,1,0:T(8,128)(2,1)S(1)} %mate_terms.26), channel_id=1, source_target_pairs={{0,2},{1,3},{2,0},{3,1},{4,6},{5,7},{6,4},{7,5},{8,10},{9,11},{10,... | collective-permute-start | bytes 196616 | tf_op jit(solution)/shard_map/ppermute | solution.py:279
  69.7 0.9 %sample_update.4 = (f32[64,1024]{1,0:T(8,128)}, f32[8,128]{1,0:T(8,128)S(1)}) custom-call(f32[64,1024]{1,0:T(8,128)S(1)} %get-tuple-element.91.samples, f32[64,1024]{1,0:T(8,128)S(1)} %get-tuple-element.118.gradient, f32[64,64]{1,0:T(8,128)S(1)} %get-tuple-element.119.gram), custom_call_target="tpu_custom_call" | custom-call | bytes 2097152 | tf_op jit(solution)/shard_map/sample_update/pallas_call | solution.py:256
  71.0 1.7 %collective-permute-done.25.refs_2_ = bf16[2,64,256]{2,1,0:T(8,128)(2,1)S(1)} collective-permute-done((bf16[2,64,256]{2,1,0:T(8,128)(2,1)S(1)}, bf16[2,64,256]{2,1,0:T(8,128)(2,1)S(1)}, u32[]{:S(2)}, u32[]{:S(2)}) %collective-permute-start.25) | collective-permute-done | bytes 65568 | tf_op jit(solution)/shard_map/ppermute | solution.py:279
  73.3 2.2 %collective-permute-start.31 = (bf16[64,640]{1,0:T(8,128)(2,1)S(1)}, bf16[64,640]{1,0:T(8,128)(2,1)S(1)}, u32[]{:S(2)}, u32[]{:S(2)}) collective-permute-start(bf16[64,640]{1,0:T(8,128)(2,1)S(1)} %get-tuple-element.125), channel_id=1, source_target_pairs={{0,8},{1,9},{2,10},{3,11},{4,12},{5,13},{6,14},{7,15},{8,0},{9,1},... | collective-permute-start | bytes 245768 | tf_op jit(solution)/shard_map/ppermute | solution.py:279
  75.5 4.7 %collective-permute-done.31 = bf16[64,640]{1,0:T(8,128)(2,1)S(1)} collective-permute-done((bf16[64,640]{1,0:T(8,128)(2,1)S(1)}, bf16[64,640]{1,0:T(8,128)(2,1)S(1)}, u32[]{:S(2)}, u32[]{:S(2)}) %collective-permute-start.31) | collective-permute-done | bytes 81952 | tf_op jit(solution)/shard_map/ppermute | solution.py:279
  80.2 0.7 add_bitcast_fusion
  (80 shorter events, 19.3 us)
Async XLA Ops:
  1.6 8.3 %collective-permute-start = (bf16[64,640]{1,0:T(8,128)(2,1)S(1)}, bf16[64,640]{1,0:T(8,128)(2,1)S(1)}, u32[]{:S(2)}, u32[]{:S(2)}) collective-permute-start(bf16[64,640]{1,0:T(8,128)(2,1)S(1)} %convert_bitcast_fusion.refs_0_), channel_id=1, source_target_pairs={{0,8},{1,9},{2,10},{3,11},{4,12},{5,13},{6,14},{7,15},{8,0},{9,1},... | collective-permute-start | bytes 245768 | tf_op jit(solution)/shard_map/ppermute | solution.py:279
  10.1 5.1 %collective-permute-start.7 = (bf16[2,64,256]{2,1,0:T(8,128)(2,1)S(1)}, bf16[2,64,256]{2,1,0:T(8,128)(2,1)S(1)}, u32[]{:S(2)}, u32[]{:S(2)}) collective-permute-start(bf16[2,64,256]{2,1,0:T(8,128)(2,1)S(1)} %get-tuple-element.73), channel_id=1, source_target_pairs={{0,7},{1,6},{2,5},{3,4},{4,3},{5,2},{6,1},{7,0},{8,15},{9,14},{10,... | collective-permute-start | bytes 196616 | tf_op jit(solution)/shard_map/ppermute | solution.py:279
  11.3 6.0 %collective-permute-start.6 = (bf16[2,64,256]{2,1,0:T(8,128)(2,1)S(1)}, bf16[2,64,256]{2,1,0:T(8,128)(2,1)S(1)}, u32[]{:S(2)}, u32[]{:S(2)}) collective-permute-start(bf16[2,64,256]{2,1,0:T(8,128)(2,1)S(1)} %get-tuple-element.72), channel_id=1, source_target_pairs={{0,6},{1,7},{2,4},{3,5},{4,2},{5,3},{6,0},{7,1},{8,14},{9,15},{10,... | collective-permute-start | bytes 196616 | tf_op jit(solution)/shard_map/ppermute | solution.py:279
  12.1 5.9 %collective-permute-start.5 = (bf16[2,64,256]{2,1,0:T(8,128)(2,1)S(1)}, bf16[2,64,256]{2,1,0:T(8,128)(2,1)S(1)}, u32[]{:S(2)}, u32[]{:S(2)}) collective-permute-start(bf16[2,64,256]{2,1,0:T(8,128)(2,1)S(1)} %get-tuple-element.71), channel_id=1, source_target_pairs={{0,5},{1,4},{2,7},{3,6},{4,1},{5,0},{6,3},{7,2},{8,13},{9,12},{10,... | collective-permute-start | bytes 196616 | tf_op jit(solution)/shard_map/ppermute | solution.py:279
  13.4 5.7 %collective-permute-start.4 = (bf16[2,64,256]{2,1,0:T(8,128)(2,1)S(1)}, bf16[2,64,256]{2,1,0:T(8,128)(2,1)S(1)}, u32[]{:S(2)}, u32[]{:S(2)}) collective-permute-start(bf16[2,64,256]{2,1,0:T(8,128)(2,1)S(1)} %get-tuple-element.70), channel_id=1, source_target_pairs={{0,4},{1,5},{2,6},{3,7},{4,0},{5,1},{6,2},{7,3},{8,12},{9,13},{10,... | collective-permute-start | bytes 196616 | tf_op jit(solution)/shard_map/ppermute | solution.py:279
  14.6 5.0 %collective-permute-start.3 = (bf16[2,64,256]{2,1,0:T(8,128)(2,1)S(1)}, bf16[2,64,256]{2,1,0:T(8,128)(2,1)S(1)}, u32[]{:S(2)}, u32[]{:S(2)}) collective-permute-start(bf16[2,64,256]{2,1,0:T(8,128)(2,1)S(1)} %get-tuple-element.69), channel_id=1, source_target_pairs={{0,3},{1,2},{2,1},{3,0},{4,7},{5,6},{6,5},{7,4},{8,11},{9,10},{10,... | collective-permute-start | bytes 196616 | tf_op jit(solution)/shard_map/ppermute | solution.py:279
  15.2 4.9 %collective-permute-start.2 = (bf16[2,64,256]{2,1,0:T(8,128)(2,1)S(1)}, bf16[2,64,256]{2,1,0:T(8,128)(2,1)S(1)}, u32[]{:S(2)}, u32[]{:S(2)}) collective-permute-start(bf16[2,64,256]{2,1,0:T(8,128)(2,1)S(1)} %get-tuple-element.68), channel_id=1, source_target_pairs={{0,2},{1,3},{2,0},{3,1},{4,6},{5,7},{6,4},{7,5},{8,10},{9,11},{10,... | collective-permute-start | bytes 196616 | tf_op jit(solution)/shard_map/ppermute | solution.py:279
  17.3 3.3 %collective-permute-start.1 = (bf16[2,64,256]{2,1,0:T(8,128)(2,1)S(1)}, bf16[2,64,256]{2,1,0:T(8,128)(2,1)S(1)}, u32[]{:S(2)}, u32[]{:S(2)}) collective-permute-start(bf16[2,64,256]{2,1,0:T(8,128)(2,1)S(1)} %get-tuple-element.67), channel_id=1, source_target_pairs={{0,1},{1,0},{2,3},{3,2},{4,5},{5,4},{6,7},{7,6},{8,9},{9,8},{10,11... | collective-permute-start | bytes 196616 | tf_op jit(solution)/shard_map/ppermute | solution.py:279
  21.8 7.7 %collective-permute-start.14 = (bf16[2,64,256]{2,1,0:T(8,128)(2,1)S(1)}, bf16[2,64,256]{2,1,0:T(8,128)(2,1)S(1)}, u32[]{:S(2)}, u32[]{:S(2)}) collective-permute-start(bf16[2,64,256]{2,1,0:T(8,128)(2,1)S(1)} %mate_terms.23), channel_id=1, source_target_pairs={{0,7},{1,6},{2,5},{3,4},{4,3},{5,2},{6,1},{7,0},{8,15},{9,14},{10,... | collective-permute-start | bytes 196616 | tf_op jit(solution)/shard_map/ppermute | solution.py:279
  23.7 7.0 %collective-permute-start.13 = (bf16[2,64,256]{2,1,0:T(8,128)(2,1)S(1)}, bf16[2,64,256]{2,1,0:T(8,128)(2,1)S(1)}, u32[]{:S(2)}, u32[]{:S(2)}) collective-permute-start(bf16[2,64,256]{2,1,0:T(8,128)(2,1)S(1)} %mate_terms.22), channel_id=1, source_target_pairs={{0,6},{1,7},{2,4},{3,5},{4,2},{5,3},{6,0},{7,1},{8,14},{9,15},{10,... | collective-permute-start | bytes 196616 | tf_op jit(solution)/shard_map/ppermute | solution.py:279
  25.4 5.6 %collective-permute-start.12 = (bf16[2,64,256]{2,1,0:T(8,128)(2,1)S(1)}, bf16[2,64,256]{2,1,0:T(8,128)(2,1)S(1)}, u32[]{:S(2)}, u32[]{:S(2)}) collective-permute-start(bf16[2,64,256]{2,1,0:T(8,128)(2,1)S(1)} %mate_terms.21), channel_id=1, source_target_pairs={{0,5},{1,4},{2,7},{3,6},{4,1},{5,0},{6,3},{7,2},{8,13},{9,12},{10,... | collective-permute-start | bytes 196616 | tf_op jit(solution)/shard_map/ppermute | solution.py:279
  27.0 4.7 %collective-permute-start.11 = (bf16[2,64,256]{2,1,0:T(8,128)(2,1)S(1)}, bf16[2,64,256]{2,1,0:T(8,128)(2,1)S(1)}, u32[]{:S(2)}, u32[]{:S(2)}) collective-permute-start(bf16[2,64,256]{2,1,0:T(8,128)(2,1)S(1)} %mate_terms.20), channel_id=1, source_target_pairs={{0,4},{1,5},{2,6},{3,7},{4,0},{5,1},{6,2},{7,3},{8,12},{9,13},{10,... | collective-permute-start | bytes 196616 | tf_op jit(solution)/shard_map/ppermute | solution.py:279
  27.9 4.1 %collective-permute-start.10 = (bf16[2,64,256]{2,1,0:T(8,128)(2,1)S(1)}, bf16[2,64,256]{2,1,0:T(8,128)(2,1)S(1)}, u32[]{:S(2)}, u32[]{:S(2)}) collective-permute-start(bf16[2,64,256]{2,1,0:T(8,128)(2,1)S(1)} %mate_terms.19), channel_id=1, source_target_pairs={{0,3},{1,2},{2,1},{3,0},{4,7},{5,6},{6,5},{7,4},{8,11},{9,10},{10,... | collective-permute-start | bytes 196616 | tf_op jit(solution)/shard_map/ppermute | solution.py:279
  29.6 4.7 %collective-permute-start.9 = (bf16[2,64,256]{2,1,0:T(8,128)(2,1)S(1)}, bf16[2,64,256]{2,1,0:T(8,128)(2,1)S(1)}, u32[]{:S(2)}, u32[]{:S(2)}) collective-permute-start(bf16[2,64,256]{2,1,0:T(8,128)(2,1)S(1)} %mate_terms.18), channel_id=1, source_target_pairs={{0,2},{1,3},{2,0},{3,1},{4,6},{5,7},{6,4},{7,5},{8,10},{9,11},{10,... | collective-permute-start | bytes 196616 | tf_op jit(solution)/shard_map/ppermute | solution.py:279
  30.7 3.6 %collective-permute-start.8 = (bf16[2,64,256]{2,1,0:T(8,128)(2,1)S(1)}, bf16[2,64,256]{2,1,0:T(8,128)(2,1)S(1)}, u32[]{:S(2)}, u32[]{:S(2)}) collective-permute-start(bf16[2,64,256]{2,1,0:T(8,128)(2,1)S(1)} %mate_terms.17), channel_id=1, source_target_pairs={{0,1},{1,0},{2,3},{3,2},{4,5},{5,4},{6,7},{7,6},{8,9},{9,8},{10,11... | collective-permute-start | bytes 196616 | tf_op jit(solution)/shard_map/ppermute | solution.py:279
  34.8 7.5 %collective-permute-start.15 = (bf16[64,640]{1,0:T(8,128)(2,1)S(1)}, bf16[64,640]{1,0:T(8,128)(2,1)S(1)}, u32[]{:S(2)}, u32[]{:S(2)}) collective-permute-start(bf16[64,640]{1,0:T(8,128)(2,1)S(1)} %get-tuple-element.95), channel_id=1, source_target_pairs={{0,8},{1,9},{2,10},{3,11},{4,12},{5,13},{6,14},{7,15},{8,0},{9,1},... | collective-permute-start | bytes 245768 | tf_op jit(solution)/shard_map/ppermute | solution.py:279
  42.3 6.5 %collective-permute-start.16 = (bf16[64,640]{1,0:T(8,128)(2,1)S(1)}, bf16[64,640]{1,0:T(8,128)(2,1)S(1)}, u32[]{:S(2)}, u32[]{:S(2)}) collective-permute-start(bf16[64,640]{1,0:T(8,128)(2,1)S(1)} %fusion.refs_0_), channel_id=1, source_target_pairs={{0,8},{1,9},{2,10},{3,11},{4,12},{5,13},{6,14},{7,15},{8,0},{9,1},... | collective-permute-start | bytes 245768 | tf_op jit(solution)/shard_map/ppermute | solution.py:279
  49.1 4.9 %collective-permute-start.23 = (bf16[2,64,256]{2,1,0:T(8,128)(2,1)S(1)}, bf16[2,64,256]{2,1,0:T(8,128)(2,1)S(1)}, u32[]{:S(2)}, u32[]{:S(2)}) collective-permute-start(bf16[2,64,256]{2,1,0:T(8,128)(2,1)S(1)} %get-tuple-element.102), channel_id=1, source_target_pairs={{0,7},{1,6},{2,5},{3,4},{4,3},{5,2},{6,1},{7,0},{8,15},{9,14},{10,... | collective-permute-start | bytes 196616 | tf_op jit(solution)/shard_map/ppermute | solution.py:279
  49.2 6.3 %collective-permute-start.22 = (bf16[2,64,256]{2,1,0:T(8,128)(2,1)S(1)}, bf16[2,64,256]{2,1,0:T(8,128)(2,1)S(1)}, u32[]{:S(2)}, u32[]{:S(2)}) collective-permute-start(bf16[2,64,256]{2,1,0:T(8,128)(2,1)S(1)} %get-tuple-element.101), channel_id=1, source_target_pairs={{0,6},{1,7},{2,4},{3,5},{4,2},{5,3},{6,0},{7,1},{8,14},{9,15},{10,... | collective-permute-start | bytes 196616 | tf_op jit(solution)/shard_map/ppermute | solution.py:279
  49.4 7.6 %collective-permute-start.21 = (bf16[2,64,256]{2,1,0:T(8,128)(2,1)S(1)}, bf16[2,64,256]{2,1,0:T(8,128)(2,1)S(1)}, u32[]{:S(2)}, u32[]{:S(2)}) collective-permute-start(bf16[2,64,256]{2,1,0:T(8,128)(2,1)S(1)} %get-tuple-element.100), channel_id=1, source_target_pairs={{0,5},{1,4},{2,7},{3,6},{4,1},{5,0},{6,3},{7,2},{8,13},{9,12},{10,... | collective-permute-start | bytes 196616 | tf_op jit(solution)/shard_map/ppermute | solution.py:279
  51.4 6.1 %collective-permute-start.20 = (bf16[2,64,256]{2,1,0:T(8,128)(2,1)S(1)}, bf16[2,64,256]{2,1,0:T(8,128)(2,1)S(1)}, u32[]{:S(2)}, u32[]{:S(2)}) collective-permute-start(bf16[2,64,256]{2,1,0:T(8,128)(2,1)S(1)} %get-tuple-element.99), channel_id=1, source_target_pairs={{0,4},{1,5},{2,6},{3,7},{4,0},{5,1},{6,2},{7,3},{8,12},{9,13},{10,... | collective-permute-start | bytes 196616 | tf_op jit(solution)/shard_map/ppermute | solution.py:279
  53.6 4.4 %collective-permute-start.19 = (bf16[2,64,256]{2,1,0:T(8,128)(2,1)S(1)}, bf16[2,64,256]{2,1,0:T(8,128)(2,1)S(1)}, u32[]{:S(2)}, u32[]{:S(2)}) collective-permute-start(bf16[2,64,256]{2,1,0:T(8,128)(2,1)S(1)} %get-tuple-element.98), channel_id=1, source_target_pairs={{0,3},{1,2},{2,1},{3,0},{4,7},{5,6},{6,5},{7,4},{8,11},{9,10},{10,... | collective-permute-start | bytes 196616 | tf_op jit(solution)/shard_map/ppermute | solution.py:279
  54.0 5.0 %collective-permute-start.18 = (bf16[2,64,256]{2,1,0:T(8,128)(2,1)S(1)}, bf16[2,64,256]{2,1,0:T(8,128)(2,1)S(1)}, u32[]{:S(2)}, u32[]{:S(2)}) collective-permute-start(bf16[2,64,256]{2,1,0:T(8,128)(2,1)S(1)} %get-tuple-element.97), channel_id=1, source_target_pairs={{0,2},{1,3},{2,0},{3,1},{4,6},{5,7},{6,4},{7,5},{8,10},{9,11},{10,... | collective-permute-start | bytes 196616 | tf_op jit(solution)/shard_map/ppermute | solution.py:279
  55.5 4.1 %collective-permute-start.17 = (bf16[2,64,256]{2,1,0:T(8,128)(2,1)S(1)}, bf16[2,64,256]{2,1,0:T(8,128)(2,1)S(1)}, u32[]{:S(2)}, u32[]{:S(2)}) collective-permute-start(bf16[2,64,256]{2,1,0:T(8,128)(2,1)S(1)} %get-tuple-element.96), channel_id=1, source_target_pairs={{0,1},{1,0},{2,3},{3,2},{4,5},{5,4},{6,7},{7,6},{8,9},{9,8},{10,11... | collective-permute-start | bytes 196616 | tf_op jit(solution)/shard_map/ppermute | solution.py:279
  60.8 7.3 %collective-permute-start.30 = (bf16[2,64,256]{2,1,0:T(8,128)(2,1)S(1)}, bf16[2,64,256]{2,1,0:T(8,128)(2,1)S(1)}, u32[]{:S(2)}, u32[]{:S(2)}) collective-permute-start(bf16[2,64,256]{2,1,0:T(8,128)(2,1)S(1)} %mate_terms.31), channel_id=1, source_target_pairs={{0,7},{1,6},{2,5},{3,4},{4,3},{5,2},{6,1},{7,0},{8,15},{9,14},{10,... | collective-permute-start | bytes 196616 | tf_op jit(solution)/shard_map/ppermute | solution.py:279
  61.3 8.3 %collective-permute-start.29 = (bf16[2,64,256]{2,1,0:T(8,128)(2,1)S(1)}, bf16[2,64,256]{2,1,0:T(8,128)(2,1)S(1)}, u32[]{:S(2)}, u32[]{:S(2)}) collective-permute-start(bf16[2,64,256]{2,1,0:T(8,128)(2,1)S(1)} %mate_terms.30), channel_id=1, source_target_pairs={{0,6},{1,7},{2,4},{3,5},{4,2},{5,3},{6,0},{7,1},{8,14},{9,15},{10,... | collective-permute-start | bytes 196616 | tf_op jit(solution)/shard_map/ppermute | solution.py:279
  64.4 6.6 %collective-permute-start.28 = (bf16[2,64,256]{2,1,0:T(8,128)(2,1)S(1)}, bf16[2,64,256]{2,1,0:T(8,128)(2,1)S(1)}, u32[]{:S(2)}, u32[]{:S(2)}) collective-permute-start(bf16[2,64,256]{2,1,0:T(8,128)(2,1)S(1)} %mate_terms.29), channel_id=1, source_target_pairs={{0,5},{1,4},{2,7},{3,6},{4,1},{5,0},{6,3},{7,2},{8,13},{9,12},{10,... | collective-permute-start | bytes 196616 | tf_op jit(solution)/shard_map/ppermute | solution.py:279
  64.8 6.2 %collective-permute-start.27 = (bf16[2,64,256]{2,1,0:T(8,128)(2,1)S(1)}, bf16[2,64,256]{2,1,0:T(8,128)(2,1)S(1)}, u32[]{:S(2)}, u32[]{:S(2)}) collective-permute-start(bf16[2,64,256]{2,1,0:T(8,128)(2,1)S(1)} %mate_terms.28), channel_id=1, source_target_pairs={{0,4},{1,5},{2,6},{3,7},{4,0},{5,1},{6,2},{7,3},{8,12},{9,13},{10,... | collective-permute-start | bytes 196616 | tf_op jit(solution)/shard_map/ppermute | solution.py:279
  66.9 4.1 %collective-permute-start.26 = (bf16[2,64,256]{2,1,0:T(8,128)(2,1)S(1)}, bf16[2,64,256]{2,1,0:T(8,128)(2,1)S(1)}, u32[]{:S(2)}, u32[]{:S(2)}) collective-permute-start(bf16[2,64,256]{2,1,0:T(8,128)(2,1)S(1)} %mate_terms.27), channel_id=1, source_target_pairs={{0,3},{1,2},{2,1},{3,0},{4,7},{5,6},{6,5},{7,4},{8,11},{9,10},{10,... | collective-permute-start | bytes 196616 | tf_op jit(solution)/shard_map/ppermute | solution.py:279
  68.1 4.7 %collective-permute-start.25 = (bf16[2,64,256]{2,1,0:T(8,128)(2,1)S(1)}, bf16[2,64,256]{2,1,0:T(8,128)(2,1)S(1)}, u32[]{:S(2)}, u32[]{:S(2)}) collective-permute-start(bf16[2,64,256]{2,1,0:T(8,128)(2,1)S(1)} %mate_terms.26), channel_id=1, source_target_pairs={{0,2},{1,3},{2,0},{3,1},{4,6},{5,7},{6,4},{7,5},{8,10},{9,11},{10,... | collective-permute-start | bytes 196616 | tf_op jit(solution)/shard_map/ppermute | solution.py:279
  69.6 3.2 %collective-permute-start.24 = (bf16[2,64,256]{2,1,0:T(8,128)(2,1)S(1)}, bf16[2,64,256]{2,1,0:T(8,128)(2,1)S(1)}, u32[]{:S(2)}, u32[]{:S(2)}) collective-permute-start(bf16[2,64,256]{2,1,0:T(8,128)(2,1)S(1)} %mate_terms.25), channel_id=1, source_target_pairs={{0,1},{1,0},{2,3},{3,2},{4,5},{5,4},{6,7},{7,6},{8,9},{9,8},{10,11... | collective-permute-start | bytes 196616 | tf_op jit(solution)/shard_map/ppermute | solution.py:279
  73.3 6.9 %collective-permute-start.31 = (bf16[64,640]{1,0:T(8,128)(2,1)S(1)}, bf16[64,640]{1,0:T(8,128)(2,1)S(1)}, u32[]{:S(2)}, u32[]{:S(2)}) collective-permute-start(bf16[64,640]{1,0:T(8,128)(2,1)S(1)} %get-tuple-element.125), channel_id=1, source_target_pairs={{0,8},{1,9},{2,10},{3,11},{4,12},{5,13},{6,14},{7,15},{8,0},{9,1},... | collective-permute-start | bytes 245768 | tf_op jit(solution)/shard_map/ppermute | solution.py:279
  (2 other events, 22.1 us)

commit v8 on v7

--- a/solution.py
+++ b/solution.py
@@ -58,14 +58,17 @@
         copy.wait()
 
 
-def steps_kernel(scale, own_blocks, pos_ref, cov, steps):
-    def step_of(block):
-        seen = (cov[...] == pos_ref[0] * own_blocks + block).astype(jnp.float32)
-        return scale / jnp.sum(jnp.sum(seen, axis=1, keepdims=True), axis=0, keepdims=True)
-
-    low = low_half(steps.shape[0])
-    for j in range(own_blocks // 2):
-        steps[:, 128 * j:128 * (j + 1)] = jnp.where(low, step_of(2 * j), step_of(2 * j + 1))
+def steps_kernel(scale, own_blocks, pos_ref, cov, *steps):
+    low = low_half(steps[0].shape[0])
+    for turn, out in enumerate(steps):
+        owner = lax.bitwise_xor(pos_ref[0], turn * PLANE)
+
+        def step_of(block):
+            seen = (cov[...] == owner * own_blocks + block).astype(jnp.float32)
+            return scale / jnp.sum(jnp.sum(seen, axis=1, keepdims=True), axis=0, keepdims=True)
+
+        for j in range(own_blocks // 2):
+            out[:, 128 * j:128 * (j + 1)] = jnp.where(low, step_of(2 * j), step_of(2 * j + 1))
 
 
 def pick_kernel(planes, per_owner, own_blocks, table, *refs):
@@ -84,8 +87,8 @@
                 packets[mate][turn, :, 128 * q:128 * (q + 1)] = pair.astype(jnp.bfloat16)
 
 
-def plane_sum_kernel(planes, per_owner, own_blocks, table, *refs):
-    terms, sums, total = refs[:PLANE], refs[-1 - planes:-1], refs[-1]
+def plane_sum_kernel(planes, n_outs, per_owner, own_blocks, table, *refs):
+    terms, sums, total = refs[:PLANE], refs[-1 - n_outs:-1], refs[-1]
     low = low_half(terms[0].shape[1])
     total[...] = jnp.zeros_like(total)
     for turn in range(planes):
@@ -100,7 +103,10 @@
         for j in range(own_blocks // 2):
             first, second = total[turn, 2 * j], total[turn, 2 * j + 1]
             both = jnp.where(low, first, second) + pltpu.roll(jnp.where(low, second, first), 64, 1)
-            sums[turn][:, 128 * j:128 * (j + 1)] = both.astype(sums[turn].dtype)
+            columns = slice(128 * j, 128 * (j + 1))
+            sums[turn][:, columns] = both.astype(sums[turn].dtype)
+            if n_outs > planes:
+                sums[planes][planes - 1 - turn, :, columns] = both.astype(jnp.bfloat16)
 
 
 def columns_of(pos, turn, mate, width):
@@ -202,11 +208,14 @@
         name="load_batch",
     )(pos, coverage, genotypes, sample_factors.T)
 
-    snp_step = pl.pallas_call(
+    by_snps = jax.ShapeDtypeStruct((rank, own_snps), jnp.float32)
+    pairwise = planes == 2
+    n_steps = 2 if pairwise else 1
+    snp_steps = pl.pallas_call(
         functools.partial(steps_kernel, 0.5 * math.sqrt(rank) / samples_here, own_blocks),
-        out_shape=jax.ShapeDtypeStruct((rank, own_snps), jnp.float32),
+        out_shape=(by_snps,) * n_steps,
         in_specs=[smem, vmem],
-        out_specs=vmem,
+        out_specs=(vmem,) * n_steps,
         compiler_params=params,
         name="snp_steps",
     )(pos, coverage)
@@ -224,15 +233,18 @@
             name="pick_blocks",
         )(table, *held)
 
-    def plane_sum(terms, after):
+    def plane_sum(terms, after, both):
+        outs = tuple(
+            jax.ShapeDtypeStruct((rank, own_snps), jnp.bfloat16 if turn % 2 and not both else jnp.float32)
+            for turn in range(planes)
+        )
+        if both:
+            outs += (jax.ShapeDtypeStruct((planes, rank, own_snps), jnp.bfloat16),)
         sums = pl.pallas_call(
-            functools.partial(plane_sum_kernel, planes, per_owner, own_blocks),
-            out_shape=tuple(
-                jax.ShapeDtypeStruct((rank, own_snps), jnp.bfloat16 if turn % 2 else jnp.float32)
-                for turn in range(planes)
-            ),
+            functools.partial(plane_sum_kernel, planes, len(outs), per_owner, own_blocks),
+            out_shape=outs,
             in_specs=[smem] + [vmem] * PLANE + [anywhere] * len(after),
-            out_specs=(vmem,) * planes,
+            out_specs=(vmem,) * len(outs),
             scratch_shapes=[dense_blocks],
             compiler_params=params,
             cost_estimate=small,
@@ -281,22 +293,28 @@
     def to_mate(x, mate):
         return swap(x, mate) if mate else x
 
+    def updated(old, step, total):
+        return (1.0 - weight_decay) * old.astype(jnp.float32) + step * total
+
     snps = snp_factors.T
+    held = None
     for iteration in range(ROUNDS):
-        held = {0: snps.astype(jnp.bfloat16)}
-        for turn in sorted(range(1, planes), key=lambda turn: (turn & (turn - 1), -turn)):
-            bit = turn & -turn
-            source = held[turn ^ bit]
-            if iteration == 0 and turn != bit:
-                source, _ = lax.optimization_barrier((source, samples))
-            held[turn] = swap(source, bit * PLANE)
+        last = iteration == ROUNDS - 1
+        if held is None:
+            held = {0: snps.astype(jnp.bfloat16)}
+            for turn in sorted(range(1, planes), key=lambda turn: (turn & (turn - 1), -turn)):
+                bit = turn & -turn
+                source = held[turn ^ bit]
+                if iteration == 0 and turn != bit:
+                    source, _ = lax.optimization_barrier((source, samples))
+                held[turn] = swap(source, bit * PLANE)
         packets = pick([held[turn] for turn in range(planes)])
         panels = [to_mate(packets[mate], mate) for mate in range(PLANE)]
         partial = ()
         for mate in (0, 7, 6, 5, 4, 3, 2, 1):
             partial = product(mate, panels[mate], partial)
         rounded = (jax.ShapeDtypeStruct((rank, samples_here), jnp.bfloat16), square)
-        if iteration < ROUNDS - 1:
+        if not last:
             samples, *current = sample_update(samples, *partial, (by_samples,) + rounded)
             after = []
         else:
@@ -305,14 +323,22 @@
                 samples, *partial, (by_samples, jax.ShapeDtypeStruct((8, 128), jnp.float32))
             )
             after = [token]
+        both = pairwise and not last
         sums = plane_sum(
-            [to_mate(terms_for(mate, *current, panels[mate]), mate) for mate in range(PLANE)], after
+            [to_mate(terms_for(mate, *current, panels[mate]), mate) for mate in range(PLANE)], after, both
         )
+        if both:
+            arrived = swap(sums[2], PLANE)
+            snps = updated(snps, snp_steps[0], sums[0] + arrived[0].astype(jnp.float32))
+            other = updated(held[1], snp_steps[1], sums[1] + arrived[1].astype(jnp.float32))
+            held = {0: snps.astype(jnp.bfloat16), 1: other.astype(jnp.bfloat16)}
+            continue
         for turn in range(planes - 1, 0, -1):
             bit = turn & -turn
             arrived = swap(sums[turn].astype(jnp.bfloat16), bit * PLANE)
             sums[turn ^ bit] = sums[turn ^ bit] + arrived.astype(jnp.float32)
-        snps = (1.0 - weight_decay) * snps + snp_step * sums[0]
+        snps = updated(snps, snp_steps[0], sums[0])
+        held = None
     return (samples.T, snps.T)
 
 

time: 81.1 us -> 78.4 us (0.967)
  waiting for transfers between devices: 21.1 us -> 18.9 us
    ppermute x32 -> x31, waiting for transfers between devices: 21.1 us -> 18.9 us  [swap(): return lax.ppermute(x, 'rows', [(r, r ^ turn) for r in range(devices)])]
    ppermute x32 -> x31, starting transfers between devices: 36.9 us -> 36.3 us  [swap(): return lax.ppermute(x, 'rows', [(r, r ^ turn) for r in range(devices)])]
  transfers between devices with their start and end apart: 32 -> 31, of which waited for: 10 -> 11; matrix products, arithmetic and copies ran while one was open for 0% -> 0% of each run, Pallas kernels for 20% -> 21%
where the time goes in v8:
time: 78.4 us; the launch traced here: 78.2 us
  starting transfers between devices  36.3 us (46%)
  Pallas kernels  20.2 us (26%)
  waiting for transfers between devices  18.9 us (24%)
  other arithmetic  1.74 us (2%)
  between operations  0.96 us (1%)
    ppermute x31, starting transfers between devices, swap(): return lax.ppermute(x, 'rows', [(r, r ^ turn) for r in range(devices)])  36.3 us
    ppermute x31, waiting for transfers between devices, swap(): return lax.ppermute(x, 'rows', [(r, r ^ turn) for r in range(devices)])  18.9 us
    pallas_call x16, Pallas kernels, product(): pl.pallas_call(functools.partial(product_kernel, mate, not before, 256),...  7.43 us
    pallas_call x16, Pallas kernels, terms_for(): pl.pallas_call(functools.partial(term_kernel, mate), out_shape=packet, in...  5.89 us
    pallas_call x1, Pallas kernels, on_device(): pl.pallas_call(functools.partial(load_kernel, planes, per_owner, own_bloc...  3.51 us
    pallas_call x3, Pallas kernels, sample_update(): pl.pallas_call(functools.partial(sample_kernel, sample_step), out_shape=o...  1.76 us
  transfers between devices with their start and end apart: 31, of which 11 were waited for; matrix products, arithmetic and copies ran while one was open for 0% of the time, Pallas kernels for 21%

profile of v8, /device:TPU:0, one launch (start us, length us, event | category | flops | bytes accessed | tf_op | source)
XLA Modules:
  0.0 78.2 jit_solution(7299052836943169879)
XLA Ops:
  0.6 0.9 %convert_bitcast_fusion.refs_0_ = bf16[64,640]{1,0:T(8,128)(2,1)S(1)} fusion(f32[640,64]{0,1:T(8,128)} %param.6), kind=kLoop, calls=%fused_computation.10 | loop fusion | flops 40960 | bytes 245760 | tf_op jit(solution)/shard_map/convert_element_type | solution.py:304
  1.6 4.1 %collective-permute-start = (bf16[64,640]{1,0:T(8,128)(2,1)S(1)}, bf16[64,640]{1,0:T(8,128)(2,1)S(1)}, u32[]{:S(2)}, u32[]{:S(2)}) collective-permute-start(bf16[64,640]{1,0:T(8,128)(2,1)S(1)} %convert_bitcast_fusion.refs_0_), channel_id=1, source_target_pairs={{0,8},{1,9},{2,10},{3,11},{4,12},{5,13},{6,14},{7,15},{8,0},{9,1},... | collective-permute-start | bytes 245768 | tf_op jit(solution)/shard_map/ppermute | solution.py:291
  5.7 3.5 %load_batch.1 = (bf16[1024,4096]{1,0:T(8,128)(2,1)S(1)}, f32[64,1024]{1,0:T(8,128)S(1)}, s32[16,4]{1,0:T(8,128)S(4)}) custom-call(s32[1]{0:T(128)} %bitcast.pos_ref, s32[16,64]{1,0:T(8,128)} %cov.3, bf16[1024,4096]{1,0:T(8,128)(2,1)} %geno.1, f32[64,1024]{1,0:T(8,128)} %bitcast.27), custom_call_target="tpu_custom_call" | custom-call | bytes 8388608 | tf_op jit(solution)/shard_map/load_batch/pallas_call | solution.py:194
  10.1 1.2 %collective-permute-start.7 = (bf16[2,64,256]{2,1,0:T(8,128)(2,1)S(1)}, bf16[2,64,256]{2,1,0:T(8,128)(2,1)S(1)}, u32[]{:S(2)}, u32[]{:S(2)}) collective-permute-start(bf16[2,64,256]{2,1,0:T(8,128)(2,1)S(1)} %get-tuple-element.76), channel_id=1, source_target_pairs={{0,7},{1,6},{2,5},{3,4},{4,3},{5,2},{6,1},{7,0},{8,15},{9,14},{10,... | collective-permute-start | bytes 196616 | tf_op jit(solution)/shard_map/ppermute | solution.py:291
  11.3 0.8 %collective-permute-start.6 = (bf16[2,64,256]{2,1,0:T(8,128)(2,1)S(1)}, bf16[2,64,256]{2,1,0:T(8,128)(2,1)S(1)}, u32[]{:S(2)}, u32[]{:S(2)}) collective-permute-start(bf16[2,64,256]{2,1,0:T(8,128)(2,1)S(1)} %get-tuple-element.75), channel_id=1, source_target_pairs={{0,6},{1,7},{2,4},{3,5},{4,2},{5,3},{6,0},{7,1},{8,14},{9,15},{10,... | collective-permute-start | bytes 196616 | tf_op jit(solution)/shard_map/ppermute | solution.py:291
  12.1 1.3 %collective-permute-start.5 = (bf16[2,64,256]{2,1,0:T(8,128)(2,1)S(1)}, bf16[2,64,256]{2,1,0:T(8,128)(2,1)S(1)}, u32[]{:S(2)}, u32[]{:S(2)}) collective-permute-start(bf16[2,64,256]{2,1,0:T(8,128)(2,1)S(1)} %get-tuple-element.74), channel_id=1, source_target_pairs={{0,5},{1,4},{2,7},{3,6},{4,1},{5,0},{6,3},{7,2},{8,13},{9,12},{10,... | collective-permute-start | bytes 196616 | tf_op jit(solution)/shard_map/ppermute | solution.py:291
  13.4 1.1 %collective-permute-start.4 = (bf16[2,64,256]{2,1,0:T(8,128)(2,1)S(1)}, bf16[2,64,256]{2,1,0:T(8,128)(2,1)S(1)}, u32[]{:S(2)}, u32[]{:S(2)}) collective-permute-start(bf16[2,64,256]{2,1,0:T(8,128)(2,1)S(1)} %get-tuple-element.73), channel_id=1, source_target_pairs={{0,4},{1,5},{2,6},{3,7},{4,0},{5,1},{6,2},{7,3},{8,12},{9,13},{10,... | collective-permute-start | bytes 196616 | tf_op jit(solution)/shard_map/ppermute | solution.py:291
  15.2 1.6 %collective-permute-start.2 = (bf16[2,64,256]{2,1,0:T(8,128)(2,1)S(1)}, bf16[2,64,256]{2,1,0:T(8,128)(2,1)S(1)}, u32[]{:S(2)}, u32[]{:S(2)}) collective-permute-start(bf16[2,64,256]{2,1,0:T(8,128)(2,1)S(1)} %get-tuple-element.71), channel_id=1, source_target_pairs={{0,2},{1,3},{2,0},{3,1},{4,6},{5,7},{6,4},{7,5},{8,10},{9,11},{10,... | collective-permute-start | bytes 196616 | tf_op jit(solution)/shard_map/ppermute | solution.py:291
  21.8 1.5 %collective-permute-start.14 = (bf16[2,64,256]{2,1,0:T(8,128)(2,1)S(1)}, bf16[2,64,256]{2,1,0:T(8,128)(2,1)S(1)}, u32[]{:S(2)}, u32[]{:S(2)}) collective-permute-start(bf16[2,64,256]{2,1,0:T(8,128)(2,1)S(1)} %mate_terms.23), channel_id=1, source_target_pairs={{0,7},{1,6},{2,5},{3,4},{4,3},{5,2},{6,1},{7,0},{8,15},{9,14},{10,... | collective-permute-start | bytes 196616 | tf_op jit(solution)/shard_map/ppermute | solution.py:291
  23.7 1.4 %collective-permute-start.13 = (bf16[2,64,256]{2,1,0:T(8,128)(2,1)S(1)}, bf16[2,64,256]{2,1,0:T(8,128)(2,1)S(1)}, u32[]{:S(2)}, u32[]{:S(2)}) collective-permute-start(bf16[2,64,256]{2,1,0:T(8,128)(2,1)S(1)} %mate_terms.22), channel_id=1, source_target_pairs={{0,6},{1,7},{2,4},{3,5},{4,2},{5,3},{6,0},{7,1},{8,14},{9,15},{10,... | collective-permute-start | bytes 196616 | tf_op jit(solution)/shard_map/ppermute | solution.py:291
  25.4 1.2 %collective-permute-start.12 = (bf16[2,64,256]{2,1,0:T(8,128)(2,1)S(1)}, bf16[2,64,256]{2,1,0:T(8,128)(2,1)S(1)}, u32[]{:S(2)}, u32[]{:S(2)}) collective-permute-start(bf16[2,64,256]{2,1,0:T(8,128)(2,1)S(1)} %mate_terms.21), channel_id=1, source_target_pairs={{0,5},{1,4},{2,7},{3,6},{4,1},{5,0},{6,3},{7,2},{8,13},{9,12},{10,... | collective-permute-start | bytes 196616 | tf_op jit(solution)/shard_map/ppermute | solution.py:291
  27.9 0.8 %collective-permute-start.10 = (bf16[2,64,256]{2,1,0:T(8,128)(2,1)S(1)}, bf16[2,64,256]{2,1,0:T(8,128)(2,1)S(1)}, u32[]{:S(2)}, u32[]{:S(2)}) collective-permute-start(bf16[2,64,256]{2,1,0:T(8,128)(2,1)S(1)} %mate_terms.19), channel_id=1, source_target_pairs={{0,3},{1,2},{2,1},{3,0},{4,7},{5,6},{6,5},{7,4},{8,11},{9,10},{10,... | collective-permute-start | bytes 196616 | tf_op jit(solution)/shard_map/ppermute | solution.py:291
  29.6 1.1 %collective-permute-start.9 = (bf16[2,64,256]{2,1,0:T(8,128)(2,1)S(1)}, bf16[2,64,256]{2,1,0:T(8,128)(2,1)S(1)}, u32[]{:S(2)}, u32[]{:S(2)}) collective-permute-start(bf16[2,64,256]{2,1,0:T(8,128)(2,1)S(1)} %mate_terms.18), channel_id=1, source_target_pairs={{0,2},{1,3},{2,0},{3,1},{4,6},{5,7},{6,4},{7,5},{8,10},{9,11},{10,... | collective-permute-start | bytes 196616 | tf_op jit(solution)/shard_map/ppermute | solution.py:291
  32.1 2.2 %collective-permute-done.9.refs_2_ = bf16[2,64,256]{2,1,0:T(8,128)(2,1)S(1)} collective-permute-done((bf16[2,64,256]{2,1,0:T(8,128)(2,1)S(1)}, bf16[2,64,256]{2,1,0:T(8,128)(2,1)S(1)}, u32[]{:S(2)}, u32[]{:S(2)}) %collective-permute-start.9) | collective-permute-done | bytes 65568 | tf_op jit(solution)/shard_map/ppermute | solution.py:291
  34.8 3.3 %collective-permute-start.15 = (bf16[2,64,640]{2,1,0:T(8,128)(2,1)S(1)}, bf16[2,64,640]{2,1,0:T(8,128)(2,1)S(1)}, u32[]{:S(2)}, u32[]{:S(2)}) collective-permute-start(bf16[2,64,640]{2,1,0:T(8,128)(2,1)S(1)} %get-tuple-element.99), channel_id=1, source_target_pairs={{0,8},{1,9},{2,10},{3,11},{4,12},{5,13},{6,14},{7,15},{8,0},{9,1},... | collective-permute-start | bytes 491528 | tf_op jit(solution)/shard_map/ppermute | solution.py:291
  38.2 7.6 %collective-permute-done.15 = bf16[2,64,640]{2,1,0:T(8,128)(2,1)S(1)} collective-permute-done((bf16[2,64,640]{2,1,0:T(8,128)(2,1)S(1)}, bf16[2,64,640]{2,1,0:T(8,128)(2,1)S(1)}, u32[]{:S(2)}, u32[]{:S(2)}) %collective-permute-start.15) | collective-permute-done | bytes 163872 | tf_op jit(solution)/shard_map/ppermute | solution.py:291
  46.5 1.6 %collective-permute-start.21 = (bf16[2,64,256]{2,1,0:T(8,128)(2,1)S(1)}, bf16[2,64,256]{2,1,0:T(8,128)(2,1)S(1)}, u32[]{:S(2)}, u32[]{:S(2)}) collective-permute-start(bf16[2,64,256]{2,1,0:T(8,128)(2,1)S(1)} %get-tuple-element.107), channel_id=1, source_target_pairs={{0,6},{1,7},{2,4},{3,5},{4,2},{5,3},{6,0},{7,1},{8,14},{9,15},{10,... | collective-permute-start | bytes 196616 | tf_op jit(solution)/shard_map/ppermute | solution.py:291
  48.1 1.0 %collective-permute-start.20 = (bf16[2,64,256]{2,1,0:T(8,128)(2,1)S(1)}, bf16[2,64,256]{2,1,0:T(8,128)(2,1)S(1)}, u32[]{:S(2)}, u32[]{:S(2)}) collective-permute-start(bf16[2,64,256]{2,1,0:T(8,128)(2,1)S(1)} %get-tuple-element.106), channel_id=1, source_target_pairs={{0,5},{1,4},{2,7},{3,6},{4,1},{5,0},{6,3},{7,2},{8,13},{9,12},{10,... | collective-permute-start | bytes 196616 | tf_op jit(solution)/shard_map/ppermute | solution.py:291
  49.0 1.5 %collective-permute-start.19 = (bf16[2,64,256]{2,1,0:T(8,128)(2,1)S(1)}, bf16[2,64,256]{2,1,0:T(8,128)(2,1)S(1)}, u32[]{:S(2)}, u32[]{:S(2)}) collective-permute-start(bf16[2,64,256]{2,1,0:T(8,128)(2,1)S(1)} %get-tuple-element.105), channel_id=1, source_target_pairs={{0,4},{1,5},{2,6},{3,7},{4,0},{5,1},{6,2},{7,3},{8,12},{9,13},{10,... | collective-permute-start | bytes 196616 | tf_op jit(solution)/shard_map/ppermute | solution.py:291
  51.1 1.0 %collective-permute-start.17 = (bf16[2,64,256]{2,1,0:T(8,128)(2,1)S(1)}, bf16[2,64,256]{2,1,0:T(8,128)(2,1)S(1)}, u32[]{:S(2)}, u32[]{:S(2)}) collective-permute-start(bf16[2,64,256]{2,1,0:T(8,128)(2,1)S(1)} %get-tuple-element.103), channel_id=1, source_target_pairs={{0,2},{1,3},{2,0},{3,1},{4,6},{5,7},{6,4},{7,5},{8,10},{9,11},{10,... | collective-permute-start | bytes 196616 | tf_op jit(solution)/shard_map/ppermute | solution.py:291
  52.6 0.9 %collective-permute-start.16 = (bf16[2,64,256]{2,1,0:T(8,128)(2,1)S(1)}, bf16[2,64,256]{2,1,0:T(8,128)(2,1)S(1)}, u32[]{:S(2)}, u32[]{:S(2)}) collective-permute-start(bf16[2,64,256]{2,1,0:T(8,128)(2,1)S(1)} %get-tuple-element.102), channel_id=1, source_target_pairs={{0,1},{1,0},{2,3},{3,2},{4,5},{5,4},{6,7},{7,6},{8,9},{9,8},{10,11... | collective-permute-start | bytes 196616 | tf_op jit(solution)/shard_map/ppermute | solution.py:291
  57.8 0.9 %collective-permute-start.29 = (bf16[2,64,256]{2,1,0:T(8,128)(2,1)S(1)}, bf16[2,64,256]{2,1,0:T(8,128)(2,1)S(1)}, u32[]{:S(2)}, u32[]{:S(2)}) collective-permute-start(bf16[2,64,256]{2,1,0:T(8,128)(2,1)S(1)} %mate_terms.31), channel_id=1, source_target_pairs={{0,7},{1,6},{2,5},{3,4},{4,3},{5,2},{6,1},{7,0},{8,15},{9,14},{10,... | collective-permute-start | bytes 196616 | tf_op jit(solution)/shard_map/ppermute | solution.py:291
  59.0 1.8 %collective-permute-start.28 = (bf16[2,64,256]{2,1,0:T(8,128)(2,1)S(1)}, bf16[2,64,256]{2,1,0:T(8,128)(2,1)S(1)}, u32[]{:S(2)}, u32[]{:S(2)}) collective-permute-start(bf16[2,64,256]{2,1,0:T(8,128)(2,1)S(1)} %mate_terms.30), channel_id=1, source_target_pairs={{0,6},{1,7},{2,4},{3,5},{4,2},{5,3},{6,0},{7,1},{8,14},{9,15},{10,... | collective-permute-start | bytes 196616 | tf_op jit(solution)/shard_map/ppermute | solution.py:291
  61.2 0.7 collective-permute-start.27
  62.3 1.2 %collective-permute-start.26 = (bf16[2,64,256]{2,1,0:T(8,128)(2,1)S(1)}, bf16[2,64,256]{2,1,0:T(8,128)(2,1)S(1)}, u32[]{:S(2)}, u32[]{:S(2)}) collective-permute-start(bf16[2,64,256]{2,1,0:T(8,128)(2,1)S(1)} %mate_terms.28), channel_id=1, source_target_pairs={{0,4},{1,5},{2,6},{3,7},{4,0},{5,1},{6,2},{7,3},{8,12},{9,13},{10,... | collective-permute-start | bytes 196616 | tf_op jit(solution)/shard_map/ppermute | solution.py:291
  63.9 0.7 collective-permute-start.25
  65.3 1.1 %collective-permute-start.24 = (bf16[2,64,256]{2,1,0:T(8,128)(2,1)S(1)}, bf16[2,64,256]{2,1,0:T(8,128)(2,1)S(1)}, u32[]{:S(2)}, u32[]{:S(2)}) collective-permute-start(bf16[2,64,256]{2,1,0:T(8,128)(2,1)S(1)} %mate_terms.26), channel_id=1, source_target_pairs={{0,2},{1,3},{2,0},{3,1},{4,6},{5,7},{6,4},{7,5},{8,10},{9,11},{10,... | collective-permute-start | bytes 196616 | tf_op jit(solution)/shard_map/ppermute | solution.py:291
  66.6 0.9 %sample_update.4 = (f32[64,1024]{1,0:T(8,128)}, f32[8,128]{1,0:T(8,128)S(1)}) custom-call(f32[64,1024]{1,0:T(8,128)S(1)} %get-tuple-element.94.samples, f32[64,1024]{1,0:T(8,128)S(1)} %get-tuple-element.124.gradient, f32[64,64]{1,0:T(8,128)S(1)} %get-tuple-element.125.gram), custom_call_target="tpu_custom_call" | custom-call | bytes 2097152 | tf_op jit(solution)/shard_map/sample_update/pallas_call | solution.py:268
  68.1 1.7 %collective-permute-done.24.refs_2_ = bf16[2,64,256]{2,1,0:T(8,128)(2,1)S(1)} collective-permute-done((bf16[2,64,256]{2,1,0:T(8,128)(2,1)S(1)}, bf16[2,64,256]{2,1,0:T(8,128)(2,1)S(1)}, u32[]{:S(2)}, u32[]{:S(2)}) %collective-permute-start.24) | collective-permute-done | bytes 65568 | tf_op jit(solution)/shard_map/ppermute | solution.py:291
  70.4 2.8 %collective-permute-start.30 = (bf16[64,640]{1,0:T(8,128)(2,1)S(1)}, bf16[64,640]{1,0:T(8,128)(2,1)S(1)}, u32[]{:S(2)}, u32[]{:S(2)}) collective-permute-start(bf16[64,640]{1,0:T(8,128)(2,1)S(1)} %get-tuple-element.131), channel_id=1, source_target_pairs={{0,8},{1,9},{2,10},{3,11},{4,12},{5,13},{6,14},{7,15},{8,0},{9,1},... | collective-permute-start | bytes 245768 | tf_op jit(solution)/shard_map/ppermute | solution.py:291
  73.2 4.2 %collective-permute-done.30 = bf16[64,640]{1,0:T(8,128)(2,1)S(1)} collective-permute-done((bf16[64,640]{1,0:T(8,128)(2,1)S(1)}, bf16[64,640]{1,0:T(8,128)(2,1)S(1)}, u32[]{:S(2)}, u32[]{:S(2)}) %collective-permute-start.30) | collective-permute-done | bytes 81952 | tf_op jit(solution)/shard_map/ppermute | solution.py:291
  77.4 0.7 add_bitcast_fusion
  (78 shorter events, 20.6 us)
Async XLA Ops:
  1.6 8.3 %collective-permute-start = (bf16[64,640]{1,0:T(8,128)(2,1)S(1)}, bf16[64,640]{1,0:T(8,128)(2,1)S(1)}, u32[]{:S(2)}, u32[]{:S(2)}) collective-permute-start(bf16[64,640]{1,0:T(8,128)(2,1)S(1)} %convert_bitcast_fusion.refs_0_), channel_id=1, source_target_pairs={{0,8},{1,9},{2,10},{3,11},{4,12},{5,13},{6,14},{7,15},{8,0},{9,1},... | collective-permute-start | bytes 245768 | tf_op jit(solution)/shard_map/ppermute | solution.py:291
  10.1 5.1 %collective-permute-start.7 = (bf16[2,64,256]{2,1,0:T(8,128)(2,1)S(1)}, bf16[2,64,256]{2,1,0:T(8,128)(2,1)S(1)}, u32[]{:S(2)}, u32[]{:S(2)}) collective-permute-start(bf16[2,64,256]{2,1,0:T(8,128)(2,1)S(1)} %get-tuple-element.76), channel_id=1, source_target_pairs={{0,7},{1,6},{2,5},{3,4},{4,3},{5,2},{6,1},{7,0},{8,15},{9,14},{10,... | collective-permute-start | bytes 196616 | tf_op jit(solution)/shard_map/ppermute | solution.py:291
  11.3 6.0 %collective-permute-start.6 = (bf16[2,64,256]{2,1,0:T(8,128)(2,1)S(1)}, bf16[2,64,256]{2,1,0:T(8,128)(2,1)S(1)}, u32[]{:S(2)}, u32[]{:S(2)}) collective-permute-start(bf16[2,64,256]{2,1,0:T(8,128)(2,1)S(1)} %get-tuple-element.75), channel_id=1, source_target_pairs={{0,6},{1,7},{2,4},{3,5},{4,2},{5,3},{6,0},{7,1},{8,14},{9,15},{10,... | collective-permute-start | bytes 196616 | tf_op jit(solution)/shard_map/ppermute | solution.py:291
  12.1 5.9 %collective-permute-start.5 = (bf16[2,64,256]{2,1,0:T(8,128)(2,1)S(1)}, bf16[2,64,256]{2,1,0:T(8,128)(2,1)S(1)}, u32[]{:S(2)}, u32[]{:S(2)}) collective-permute-start(bf16[2,64,256]{2,1,0:T(8,128)(2,1)S(1)} %get-tuple-element.74), channel_id=1, source_target_pairs={{0,5},{1,4},{2,7},{3,6},{4,1},{5,0},{6,3},{7,2},{8,13},{9,12},{10,... | collective-permute-start | bytes 196616 | tf_op jit(solution)/shard_map/ppermute | solution.py:291
  13.4 5.7 %collective-permute-start.4 = (bf16[2,64,256]{2,1,0:T(8,128)(2,1)S(1)}, bf16[2,64,256]{2,1,0:T(8,128)(2,1)S(1)}, u32[]{:S(2)}, u32[]{:S(2)}) collective-permute-start(bf16[2,64,256]{2,1,0:T(8,128)(2,1)S(1)} %get-tuple-element.73), channel_id=1, source_target_pairs={{0,4},{1,5},{2,6},{3,7},{4,0},{5,1},{6,2},{7,3},{8,12},{9,13},{10,... | collective-permute-start | bytes 196616 | tf_op jit(solution)/shard_map/ppermute | solution.py:291
  14.6 5.0 %collective-permute-start.3 = (bf16[2,64,256]{2,1,0:T(8,128)(2,1)S(1)}, bf16[2,64,256]{2,1,0:T(8,128)(2,1)S(1)}, u32[]{:S(2)}, u32[]{:S(2)}) collective-permute-start(bf16[2,64,256]{2,1,0:T(8,128)(2,1)S(1)} %get-tuple-element.72), channel_id=1, source_target_pairs={{0,3},{1,2},{2,1},{3,0},{4,7},{5,6},{6,5},{7,4},{8,11},{9,10},{10,... | collective-permute-start | bytes 196616 | tf_op jit(solution)/shard_map/ppermute | solution.py:291
  15.2 4.9 %collective-permute-start.2 = (bf16[2,64,256]{2,1,0:T(8,128)(2,1)S(1)}, bf16[2,64,256]{2,1,0:T(8,128)(2,1)S(1)}, u32[]{:S(2)}, u32[]{:S(2)}) collective-permute-start(bf16[2,64,256]{2,1,0:T(8,128)(2,1)S(1)} %get-tuple-element.71), channel_id=1, source_target_pairs={{0,2},{1,3},{2,0},{3,1},{4,6},{5,7},{6,4},{7,5},{8,10},{9,11},{10,... | collective-permute-start | bytes 196616 | tf_op jit(solution)/shard_map/ppermute | solution.py:291
  17.3 3.3 %collective-permute-start.1 = (bf16[2,64,256]{2,1,0:T(8,128)(2,1)S(1)}, bf16[2,64,256]{2,1,0:T(8,128)(2,1)S(1)}, u32[]{:S(2)}, u32[]{:S(2)}) collective-permute-start(bf16[2,64,256]{2,1,0:T(8,128)(2,1)S(1)} %get-tuple-element.70), channel_id=1, source_target_pairs={{0,1},{1,0},{2,3},{3,2},{4,5},{5,4},{6,7},{7,6},{8,9},{9,8},{10,11... | collective-permute-start | bytes 196616 | tf_op jit(solution)/shard_map/ppermute | solution.py:291
  21.8 7.7 %collective-permute-start.14 = (bf16[2,64,256]{2,1,0:T(8,128)(2,1)S(1)}, bf16[2,64,256]{2,1,0:T(8,128)(2,1)S(1)}, u32[]{:S(2)}, u32[]{:S(2)}) collective-permute-start(bf16[2,64,256]{2,1,0:T(8,128)(2,1)S(1)} %mate_terms.23), channel_id=1, source_target_pairs={{0,7},{1,6},{2,5},{3,4},{4,3},{5,2},{6,1},{7,0},{8,15},{9,14},{10,... | collective-permute-start | bytes 196616 | tf_op jit(solution)/shard_map/ppermute | solution.py:291
  23.7 7.0 %collective-permute-start.13 = (bf16[2,64,256]{2,1,0:T(8,128)(2,1)S(1)}, bf16[2,64,256]{2,1,0:T(8,128)(2,1)S(1)}, u32[]{:S(2)}, u32[]{:S(2)}) collective-permute-start(bf16[2,64,256]{2,1,0:T(8,128)(2,1)S(1)} %mate_terms.22), channel_id=1, source_target_pairs={{0,6},{1,7},{2,4},{3,5},{4,2},{5,3},{6,0},{7,1},{8,14},{9,15},{10,... | collective-permute-start | bytes 196616 | tf_op jit(solution)/shard_map/ppermute | solution.py:291
  25.4 5.7 %collective-permute-start.12 = (bf16[2,64,256]{2,1,0:T(8,128)(2,1)S(1)}, bf16[2,64,256]{2,1,0:T(8,128)(2,1)S(1)}, u32[]{:S(2)}, u32[]{:S(2)}) collective-permute-start(bf16[2,64,256]{2,1,0:T(8,128)(2,1)S(1)} %mate_terms.21), channel_id=1, source_target_pairs={{0,5},{1,4},{2,7},{3,6},{4,1},{5,0},{6,3},{7,2},{8,13},{9,12},{10,... | collective-permute-start | bytes 196616 | tf_op jit(solution)/shard_map/ppermute | solution.py:291
  27.0 4.7 %collective-permute-start.11 = (bf16[2,64,256]{2,1,0:T(8,128)(2,1)S(1)}, bf16[2,64,256]{2,1,0:T(8,128)(2,1)S(1)}, u32[]{:S(2)}, u32[]{:S(2)}) collective-permute-start(bf16[2,64,256]{2,1,0:T(8,128)(2,1)S(1)} %mate_terms.20), channel_id=1, source_target_pairs={{0,4},{1,5},{2,6},{3,7},{4,0},{5,1},{6,2},{7,3},{8,12},{9,13},{10,... | collective-permute-start | bytes 196616 | tf_op jit(solution)/shard_map/ppermute | solution.py:291
  27.9 4.2 %collective-permute-start.10 = (bf16[2,64,256]{2,1,0:T(8,128)(2,1)S(1)}, bf16[2,64,256]{2,1,0:T(8,128)(2,1)S(1)}, u32[]{:S(2)}, u32[]{:S(2)}) collective-permute-start(bf16[2,64,256]{2,1,0:T(8,128)(2,1)S(1)} %mate_terms.19), channel_id=1, source_target_pairs={{0,3},{1,2},{2,1},{3,0},{4,7},{5,6},{6,5},{7,4},{8,11},{9,10},{10,... | collective-permute-start | bytes 196616 | tf_op jit(solution)/shard_map/ppermute | solution.py:291
  29.2 16.6 %copy-start.1 = (f32[640,64]{0,1:T(8,128)S(1)}, f32[640,64]{0,1:T(8,128)}, u32[]{:S(2)}) copy-start(f32[640,64]{0,1:T(8,128)} %param.6) | copy-start | bytes 491524
  29.6 4.7 %collective-permute-start.9 = (bf16[2,64,256]{2,1,0:T(8,128)(2,1)S(1)}, bf16[2,64,256]{2,1,0:T(8,128)(2,1)S(1)}, u32[]{:S(2)}, u32[]{:S(2)}) collective-permute-start(bf16[2,64,256]{2,1,0:T(8,128)(2,1)S(1)} %mate_terms.18), channel_id=1, source_target_pairs={{0,2},{1,3},{2,0},{3,1},{4,6},{5,7},{6,4},{7,5},{8,10},{9,11},{10,... | collective-permute-start | bytes 196616 | tf_op jit(solution)/shard_map/ppermute | solution.py:291
  30.7 3.6 %collective-permute-start.8 = (bf16[2,64,256]{2,1,0:T(8,128)(2,1)S(1)}, bf16[2,64,256]{2,1,0:T(8,128)(2,1)S(1)}, u32[]{:S(2)}, u32[]{:S(2)}) collective-permute-start(bf16[2,64,256]{2,1,0:T(8,128)(2,1)S(1)} %mate_terms.17), channel_id=1, source_target_pairs={{0,1},{1,0},{2,3},{3,2},{4,5},{5,4},{6,7},{7,6},{8,9},{9,8},{10,11... | collective-permute-start | bytes 196616 | tf_op jit(solution)/shard_map/ppermute | solution.py:291
  34.8 11.0 %collective-permute-start.15 = (bf16[2,64,640]{2,1,0:T(8,128)(2,1)S(1)}, bf16[2,64,640]{2,1,0:T(8,128)(2,1)S(1)}, u32[]{:S(2)}, u32[]{:S(2)}) collective-permute-start(bf16[2,64,640]{2,1,0:T(8,128)(2,1)S(1)} %get-tuple-element.99), channel_id=1, source_target_pairs={{0,8},{1,9},{2,10},{3,11},{4,12},{5,13},{6,14},{7,15},{8,0},{9,1},... | collective-permute-start | bytes 491528 | tf_op jit(solution)/shard_map/ppermute | solution.py:291
  46.1 5.0 %collective-permute-start.22 = (bf16[2,64,256]{2,1,0:T(8,128)(2,1)S(1)}, bf16[2,64,256]{2,1,0:T(8,128)(2,1)S(1)}, u32[]{:S(2)}, u32[]{:S(2)}) collective-permute-start(bf16[2,64,256]{2,1,0:T(8,128)(2,1)S(1)} %get-tuple-element.108), channel_id=1, source_target_pairs={{0,7},{1,6},{2,5},{3,4},{4,3},{5,2},{6,1},{7,0},{8,15},{9,14},{10,... | collective-permute-start | bytes 196616 | tf_op jit(solution)/shard_map/ppermute | solution.py:291
  46.5 6.1 %collective-permute-start.21 = (bf16[2,64,256]{2,1,0:T(8,128)(2,1)S(1)}, bf16[2,64,256]{2,1,0:T(8,128)(2,1)S(1)}, u32[]{:S(2)}, u32[]{:S(2)}) collective-permute-start(bf16[2,64,256]{2,1,0:T(8,128)(2,1)S(1)} %get-tuple-element.107), channel_id=1, source_target_pairs={{0,6},{1,7},{2,4},{3,5},{4,2},{5,3},{6,0},{7,1},{8,14},{9,15},{10,... | collective-permute-start | bytes 196616 | tf_op jit(solution)/shard_map/ppermute | solution.py:291
  48.1 5.9 %collective-permute-start.20 = (bf16[2,64,256]{2,1,0:T(8,128)(2,1)S(1)}, bf16[2,64,256]{2,1,0:T(8,128)(2,1)S(1)}, u32[]{:S(2)}, u32[]{:S(2)}) collective-permute-start(bf16[2,64,256]{2,1,0:T(8,128)(2,1)S(1)} %get-tuple-element.106), channel_id=1, source_target_pairs={{0,5},{1,4},{2,7},{3,6},{4,1},{5,0},{6,3},{7,2},{8,13},{9,12},{10,... | collective-permute-start | bytes 196616 | tf_op jit(solution)/shard_map/ppermute | solution.py:291
  49.0 5.5 %collective-permute-start.19 = (bf16[2,64,256]{2,1,0:T(8,128)(2,1)S(1)}, bf16[2,64,256]{2,1,0:T(8,128)(2,1)S(1)}, u32[]{:S(2)}, u32[]{:S(2)}) collective-permute-start(bf16[2,64,256]{2,1,0:T(8,128)(2,1)S(1)} %get-tuple-element.105), channel_id=1, source_target_pairs={{0,4},{1,5},{2,6},{3,7},{4,0},{5,1},{6,2},{7,3},{8,12},{9,13},{10,... | collective-permute-start | bytes 196616 | tf_op jit(solution)/shard_map/ppermute | solution.py:291
  50.6 4.4 %collective-permute-start.18 = (bf16[2,64,256]{2,1,0:T(8,128)(2,1)S(1)}, bf16[2,64,256]{2,1,0:T(8,128)(2,1)S(1)}, u32[]{:S(2)}, u32[]{:S(2)}) collective-permute-start(bf16[2,64,256]{2,1,0:T(8,128)(2,1)S(1)} %get-tuple-element.104), channel_id=1, source_target_pairs={{0,3},{1,2},{2,1},{3,0},{4,7},{5,6},{6,5},{7,4},{8,11},{9,10},{10,... | collective-permute-start | bytes 196616 | tf_op jit(solution)/shard_map/ppermute | solution.py:291
  51.1 4.9 %collective-permute-start.17 = (bf16[2,64,256]{2,1,0:T(8,128)(2,1)S(1)}, bf16[2,64,256]{2,1,0:T(8,128)(2,1)S(1)}, u32[]{:S(2)}, u32[]{:S(2)}) collective-permute-start(bf16[2,64,256]{2,1,0:T(8,128)(2,1)S(1)} %get-tuple-element.103), channel_id=1, source_target_pairs={{0,2},{1,3},{2,0},{3,1},{4,6},{5,7},{6,4},{7,5},{8,10},{9,11},{10,... | collective-permute-start | bytes 196616 | tf_op jit(solution)/shard_map/ppermute | solution.py:291
  52.6 3.9 %collective-permute-start.16 = (bf16[2,64,256]{2,1,0:T(8,128)(2,1)S(1)}, bf16[2,64,256]{2,1,0:T(8,128)(2,1)S(1)}, u32[]{:S(2)}, u32[]{:S(2)}) collective-permute-start(bf16[2,64,256]{2,1,0:T(8,128)(2,1)S(1)} %get-tuple-element.102), channel_id=1, source_target_pairs={{0,1},{1,0},{2,3},{3,2},{4,5},{5,4},{6,7},{7,6},{8,9},{9,8},{10,11... | collective-permute-start | bytes 196616 | tf_op jit(solution)/shard_map/ppermute | solution.py:291
  57.8 7.6 %collective-permute-start.29 = (bf16[2,64,256]{2,1,0:T(8,128)(2,1)S(1)}, bf16[2,64,256]{2,1,0:T(8,128)(2,1)S(1)}, u32[]{:S(2)}, u32[]{:S(2)}) collective-permute-start(bf16[2,64,256]{2,1,0:T(8,128)(2,1)S(1)} %mate_terms.31), channel_id=1, source_target_pairs={{0,7},{1,6},{2,5},{3,4},{4,3},{5,2},{6,1},{7,0},{8,15},{9,14},{10,... | collective-permute-start | bytes 196616 | tf_op jit(solution)/shard_map/ppermute | solution.py:291
  59.0 7.4 %collective-permute-start.28 = (bf16[2,64,256]{2,1,0:T(8,128)(2,1)S(1)}, bf16[2,64,256]{2,1,0:T(8,128)(2,1)S(1)}, u32[]{:S(2)}, u32[]{:S(2)}) collective-permute-start(bf16[2,64,256]{2,1,0:T(8,128)(2,1)S(1)} %mate_terms.30), channel_id=1, source_target_pairs={{0,6},{1,7},{2,4},{3,5},{4,2},{5,3},{6,0},{7,1},{8,14},{9,15},{10,... | collective-permute-start | bytes 196616 | tf_op jit(solution)/shard_map/ppermute | solution.py:291
  61.2 6.8 %collective-permute-start.27 = (bf16[2,64,256]{2,1,0:T(8,128)(2,1)S(1)}, bf16[2,64,256]{2,1,0:T(8,128)(2,1)S(1)}, u32[]{:S(2)}, u32[]{:S(2)}) collective-permute-start(bf16[2,64,256]{2,1,0:T(8,128)(2,1)S(1)} %mate_terms.29), channel_id=1, source_target_pairs={{0,5},{1,4},{2,7},{3,6},{4,1},{5,0},{6,3},{7,2},{8,13},{9,12},{10,... | collective-permute-start | bytes 196616 | tf_op jit(solution)/shard_map/ppermute | solution.py:291
  62.3 5.7 %collective-permute-start.26 = (bf16[2,64,256]{2,1,0:T(8,128)(2,1)S(1)}, bf16[2,64,256]{2,1,0:T(8,128)(2,1)S(1)}, u32[]{:S(2)}, u32[]{:S(2)}) collective-permute-start(bf16[2,64,256]{2,1,0:T(8,128)(2,1)S(1)} %mate_terms.28), channel_id=1, source_target_pairs={{0,4},{1,5},{2,6},{3,7},{4,0},{5,1},{6,2},{7,3},{8,12},{9,13},{10,... | collective-permute-start | bytes 196616 | tf_op jit(solution)/shard_map/ppermute | solution.py:291
  63.9 4.3 %collective-permute-start.25 = (bf16[2,64,256]{2,1,0:T(8,128)(2,1)S(1)}, bf16[2,64,256]{2,1,0:T(8,128)(2,1)S(1)}, u32[]{:S(2)}, u32[]{:S(2)}) collective-permute-start(bf16[2,64,256]{2,1,0:T(8,128)(2,1)S(1)} %mate_terms.27), channel_id=1, source_target_pairs={{0,3},{1,2},{2,1},{3,0},{4,7},{5,6},{6,5},{7,4},{8,11},{9,10},{10,... | collective-permute-start | bytes 196616 | tf_op jit(solution)/shard_map/ppermute | solution.py:291
  65.3 4.5 %collective-permute-start.24 = (bf16[2,64,256]{2,1,0:T(8,128)(2,1)S(1)}, bf16[2,64,256]{2,1,0:T(8,128)(2,1)S(1)}, u32[]{:S(2)}, u32[]{:S(2)}) collective-permute-start(bf16[2,64,256]{2,1,0:T(8,128)(2,1)S(1)} %mate_terms.26), channel_id=1, source_target_pairs={{0,2},{1,3},{2,0},{3,1},{4,6},{5,7},{6,4},{7,5},{8,10},{9,11},{10,... | collective-permute-start | bytes 196616 | tf_op jit(solution)/shard_map/ppermute | solution.py:291
  66.4 3.4 %collective-permute-start.23 = (bf16[2,64,256]{2,1,0:T(8,128)(2,1)S(1)}, bf16[2,64,256]{2,1,0:T(8,128)(2,1)S(1)}, u32[]{:S(2)}, u32[]{:S(2)}) collective-permute-start(bf16[2,64,256]{2,1,0:T(8,128)(2,1)S(1)} %mate_terms.25), channel_id=1, source_target_pairs={{0,1},{1,0},{2,3},{3,2},{4,5},{5,4},{6,7},{7,6},{8,9},{9,8},{10,11... | collective-permute-start | bytes 196616 | tf_op jit(solution)/shard_map/ppermute | solution.py:291
  70.4 7.1 %collective-permute-start.30 = (bf16[64,640]{1,0:T(8,128)(2,1)S(1)}, bf16[64,640]{1,0:T(8,128)(2,1)S(1)}, u32[]{:S(2)}, u32[]{:S(2)}) collective-permute-start(bf16[64,640]{1,0:T(8,128)(2,1)S(1)} %get-tuple-element.131), channel_id=1, source_target_pairs={{0,8},{1,9},{2,10},{3,11},{4,12},{5,13},{6,14},{7,15},{8,0},{9,1},... | collective-permute-start | bytes 245768 | tf_op jit(solution)/shard_map/ppermute | solution.py:291
  (1 other events, 8.9 us)

commit v9 on v8

v9 whole, which is shorter than its diff:
```python
import functools
import math

import jax
import jax.numpy as jnp
from jax import lax
from jax.experimental import pallas as pl
from jax.experimental.pallas import tpu as pltpu
from jax.sharding import PartitionSpec as P

ROUNDS = 2

weight_decay = 0.02

MATES = (0, 2, 4, 6)
REST = 8
NT = (((1,), (1,)), ((), ()))
NN = (((1,), (0,)), ((), ()))
VMEM_LIMIT = 24 * 1024 * 1024


def dot(a, b, dims):
    return lax.dot_general(a, b, dims, preferred_element_type=jnp.float32)


def split3(x):
    hi = x.astype(jnp.bfloat16)
    rest = x - hi.astype(jnp.float32)
    mid = rest.astype(jnp.bfloat16)
    lo = (rest - mid.astype(jnp.float32)).astype(jnp.bfloat16)
    return hi, mid, lo


def low_half(rows):
    return lax.broadcasted_iota(jnp.int32, (rows, 128), 1) < 64


def double(x, low):
    turned = pltpu.roll(x, 64, 1)
    return jnp.where(low, x, turned), jnp.where(low, turned, x)


def load_kernel(turns, per_owner, own_blocks, pos_ref, cov, geno, samples, geno_out, samples_out, table, listed, sems):
    copies = [
        pltpu.make_async_copy(cov, listed, sems.at[0]),
        pltpu.make_async_copy(samples, samples_out, sems.at[1]),
        pltpu.make_async_copy(geno, geno_out, sems.at[2]),
    ]
    for copy in copies:
        copy.start()
    copies[0].wait()
    for m, mate in enumerate(MATES):
        batch = lax.bitwise_xor(pos_ref[0], mate)
        for t, turn in enumerate(turns):
            owner = lax.bitwise_xor(pos_ref[0], turn)
            for p in range(per_owner):
                table[m * len(turns) + t, p] = listed[batch, owner * per_owner + p] - owner * own_blocks
    for copy in copies[1:]:
        copy.wait()


def steps_kernel(scale, own_blocks, pos_ref, cov, *steps):
    low = low_half(steps[0].shape[0])
    for turn, out in enumerate(steps):
        owner = lax.bitwise_xor(pos_ref[0], turn * REST)

        def step_of(block):
            seen = (cov[...] == owner * own_blocks + block).astype(jnp.float32)
            return scale / jnp.sum(jnp.sum(seen, axis=1, keepdims=True), axis=0, keepdims=True)

        for j in range(own_blocks // 2):
            out[:, 128 * j:128 * (j + 1)] = jnp.where(low, step_of(2 * j), step_of(2 * j + 1))


def pick_kernel(places, per_owner, own_blocks, table, *refs):
    packets, blocks = refs[-1 - len(MATES):-1], refs[-1]
    turns = len(places)
    low = low_half(blocks.shape[2])
    for t, (ref, at) in enumerate(places):
        for j in range(own_blocks // 2):
            columns = slice(128 * j, 128 * (j + 1))
            x = (refs[ref][:, columns] if at is None else refs[ref][at, :, columns]).astype(jnp.float32)
            blocks[t, 2 * j], blocks[t, 2 * j + 1] = double(x, low)
    for m in range(len(MATES)):
        for t in range(turns):
            for q in range(per_owner // 2):
                first, second = table[m * turns + t, 2 * q], table[m * turns + t, 2 * q + 1]
                pair = jnp.where(low, blocks[t, first], blocks[t, second])
                packets[m][t, :, 128 * q:128 * (q + 1)] = pair.astype(jnp.bfloat16)


def mates_sum_kernel(turns, per_owner, own_blocks, table, *refs):
    terms, sums, total = refs[:len(MATES)], refs[-2 - turns // 2:-1], refs[-1]
    low = low_half(terms[0].shape[1])
    total[...] = jnp.zeros_like(total)
    for t in range(turns):
        for m in range(len(MATES)):
            for q in range(per_owner // 2):
                first, second = table[m * turns + t, 2 * q], table[m * turns + t, 2 * q + 1]
                pair = terms[m][t, :, 128 * q:128 * (q + 1)].astype(jnp.float32)
                total[t, first] += jnp.where(low, pair, 0.0)
                total[t, second] += jnp.where(low, 0.0, pair)
    for t in range(turns):
        for j in range(own_blocks // 2):
            first, second = total[t, 2 * j], total[t, 2 * j + 1]
            both = jnp.where(low, first, second) + pltpu.roll(jnp.where(low, second, first), 64, 1)
            columns = slice(128 * j, 128 * (j + 1))
            if t % 2:
                sums[-1][t // 2, :, columns] = both.astype(jnp.bfloat16)
            else:
                sums[t // 2][:, columns] = both


def add_kernel(own, other, arrived, own_sum, other_sum, swapped):
    own_sum[...] = own[...] + arrived[0].astype(jnp.float32)
    other_sum[...] = other[...] + arrived[1].astype(jnp.float32)
    swapped[0] = other_sum[...].astype(jnp.bfloat16)
    swapped[1] = own_sum[...].astype(jnp.bfloat16)


def update_kernel(own_sum, other_sum, arrived, own_step, other_step, snps, other_snps, new_snps, held):
    kept = 1.0 - weight_decay
    own_total = own_sum[...] + arrived[0].astype(jnp.float32)
    other_total = other_sum[...] + arrived[1].astype(jnp.float32)
    new_snps[...] = kept * snps[...] + own_step[...] * own_total
    held[0] = new_snps[...].astype(jnp.bfloat16)
    other = kept * other_snps[...].astype(jnp.float32) + other_step[...] * other_total
    held[1] = other.astype(jnp.bfloat16)


def turns_of(devices):
    return [high + core for high in range(0, devices, REST) for core in (0, 1)]


def columns_of(pos, turn, mate, width):
    owner = lax.bitwise_xor(pos, turn ^ mate)
    return pl.ds(pl.multiple_of(owner * width, width), width)


def product_kernel(turns, mate, first, rows, pos_ref, geno, packet, *refs):
    before, (gradient, gram) = refs[:-2], refs[-2:]
    pos = pos_ref[0]
    width = packet.shape[2]
    total = None if first else before[1][...]
    for t in range(len(turns)):
        term = dot(packet[t], packet[t], NT)
        total = term if total is None else total + term
    gram[...] = total
    for r in range(geno.shape[0] // rows):
        here = slice(r * rows, (r + 1) * rows)
        total = None if first else before[0][:, here]
        for t, turn in enumerate(turns):
            term = dot(packet[t], geno[here, columns_of(pos, turn, mate, width)], NT)
            total = term if total is None else total + term
        gradient[:, here] = total


def sample_kernel(sample_step, samples, gradient, gram, *outs):
    old = samples[...]
    old_bf16 = old.astype(jnp.bfloat16)
    total = gradient[...]
    for part in split3(gram[...]):
        total -= dot(part, old_bf16, NN)
    new = (1.0 - weight_decay) * old + sample_step * total
    *full, last = outs
    rounded = new.astype(jnp.bfloat16)
    for out in full:
        out[...] = new if out.dtype == jnp.float32 else rounded
    if last.shape[0] == last.shape[1]:
        last[...] = dot(rounded, rounded, NT)
    else:
        last[...] = jnp.zeros_like(last)


def term_kernel(turns, mate, pos_ref, geno, samples, gram, packet, terms):
    pos = pos_ref[0]
    width = packet.shape[2]
    parts = split3(gram[...])
    for t, turn in enumerate(turns):
        term = dot(samples[...], geno[:, columns_of(pos, turn, mate, width)], NN)
        for part in parts:
            term -= dot(part, packet[t], NN)
        terms[t] = term.astype(jnp.bfloat16)


def on_device(genotypes, sample_factors, snp_factors, coverage):
    devices = lax.axis_size("rows")
    turns = turns_of(devices)
    highs = len(turns) // 2
    position = lax.axis_index("rows").astype(jnp.int32)
    samples_here, snps_here = genotypes.shape
    rank = sample_factors.shape[1]
    covered = coverage.shape[1]
    tile_size = snps_here // covered
    per_owner = covered // devices
    own_snps = snp_factors.shape[0]
    own_blocks = own_snps // tile_size
    width = per_owner * tile_size
    assert tile_size == 64 and per_owner % 2 == 0 and own_blocks % 2 == 0
    assert devices % REST == 0 and devices & (devices - 1) == 0

    sample_step = 0.5 * math.sqrt(rank) / (covered * tile_size)

    smem = pl.BlockSpec(memory_space=pltpu.SMEM)
    vmem = pl.BlockSpec(memory_space=pltpu.VMEM)
    hbm = pl.BlockSpec(memory_space=pltpu.HBM)
    anywhere = pl.BlockSpec(memory_space=pl.ANY)
    params = pltpu.CompilerParams(vmem_limit_bytes=VMEM_LIMIT)
    pos = position.reshape(1)
    packet = jax.ShapeDtypeStruct((len(turns), rank, width), jnp.bfloat16)
    dense_blocks = pltpu.VMEM((len(turns), own_blocks, rank, 128), jnp.float32)
    by_samples = jax.ShapeDtypeStruct((rank, samples_here), jnp.float32)
    square = jax.ShapeDtypeStruct((rank, rank), jnp.float32)

    def cost(flops, bytes_accessed):
        return pl.CostEstimate(flops=flops, bytes_accessed=bytes_accessed, transcendentals=0)

    geno, samples, table = pl.pallas_call(
        functools.partial(load_kernel, turns, per_owner, own_blocks),
        out_shape=(
            pltpu.VMEM((samples_here, snps_here), jnp.bfloat16),
            pltpu.VMEM((rank, samples_here), jnp.float32),
            pltpu.SMEM((len(MATES) * len(turns), per_owner), jnp.int32),
        ),
        in_specs=[smem, hbm, hbm, hbm],
        out_specs=(vmem, vmem, smem),
        scratch_shapes=[pltpu.SMEM(coverage.shape, jnp.int32), pltpu.SemaphoreType.DMA((3,))],
        compiler_params=pltpu.CompilerParams(
            vmem_limit_bytes=58 * 1024 * 1024 - 2 * samples_here * snps_here
        ),
        cost_estimate=cost(0, 2 * samples_here * snps_here),
        name="load_batch",
    )(pos, coverage, genotypes, sample_factors.T)

    by_snps = jax.ShapeDtypeStruct((rank, own_snps), jnp.float32)
    pairwise = highs == 2
    n_steps = 2 if pairwise else 1
    snp_steps = pl.pallas_call(
        functools.partial(steps_kernel, 0.5 * math.sqrt(rank) / samples_here, own_blocks),
        out_shape=(by_snps,) * n_steps,
        in_specs=[smem, vmem],
        out_specs=(vmem,) * n_steps,
        compiler_params=params,
        name="snp_steps",
    )(pos, coverage)
    small = cost(0, 2 * 1024 * 1024)

    def pick(arrays, places):
        return pl.pallas_call(
            functools.partial(pick_kernel, places, per_owner, own_blocks),
            out_shape=(packet,) * len(MATES),
            in_specs=[smem] + [vmem] * len(arrays),
            out_specs=(vmem,) * len(MATES),
            scratch_shapes=[dense_blocks],
            compiler_params=params,
            cost_estimate=small,
            name="pick_blocks",
        )(table, *arrays)

    def mates_sum(terms, after):
        *sums, for_core = pl.pallas_call(
            functools.partial(mates_sum_kernel, len(turns), per_owner, own_blocks),
            out_shape=(by_snps,) * highs + (jax.ShapeDtypeStruct((highs, rank, own_snps), jnp.bfloat16),),
            in_specs=[smem] + [vmem] * len(MATES) + [anywhere] * len(after),
            out_specs=(vmem,) * (highs + 1),
            scratch_shapes=[dense_blocks],
            compiler_params=params,
            cost_estimate=small,
            name="mates_sum",
        )(table, *terms, *after)
        return sums, for_core

    two_snps = jax.ShapeDtypeStruct((2, rank, own_snps), jnp.bfloat16)
    add_core = pl.pallas_call(
        add_kernel,
        out_shape=(by_snps, by_snps, two_snps),
        in_specs=[vmem] * 3,
        out_specs=(vmem,) * 3,
        compiler_params=params,
        name="add_core",
    )
    owners_update = pl.pallas_call(
        update_kernel,
        out_shape=(by_snps, two_snps),
        in_specs=[vmem] * 7,
        out_specs=(vmem,) * 2,
        compiler_params=params,
        name="owners_update",
    )

    def product(mate, panel, before):
        share = samples_here * snps_here // len(MATES)
        return pl.pallas_call(
            functools.partial(product_kernel, turns, mate, not before, 256),
            out_shape=(by_samples, square),
            in_specs=[smem] + [vmem] * (2 + len(before)),
            out_specs=(vmem, vmem),
            compiler_params=params,
            cost_estimate=cost(8 * rank * share, 2 * share),
            name="panel_product",
        )(pos, geno, panel, *before)

    def sample_update(samples, gradient, gram, outs):
        return pl.pallas_call(
            functools.partial(sample_kernel, sample_step),
            out_shape=outs,
            in_specs=[vmem] * 3,
            out_specs=(vmem,) * len(outs),
            compiler_params=params,
            cost_estimate=small,
            name="sample_update",
        )(samples, gradient, gram)

    def terms_for(mate, samples_bf16, gram, panel):
        share = samples_here * snps_here // len(MATES)
        return pl.pallas_call(
            functools.partial(term_kernel, turns, mate),
            out_shape=packet,
            in_specs=[smem] + [vmem] * 4,
            out_specs=vmem,
            compiler_params=params,
            cost_estimate=cost(8 * rank * share, 2 * share),
            name="mate_terms",
        )(pos, geno, samples_bf16, gram, panel)

    def swap(x, turn):
        return lax.ppermute(x, "rows", [(r, r ^ turn) for r in range(devices)])

    def to_mate(x, mate):
        return swap(x, mate) if mate else x

    snps = snp_factors.T
    held = None
    for iteration in range(ROUNDS):
        last = iteration == ROUNDS - 1
        if held is None:
            held = {0: snps.astype(jnp.bfloat16)}
            for high in sorted(range(1, highs), key=lambda high: (high & (high - 1), -high)):
                bit = high & -high
                held[high] = swap(held[high ^ bit], bit * REST)
            arrays = []
            for high in range(highs):
                source = held[high]
                if iteration == 0 and high:
                    source, _ = lax.optimization_barrier((source, samples))
                arrays += [held[high], swap(source, 1)]
            places = [(i, None) for i in range(len(turns))]
        else:
            arrays = [held, swap(held, 1)]
            places = [(t % 2, t // 2) for t in range(len(turns))]
        packets = pick(arrays, places)
        panels = [to_mate(x, mate) for x, mate in zip(packets, MATES)]
        partial = ()
        for m in (0, 3, 2, 1):
            partial = product(MATES[m], panels[m], partial)
        rounded = (jax.ShapeDtypeStruct((rank, samples_here), jnp.bfloat16), square)
        if not last:
            samples, *current = sample_update(samples, *partial, (by_samples,) + rounded)
            after = []
        else:
            current = sample_update(samples, *partial, rounded)
            samples, token = sample_update(
                samples, *partial, (by_samples, jax.ShapeDtypeStruct((8, 128), jnp.float32))
            )
            after = [token]
        sums, for_core = mates_sum(
            [to_mate(terms_for(mate, *current, x), mate) for x, mate in zip(panels, MATES)], after
        )
        arrived = swap(for_core, 1)
        if pairwise and not last:
            own_sum, other_sum, swapped = add_core(*sums, arrived)
            snps, held = owners_update(
                own_sum, other_sum, swap(swapped, REST), *snp_steps, snps, held[1]
            )
            continue
        sums = [x + arrived[high].astype(jnp.float32) for high, x in enumerate(sums)]
        for high in range(highs - 1, 0, -1):
            bit = high & -high
            sums[high ^ bit] += swap(sums[high].astype(jnp.bfloat16), bit * REST).astype(jnp.float32)
        snps = (1.0 - weight_decay) * snps + snp_steps[0] * sums[0]
        held = None
    return (samples.T, snps.T)


def solution(mesh):
    placed = (
        P(("groups", "rows"), None),
        P(("groups", "rows"), None),
        P(("groups", "rows"), None),
        P("groups", None),
    )
    return jax.shard_map(
        on_device,
        mesh=mesh,
        in_specs=placed,
        out_specs=(P(("groups", "rows"), None), P(("groups", "rows"), None)),
        check_vma=False,
    )
```

time: 78.4 us -> 78.4 us (level)
  waiting for transfers between devices: 18.9 us -> 35.5 us
  starting transfers between devices: 36.3 us -> 21.5 us
  Pallas kernels: 20.2 us -> 18.6 us
    ppermute x31 -> x20, waiting for transfers between devices: 18.9 us -> 35.5 us  [swap(): return lax.ppermute(x, 'rows', [(r, r ^ turn) for r in range(devices)])]
    ppermute x31 -> x20, starting transfers between devices: 36.3 us -> 21.5 us  [swap(): return lax.ppermute(x, 'rows', [(r, r ^ turn) for r in range(devices)])]
    pallas_call x37 -> x23, Pallas kernels: 18.3 us -> 16.7 us  [the longest x8 6.38 us: product(): pl.pallas_call(functools.partial(product_kernel, turns, mate, not before,...]
  transfers between devices with their start and end apart: 31 -> 20, of which waited for: 11 -> 17; matrix products, arithmetic and copies ran while one was open for 0% -> 0% of each run, Pallas kernels for 21% -> 17%
where the time goes in v9:
time: 78.4 us; the launch traced here: 78.2 us
  waiting for transfers between devices  35.5 us (45%)
  starting transfers between devices  21.5 us (27%)
  Pallas kernels  18.6 us (24%)
  other arithmetic  1.66 us (2%)
  between operations  0.84 us (1%)
    ppermute x20, waiting for transfers between devices, swap(): return lax.ppermute(x, 'rows', [(r, r ^ turn) for r in range(devices)])  35.5 us
    ppermute x20, starting transfers between devices, swap(): return lax.ppermute(x, 'rows', [(r, r ^ turn) for r in range(devices)])  21.5 us
    pallas_call x8, Pallas kernels, product(): pl.pallas_call(functools.partial(product_kernel, turns, mate, not before,...  6.38 us
    pallas_call x8, Pallas kernels, terms_for(): pl.pallas_call(functools.partial(term_kernel, turns, mate), out_shape=pac...  4.9 us
    pallas_call x1, Pallas kernels, on_device(): pl.pallas_call(functools.partial(load_kernel, turns, per_owner, own_block...  3.51 us
    pallas_call x3, Pallas kernels, sample_update(): pl.pallas_call(functools.partial(sample_kernel, sample_step), out_shape=o...  1.77 us
  transfers between devices with their start and end apart: 20, of which 17 were waited for; matrix products, arithmetic and copies ran while one was open for 0% of the time, Pallas kernels for 17%

profile of v9, /device:TPU:0, one launch (start us, length us, event | category | flops | bytes accessed | tf_op | source)
XLA Modules:
  0.0 78.2 jit_solution(15796115118068837207)
XLA Ops:
  0.6 0.9 %bitcast_convert_fusion.refs_0_ = bf16[64,640]{1,0:T(8,128)(2,1)S(1)} fusion(f32[640,64]{0,1:T(8,128)} %param.6), kind=kLoop, calls=%fused_computation.9 | loop fusion | flops 40960 | bytes 245760 | tf_op jit(solution)/shard_map/convert_element_type | solution.py:337
  1.6 4.1 %collective-permute-start.1 = (bf16[64,640]{1,0:T(8,128)(2,1)S(1)}, bf16[64,640]{1,0:T(8,128)(2,1)S(1)}, u32[]{:S(2)}, u32[]{:S(2)}) collective-permute-start(bf16[64,640]{1,0:T(8,128)(2,1)S(1)} %bitcast_convert_fusion.refs_0_), channel_id=1, source_target_pairs={{0,8},{1,9},{2,10},{3,11},{4,12},{5,13},{6,14},{7,15},{8,0},{9,1},... | collective-permute-start | bytes 245768 | tf_op jit(solution)/shard_map/ppermute | solution.py:327
  5.7 3.5 %load_batch.1 = (bf16[1024,4096]{1,0:T(8,128)(2,1)S(1)}, f32[64,1024]{1,0:T(8,128)S(1)}, s32[16,4]{1,0:T(8,128)S(4)}) custom-call(s32[1]{0:T(128)} %bitcast.pos_ref, s32[16,64]{1,0:T(8,128)} %cov.3, bf16[1024,4096]{1,0:T(8,128)(2,1)} %geno.1, f32[64,1024]{1,0:T(8,128)} %bitcast.18), custom_call_target="tpu_custom_call" | custom-call | bytes 8388608 | tf_op jit(solution)/shard_map/load_batch/pallas_call | solution.py:218
  9.9 1.3 %collective-permute-done.2.refs_3_ = bf16[64,640]{1,0:T(8,128)(2,1)S(1)} collective-permute-done((bf16[64,640]{1,0:T(8,128)(2,1)S(1)}, bf16[64,640]{1,0:T(8,128)(2,1)S(1)}, u32[]{:S(2)}, u32[]{:S(2)}) %collective-permute-start.2) | collective-permute-done | bytes 81952 | tf_op jit(solution)/shard_map/ppermute | solution.py:327
  11.4 2.1 %collective-permute-start.5 = (bf16[4,64,256]{2,1,0:T(8,128)(2,1)S(1)}, bf16[4,64,256]{2,1,0:T(8,128)(2,1)S(1)}, u32[]{:S(2)}, u32[]{:S(2)}) collective-permute-start(bf16[4,64,256]{2,1,0:T(8,128)(2,1)S(1)} %get-tuple-element.56), channel_id=1, source_target_pairs={{0,6},{1,7},{2,4},{3,5},{4,2},{5,3},{6,0},{7,1},{8,14},{9,15},{10,... | collective-permute-start | bytes 393224 | tf_op jit(solution)/shard_map/ppermute | solution.py:327
  13.6 1.1 %collective-permute-start.4 = (bf16[4,64,256]{2,1,0:T(8,128)(2,1)S(1)}, bf16[4,64,256]{2,1,0:T(8,128)(2,1)S(1)}, u32[]{:S(2)}, u32[]{:S(2)}) collective-permute-start(bf16[4,64,256]{2,1,0:T(8,128)(2,1)S(1)} %get-tuple-element.55), channel_id=1, source_target_pairs={{0,4},{1,5},{2,6},{3,7},{4,0},{5,1},{6,2},{7,3},{8,12},{9,13},{10,... | collective-permute-start | bytes 393224 | tf_op jit(solution)/shard_map/ppermute | solution.py:327
  15.8 3.0 %collective-permute-done.5.packet = bf16[4,64,256]{2,1,0:T(8,128)(2,1)S(1)} collective-permute-done((bf16[4,64,256]{2,1,0:T(8,128)(2,1)S(1)}, bf16[4,64,256]{2,1,0:T(8,128)(2,1)S(1)}, u32[]{:S(2)}, u32[]{:S(2)}) %collective-permute-start.5) | collective-permute-done | bytes 131104 | tf_op jit(solution)/shard_map/ppermute | solution.py:327
  19.5 1.5 %collective-permute-done.4.packet = bf16[4,64,256]{2,1,0:T(8,128)(2,1)S(1)} collective-permute-done((bf16[4,64,256]{2,1,0:T(8,128)(2,1)S(1)}, bf16[4,64,256]{2,1,0:T(8,128)(2,1)S(1)}, u32[]{:S(2)}, u32[]{:S(2)}) %collective-permute-start.4) | collective-permute-done | bytes 131104 | tf_op jit(solution)/shard_map/ppermute | solution.py:327
  21.8 0.8 %panel_product.11 = (f32[64,1024]{1,0:T(8,128)S(1)}, f32[64,64]{1,0:T(8,128)S(1)}) custom-call(s32[1]{0:T(128)} %bitcast.pos_ref, bf16[1024,4096]{1,0:T(8,128)(2,1)S(1)} %get-tuple-element.51.geno, bf16[4,64,256]{2,1,0:T(8,128)(2,1)S(1)} %collective-permute-done.3.packet, f32[64,1024]{1,0:T(8,128)S(1)} %get-tuple-element.62.refs_0_, ...), custom_call_target="tpu_custom_call" | custom-call | flops 536870912 | bytes 2097152 | tf_op jit(solution)/shard_map/panel_product/pallas_call | solution.py:293
  23.7 1.3 %collective-permute-start.8 = (bf16[4,64,256]{2,1,0:T(8,128)(2,1)S(1)}, bf16[4,64,256]{2,1,0:T(8,128)(2,1)S(1)}, u32[]{:S(2)}, u32[]{:S(2)}) collective-permute-start(bf16[4,64,256]{2,1,0:T(8,128)(2,1)S(1)} %mate_terms.11), channel_id=1, source_target_pairs={{0,6},{1,7},{2,4},{3,5},{4,2},{5,3},{6,0},{7,1},{8,14},{9,15},{10,... | collective-permute-start | bytes 393224 | tf_op jit(solution)/shard_map/ppermute | solution.py:327
  25.6 0.9 %collective-permute-start.7 = (bf16[4,64,256]{2,1,0:T(8,128)(2,1)S(1)}, bf16[4,64,256]{2,1,0:T(8,128)(2,1)S(1)}, u32[]{:S(2)}, u32[]{:S(2)}) collective-permute-start(bf16[4,64,256]{2,1,0:T(8,128)(2,1)S(1)} %mate_terms.10), channel_id=1, source_target_pairs={{0,4},{1,5},{2,6},{3,7},{4,0},{5,1},{6,2},{7,3},{8,12},{9,13},{10,... | collective-permute-start | bytes 393224 | tf_op jit(solution)/shard_map/ppermute | solution.py:327
  27.1 1.5 %collective-permute-start.6 = (bf16[4,64,256]{2,1,0:T(8,128)(2,1)S(1)}, bf16[4,64,256]{2,1,0:T(8,128)(2,1)S(1)}, u32[]{:S(2)}, u32[]{:S(2)}) collective-permute-start(bf16[4,64,256]{2,1,0:T(8,128)(2,1)S(1)} %mate_terms.9), channel_id=1, source_target_pairs={{0,2},{1,3},{2,0},{3,1},{4,6},{5,7},{6,4},{7,5},{8,10},{9,11},{10,... | collective-permute-start | bytes 393224 | tf_op jit(solution)/shard_map/ppermute | solution.py:327
  29.2 1.6 %collective-permute-done.8.refs_3_ = bf16[4,64,256]{2,1,0:T(8,128)(2,1)S(1)} collective-permute-done((bf16[4,64,256]{2,1,0:T(8,128)(2,1)S(1)}, bf16[4,64,256]{2,1,0:T(8,128)(2,1)S(1)}, u32[]{:S(2)}, u32[]{:S(2)}) %collective-permute-start.8) | collective-permute-done | bytes 131104 | tf_op jit(solution)/shard_map/ppermute | solution.py:327
  30.9 1.2 %collective-permute-done.7.refs_2_ = bf16[4,64,256]{2,1,0:T(8,128)(2,1)S(1)} collective-permute-done((bf16[4,64,256]{2,1,0:T(8,128)(2,1)S(1)}, bf16[4,64,256]{2,1,0:T(8,128)(2,1)S(1)}, u32[]{:S(2)}, u32[]{:S(2)}) %collective-permute-start.7) | collective-permute-done | bytes 131104 | tf_op jit(solution)/shard_map/ppermute | solution.py:327
  32.0 0.8 %collective-permute-done.6.refs_1_ = bf16[4,64,256]{2,1,0:T(8,128)(2,1)S(1)} collective-permute-done((bf16[4,64,256]{2,1,0:T(8,128)(2,1)S(1)}, bf16[4,64,256]{2,1,0:T(8,128)(2,1)S(1)}, u32[]{:S(2)}, u32[]{:S(2)}) %collective-permute-start.6) | collective-permute-done | bytes 131104 | tf_op jit(solution)/shard_map/ppermute | solution.py:327
  33.6 1.4 %collective-permute-done.9.arrived = bf16[2,64,640]{2,1,0:T(8,128)(2,1)S(1)} collective-permute-done((bf16[2,64,640]{2,1,0:T(8,128)(2,1)S(1)}, bf16[2,64,640]{2,1,0:T(8,128)(2,1)S(1)}, u32[]{:S(2)}, u32[]{:S(2)}) %collective-permute-start.9) | collective-permute-done | bytes 163872 | tf_op jit(solution)/shard_map/ppermute | solution.py:327
  35.0 1.7 %collective-permute-start.10 = (bf16[2,64,640]{2,1,0:T(8,128)(2,1)S(1)}, bf16[2,64,640]{2,1,0:T(8,128)(2,1)S(1)}, u32[]{:S(2)}, u32[]{:S(2)}) collective-permute-start(bf16[2,64,640]{2,1,0:T(8,128)(2,1)S(1)} %get-tuple-element.74), channel_id=1, source_target_pairs={{0,8},{1,9},{2,10},{3,11},{4,12},{5,13},{6,14},{7,15},{8,0},{9,1},... | collective-permute-start | bytes 491528 | tf_op jit(solution)/shard_map/ppermute | solution.py:327
  36.8 8.9 %collective-permute-done.10.arrived = bf16[2,64,640]{2,1,0:T(8,128)(2,1)S(1)} collective-permute-done((bf16[2,64,640]{2,1,0:T(8,128)(2,1)S(1)}, bf16[2,64,640]{2,1,0:T(8,128)(2,1)S(1)}, u32[]{:S(2)}, u32[]{:S(2)}) %collective-permute-start.10) | collective-permute-done | bytes 163872 | tf_op jit(solution)/shard_map/ppermute | solution.py:327
  45.9 1.4 %collective-permute-done.11.refs_1_ = bf16[2,64,640]{2,1,0:T(8,128)(2,1)S(1)} collective-permute-done((bf16[2,64,640]{2,1,0:T(8,128)(2,1)S(1)}, bf16[2,64,640]{2,1,0:T(8,128)(2,1)S(1)}, u32[]{:S(2)}, u32[]{:S(2)}) %collective-permute-start.11) | collective-permute-done | bytes 163872 | tf_op jit(solution)/shard_map/ppermute | solution.py:327
  47.8 2.1 %collective-permute-start.13 = (bf16[4,64,256]{2,1,0:T(8,128)(2,1)S(1)}, bf16[4,64,256]{2,1,0:T(8,128)(2,1)S(1)}, u32[]{:S(2)}, u32[]{:S(2)}) collective-permute-start(bf16[4,64,256]{2,1,0:T(8,128)(2,1)S(1)} %get-tuple-element.79), channel_id=1, source_target_pairs={{0,4},{1,5},{2,6},{3,7},{4,0},{5,1},{6,2},{7,3},{8,12},{9,13},{10,... | collective-permute-start | bytes 393224 | tf_op jit(solution)/shard_map/ppermute | solution.py:327
  49.9 1.3 %collective-permute-start.12 = (bf16[4,64,256]{2,1,0:T(8,128)(2,1)S(1)}, bf16[4,64,256]{2,1,0:T(8,128)(2,1)S(1)}, u32[]{:S(2)}, u32[]{:S(2)}) collective-permute-start(bf16[4,64,256]{2,1,0:T(8,128)(2,1)S(1)} %get-tuple-element.78), channel_id=1, source_target_pairs={{0,2},{1,3},{2,0},{3,1},{4,6},{5,7},{6,4},{7,5},{8,10},{9,11},{10,... | collective-permute-start | bytes 393224 | tf_op jit(solution)/shard_map/ppermute | solution.py:327
  51.9 3.0 %collective-permute-done.14.packet = bf16[4,64,256]{2,1,0:T(8,128)(2,1)S(1)} collective-permute-done((bf16[4,64,256]{2,1,0:T(8,128)(2,1)S(1)}, bf16[4,64,256]{2,1,0:T(8,128)(2,1)S(1)}, u32[]{:S(2)}, u32[]{:S(2)}) %collective-permute-start.14) | collective-permute-done | bytes 131104 | tf_op jit(solution)/shard_map/ppermute | solution.py:327
  57.0 0.8 %panel_product.15 = (f32[64,1024]{1,0:T(8,128)S(1)}, f32[64,64]{1,0:T(8,128)S(1)}) custom-call(s32[1]{0:T(128)} %bitcast.pos_ref, bf16[1024,4096]{1,0:T(8,128)(2,1)S(1)} %get-tuple-element.51.geno, bf16[4,64,256]{2,1,0:T(8,128)(2,1)S(1)} %collective-permute-done.12.packet, f32[64,1024]{1,0:T(8,128)S(1)} %get-tuple-element.86.refs_0_, ...), custom_call_target="tpu_custom_call" | custom-call | flops 536870912 | bytes 2097152 | tf_op jit(solution)/shard_map/panel_product/pallas_call | solution.py:293
  59.9 2.4 %collective-permute-start.16 = (bf16[4,64,256]{2,1,0:T(8,128)(2,1)S(1)}, bf16[4,64,256]{2,1,0:T(8,128)(2,1)S(1)}, u32[]{:S(2)}, u32[]{:S(2)}) collective-permute-start(bf16[4,64,256]{2,1,0:T(8,128)(2,1)S(1)} %mate_terms.14), channel_id=1, source_target_pairs={{0,4},{1,5},{2,6},{3,7},{4,0},{5,1},{6,2},{7,3},{8,12},{9,13},{10,... | collective-permute-start | bytes 393224 | tf_op jit(solution)/shard_map/ppermute | solution.py:327
  62.9 0.8 %collective-permute-start.15 = (bf16[4,64,256]{2,1,0:T(8,128)(2,1)S(1)}, bf16[4,64,256]{2,1,0:T(8,128)(2,1)S(1)}, u32[]{:S(2)}, u32[]{:S(2)}) collective-permute-start(bf16[4,64,256]{2,1,0:T(8,128)(2,1)S(1)} %mate_terms.13), channel_id=1, source_target_pairs={{0,2},{1,3},{2,0},{3,1},{4,6},{5,7},{6,4},{7,5},{8,10},{9,11},{10,... | collective-permute-start | bytes 393224 | tf_op jit(solution)/shard_map/ppermute | solution.py:327
  63.8 1.0 %sample_update.4 = (f32[64,1024]{1,0:T(8,128)}, f32[8,128]{1,0:T(8,128)S(1)}) custom-call(f32[64,1024]{1,0:T(8,128)S(1)} %get-tuple-element.66.samples, f32[64,1024]{1,0:T(8,128)S(1)} %get-tuple-element.88.gradient, f32[64,64]{1,0:T(8,128)S(1)} %get-tuple-element.89.gram), custom_call_target="tpu_custom_call" | custom-call | bytes 2097152 | tf_op jit(solution)/shard_map/sample_update/pallas_call | solution.py:304
  65.3 0.9 %collective-permute-done.17.refs_3_ = bf16[4,64,256]{2,1,0:T(8,128)(2,1)S(1)} collective-permute-done((bf16[4,64,256]{2,1,0:T(8,128)(2,1)S(1)}, bf16[4,64,256]{2,1,0:T(8,128)(2,1)S(1)}, u32[]{:S(2)}, u32[]{:S(2)}) %collective-permute-start.17) | collective-permute-done | bytes 131104 | tf_op jit(solution)/shard_map/ppermute | solution.py:327
  66.2 1.0 %collective-permute-done.16.refs_2_ = bf16[4,64,256]{2,1,0:T(8,128)(2,1)S(1)} collective-permute-done((bf16[4,64,256]{2,1,0:T(8,128)(2,1)S(1)}, bf16[4,64,256]{2,1,0:T(8,128)(2,1)S(1)}, u32[]{:S(2)}, u32[]{:S(2)}) %collective-permute-start.16) | collective-permute-done | bytes 131104 | tf_op jit(solution)/shard_map/ppermute | solution.py:327
  67.2 0.9 %collective-permute-done.15.refs_1_ = bf16[4,64,256]{2,1,0:T(8,128)(2,1)S(1)} collective-permute-done((bf16[4,64,256]{2,1,0:T(8,128)(2,1)S(1)}, bf16[4,64,256]{2,1,0:T(8,128)(2,1)S(1)}, u32[]{:S(2)}, u32[]{:S(2)}) %collective-permute-start.15) | collective-permute-done | bytes 131104 | tf_op jit(solution)/shard_map/ppermute | solution.py:327
  68.8 1.4 %collective-permute-done.18 = bf16[2,64,640]{2,1,0:T(8,128)(2,1)S(1)} collective-permute-done((bf16[2,64,640]{2,1,0:T(8,128)(2,1)S(1)}, bf16[2,64,640]{2,1,0:T(8,128)(2,1)S(1)}, u32[]{:S(2)}, u32[]{:S(2)}) %collective-permute-start.18) | collective-permute-done | bytes 163872 | tf_op jit(solution)/shard_map/ppermute | solution.py:327
  70.2 1.0 %collective-permute-start.19 = (bf16[64,640]{1,0:T(8,128)(2,1)S(1)}, bf16[64,640]{1,0:T(8,128)(2,1)S(1)}, u32[]{:S(2)}, u32[]{:S(2)}) collective-permute-start(bf16[64,640]{1,0:T(8,128)(2,1)S(1)} %fusion), channel_id=1, source_target_pairs={{0,8},{1,9},{2,10},{3,11},{4,12},{5,13},{6,14},{7,15},{8,0},{9,1},... | collective-permute-start | bytes 245768 | tf_op jit(solution)/shard_map/ppermute | solution.py:327
  71.2 6.2 %collective-permute-done.19 = bf16[64,640]{1,0:T(8,128)(2,1)S(1)} collective-permute-done((bf16[64,640]{1,0:T(8,128)(2,1)S(1)}, bf16[64,640]{1,0:T(8,128)(2,1)S(1)}, u32[]{:S(2)}, u32[]{:S(2)}) %collective-permute-start.19) | collective-permute-done | bytes 81952 | tf_op jit(solution)/shard_map/ppermute | solution.py:327
  (42 shorter events, 15.7 us)
Async XLA Ops:
  1.6 8.3 %collective-permute-start.1 = (bf16[64,640]{1,0:T(8,128)(2,1)S(1)}, bf16[64,640]{1,0:T(8,128)(2,1)S(1)}, u32[]{:S(2)}, u32[]{:S(2)}) collective-permute-start(bf16[64,640]{1,0:T(8,128)(2,1)S(1)} %bitcast_convert_fusion.refs_0_), channel_id=1, source_target_pairs={{0,8},{1,9},{2,10},{3,11},{4,12},{5,13},{6,14},{7,15},{8,0},{9,1},... | collective-permute-start | bytes 245768 | tf_op jit(solution)/shard_map/ppermute | solution.py:327
  5.7 4.2 %collective-permute-start = (bf16[64,640]{1,0:T(8,128)(2,1)S(1)}, bf16[64,640]{1,0:T(8,128)(2,1)S(1)}, u32[]{:S(2)}, u32[]{:S(2)}) collective-permute-start(bf16[64,640]{1,0:T(8,128)(2,1)S(1)} %bitcast_convert_fusion.refs_0_), channel_id=1, source_target_pairs={{0,1},{1,0},{2,3},{3,2},{4,5},{5,4},{6,7},{7,6},{8,9},{9,8},{10,11... | collective-permute-start | bytes 245768 | tf_op jit(solution)/shard_map/ppermute | solution.py:327
  9.9 1.3 %collective-permute-start.2 = (bf16[64,640]{1,0:T(8,128)(2,1)S(1)}, bf16[64,640]{1,0:T(8,128)(2,1)S(1)}, u32[]{:S(2)}, u32[]{:S(2)}) collective-permute-start(bf16[64,640]{1,0:T(8,128)(2,1)S(1)} %collective-permute-done.1.refs_2_.other_snps), channel_id=1, source_target_pairs={{0,1},{1,0},{2,3},{3,2},{4,5},{5,4},{6,7},{7,6},{8,9},{9,8},{10,11... | collective-permute-start | bytes 245768 | tf_op jit(solution)/shard_map/ppermute | solution.py:327
  11.4 7.3 %collective-permute-start.5 = (bf16[4,64,256]{2,1,0:T(8,128)(2,1)S(1)}, bf16[4,64,256]{2,1,0:T(8,128)(2,1)S(1)}, u32[]{:S(2)}, u32[]{:S(2)}) collective-permute-start(bf16[4,64,256]{2,1,0:T(8,128)(2,1)S(1)} %get-tuple-element.56), channel_id=1, source_target_pairs={{0,6},{1,7},{2,4},{3,5},{4,2},{5,3},{6,0},{7,1},{8,14},{9,15},{10,... | collective-permute-start | bytes 393224 | tf_op jit(solution)/shard_map/ppermute | solution.py:327
  13.6 7.5 %collective-permute-start.4 = (bf16[4,64,256]{2,1,0:T(8,128)(2,1)S(1)}, bf16[4,64,256]{2,1,0:T(8,128)(2,1)S(1)}, u32[]{:S(2)}, u32[]{:S(2)}) collective-permute-start(bf16[4,64,256]{2,1,0:T(8,128)(2,1)S(1)} %get-tuple-element.55), channel_id=1, source_target_pairs={{0,4},{1,5},{2,6},{3,7},{4,0},{5,1},{6,2},{7,3},{8,12},{9,13},{10,... | collective-permute-start | bytes 393224 | tf_op jit(solution)/shard_map/ppermute | solution.py:327
  14.6 7.2 %collective-permute-start.3 = (bf16[4,64,256]{2,1,0:T(8,128)(2,1)S(1)}, bf16[4,64,256]{2,1,0:T(8,128)(2,1)S(1)}, u32[]{:S(2)}, u32[]{:S(2)}) collective-permute-start(bf16[4,64,256]{2,1,0:T(8,128)(2,1)S(1)} %get-tuple-element.54), channel_id=1, source_target_pairs={{0,2},{1,3},{2,0},{3,1},{4,6},{5,7},{6,4},{7,5},{8,10},{9,11},{10,... | collective-permute-start | bytes 393224 | tf_op jit(solution)/shard_map/ppermute | solution.py:327
  23.7 7.2 %collective-permute-start.8 = (bf16[4,64,256]{2,1,0:T(8,128)(2,1)S(1)}, bf16[4,64,256]{2,1,0:T(8,128)(2,1)S(1)}, u32[]{:S(2)}, u32[]{:S(2)}) collective-permute-start(bf16[4,64,256]{2,1,0:T(8,128)(2,1)S(1)} %mate_terms.11), channel_id=1, source_target_pairs={{0,6},{1,7},{2,4},{3,5},{4,2},{5,3},{6,0},{7,1},{8,14},{9,15},{10,... | collective-permute-start | bytes 393224 | tf_op jit(solution)/shard_map/ppermute | solution.py:327
  25.5 11.2 %copy-start.1 = (s32[16,64]{1,0:T(8,128)S(1)}, s32[16,64]{1,0:T(8,128)}, u32[]{:S(2)}) copy-start(s32[16,64]{1,0:T(8,128)} %cov.3) | copy-start | bytes 12292
  25.6 20.2 %copy-start = (f32[640,64]{0,1:T(8,128)S(1)}, f32[640,64]{0,1:T(8,128)}, u32[]{:S(2)}) copy-start(f32[640,64]{0,1:T(8,128)} %param.6) | copy-start | bytes 491524
  25.6 6.5 %collective-permute-start.7 = (bf16[4,64,256]{2,1,0:T(8,128)(2,1)S(1)}, bf16[4,64,256]{2,1,0:T(8,128)(2,1)S(1)}, u32[]{:S(2)}, u32[]{:S(2)}) collective-permute-start(bf16[4,64,256]{2,1,0:T(8,128)(2,1)S(1)} %mate_terms.10), channel_id=1, source_target_pairs={{0,4},{1,5},{2,6},{3,7},{4,0},{5,1},{6,2},{7,3},{8,12},{9,13},{10,... | collective-permute-start | bytes 393224 | tf_op jit(solution)/shard_map/ppermute | solution.py:327
  27.1 5.7 %collective-permute-start.6 = (bf16[4,64,256]{2,1,0:T(8,128)(2,1)S(1)}, bf16[4,64,256]{2,1,0:T(8,128)(2,1)S(1)}, u32[]{:S(2)}, u32[]{:S(2)}) collective-permute-start(bf16[4,64,256]{2,1,0:T(8,128)(2,1)S(1)} %mate_terms.9), channel_id=1, source_target_pairs={{0,2},{1,3},{2,0},{3,1},{4,6},{5,7},{6,4},{7,5},{8,10},{9,11},{10,... | collective-permute-start | bytes 393224 | tf_op jit(solution)/shard_map/ppermute | solution.py:327
  33.5 1.5 %collective-permute-start.9 = (bf16[2,64,640]{2,1,0:T(8,128)(2,1)S(1)}, bf16[2,64,640]{2,1,0:T(8,128)(2,1)S(1)}, u32[]{:S(2)}, u32[]{:S(2)}) collective-permute-start(bf16[2,64,640]{2,1,0:T(8,128)(2,1)S(1)} %get-tuple-element.71), channel_id=1, source_target_pairs={{0,1},{1,0},{2,3},{3,2},{4,5},{5,4},{6,7},{7,6},{8,9},{9,8},{10,11... | collective-permute-start | bytes 491528 | tf_op jit(solution)/shard_map/ppermute | solution.py:327
  35.0 10.7 %collective-permute-start.10 = (bf16[2,64,640]{2,1,0:T(8,128)(2,1)S(1)}, bf16[2,64,640]{2,1,0:T(8,128)(2,1)S(1)}, u32[]{:S(2)}, u32[]{:S(2)}) collective-permute-start(bf16[2,64,640]{2,1,0:T(8,128)(2,1)S(1)} %get-tuple-element.74), channel_id=1, source_target_pairs={{0,8},{1,9},{2,10},{3,11},{4,12},{5,13},{6,14},{7,15},{8,0},{9,1},... | collective-permute-start | bytes 491528 | tf_op jit(solution)/shard_map/ppermute | solution.py:327
  45.9 1.5 %collective-permute-start.11 = (bf16[2,64,640]{2,1,0:T(8,128)(2,1)S(1)}, bf16[2,64,640]{2,1,0:T(8,128)(2,1)S(1)}, u32[]{:S(2)}, u32[]{:S(2)}) collective-permute-start(bf16[2,64,640]{2,1,0:T(8,128)(2,1)S(1)} %get-tuple-element.77.refs_0_), channel_id=1, source_target_pairs={{0,1},{1,0},{2,3},{3,2},{4,5},{5,4},{6,7},{7,6},{8,9},{9,8},{10,11... | collective-permute-start | bytes 491528 | tf_op jit(solution)/shard_map/ppermute | solution.py:327
  47.6 7.3 %collective-permute-start.14 = (bf16[4,64,256]{2,1,0:T(8,128)(2,1)S(1)}, bf16[4,64,256]{2,1,0:T(8,128)(2,1)S(1)}, u32[]{:S(2)}, u32[]{:S(2)}) collective-permute-start(bf16[4,64,256]{2,1,0:T(8,128)(2,1)S(1)} %get-tuple-element.80), channel_id=1, source_target_pairs={{0,6},{1,7},{2,4},{3,5},{4,2},{5,3},{6,0},{7,1},{8,14},{9,15},{10,... | collective-permute-start | bytes 393224 | tf_op jit(solution)/shard_map/ppermute | solution.py:327
  47.8 8.4 %collective-permute-start.13 = (bf16[4,64,256]{2,1,0:T(8,128)(2,1)S(1)}, bf16[4,64,256]{2,1,0:T(8,128)(2,1)S(1)}, u32[]{:S(2)}, u32[]{:S(2)}) collective-permute-start(bf16[4,64,256]{2,1,0:T(8,128)(2,1)S(1)} %get-tuple-element.79), channel_id=1, source_target_pairs={{0,4},{1,5},{2,6},{3,7},{4,0},{5,1},{6,2},{7,3},{8,12},{9,13},{10,... | collective-permute-start | bytes 393224 | tf_op jit(solution)/shard_map/ppermute | solution.py:327
  49.9 7.1 %collective-permute-start.12 = (bf16[4,64,256]{2,1,0:T(8,128)(2,1)S(1)}, bf16[4,64,256]{2,1,0:T(8,128)(2,1)S(1)}, u32[]{:S(2)}, u32[]{:S(2)}) collective-permute-start(bf16[4,64,256]{2,1,0:T(8,128)(2,1)S(1)} %get-tuple-element.78), channel_id=1, source_target_pairs={{0,2},{1,3},{2,0},{3,1},{4,6},{5,7},{6,4},{7,5},{8,10},{9,11},{10,... | collective-permute-start | bytes 393224 | tf_op jit(solution)/shard_map/ppermute | solution.py:327
  58.9 7.3 %collective-permute-start.17 = (bf16[4,64,256]{2,1,0:T(8,128)(2,1)S(1)}, bf16[4,64,256]{2,1,0:T(8,128)(2,1)S(1)}, u32[]{:S(2)}, u32[]{:S(2)}) collective-permute-start(bf16[4,64,256]{2,1,0:T(8,128)(2,1)S(1)} %mate_terms.15), channel_id=1, source_target_pairs={{0,6},{1,7},{2,4},{3,5},{4,2},{5,3},{6,0},{7,1},{8,14},{9,15},{10,... | collective-permute-start | bytes 393224 | tf_op jit(solution)/shard_map/ppermute | solution.py:327
  59.9 7.2 %collective-permute-start.16 = (bf16[4,64,256]{2,1,0:T(8,128)(2,1)S(1)}, bf16[4,64,256]{2,1,0:T(8,128)(2,1)S(1)}, u32[]{:S(2)}, u32[]{:S(2)}) collective-permute-start(bf16[4,64,256]{2,1,0:T(8,128)(2,1)S(1)} %mate_terms.14), channel_id=1, source_target_pairs={{0,4},{1,5},{2,6},{3,7},{4,0},{5,1},{6,2},{7,3},{8,12},{9,13},{10,... | collective-permute-start | bytes 393224 | tf_op jit(solution)/shard_map/ppermute | solution.py:327
  62.9 5.1 %collective-permute-start.15 = (bf16[4,64,256]{2,1,0:T(8,128)(2,1)S(1)}, bf16[4,64,256]{2,1,0:T(8,128)(2,1)S(1)}, u32[]{:S(2)}, u32[]{:S(2)}) collective-permute-start(bf16[4,64,256]{2,1,0:T(8,128)(2,1)S(1)} %mate_terms.13), channel_id=1, source_target_pairs={{0,2},{1,3},{2,0},{3,1},{4,6},{5,7},{6,4},{7,5},{8,10},{9,11},{10,... | collective-permute-start | bytes 393224 | tf_op jit(solution)/shard_map/ppermute | solution.py:327
  68.7 1.5 %collective-permute-start.18 = (bf16[2,64,640]{2,1,0:T(8,128)(2,1)S(1)}, bf16[2,64,640]{2,1,0:T(8,128)(2,1)S(1)}, u32[]{:S(2)}, u32[]{:S(2)}) collective-permute-start(bf16[2,64,640]{2,1,0:T(8,128)(2,1)S(1)} %get-tuple-element.96), channel_id=1, source_target_pairs={{0,1},{1,0},{2,3},{3,2},{4,5},{5,4},{6,7},{7,6},{8,9},{9,8},{10,11... | collective-permute-start | bytes 491528 | tf_op jit(solution)/shard_map/ppermute | solution.py:327
  70.2 7.2 %collective-permute-start.19 = (bf16[64,640]{1,0:T(8,128)(2,1)S(1)}, bf16[64,640]{1,0:T(8,128)(2,1)S(1)}, u32[]{:S(2)}, u32[]{:S(2)}) collective-permute-start(bf16[64,640]{1,0:T(8,128)(2,1)S(1)} %fusion), channel_id=1, source_target_pairs={{0,8},{1,9},{2,10},{3,11},{4,12},{5,13},{6,14},{7,15},{8,0},{9,1},... | collective-permute-start | bytes 245768 | tf_op jit(solution)/shard_map/ppermute | solution.py:327

commit v10 on v9

--- a/solution.py
+++ b/solution.py
@@ -72,21 +72,20 @@
             out[:, 128 * j:128 * (j + 1)] = jnp.where(low, step_of(2 * j), step_of(2 * j + 1))
 
 
-def pick_kernel(places, per_owner, own_blocks, table, *refs):
+def pick_kernel(turns, group, places, per_owner, own_blocks, table, *refs):
     packets, blocks = refs[-1 - len(MATES):-1], refs[-1]
-    turns = len(places)
     low = low_half(blocks.shape[2])
-    for t, (ref, at) in enumerate(places):
+    for i, (ref, at) in enumerate(places):
         for j in range(own_blocks // 2):
             columns = slice(128 * j, 128 * (j + 1))
             x = (refs[ref][:, columns] if at is None else refs[ref][at, :, columns]).astype(jnp.float32)
-            blocks[t, 2 * j], blocks[t, 2 * j + 1] = double(x, low)
+            blocks[i, 2 * j], blocks[i, 2 * j + 1] = double(x, low)
     for m in range(len(MATES)):
-        for t in range(turns):
+        for i, t in enumerate(group):
             for q in range(per_owner // 2):
                 first, second = table[m * turns + t, 2 * q], table[m * turns + t, 2 * q + 1]
-                pair = jnp.where(low, blocks[t, first], blocks[t, second])
-                packets[m][t, :, 128 * q:128 * (q + 1)] = pair.astype(jnp.bfloat16)
+                pair = jnp.where(low, blocks[i, first], blocks[i, second])
+                packets[m][i, :, 128 * q:128 * (q + 1)] = pair.astype(jnp.bfloat16)
 
 
 def mates_sum_kernel(turns, per_owner, own_blocks, table, *refs):
@@ -172,15 +171,17 @@
         last[...] = jnp.zeros_like(last)
 
 
-def term_kernel(turns, mate, pos_ref, geno, samples, gram, packet, terms):
+def term_kernel(turns, groups, mate, pos_ref, geno, samples, gram, *refs):
+    packets, terms = refs[:-1], refs[-1]
     pos = pos_ref[0]
-    width = packet.shape[2]
+    width = terms.shape[2]
     parts = split3(gram[...])
-    for t, turn in enumerate(turns):
-        term = dot(samples[...], geno[:, columns_of(pos, turn, mate, width)], NN)
-        for part in parts:
-            term -= dot(part, packet[t], NN)
-        terms[t] = term.astype(jnp.bfloat16)
+    for packet, group in zip(packets, groups):
+        for i, t in enumerate(group):
+            term = dot(samples[...], geno[:, columns_of(pos, turns[t], mate, width)], NN)
+            for part in parts:
+                term -= dot(part, packet[i], NN)
+            terms[t] = term.astype(jnp.bfloat16)
 
 
 def on_device(genotypes, sample_factors, snp_factors, coverage):
@@ -245,13 +246,15 @@
     )(pos, coverage)
     small = cost(0, 2 * 1024 * 1024)
 
-    def pick(arrays, places):
+    half_packet = jax.ShapeDtypeStruct((highs, rank, width), jnp.bfloat16)
+
+    def pick(arrays, group, places):
         return pl.pallas_call(
-            functools.partial(pick_kernel, places, per_owner, own_blocks),
-            out_shape=(packet,) * len(MATES),
+            functools.partial(pick_kernel, len(turns), group, places, per_owner, own_blocks),
+            out_shape=(half_packet,) * len(MATES),
             in_specs=[smem] + [vmem] * len(arrays),
             out_specs=(vmem,) * len(MATES),
-            scratch_shapes=[dense_blocks],
+            scratch_shapes=[pltpu.VMEM((highs, own_blocks, rank, 128), jnp.float32)],
             compiler_params=params,
             cost_estimate=small,
             name="pick_blocks",
@@ -288,10 +291,10 @@
         name="owners_update",
     )
 
-    def product(mate, panel, before):
-        share = samples_here * snps_here // len(MATES)
+    def product(mate, group, panel, before):
+        share = samples_here * snps_here // len(MATES) // 2
         return pl.pallas_call(
-            functools.partial(product_kernel, turns, mate, not before, 256),
+            functools.partial(product_kernel, [turns[t] for t in group], mate, not before, 256),
             out_shape=(by_samples, square),
             in_specs=[smem] + [vmem] * (2 + len(before)),
             out_specs=(vmem, vmem),
@@ -311,17 +314,17 @@
             name="sample_update",
         )(samples, gradient, gram)
 
-    def terms_for(mate, samples_bf16, gram, panel):
+    def terms_for(mate, samples_bf16, gram, groups, panels):
         share = samples_here * snps_here // len(MATES)
         return pl.pallas_call(
-            functools.partial(term_kernel, turns, mate),
+            functools.partial(term_kernel, turns, groups, mate),
             out_shape=packet,
-            in_specs=[smem] + [vmem] * 4,
+            in_specs=[smem] + [vmem] * (3 + len(panels)),
             out_specs=vmem,
             compiler_params=params,
             cost_estimate=cost(8 * rank * share, 2 * share),
             name="mate_terms",
-        )(pos, geno, samples_bf16, gram, panel)
+        )(pos, geno, samples_bf16, gram, *panels)
 
     def swap(x, turn):
         return lax.ppermute(x, "rows", [(r, r ^ turn) for r in range(devices)])
@@ -338,21 +341,26 @@
             for high in sorted(range(1, highs), key=lambda high: (high & (high - 1), -high)):
                 bit = high & -high
                 held[high] = swap(held[high ^ bit], bit * REST)
-            arrays = []
+            groups = [list(range(highs)), list(range(highs, 2 * highs))]
+            sources = {}
             for high in range(highs):
                 source = held[high]
                 if iteration == 0 and high:
                     source, _ = lax.optimization_barrier((source, samples))
-                arrays += [held[high], swap(source, 1)]
-            places = [(i, None) for i in range(len(turns))]
+                sources[2 * high], sources[2 * high + 1] = held[high], swap(source, 1)
+            picked = [
+                pick([sources[t] for t in group], group, [(i, None) for i in range(highs)]) for group in groups
+            ]
         else:
-            arrays = [held, swap(held, 1)]
-            places = [(t % 2, t // 2) for t in range(len(turns))]
-        packets = pick(arrays, places)
-        panels = [to_mate(x, mate) for x, mate in zip(packets, MATES)]
+            groups = [[2 * high + core for high in range(highs)] for core in (0, 1)]
+            picked = [
+                pick([x], group, [(0, high) for high in range(highs)])
+                for x, group in zip((held, swap(held, 1)), groups)
+            ]
+        panels = [[to_mate(x, mate) for x, mate in zip(packets, MATES)] for packets in picked]
         partial = ()
-        for m in (0, 3, 2, 1):
-            partial = product(MATES[m], panels[m], partial)
+        for g, m in ((0, 0), (1, 0), (0, 3), (0, 2), (0, 1), (1, 3), (1, 2), (1, 1)):
+            partial = product(MATES[m], groups[g], panels[g][m], partial)
         rounded = (jax.ShapeDtypeStruct((rank, samples_here), jnp.bfloat16), square)
         if not last:
             samples, *current = sample_update(samples, *partial, (by_samples,) + rounded)
@@ -364,7 +372,11 @@
             )
             after = [token]
         sums, for_core = mates_sum(
-            [to_mate(terms_for(mate, *current, x), mate) for x, mate in zip(panels, MATES)], after
+            [
+                to_mate(terms_for(mate, *current, groups, [x[m] for x in panels]), mate)
+                for m, mate in enumerate(MATES)
+            ],
+            after,
         )
         arrived = swap(for_core, 1)
         if pairwise and not last:

time: 78.4 us -> 77.7 us (level)
  waiting for transfers between devices: 35.5 us -> 24.8 us
  starting transfers between devices: 21.5 us -> 30.2 us
  Pallas kernels: 18.6 us -> 19.8 us
    ppermute x20 -> x26, waiting for transfers between devices: 35.5 us -> 24.8 us  [swap(): return lax.ppermute(x, 'rows', [(r, r ^ turn) for r in range(devices)])]
    ppermute x20 -> x26, starting transfers between devices: 21.5 us -> 30.2 us  [swap(): return lax.ppermute(x, 'rows', [(r, r ^ turn) for r in range(devices)])]
    pallas_call x18 -> x28, Pallas kernels: 11.8 us -> 13 us  [the longest x16 7.41 us: product(): pl.pallas_call(functools.partial(product_kernel, [turns[t] for t in group...]
  transfers between devices with their start and end apart: 20 -> 26, of which waited for: 17 -> 13; matrix products, arithmetic and copies ran while one was open for 0% -> 0% of each run, Pallas kernels for 17% -> 20%
where the time goes in v10:
time: 77.7 us; the launch traced here: 77.5 us
  starting transfers between devices  30.2 us (39%)
  waiting for transfers between devices  24.8 us (32%)
  Pallas kernels  19.8 us (25%)
  other arithmetic  1.66 us (2%)
  between operations  0.97 us (1%)
    ppermute x26, starting transfers between devices, swap(): return lax.ppermute(x, 'rows', [(r, r ^ turn) for r in range(devices)])  30.2 us
    ppermute x26, waiting for transfers between devices, swap(): return lax.ppermute(x, 'rows', [(r, r ^ turn) for r in range(devices)])  24.8 us
    pallas_call x16, Pallas kernels, product(): pl.pallas_call(functools.partial(product_kernel, [turns[t] for t in group...  7.41 us
    pallas_call x8, Pallas kernels, terms_for(): pl.pallas_call(functools.partial(term_kernel, turns, groups, mate), out_s...  4.9 us
    pallas_call x1, Pallas kernels, on_device(): pl.pallas_call(functools.partial(load_kernel, turns, per_owner, own_block...  3.51 us
    pallas_call x3, Pallas kernels, sample_update(): pl.pallas_call(functools.partial(sample_kernel, sample_step), out_shape=o...  1.76 us
  transfers between devices with their start and end apart: 26, of which 13 were waited for; matrix products, arithmetic and copies ran while one was open for 0% of the time, Pallas kernels for 20%

profile of v10, /device:TPU:0, one launch (start us, length us, event | category | flops | bytes accessed | tf_op | source)
XLA Modules:
  0.0 77.5 jit_solution(12290543967920076504)
XLA Ops:
  0.6 0.9 %bitcast_convert_fusion.refs_0_ = bf16[64,640]{1,0:T(8,128)(2,1)S(1)} fusion(f32[640,64]{0,1:T(8,128)} %param.6), kind=kLoop, calls=%fused_computation.9 | loop fusion | flops 40960 | bytes 245760 | tf_op jit(solution)/shard_map/convert_element_type | solution.py:340
  1.6 4.1 %collective-permute-start = (bf16[64,640]{1,0:T(8,128)(2,1)S(1)}, bf16[64,640]{1,0:T(8,128)(2,1)S(1)}, u32[]{:S(2)}, u32[]{:S(2)}) collective-permute-start(bf16[64,640]{1,0:T(8,128)(2,1)S(1)} %bitcast_convert_fusion.refs_0_), channel_id=1, source_target_pairs={{0,8},{1,9},{2,10},{3,11},{4,12},{5,13},{6,14},{7,15},{8,0},{9,1},... | collective-permute-start | bytes 245768 | tf_op jit(solution)/shard_map/ppermute | solution.py:330
  5.7 3.5 %load_batch.1 = (bf16[1024,4096]{1,0:T(8,128)(2,1)S(1)}, f32[64,1024]{1,0:T(8,128)S(1)}, s32[16,4]{1,0:T(8,128)S(4)}) custom-call(s32[1]{0:T(128)} %bitcast.pos_ref, s32[16,64]{1,0:T(8,128)} %cov.3, bf16[1024,4096]{1,0:T(8,128)(2,1)} %geno.1, f32[64,1024]{1,0:T(8,128)} %bitcast.18), custom_call_target="tpu_custom_call" | custom-call | bytes 8388608 | tf_op jit(solution)/shard_map/load_batch/pallas_call | solution.py:219
  9.2 0.7 collective-permute-done.refs_0_.other_snps
  10.0 2.5 %collective-permute-start.8 = (bf16[2,64,256]{2,1,0:T(8,128)(2,1)S(1)}, bf16[2,64,256]{2,1,0:T(8,128)(2,1)S(1)}, u32[]{:S(2)}, u32[]{:S(2)}) collective-permute-start(bf16[2,64,256]{2,1,0:T(8,128)(2,1)S(1)} %get-tuple-element.83), channel_id=1, source_target_pairs={{0,6},{1,7},{2,4},{3,5},{4,2},{5,3},{6,0},{7,1},{8,14},{9,15},{10,... | collective-permute-start | bytes 196616 | tf_op jit(solution)/shard_map/ppermute | solution.py:330
  12.5 0.7 collective-permute-start.7
  14.2 2.5 %collective-permute-start.4 = (bf16[2,64,256]{2,1,0:T(8,128)(2,1)S(1)}, bf16[2,64,256]{2,1,0:T(8,128)(2,1)S(1)}, u32[]{:S(2)}, u32[]{:S(2)}) collective-permute-start(bf16[2,64,256]{2,1,0:T(8,128)(2,1)S(1)} %get-tuple-element.80), channel_id=1, source_target_pairs={{0,6},{1,7},{2,4},{3,5},{4,2},{5,3},{6,0},{7,1},{8,14},{9,15},{10,... | collective-permute-start | bytes 196616 | tf_op jit(solution)/shard_map/ppermute | solution.py:330
  16.7 0.7 collective-permute-start.3
  20.3 0.7 collective-permute-done.3.packet.refs_1_
  21.5 0.8 %collective-permute-done.2.packet.refs_1_ = bf16[2,64,256]{2,1,0:T(8,128)(2,1)S(1)} collective-permute-done((bf16[2,64,256]{2,1,0:T(8,128)(2,1)S(1)}, bf16[2,64,256]{2,1,0:T(8,128)(2,1)S(1)}, u32[]{:S(2)}, u32[]{:S(2)}) %collective-permute-start.2) | collective-permute-done | bytes 65568 | tf_op jit(solution)/shard_map/ppermute | solution.py:330
  23.2 0.6 mate_terms.11
  23.8 1.3 %collective-permute-start.11 = (bf16[4,64,256]{2,1,0:T(8,128)(2,1)S(1)}, bf16[4,64,256]{2,1,0:T(8,128)(2,1)S(1)}, u32[]{:S(2)}, u32[]{:S(2)}) collective-permute-start(bf16[4,64,256]{2,1,0:T(8,128)(2,1)S(1)} %mate_terms.11), channel_id=1, source_target_pairs={{0,6},{1,7},{2,4},{3,5},{4,2},{5,3},{6,0},{7,1},{8,14},{9,15},{10,... | collective-permute-start | bytes 393224 | tf_op jit(solution)/shard_map/ppermute | solution.py:330
  26.9 1.8 %collective-permute-start.9 = (bf16[4,64,256]{2,1,0:T(8,128)(2,1)S(1)}, bf16[4,64,256]{2,1,0:T(8,128)(2,1)S(1)}, u32[]{:S(2)}, u32[]{:S(2)}) collective-permute-start(bf16[4,64,256]{2,1,0:T(8,128)(2,1)S(1)} %mate_terms.9), channel_id=1, source_target_pairs={{0,2},{1,3},{2,0},{3,1},{4,6},{5,7},{6,4},{7,5},{8,10},{9,11},{10,... | collective-permute-start | bytes 393224 | tf_op jit(solution)/shard_map/ppermute | solution.py:330
  29.4 0.8 %collective-permute-done.11.refs_3_ = bf16[4,64,256]{2,1,0:T(8,128)(2,1)S(1)} collective-permute-done((bf16[4,64,256]{2,1,0:T(8,128)(2,1)S(1)}, bf16[4,64,256]{2,1,0:T(8,128)(2,1)S(1)}, u32[]{:S(2)}, u32[]{:S(2)}) %collective-permute-start.11) | collective-permute-done | bytes 131104 | tf_op jit(solution)/shard_map/ppermute | solution.py:330
  30.8 1.4 %collective-permute-done.9.refs_1_ = bf16[4,64,256]{2,1,0:T(8,128)(2,1)S(1)} collective-permute-done((bf16[4,64,256]{2,1,0:T(8,128)(2,1)S(1)}, bf16[4,64,256]{2,1,0:T(8,128)(2,1)S(1)}, u32[]{:S(2)}, u32[]{:S(2)}) %collective-permute-start.9) | collective-permute-done | bytes 131104 | tf_op jit(solution)/shard_map/ppermute | solution.py:330
  33.0 1.4 %collective-permute-done.12.arrived = bf16[2,64,640]{2,1,0:T(8,128)(2,1)S(1)} collective-permute-done((bf16[2,64,640]{2,1,0:T(8,128)(2,1)S(1)}, bf16[2,64,640]{2,1,0:T(8,128)(2,1)S(1)}, u32[]{:S(2)}, u32[]{:S(2)}) %collective-permute-start.12) | collective-permute-done | bytes 163872 | tf_op jit(solution)/shard_map/ppermute | solution.py:330
  34.4 2.3 %collective-permute-start.13 = (bf16[2,64,640]{2,1,0:T(8,128)(2,1)S(1)}, bf16[2,64,640]{2,1,0:T(8,128)(2,1)S(1)}, u32[]{:S(2)}, u32[]{:S(2)}) collective-permute-start(bf16[2,64,640]{2,1,0:T(8,128)(2,1)S(1)} %get-tuple-element.110), channel_id=1, source_target_pairs={{0,8},{1,9},{2,10},{3,11},{4,12},{5,13},{6,14},{7,15},{8,0},{9,1},... | collective-permute-start | bytes 491528 | tf_op jit(solution)/shard_map/ppermute | solution.py:330
  36.9 8.3 %collective-permute-done.13.arrived = bf16[2,64,640]{2,1,0:T(8,128)(2,1)S(1)} collective-permute-done((bf16[2,64,640]{2,1,0:T(8,128)(2,1)S(1)}, bf16[2,64,640]{2,1,0:T(8,128)(2,1)S(1)}, u32[]{:S(2)}, u32[]{:S(2)}) %collective-permute-start.13) | collective-permute-done | bytes 163872 | tf_op jit(solution)/shard_map/ppermute | solution.py:330
  45.5 1.0 %collective-permute-start.20 = (bf16[2,64,256]{2,1,0:T(8,128)(2,1)S(1)}, bf16[2,64,256]{2,1,0:T(8,128)(2,1)S(1)}, u32[]{:S(2)}, u32[]{:S(2)}) collective-permute-start(bf16[2,64,256]{2,1,0:T(8,128)(2,1)S(1)} %get-tuple-element.119), channel_id=1, source_target_pairs={{0,6},{1,7},{2,4},{3,5},{4,2},{5,3},{6,0},{7,1},{8,14},{9,15},{10,... | collective-permute-start | bytes 196616 | tf_op jit(solution)/shard_map/ppermute | solution.py:330
  46.5 2.0 %collective-permute-start.19 = (bf16[2,64,256]{2,1,0:T(8,128)(2,1)S(1)}, bf16[2,64,256]{2,1,0:T(8,128)(2,1)S(1)}, u32[]{:S(2)}, u32[]{:S(2)}) collective-permute-start(bf16[2,64,256]{2,1,0:T(8,128)(2,1)S(1)} %get-tuple-element.118), channel_id=1, source_target_pairs={{0,4},{1,5},{2,6},{3,7},{4,0},{5,1},{6,2},{7,3},{8,12},{9,13},{10,... | collective-permute-start | bytes 196616 | tf_op jit(solution)/shard_map/ppermute | solution.py:330
  49.7 1.0 %collective-permute-start.17 = (bf16[2,64,256]{2,1,0:T(8,128)(2,1)S(1)}, bf16[2,64,256]{2,1,0:T(8,128)(2,1)S(1)}, u32[]{:S(2)}, u32[]{:S(2)}) collective-permute-start(bf16[2,64,256]{2,1,0:T(8,128)(2,1)S(1)} %get-tuple-element.116), channel_id=1, source_target_pairs={{0,6},{1,7},{2,4},{3,5},{4,2},{5,3},{6,0},{7,1},{8,14},{9,15},{10,... | collective-permute-start | bytes 196616 | tf_op jit(solution)/shard_map/ppermute | solution.py:330
  50.7 2.0 %collective-permute-start.16 = (bf16[2,64,256]{2,1,0:T(8,128)(2,1)S(1)}, bf16[2,64,256]{2,1,0:T(8,128)(2,1)S(1)}, u32[]{:S(2)}, u32[]{:S(2)}) collective-permute-start(bf16[2,64,256]{2,1,0:T(8,128)(2,1)S(1)} %get-tuple-element.115), channel_id=1, source_target_pairs={{0,4},{1,5},{2,6},{3,7},{4,0},{5,1},{6,2},{7,3},{8,12},{9,13},{10,... | collective-permute-start | bytes 196616 | tf_op jit(solution)/shard_map/ppermute | solution.py:330
  56.2 1.3 %collective-permute-done.15.packet.refs_1_ = bf16[2,64,256]{2,1,0:T(8,128)(2,1)S(1)} collective-permute-done((bf16[2,64,256]{2,1,0:T(8,128)(2,1)S(1)}, bf16[2,64,256]{2,1,0:T(8,128)(2,1)S(1)}, u32[]{:S(2)}, u32[]{:S(2)}) %collective-permute-start.15) | collective-permute-done | bytes 65568 | tf_op jit(solution)/shard_map/ppermute | solution.py:330
  58.4 0.6 mate_terms.15
  60.0 1.7 %collective-permute-start.22 = (bf16[4,64,256]{2,1,0:T(8,128)(2,1)S(1)}, bf16[4,64,256]{2,1,0:T(8,128)(2,1)S(1)}, u32[]{:S(2)}, u32[]{:S(2)}) collective-permute-start(bf16[4,64,256]{2,1,0:T(8,128)(2,1)S(1)} %mate_terms.14), channel_id=1, source_target_pairs={{0,4},{1,5},{2,6},{3,7},{4,0},{5,1},{6,2},{7,3},{8,12},{9,13},{10,... | collective-permute-start | bytes 393224 | tf_op jit(solution)/shard_map/ppermute | solution.py:330
  62.4 1.6 %collective-permute-start.21 = (bf16[4,64,256]{2,1,0:T(8,128)(2,1)S(1)}, bf16[4,64,256]{2,1,0:T(8,128)(2,1)S(1)}, u32[]{:S(2)}, u32[]{:S(2)}) collective-permute-start(bf16[4,64,256]{2,1,0:T(8,128)(2,1)S(1)} %mate_terms.13), channel_id=1, source_target_pairs={{0,2},{1,3},{2,0},{3,1},{4,6},{5,7},{6,4},{7,5},{8,10},{9,11},{10,... | collective-permute-start | bytes 393224 | tf_op jit(solution)/shard_map/ppermute | solution.py:330
  63.9 0.9 %sample_update.4 = (f32[64,1024]{1,0:T(8,128)}, f32[8,128]{1,0:T(8,128)S(1)}) custom-call(f32[64,1024]{1,0:T(8,128)S(1)} %get-tuple-element.102.samples, f32[64,1024]{1,0:T(8,128)S(1)} %get-tuple-element.136.gradient, f32[64,64]{1,0:T(8,128)S(1)} %get-tuple-element.137.gram), custom_call_target="tpu_custom_call" | custom-call | bytes 2097152 | tf_op jit(solution)/shard_map/sample_update/pallas_call | solution.py:307
  66.0 1.4 %collective-permute-done.21.refs_1_ = bf16[4,64,256]{2,1,0:T(8,128)(2,1)S(1)} collective-permute-done((bf16[4,64,256]{2,1,0:T(8,128)(2,1)S(1)}, bf16[4,64,256]{2,1,0:T(8,128)(2,1)S(1)}, u32[]{:S(2)}, u32[]{:S(2)}) %collective-permute-start.21) | collective-permute-done | bytes 131104 | tf_op jit(solution)/shard_map/ppermute | solution.py:330
  68.1 1.4 %collective-permute-done.24 = bf16[2,64,640]{2,1,0:T(8,128)(2,1)S(1)} collective-permute-done((bf16[2,64,640]{2,1,0:T(8,128)(2,1)S(1)}, bf16[2,64,640]{2,1,0:T(8,128)(2,1)S(1)}, u32[]{:S(2)}, u32[]{:S(2)}) %collective-permute-start.24) | collective-permute-done | bytes 163872 | tf_op jit(solution)/shard_map/ppermute | solution.py:330
  69.5 1.9 %collective-permute-start.25 = (bf16[64,640]{1,0:T(8,128)(2,1)S(1)}, bf16[64,640]{1,0:T(8,128)(2,1)S(1)}, u32[]{:S(2)}, u32[]{:S(2)}) collective-permute-start(bf16[64,640]{1,0:T(8,128)(2,1)S(1)} %fusion), channel_id=1, source_target_pairs={{0,8},{1,9},{2,10},{3,11},{4,12},{5,13},{6,14},{7,15},{8,0},{9,1},... | collective-permute-start | bytes 245768 | tf_op jit(solution)/shard_map/ppermute | solution.py:330
  71.4 5.4 %collective-permute-done.25 = bf16[64,640]{1,0:T(8,128)(2,1)S(1)} collective-permute-done((bf16[64,640]{1,0:T(8,128)(2,1)S(1)}, bf16[64,640]{1,0:T(8,128)(2,1)S(1)}, u32[]{:S(2)}, u32[]{:S(2)}) %collective-permute-start.25) | collective-permute-done | bytes 81952 | tf_op jit(solution)/shard_map/ppermute | solution.py:330
  76.8 0.7 fusion.4
  (64 shorter events, 18.4 us)
Async XLA Ops:
  1.6 8.3 %collective-permute-start = (bf16[64,640]{1,0:T(8,128)(2,1)S(1)}, bf16[64,640]{1,0:T(8,128)(2,1)S(1)}, u32[]{:S(2)}, u32[]{:S(2)}) collective-permute-start(bf16[64,640]{1,0:T(8,128)(2,1)S(1)} %bitcast_convert_fusion.refs_0_), channel_id=1, source_target_pairs={{0,8},{1,9},{2,10},{3,11},{4,12},{5,13},{6,14},{7,15},{8,0},{9,1},... | collective-permute-start | bytes 245768 | tf_op jit(solution)/shard_map/ppermute | solution.py:330
  5.7 4.2 %collective-permute-start.5 = (bf16[64,640]{1,0:T(8,128)(2,1)S(1)}, bf16[64,640]{1,0:T(8,128)(2,1)S(1)}, u32[]{:S(2)}, u32[]{:S(2)}) collective-permute-start(bf16[64,640]{1,0:T(8,128)(2,1)S(1)} %bitcast_convert_fusion.refs_0_), channel_id=1, source_target_pairs={{0,1},{1,0},{2,3},{3,2},{4,5},{5,4},{6,7},{7,6},{8,9},{9,8},{10,11... | collective-permute-start | bytes 245768 | tf_op jit(solution)/shard_map/ppermute | solution.py:330
  9.9 4.2 %collective-permute-start.1 = (bf16[64,640]{1,0:T(8,128)(2,1)S(1)}, bf16[64,640]{1,0:T(8,128)(2,1)S(1)}, u32[]{:S(2)}, u32[]{:S(2)}) collective-permute-start(bf16[64,640]{1,0:T(8,128)(2,1)S(1)} %collective-permute-done.refs_0_.other_snps), channel_id=1, source_target_pairs={{0,1},{1,0},{2,3},{3,2},{4,5},{5,4},{6,7},{7,6},{8,9},{9,8},{10,11... | collective-permute-start | bytes 245768 | tf_op jit(solution)/shard_map/ppermute | solution.py:330
  10.0 7.9 %collective-permute-start.8 = (bf16[2,64,256]{2,1,0:T(8,128)(2,1)S(1)}, bf16[2,64,256]{2,1,0:T(8,128)(2,1)S(1)}, u32[]{:S(2)}, u32[]{:S(2)}) collective-permute-start(bf16[2,64,256]{2,1,0:T(8,128)(2,1)S(1)} %get-tuple-element.83), channel_id=1, source_target_pairs={{0,6},{1,7},{2,4},{3,5},{4,2},{5,3},{6,0},{7,1},{8,14},{9,15},{10,... | collective-permute-start | bytes 196616 | tf_op jit(solution)/shard_map/ppermute | solution.py:330
  12.5 6.3 %collective-permute-start.7 = (bf16[2,64,256]{2,1,0:T(8,128)(2,1)S(1)}, bf16[2,64,256]{2,1,0:T(8,128)(2,1)S(1)}, u32[]{:S(2)}, u32[]{:S(2)}) collective-permute-start(bf16[2,64,256]{2,1,0:T(8,128)(2,1)S(1)} %get-tuple-element.82), channel_id=1, source_target_pairs={{0,4},{1,5},{2,6},{3,7},{4,0},{5,1},{6,2},{7,3},{8,12},{9,13},{10,... | collective-permute-start | bytes 196616 | tf_op jit(solution)/shard_map/ppermute | solution.py:330
  13.3 6.0 %collective-permute-start.6 = (bf16[2,64,256]{2,1,0:T(8,128)(2,1)S(1)}, bf16[2,64,256]{2,1,0:T(8,128)(2,1)S(1)}, u32[]{:S(2)}, u32[]{:S(2)}) collective-permute-start(bf16[2,64,256]{2,1,0:T(8,128)(2,1)S(1)} %get-tuple-element.81), channel_id=1, source_target_pairs={{0,2},{1,3},{2,0},{3,1},{4,6},{5,7},{6,4},{7,5},{8,10},{9,11},{10,... | collective-permute-start | bytes 196616 | tf_op jit(solution)/shard_map/ppermute | solution.py:330
  14.2 5.5 %collective-permute-start.4 = (bf16[2,64,256]{2,1,0:T(8,128)(2,1)S(1)}, bf16[2,64,256]{2,1,0:T(8,128)(2,1)S(1)}, u32[]{:S(2)}, u32[]{:S(2)}) collective-permute-start(bf16[2,64,256]{2,1,0:T(8,128)(2,1)S(1)} %get-tuple-element.80), channel_id=1, source_target_pairs={{0,6},{1,7},{2,4},{3,5},{4,2},{5,3},{6,0},{7,1},{8,14},{9,15},{10,... | collective-permute-start | bytes 196616 | tf_op jit(solution)/shard_map/ppermute | solution.py:330
  16.7 4.3 %collective-permute-start.3 = (bf16[2,64,256]{2,1,0:T(8,128)(2,1)S(1)}, bf16[2,64,256]{2,1,0:T(8,128)(2,1)S(1)}, u32[]{:S(2)}, u32[]{:S(2)}) collective-permute-start(bf16[2,64,256]{2,1,0:T(8,128)(2,1)S(1)} %get-tuple-element.79), channel_id=1, source_target_pairs={{0,4},{1,5},{2,6},{3,7},{4,0},{5,1},{6,2},{7,3},{8,12},{9,13},{10,... | collective-permute-start | bytes 196616 | tf_op jit(solution)/shard_map/ppermute | solution.py:330
  18.0 4.3 %collective-permute-start.2 = (bf16[2,64,256]{2,1,0:T(8,128)(2,1)S(1)}, bf16[2,64,256]{2,1,0:T(8,128)(2,1)S(1)}, u32[]{:S(2)}, u32[]{:S(2)}) collective-permute-start(bf16[2,64,256]{2,1,0:T(8,128)(2,1)S(1)} %get-tuple-element.78), channel_id=1, source_target_pairs={{0,2},{1,3},{2,0},{3,1},{4,6},{5,7},{6,4},{7,5},{8,10},{9,11},{10,... | collective-permute-start | bytes 196616 | tf_op jit(solution)/shard_map/ppermute | solution.py:330
  23.8 6.4 %collective-permute-start.11 = (bf16[4,64,256]{2,1,0:T(8,128)(2,1)S(1)}, bf16[4,64,256]{2,1,0:T(8,128)(2,1)S(1)}, u32[]{:S(2)}, u32[]{:S(2)}) collective-permute-start(bf16[4,64,256]{2,1,0:T(8,128)(2,1)S(1)} %mate_terms.11), channel_id=1, source_target_pairs={{0,6},{1,7},{2,4},{3,5},{4,2},{5,3},{6,0},{7,1},{8,14},{9,15},{10,... | collective-permute-start | bytes 393224 | tf_op jit(solution)/shard_map/ppermute | solution.py:330
  25.7 11.0 %copy-start.1 = (s32[16,64]{1,0:T(8,128)S(1)}, s32[16,64]{1,0:T(8,128)}, u32[]{:S(2)}) copy-start(s32[16,64]{1,0:T(8,128)} %cov.3) | copy-start | bytes 12292
  25.7 19.4 %copy-start = (f32[640,64]{0,1:T(8,128)S(1)}, f32[640,64]{0,1:T(8,128)}, u32[]{:S(2)}) copy-start(f32[640,64]{0,1:T(8,128)} %param.6) | copy-start | bytes 491524
  25.7 5.1 %collective-permute-start.10 = (bf16[4,64,256]{2,1,0:T(8,128)(2,1)S(1)}, bf16[4,64,256]{2,1,0:T(8,128)(2,1)S(1)}, u32[]{:S(2)}, u32[]{:S(2)}) collective-permute-start(bf16[4,64,256]{2,1,0:T(8,128)(2,1)S(1)} %mate_terms.10), channel_id=1, source_target_pairs={{0,4},{1,5},{2,6},{3,7},{4,0},{5,1},{6,2},{7,3},{8,12},{9,13},{10,... | collective-permute-start | bytes 393224 | tf_op jit(solution)/shard_map/ppermute | solution.py:330
  26.9 5.3 %collective-permute-start.9 = (bf16[4,64,256]{2,1,0:T(8,128)(2,1)S(1)}, bf16[4,64,256]{2,1,0:T(8,128)(2,1)S(1)}, u32[]{:S(2)}, u32[]{:S(2)}) collective-permute-start(bf16[4,64,256]{2,1,0:T(8,128)(2,1)S(1)} %mate_terms.9), channel_id=1, source_target_pairs={{0,2},{1,3},{2,0},{3,1},{4,6},{5,7},{6,4},{7,5},{8,10},{9,11},{10,... | collective-permute-start | bytes 393224 | tf_op jit(solution)/shard_map/ppermute | solution.py:330
  32.9 1.5 %collective-permute-start.12 = (bf16[2,64,640]{2,1,0:T(8,128)(2,1)S(1)}, bf16[2,64,640]{2,1,0:T(8,128)(2,1)S(1)}, u32[]{:S(2)}, u32[]{:S(2)}) collective-permute-start(bf16[2,64,640]{2,1,0:T(8,128)(2,1)S(1)} %get-tuple-element.107), channel_id=1, source_target_pairs={{0,1},{1,0},{2,3},{3,2},{4,5},{5,4},{6,7},{7,6},{8,9},{9,8},{10,11... | collective-permute-start | bytes 491528 | tf_op jit(solution)/shard_map/ppermute | solution.py:330
  34.4 10.7 %collective-permute-start.13 = (bf16[2,64,640]{2,1,0:T(8,128)(2,1)S(1)}, bf16[2,64,640]{2,1,0:T(8,128)(2,1)S(1)}, u32[]{:S(2)}, u32[]{:S(2)}) collective-permute-start(bf16[2,64,640]{2,1,0:T(8,128)(2,1)S(1)} %get-tuple-element.110), channel_id=1, source_target_pairs={{0,8},{1,9},{2,10},{3,11},{4,12},{5,13},{6,14},{7,15},{8,0},{9,1},... | collective-permute-start | bytes 491528 | tf_op jit(solution)/shard_map/ppermute | solution.py:330
  45.2 4.3 %collective-permute-start.14 = (bf16[2,64,640]{2,1,0:T(8,128)(2,1)S(1)}, bf16[2,64,640]{2,1,0:T(8,128)(2,1)S(1)}, u32[]{:S(2)}, u32[]{:S(2)}) collective-permute-start(bf16[2,64,640]{2,1,0:T(8,128)(2,1)S(1)} %get-tuple-element.113.refs_0_), channel_id=1, source_target_pairs={{0,1},{1,0},{2,3},{3,2},{4,5},{5,4},{6,7},{7,6},{8,9},{9,8},{10,11... | collective-permute-start | bytes 491528 | tf_op jit(solution)/shard_map/ppermute | solution.py:330
  45.5 7.7 %collective-permute-start.20 = (bf16[2,64,256]{2,1,0:T(8,128)(2,1)S(1)}, bf16[2,64,256]{2,1,0:T(8,128)(2,1)S(1)}, u32[]{:S(2)}, u32[]{:S(2)}) collective-permute-start(bf16[2,64,256]{2,1,0:T(8,128)(2,1)S(1)} %get-tuple-element.119), channel_id=1, source_target_pairs={{0,6},{1,7},{2,4},{3,5},{4,2},{5,3},{6,0},{7,1},{8,14},{9,15},{10,... | collective-permute-start | bytes 196616 | tf_op jit(solution)/shard_map/ppermute | solution.py:330
  46.5 7.8 %collective-permute-start.19 = (bf16[2,64,256]{2,1,0:T(8,128)(2,1)S(1)}, bf16[2,64,256]{2,1,0:T(8,128)(2,1)S(1)}, u32[]{:S(2)}, u32[]{:S(2)}) collective-permute-start(bf16[2,64,256]{2,1,0:T(8,128)(2,1)S(1)} %get-tuple-element.118), channel_id=1, source_target_pairs={{0,4},{1,5},{2,6},{3,7},{4,0},{5,1},{6,2},{7,3},{8,12},{9,13},{10,... | collective-permute-start | bytes 196616 | tf_op jit(solution)/shard_map/ppermute | solution.py:330
  48.5 6.3 %collective-permute-start.18 = (bf16[2,64,256]{2,1,0:T(8,128)(2,1)S(1)}, bf16[2,64,256]{2,1,0:T(8,128)(2,1)S(1)}, u32[]{:S(2)}, u32[]{:S(2)}) collective-permute-start(bf16[2,64,256]{2,1,0:T(8,128)(2,1)S(1)} %get-tuple-element.117), channel_id=1, source_target_pairs={{0,2},{1,3},{2,0},{3,1},{4,6},{5,7},{6,4},{7,5},{8,10},{9,11},{10,... | collective-permute-start | bytes 196616 | tf_op jit(solution)/shard_map/ppermute | solution.py:330
  49.7 5.5 %collective-permute-start.17 = (bf16[2,64,256]{2,1,0:T(8,128)(2,1)S(1)}, bf16[2,64,256]{2,1,0:T(8,128)(2,1)S(1)}, u32[]{:S(2)}, u32[]{:S(2)}) collective-permute-start(bf16[2,64,256]{2,1,0:T(8,128)(2,1)S(1)} %get-tuple-element.116), channel_id=1, source_target_pairs={{0,6},{1,7},{2,4},{3,5},{4,2},{5,3},{6,0},{7,1},{8,14},{9,15},{10,... | collective-permute-start | bytes 196616 | tf_op jit(solution)/shard_map/ppermute | solution.py:330
  50.7 5.0 %collective-permute-start.16 = (bf16[2,64,256]{2,1,0:T(8,128)(2,1)S(1)}, bf16[2,64,256]{2,1,0:T(8,128)(2,1)S(1)}, u32[]{:S(2)}, u32[]{:S(2)}) collective-permute-start(bf16[2,64,256]{2,1,0:T(8,128)(2,1)S(1)} %get-tuple-element.115), channel_id=1, source_target_pairs={{0,4},{1,5},{2,6},{3,7},{4,0},{5,1},{6,2},{7,3},{8,12},{9,13},{10,... | collective-permute-start | bytes 196616 | tf_op jit(solution)/shard_map/ppermute | solution.py:330
  53.2 4.3 %collective-permute-start.15 = (bf16[2,64,256]{2,1,0:T(8,128)(2,1)S(1)}, bf16[2,64,256]{2,1,0:T(8,128)(2,1)S(1)}, u32[]{:S(2)}, u32[]{:S(2)}) collective-permute-start(bf16[2,64,256]{2,1,0:T(8,128)(2,1)S(1)} %get-tuple-element.114), channel_id=1, source_target_pairs={{0,2},{1,3},{2,0},{3,1},{4,6},{5,7},{6,4},{7,5},{8,10},{9,11},{10,... | collective-permute-start | bytes 196616 | tf_op jit(solution)/shard_map/ppermute | solution.py:330
  59.0 6.5 %collective-permute-start.23 = (bf16[4,64,256]{2,1,0:T(8,128)(2,1)S(1)}, bf16[4,64,256]{2,1,0:T(8,128)(2,1)S(1)}, u32[]{:S(2)}, u32[]{:S(2)}) collective-permute-start(bf16[4,64,256]{2,1,0:T(8,128)(2,1)S(1)} %mate_terms.15), channel_id=1, source_target_pairs={{0,6},{1,7},{2,4},{3,5},{4,2},{5,3},{6,0},{7,1},{8,14},{9,15},{10,... | collective-permute-start | bytes 393224 | tf_op jit(solution)/shard_map/ppermute | solution.py:330
  60.0 5.9 %collective-permute-start.22 = (bf16[4,64,256]{2,1,0:T(8,128)(2,1)S(1)}, bf16[4,64,256]{2,1,0:T(8,128)(2,1)S(1)}, u32[]{:S(2)}, u32[]{:S(2)}) collective-permute-start(bf16[4,64,256]{2,1,0:T(8,128)(2,1)S(1)} %mate_terms.14), channel_id=1, source_target_pairs={{0,4},{1,5},{2,6},{3,7},{4,0},{5,1},{6,2},{7,3},{8,12},{9,13},{10,... | collective-permute-start | bytes 393224 | tf_op jit(solution)/shard_map/ppermute | solution.py:330
  62.4 5.0 %collective-permute-start.21 = (bf16[4,64,256]{2,1,0:T(8,128)(2,1)S(1)}, bf16[4,64,256]{2,1,0:T(8,128)(2,1)S(1)}, u32[]{:S(2)}, u32[]{:S(2)}) collective-permute-start(bf16[4,64,256]{2,1,0:T(8,128)(2,1)S(1)} %mate_terms.13), channel_id=1, source_target_pairs={{0,2},{1,3},{2,0},{3,1},{4,6},{5,7},{6,4},{7,5},{8,10},{9,11},{10,... | collective-permute-start | bytes 393224 | tf_op jit(solution)/shard_map/ppermute | solution.py:330
  68.1 1.5 %collective-permute-start.24 = (bf16[2,64,640]{2,1,0:T(8,128)(2,1)S(1)}, bf16[2,64,640]{2,1,0:T(8,128)(2,1)S(1)}, u32[]{:S(2)}, u32[]{:S(2)}) collective-permute-start(bf16[2,64,640]{2,1,0:T(8,128)(2,1)S(1)} %get-tuple-element.144), channel_id=1, source_target_pairs={{0,1},{1,0},{2,3},{3,2},{4,5},{5,4},{6,7},{7,6},{8,9},{9,8},{10,11... | collective-permute-start | bytes 491528 | tf_op jit(solution)/shard_map/ppermute | solution.py:330
  69.5 7.2 %collective-permute-start.25 = (bf16[64,640]{1,0:T(8,128)(2,1)S(1)}, bf16[64,640]{1,0:T(8,128)(2,1)S(1)}, u32[]{:S(2)}, u32[]{:S(2)}) collective-permute-start(bf16[64,640]{1,0:T(8,128)(2,1)S(1)} %fusion), channel_id=1, source_target_pairs={{0,8},{1,9},{2,10},{3,11},{4,12},{5,13},{6,14},{7,15},{8,0},{9,1},... | collective-permute-start | bytes 245768 | tf_op jit(solution)/shard_map/ppermute | solution.py:330

commit v11 on v10

--- a/solution.py
+++ b/solution.py
@@ -88,31 +88,27 @@
                 packets[m][i, :, 128 * q:128 * (q + 1)] = pair.astype(jnp.bfloat16)
 
 
-def mates_sum_kernel(turns, per_owner, own_blocks, table, *refs):
-    terms, sums, total = refs[:len(MATES)], refs[-2 - turns // 2:-1], refs[-1]
+def mates_sum_kernel(turns, group, per_owner, own_blocks, table, *refs):
+    terms, sums, total = refs[:len(MATES)], refs[-2], refs[-1]
     low = low_half(terms[0].shape[1])
     total[...] = jnp.zeros_like(total)
-    for t in range(turns):
+    for i, t in enumerate(group):
         for m in range(len(MATES)):
             for q in range(per_owner // 2):
                 first, second = table[m * turns + t, 2 * q], table[m * turns + t, 2 * q + 1]
                 pair = terms[m][t, :, 128 * q:128 * (q + 1)].astype(jnp.float32)
-                total[t, first] += jnp.where(low, pair, 0.0)
-                total[t, second] += jnp.where(low, 0.0, pair)
-    for t in range(turns):
+                total[i, first] += jnp.where(low, pair, 0.0)
+                total[i, second] += jnp.where(low, 0.0, pair)
+    for i in range(len(group)):
         for j in range(own_blocks // 2):
-            first, second = total[t, 2 * j], total[t, 2 * j + 1]
+            first, second = total[i, 2 * j], total[i, 2 * j + 1]
             both = jnp.where(low, first, second) + pltpu.roll(jnp.where(low, second, first), 64, 1)
-            columns = slice(128 * j, 128 * (j + 1))
-            if t % 2:
-                sums[-1][t // 2, :, columns] = both.astype(jnp.bfloat16)
-            else:
-                sums[t // 2][:, columns] = both
-
-
-def add_kernel(own, other, arrived, own_sum, other_sum, swapped):
-    own_sum[...] = own[...] + arrived[0].astype(jnp.float32)
-    other_sum[...] = other[...] + arrived[1].astype(jnp.float32)
+            sums[i, :, 128 * j:128 * (j + 1)] = both.astype(sums.dtype)
+
+
+def add_kernel(sums, arrived, own_sum, other_sum, swapped):
+    own_sum[...] = sums[0] + arrived[0].astype(jnp.float32)
+    other_sum[...] = sums[1] + arrived[1].astype(jnp.float32)
     swapped[0] = other_sum[...].astype(jnp.bfloat16)
     swapped[1] = own_sum[...].astype(jnp.bfloat16)
 
@@ -260,24 +256,23 @@
             name="pick_blocks",
         )(table, *arrays)
 
-    def mates_sum(terms, after):
-        *sums, for_core = pl.pallas_call(
-            functools.partial(mates_sum_kernel, len(turns), per_owner, own_blocks),
-            out_shape=(by_snps,) * highs + (jax.ShapeDtypeStruct((highs, rank, own_snps), jnp.bfloat16),),
+    def mates_sum(terms, group, dtype, after):
+        return pl.pallas_call(
+            functools.partial(mates_sum_kernel, len(turns), group, per_owner, own_blocks),
+            out_shape=jax.ShapeDtypeStruct((len(group), rank, own_snps), dtype),
             in_specs=[smem] + [vmem] * len(MATES) + [anywhere] * len(after),
-            out_specs=(vmem,) * (highs + 1),
-            scratch_shapes=[dense_blocks],
+            out_specs=vmem,
+            scratch_shapes=[pltpu.VMEM((len(group), own_blocks, rank, 128), jnp.float32)],
             compiler_params=params,
             cost_estimate=small,
             name="mates_sum",
         )(table, *terms, *after)
-        return sums, for_core
 
     two_snps = jax.ShapeDtypeStruct((2, rank, own_snps), jnp.bfloat16)
     add_core = pl.pallas_call(
         add_kernel,
         out_shape=(by_snps, by_snps, two_snps),
-        in_specs=[vmem] * 3,
+        in_specs=[vmem] * 2,
         out_specs=(vmem,) * 3,
         compiler_params=params,
         name="add_core",
@@ -371,21 +366,20 @@
                 samples, *partial, (by_samples, jax.ShapeDtypeStruct((8, 128), jnp.float32))
             )
             after = [token]
-        sums, for_core = mates_sum(
-            [
-                to_mate(terms_for(mate, *current, groups, [x[m] for x in panels]), mate)
-                for m, mate in enumerate(MATES)
-            ],
-            after,
-        )
+        sent = [
+            to_mate(terms_for(mate, *current, groups, [x[m] for x in panels]), mate)
+            for m, mate in enumerate(MATES)
+        ]
+        for_core = mates_sum(sent, list(range(1, len(turns), 2)), jnp.bfloat16, after)
         arrived = swap(for_core, 1)
+        sums = mates_sum(sent, list(range(0, len(turns), 2)), jnp.float32, [for_core])
         if pairwise and not last:
-            own_sum, other_sum, swapped = add_core(*sums, arrived)
+            own_sum, other_sum, swapped = add_core(sums, arrived)
             snps, held = owners_update(
                 own_sum, other_sum, swap(swapped, REST), *snp_steps, snps, held[1]
             )
             continue
-        sums = [x + arrived[high].astype(jnp.float32) for high, x in enumerate(sums)]
+        sums = [sums[high] + arrived[high].astype(jnp.float32) for high in range(highs)]
         for high in range(highs - 1, 0, -1):
             bit = high & -high
             sums[high ^ bit] += swap(sums[high].astype(jnp.bfloat16), bit * REST).astype(jnp.float32)

time: 77.7 us -> 77.1 us (level)
  transfers between devices with their start and end apart: 26 -> 26, of which waited for: 13 -> 13; matrix products, arithmetic and copies ran while one was open for 0% -> 0% of each run, Pallas kernels for 20% -> 21%
where the time goes in v11:
time: 77.1 us; the launch traced here: 76.9 us
  starting transfers between devices  30.2 us (39%)
  waiting for transfers between devices  24.1 us (31%)
  Pallas kernels  19.9 us (26%)
  other arithmetic  1.65 us (2%)
  between operations  0.98 us (1%)
    ppermute x26, starting transfers between devices, swap(): return lax.ppermute(x, 'rows', [(r, r ^ turn) for r in range(devices)])  30.2 us
    ppermute x26, waiting for transfers between devices, swap(): return lax.ppermute(x, 'rows', [(r, r ^ turn) for r in range(devices)])  24.1 us
    pallas_call x16, Pallas kernels, product(): pl.pallas_call(functools.partial(product_kernel, [turns[t] for t in group...  7.42 us
    pallas_call x8, Pallas kernels, terms_for(): pl.pallas_call(functools.partial(term_kernel, turns, groups, mate), out_s...  4.91 us
    pallas_call x1, Pallas kernels, on_device(): pl.pallas_call(functools.partial(load_kernel, turns, per_owner, own_block...  3.51 us
    pallas_call x3, Pallas kernels, sample_update(): pl.pallas_call(functools.partial(sample_kernel, sample_step), out_shape=o...  1.76 us
  transfers between devices with their start and end apart: 26, of which 13 were waited for; matrix products, arithmetic and copies ran while one was open for 0% of the time, Pallas kernels for 21%

profile of v11, /device:TPU:0, one launch (start us, length us, event | category | flops | bytes accessed | tf_op | source)
XLA Modules:
  0.0 76.9 jit_solution(10338564217970113966)
XLA Ops:
  0.6 0.9 %bitcast_convert_fusion.refs_0_ = bf16[64,640]{1,0:T(8,128)(2,1)S(1)} fusion(f32[640,64]{0,1:T(8,128)} %param.6), kind=kLoop, calls=%fused_computation.9 | loop fusion | flops 40960 | bytes 245760 | tf_op jit(solution)/shard_map/convert_element_type | solution.py:335
  1.6 4.1 %collective-permute-start = (bf16[64,640]{1,0:T(8,128)(2,1)S(1)}, bf16[64,640]{1,0:T(8,128)(2,1)S(1)}, u32[]{:S(2)}, u32[]{:S(2)}) collective-permute-start(bf16[64,640]{1,0:T(8,128)(2,1)S(1)} %bitcast_convert_fusion.refs_0_), channel_id=1, source_target_pairs={{0,8},{1,9},{2,10},{3,11},{4,12},{5,13},{6,14},{7,15},{8,0},{9,1},... | collective-permute-start | bytes 245768 | tf_op jit(solution)/shard_map/ppermute | solution.py:325
  5.7 3.5 %load_batch.1 = (bf16[1024,4096]{1,0:T(8,128)(2,1)S(1)}, f32[64,1024]{1,0:T(8,128)S(1)}, s32[16,4]{1,0:T(8,128)S(4)}) custom-call(s32[1]{0:T(128)} %bitcast.pos_ref, s32[16,64]{1,0:T(8,128)} %cov.3, bf16[1024,4096]{1,0:T(8,128)(2,1)} %geno.1, f32[64,1024]{1,0:T(8,128)} %bitcast.20), custom_call_target="tpu_custom_call" | custom-call | bytes 8388608 | tf_op jit(solution)/shard_map/load_batch/pallas_call | solution.py:215
  9.2 0.7 collective-permute-done.refs_0_.other_snps
  10.0 2.5 %collective-permute-start.8 = (bf16[2,64,256]{2,1,0:T(8,128)(2,1)S(1)}, bf16[2,64,256]{2,1,0:T(8,128)(2,1)S(1)}, u32[]{:S(2)}, u32[]{:S(2)}) collective-permute-start(bf16[2,64,256]{2,1,0:T(8,128)(2,1)S(1)} %get-tuple-element.77), channel_id=1, source_target_pairs={{0,6},{1,7},{2,4},{3,5},{4,2},{5,3},{6,0},{7,1},{8,14},{9,15},{10,... | collective-permute-start | bytes 196616 | tf_op jit(solution)/shard_map/ppermute | solution.py:325
  12.5 0.7 collective-permute-start.7
  14.2 2.5 %collective-permute-start.4 = (bf16[2,64,256]{2,1,0:T(8,128)(2,1)S(1)}, bf16[2,64,256]{2,1,0:T(8,128)(2,1)S(1)}, u32[]{:S(2)}, u32[]{:S(2)}) collective-permute-start(bf16[2,64,256]{2,1,0:T(8,128)(2,1)S(1)} %get-tuple-element.74), channel_id=1, source_target_pairs={{0,6},{1,7},{2,4},{3,5},{4,2},{5,3},{6,0},{7,1},{8,14},{9,15},{10,... | collective-permute-start | bytes 196616 | tf_op jit(solution)/shard_map/ppermute | solution.py:325
  16.7 0.7 collective-permute-start.3
  20.3 0.7 collective-permute-done.3.packet.refs_1_
  21.5 0.8 %collective-permute-done.2.packet.refs_1_ = bf16[2,64,256]{2,1,0:T(8,128)(2,1)S(1)} collective-permute-done((bf16[2,64,256]{2,1,0:T(8,128)(2,1)S(1)}, bf16[2,64,256]{2,1,0:T(8,128)(2,1)S(1)}, u32[]{:S(2)}, u32[]{:S(2)}) %collective-permute-start.2) | collective-permute-done | bytes 65568 | tf_op jit(solution)/shard_map/ppermute | solution.py:325
  23.2 0.6 mate_terms.11
  23.8 1.3 %collective-permute-start.11 = (bf16[4,64,256]{2,1,0:T(8,128)(2,1)S(1)}, bf16[4,64,256]{2,1,0:T(8,128)(2,1)S(1)}, u32[]{:S(2)}, u32[]{:S(2)}) collective-permute-start(bf16[4,64,256]{2,1,0:T(8,128)(2,1)S(1)} %mate_terms.11), channel_id=1, source_target_pairs={{0,6},{1,7},{2,4},{3,5},{4,2},{5,3},{6,0},{7,1},{8,14},{9,15},{10,... | collective-permute-start | bytes 393224 | tf_op jit(solution)/shard_map/ppermute | solution.py:325
  26.9 1.8 %collective-permute-start.9 = (bf16[4,64,256]{2,1,0:T(8,128)(2,1)S(1)}, bf16[4,64,256]{2,1,0:T(8,128)(2,1)S(1)}, u32[]{:S(2)}, u32[]{:S(2)}) collective-permute-start(bf16[4,64,256]{2,1,0:T(8,128)(2,1)S(1)} %mate_terms.9), channel_id=1, source_target_pairs={{0,2},{1,3},{2,0},{3,1},{4,6},{5,7},{6,4},{7,5},{8,10},{9,11},{10,... | collective-permute-start | bytes 393224 | tf_op jit(solution)/shard_map/ppermute | solution.py:325
  29.4 0.8 %collective-permute-done.11.refs_3_ = bf16[4,64,256]{2,1,0:T(8,128)(2,1)S(1)} collective-permute-done((bf16[4,64,256]{2,1,0:T(8,128)(2,1)S(1)}, bf16[4,64,256]{2,1,0:T(8,128)(2,1)S(1)}, u32[]{:S(2)}, u32[]{:S(2)}) %collective-permute-start.11) | collective-permute-done | bytes 131104 | tf_op jit(solution)/shard_map/ppermute | solution.py:325
  30.8 1.4 %collective-permute-done.9.refs_1_ = bf16[4,64,256]{2,1,0:T(8,128)(2,1)S(1)} collective-permute-done((bf16[4,64,256]{2,1,0:T(8,128)(2,1)S(1)}, bf16[4,64,256]{2,1,0:T(8,128)(2,1)S(1)}, u32[]{:S(2)}, u32[]{:S(2)}) %collective-permute-start.9) | collective-permute-done | bytes 131104 | tf_op jit(solution)/shard_map/ppermute | solution.py:325
  33.0 1.0 %collective-permute-done.12.arrived = bf16[2,64,640]{2,1,0:T(8,128)(2,1)S(1)} collective-permute-done((bf16[2,64,640]{2,1,0:T(8,128)(2,1)S(1)}, bf16[2,64,640]{2,1,0:T(8,128)(2,1)S(1)}, u32[]{:S(2)}, u32[]{:S(2)}) %collective-permute-start.12) | collective-permute-done | bytes 163872 | tf_op jit(solution)/shard_map/ppermute | solution.py:325
  34.1 2.3 %collective-permute-start.13 = (bf16[2,64,640]{2,1,0:T(8,128)(2,1)S(1)}, bf16[2,64,640]{2,1,0:T(8,128)(2,1)S(1)}, u32[]{:S(2)}, u32[]{:S(2)}) collective-permute-start(bf16[2,64,640]{2,1,0:T(8,128)(2,1)S(1)} %get-tuple-element.101), channel_id=1, source_target_pairs={{0,8},{1,9},{2,10},{3,11},{4,12},{5,13},{6,14},{7,15},{8,0},{9,1},... | collective-permute-start | bytes 491528 | tf_op jit(solution)/shard_map/ppermute | solution.py:325
  36.6 8.2 %collective-permute-done.13.arrived = bf16[2,64,640]{2,1,0:T(8,128)(2,1)S(1)} collective-permute-done((bf16[2,64,640]{2,1,0:T(8,128)(2,1)S(1)}, bf16[2,64,640]{2,1,0:T(8,128)(2,1)S(1)}, u32[]{:S(2)}, u32[]{:S(2)}) %collective-permute-start.13) | collective-permute-done | bytes 163872 | tf_op jit(solution)/shard_map/ppermute | solution.py:325
  45.2 1.0 %collective-permute-start.20 = (bf16[2,64,256]{2,1,0:T(8,128)(2,1)S(1)}, bf16[2,64,256]{2,1,0:T(8,128)(2,1)S(1)}, u32[]{:S(2)}, u32[]{:S(2)}) collective-permute-start(bf16[2,64,256]{2,1,0:T(8,128)(2,1)S(1)} %get-tuple-element.110), channel_id=1, source_target_pairs={{0,6},{1,7},{2,4},{3,5},{4,2},{5,3},{6,0},{7,1},{8,14},{9,15},{10,... | collective-permute-start | bytes 196616 | tf_op jit(solution)/shard_map/ppermute | solution.py:325
  46.2 2.0 %collective-permute-start.19 = (bf16[2,64,256]{2,1,0:T(8,128)(2,1)S(1)}, bf16[2,64,256]{2,1,0:T(8,128)(2,1)S(1)}, u32[]{:S(2)}, u32[]{:S(2)}) collective-permute-start(bf16[2,64,256]{2,1,0:T(8,128)(2,1)S(1)} %get-tuple-element.109), channel_id=1, source_target_pairs={{0,4},{1,5},{2,6},{3,7},{4,0},{5,1},{6,2},{7,3},{8,12},{9,13},{10,... | collective-permute-start | bytes 196616 | tf_op jit(solution)/shard_map/ppermute | solution.py:325
  49.4 1.0 %collective-permute-start.17 = (bf16[2,64,256]{2,1,0:T(8,128)(2,1)S(1)}, bf16[2,64,256]{2,1,0:T(8,128)(2,1)S(1)}, u32[]{:S(2)}, u32[]{:S(2)}) collective-permute-start(bf16[2,64,256]{2,1,0:T(8,128)(2,1)S(1)} %get-tuple-element.107), channel_id=1, source_target_pairs={{0,6},{1,7},{2,4},{3,5},{4,2},{5,3},{6,0},{7,1},{8,14},{9,15},{10,... | collective-permute-start | bytes 196616 | tf_op jit(solution)/shard_map/ppermute | solution.py:325
  50.4 2.0 %collective-permute-start.16 = (bf16[2,64,256]{2,1,0:T(8,128)(2,1)S(1)}, bf16[2,64,256]{2,1,0:T(8,128)(2,1)S(1)}, u32[]{:S(2)}, u32[]{:S(2)}) collective-permute-start(bf16[2,64,256]{2,1,0:T(8,128)(2,1)S(1)} %get-tuple-element.106), channel_id=1, source_target_pairs={{0,4},{1,5},{2,6},{3,7},{4,0},{5,1},{6,2},{7,3},{8,12},{9,13},{10,... | collective-permute-start | bytes 196616 | tf_op jit(solution)/shard_map/ppermute | solution.py:325
  55.9 1.3 %collective-permute-done.15.packet.refs_1_ = bf16[2,64,256]{2,1,0:T(8,128)(2,1)S(1)} collective-permute-done((bf16[2,64,256]{2,1,0:T(8,128)(2,1)S(1)}, bf16[2,64,256]{2,1,0:T(8,128)(2,1)S(1)}, u32[]{:S(2)}, u32[]{:S(2)}) %collective-permute-start.15) | collective-permute-done | bytes 65568 | tf_op jit(solution)/shard_map/ppermute | solution.py:325
  58.1 0.6 mate_terms.15
  59.7 1.7 %collective-permute-start.22 = (bf16[4,64,256]{2,1,0:T(8,128)(2,1)S(1)}, bf16[4,64,256]{2,1,0:T(8,128)(2,1)S(1)}, u32[]{:S(2)}, u32[]{:S(2)}) collective-permute-start(bf16[4,64,256]{2,1,0:T(8,128)(2,1)S(1)} %mate_terms.14), channel_id=1, source_target_pairs={{0,4},{1,5},{2,6},{3,7},{4,0},{5,1},{6,2},{7,3},{8,12},{9,13},{10,... | collective-permute-start | bytes 393224 | tf_op jit(solution)/shard_map/ppermute | solution.py:325
  62.1 1.5 %collective-permute-start.21 = (bf16[4,64,256]{2,1,0:T(8,128)(2,1)S(1)}, bf16[4,64,256]{2,1,0:T(8,128)(2,1)S(1)}, u32[]{:S(2)}, u32[]{:S(2)}) collective-permute-start(bf16[4,64,256]{2,1,0:T(8,128)(2,1)S(1)} %mate_terms.13), channel_id=1, source_target_pairs={{0,2},{1,3},{2,0},{3,1},{4,6},{5,7},{6,4},{7,5},{8,10},{9,11},{10,... | collective-permute-start | bytes 393224 | tf_op jit(solution)/shard_map/ppermute | solution.py:325
  63.6 0.9 %sample_update.4 = (f32[64,1024]{1,0:T(8,128)}, f32[8,128]{1,0:T(8,128)S(1)}) custom-call(f32[64,1024]{1,0:T(8,128)S(1)} %get-tuple-element.96.samples, f32[64,1024]{1,0:T(8,128)S(1)} %get-tuple-element.127.gradient, f32[64,64]{1,0:T(8,128)S(1)} %get-tuple-element.128.gram), custom_call_target="tpu_custom_call" | custom-call | bytes 2097152 | tf_op jit(solution)/shard_map/sample_update/pallas_call | solution.py:302
  65.7 1.4 %collective-permute-done.21.refs_1_ = bf16[4,64,256]{2,1,0:T(8,128)(2,1)S(1)} collective-permute-done((bf16[4,64,256]{2,1,0:T(8,128)(2,1)S(1)}, bf16[4,64,256]{2,1,0:T(8,128)(2,1)S(1)}, u32[]{:S(2)}, u32[]{:S(2)}) %collective-permute-start.21) | collective-permute-done | bytes 131104 | tf_op jit(solution)/shard_map/ppermute | solution.py:325
  67.9 1.0 %collective-permute-done.24 = bf16[2,64,640]{2,1,0:T(8,128)(2,1)S(1)} collective-permute-done((bf16[2,64,640]{2,1,0:T(8,128)(2,1)S(1)}, bf16[2,64,640]{2,1,0:T(8,128)(2,1)S(1)}, u32[]{:S(2)}, u32[]{:S(2)}) %collective-permute-start.24) | collective-permute-done | bytes 163872 | tf_op jit(solution)/shard_map/ppermute | solution.py:325
  68.9 1.9 %collective-permute-start.25 = (bf16[64,640]{1,0:T(8,128)(2,1)S(1)}, bf16[64,640]{1,0:T(8,128)(2,1)S(1)}, u32[]{:S(2)}, u32[]{:S(2)}) collective-permute-start(bf16[64,640]{1,0:T(8,128)(2,1)S(1)} %fusion.6), channel_id=1, source_target_pairs={{0,8},{1,9},{2,10},{3,11},{4,12},{5,13},{6,14},{7,15},{8,0},{9,1},... | collective-permute-start | bytes 245768 | tf_op jit(solution)/shard_map/ppermute | solution.py:325
  70.8 5.4 %collective-permute-done.25 = bf16[64,640]{1,0:T(8,128)(2,1)S(1)} collective-permute-done((bf16[64,640]{1,0:T(8,128)(2,1)S(1)}, bf16[64,640]{1,0:T(8,128)(2,1)S(1)}, u32[]{:S(2)}, u32[]{:S(2)}) %collective-permute-start.25) | collective-permute-done | bytes 81952 | tf_op jit(solution)/shard_map/ppermute | solution.py:325
  76.2 0.7 fusion.5
  (66 shorter events, 18.5 us)
Async XLA Ops:
  1.6 8.3 %collective-permute-start = (bf16[64,640]{1,0:T(8,128)(2,1)S(1)}, bf16[64,640]{1,0:T(8,128)(2,1)S(1)}, u32[]{:S(2)}, u32[]{:S(2)}) collective-permute-start(bf16[64,640]{1,0:T(8,128)(2,1)S(1)} %bitcast_convert_fusion.refs_0_), channel_id=1, source_target_pairs={{0,8},{1,9},{2,10},{3,11},{4,12},{5,13},{6,14},{7,15},{8,0},{9,1},... | collective-permute-start | bytes 245768 | tf_op jit(solution)/shard_map/ppermute | solution.py:325
  5.7 4.2 %collective-permute-start.5 = (bf16[64,640]{1,0:T(8,128)(2,1)S(1)}, bf16[64,640]{1,0:T(8,128)(2,1)S(1)}, u32[]{:S(2)}, u32[]{:S(2)}) collective-permute-start(bf16[64,640]{1,0:T(8,128)(2,1)S(1)} %bitcast_convert_fusion.refs_0_), channel_id=1, source_target_pairs={{0,1},{1,0},{2,3},{3,2},{4,5},{5,4},{6,7},{7,6},{8,9},{9,8},{10,11... | collective-permute-start | bytes 245768 | tf_op jit(solution)/shard_map/ppermute | solution.py:325
  9.9 4.2 %collective-permute-start.1 = (bf16[64,640]{1,0:T(8,128)(2,1)S(1)}, bf16[64,640]{1,0:T(8,128)(2,1)S(1)}, u32[]{:S(2)}, u32[]{:S(2)}) collective-permute-start(bf16[64,640]{1,0:T(8,128)(2,1)S(1)} %collective-permute-done.refs_0_.other_snps), channel_id=1, source_target_pairs={{0,1},{1,0},{2,3},{3,2},{4,5},{5,4},{6,7},{7,6},{8,9},{9,8},{10,11... | collective-permute-start | bytes 245768 | tf_op jit(solution)/shard_map/ppermute | solution.py:325
  10.0 7.9 %collective-permute-start.8 = (bf16[2,64,256]{2,1,0:T(8,128)(2,1)S(1)}, bf16[2,64,256]{2,1,0:T(8,128)(2,1)S(1)}, u32[]{:S(2)}, u32[]{:S(2)}) collective-permute-start(bf16[2,64,256]{2,1,0:T(8,128)(2,1)S(1)} %get-tuple-element.77), channel_id=1, source_target_pairs={{0,6},{1,7},{2,4},{3,5},{4,2},{5,3},{6,0},{7,1},{8,14},{9,15},{10,... | collective-permute-start | bytes 196616 | tf_op jit(solution)/shard_map/ppermute | solution.py:325
  12.5 6.3 %collective-permute-start.7 = (bf16[2,64,256]{2,1,0:T(8,128)(2,1)S(1)}, bf16[2,64,256]{2,1,0:T(8,128)(2,1)S(1)}, u32[]{:S(2)}, u32[]{:S(2)}) collective-permute-start(bf16[2,64,256]{2,1,0:T(8,128)(2,1)S(1)} %get-tuple-element.76), channel_id=1, source_target_pairs={{0,4},{1,5},{2,6},{3,7},{4,0},{5,1},{6,2},{7,3},{8,12},{9,13},{10,... | collective-permute-start | bytes 196616 | tf_op jit(solution)/shard_map/ppermute | solution.py:325
  13.3 6.0 %collective-permute-start.6 = (bf16[2,64,256]{2,1,0:T(8,128)(2,1)S(1)}, bf16[2,64,256]{2,1,0:T(8,128)(2,1)S(1)}, u32[]{:S(2)}, u32[]{:S(2)}) collective-permute-start(bf16[2,64,256]{2,1,0:T(8,128)(2,1)S(1)} %get-tuple-element.75), channel_id=1, source_target_pairs={{0,2},{1,3},{2,0},{3,1},{4,6},{5,7},{6,4},{7,5},{8,10},{9,11},{10,... | collective-permute-start | bytes 196616 | tf_op jit(solution)/shard_map/ppermute | solution.py:325
  14.2 5.5 %collective-permute-start.4 = (bf16[2,64,256]{2,1,0:T(8,128)(2,1)S(1)}, bf16[2,64,256]{2,1,0:T(8,128)(2,1)S(1)}, u32[]{:S(2)}, u32[]{:S(2)}) collective-permute-start(bf16[2,64,256]{2,1,0:T(8,128)(2,1)S(1)} %get-tuple-element.74), channel_id=1, source_target_pairs={{0,6},{1,7},{2,4},{3,5},{4,2},{5,3},{6,0},{7,1},{8,14},{9,15},{10,... | collective-permute-start | bytes 196616 | tf_op jit(solution)/shard_map/ppermute | solution.py:325
  16.7 4.3 %collective-permute-start.3 = (bf16[2,64,256]{2,1,0:T(8,128)(2,1)S(1)}, bf16[2,64,256]{2,1,0:T(8,128)(2,1)S(1)}, u32[]{:S(2)}, u32[]{:S(2)}) collective-permute-start(bf16[2,64,256]{2,1,0:T(8,128)(2,1)S(1)} %get-tuple-element.73), channel_id=1, source_target_pairs={{0,4},{1,5},{2,6},{3,7},{4,0},{5,1},{6,2},{7,3},{8,12},{9,13},{10,... | collective-permute-start | bytes 196616 | tf_op jit(solution)/shard_map/ppermute | solution.py:325
  18.0 4.3 %collective-permute-start.2 = (bf16[2,64,256]{2,1,0:T(8,128)(2,1)S(1)}, bf16[2,64,256]{2,1,0:T(8,128)(2,1)S(1)}, u32[]{:S(2)}, u32[]{:S(2)}) collective-permute-start(bf16[2,64,256]{2,1,0:T(8,128)(2,1)S(1)} %get-tuple-element.72), channel_id=1, source_target_pairs={{0,2},{1,3},{2,0},{3,1},{4,6},{5,7},{6,4},{7,5},{8,10},{9,11},{10,... | collective-permute-start | bytes 196616 | tf_op jit(solution)/shard_map/ppermute | solution.py:325
  23.8 6.4 %collective-permute-start.11 = (bf16[4,64,256]{2,1,0:T(8,128)(2,1)S(1)}, bf16[4,64,256]{2,1,0:T(8,128)(2,1)S(1)}, u32[]{:S(2)}, u32[]{:S(2)}) collective-permute-start(bf16[4,64,256]{2,1,0:T(8,128)(2,1)S(1)} %mate_terms.11), channel_id=1, source_target_pairs={{0,6},{1,7},{2,4},{3,5},{4,2},{5,3},{6,0},{7,1},{8,14},{9,15},{10,... | collective-permute-start | bytes 393224 | tf_op jit(solution)/shard_map/ppermute | solution.py:325
  25.7 10.7 %copy-start.1 = (s32[16,64]{1,0:T(8,128)S(1)}, s32[16,64]{1,0:T(8,128)}, u32[]{:S(2)}) copy-start(s32[16,64]{1,0:T(8,128)} %cov.3) | copy-start | bytes 12292
  25.7 19.1 %copy-start = (f32[640,64]{0,1:T(8,128)S(1)}, f32[640,64]{0,1:T(8,128)}, u32[]{:S(2)}) copy-start(f32[640,64]{0,1:T(8,128)} %param.6) | copy-start | bytes 491524
  25.7 5.1 %collective-permute-start.10 = (bf16[4,64,256]{2,1,0:T(8,128)(2,1)S(1)}, bf16[4,64,256]{2,1,0:T(8,128)(2,1)S(1)}, u32[]{:S(2)}, u32[]{:S(2)}) collective-permute-start(bf16[4,64,256]{2,1,0:T(8,128)(2,1)S(1)} %mate_terms.10), channel_id=1, source_target_pairs={{0,4},{1,5},{2,6},{3,7},{4,0},{5,1},{6,2},{7,3},{8,12},{9,13},{10,... | collective-permute-start | bytes 393224 | tf_op jit(solution)/shard_map/ppermute | solution.py:325
  26.9 5.3 %collective-permute-start.9 = (bf16[4,64,256]{2,1,0:T(8,128)(2,1)S(1)}, bf16[4,64,256]{2,1,0:T(8,128)(2,1)S(1)}, u32[]{:S(2)}, u32[]{:S(2)}) collective-permute-start(bf16[4,64,256]{2,1,0:T(8,128)(2,1)S(1)} %mate_terms.9), channel_id=1, source_target_pairs={{0,2},{1,3},{2,0},{3,1},{4,6},{5,7},{6,4},{7,5},{8,10},{9,11},{10,... | collective-permute-start | bytes 393224 | tf_op jit(solution)/shard_map/ppermute | solution.py:325
  32.6 1.5 %collective-permute-start.12 = (bf16[2,64,640]{2,1,0:T(8,128)(2,1)S(1)}, bf16[2,64,640]{2,1,0:T(8,128)(2,1)S(1)}, u32[]{:S(2)}, u32[]{:S(2)}) collective-permute-start(bf16[2,64,640]{2,1,0:T(8,128)(2,1)S(1)} %mates_sum.4.refs_4_), channel_id=1, source_target_pairs={{0,1},{1,0},{2,3},{3,2},{4,5},{5,4},{6,7},{7,6},{8,9},{9,8},{10,11... | collective-permute-start | bytes 491528 | tf_op jit(solution)/shard_map/ppermute | solution.py:325
  34.1 10.7 %collective-permute-start.13 = (bf16[2,64,640]{2,1,0:T(8,128)(2,1)S(1)}, bf16[2,64,640]{2,1,0:T(8,128)(2,1)S(1)}, u32[]{:S(2)}, u32[]{:S(2)}) collective-permute-start(bf16[2,64,640]{2,1,0:T(8,128)(2,1)S(1)} %get-tuple-element.101), channel_id=1, source_target_pairs={{0,8},{1,9},{2,10},{3,11},{4,12},{5,13},{6,14},{7,15},{8,0},{9,1},... | collective-permute-start | bytes 491528 | tf_op jit(solution)/shard_map/ppermute | solution.py:325
  44.9 4.3 %collective-permute-start.14 = (bf16[2,64,640]{2,1,0:T(8,128)(2,1)S(1)}, bf16[2,64,640]{2,1,0:T(8,128)(2,1)S(1)}, u32[]{:S(2)}, u32[]{:S(2)}) collective-permute-start(bf16[2,64,640]{2,1,0:T(8,128)(2,1)S(1)} %get-tuple-element.104.refs_0_), channel_id=1, source_target_pairs={{0,1},{1,0},{2,3},{3,2},{4,5},{5,4},{6,7},{7,6},{8,9},{9,8},{10,11... | collective-permute-start | bytes 491528 | tf_op jit(solution)/shard_map/ppermute | solution.py:325
  45.2 7.7 %collective-permute-start.20 = (bf16[2,64,256]{2,1,0:T(8,128)(2,1)S(1)}, bf16[2,64,256]{2,1,0:T(8,128)(2,1)S(1)}, u32[]{:S(2)}, u32[]{:S(2)}) collective-permute-start(bf16[2,64,256]{2,1,0:T(8,128)(2,1)S(1)} %get-tuple-element.110), channel_id=1, source_target_pairs={{0,6},{1,7},{2,4},{3,5},{4,2},{5,3},{6,0},{7,1},{8,14},{9,15},{10,... | collective-permute-start | bytes 196616 | tf_op jit(solution)/shard_map/ppermute | solution.py:325
  46.2 7.8 %collective-permute-start.19 = (bf16[2,64,256]{2,1,0:T(8,128)(2,1)S(1)}, bf16[2,64,256]{2,1,0:T(8,128)(2,1)S(1)}, u32[]{:S(2)}, u32[]{:S(2)}) collective-permute-start(bf16[2,64,256]{2,1,0:T(8,128)(2,1)S(1)} %get-tuple-element.109), channel_id=1, source_target_pairs={{0,4},{1,5},{2,6},{3,7},{4,0},{5,1},{6,2},{7,3},{8,12},{9,13},{10,... | collective-permute-start | bytes 196616 | tf_op jit(solution)/shard_map/ppermute | solution.py:325
  48.2 6.2 %collective-permute-start.18 = (bf16[2,64,256]{2,1,0:T(8,128)(2,1)S(1)}, bf16[2,64,256]{2,1,0:T(8,128)(2,1)S(1)}, u32[]{:S(2)}, u32[]{:S(2)}) collective-permute-start(bf16[2,64,256]{2,1,0:T(8,128)(2,1)S(1)} %get-tuple-element.108), channel_id=1, source_target_pairs={{0,2},{1,3},{2,0},{3,1},{4,6},{5,7},{6,4},{7,5},{8,10},{9,11},{10,... | collective-permute-start | bytes 196616 | tf_op jit(solution)/shard_map/ppermute | solution.py:325
  49.4 5.5 %collective-permute-start.17 = (bf16[2,64,256]{2,1,0:T(8,128)(2,1)S(1)}, bf16[2,64,256]{2,1,0:T(8,128)(2,1)S(1)}, u32[]{:S(2)}, u32[]{:S(2)}) collective-permute-start(bf16[2,64,256]{2,1,0:T(8,128)(2,1)S(1)} %get-tuple-element.107), channel_id=1, source_target_pairs={{0,6},{1,7},{2,4},{3,5},{4,2},{5,3},{6,0},{7,1},{8,14},{9,15},{10,... | collective-permute-start | bytes 196616 | tf_op jit(solution)/shard_map/ppermute | solution.py:325
  50.4 5.0 %collective-permute-start.16 = (bf16[2,64,256]{2,1,0:T(8,128)(2,1)S(1)}, bf16[2,64,256]{2,1,0:T(8,128)(2,1)S(1)}, u32[]{:S(2)}, u32[]{:S(2)}) collective-permute-start(bf16[2,64,256]{2,1,0:T(8,128)(2,1)S(1)} %get-tuple-element.106), channel_id=1, source_target_pairs={{0,4},{1,5},{2,6},{3,7},{4,0},{5,1},{6,2},{7,3},{8,12},{9,13},{10,... | collective-permute-start | bytes 196616 | tf_op jit(solution)/shard_map/ppermute | solution.py:325
  52.9 4.3 %collective-permute-start.15 = (bf16[2,64,256]{2,1,0:T(8,128)(2,1)S(1)}, bf16[2,64,256]{2,1,0:T(8,128)(2,1)S(1)}, u32[]{:S(2)}, u32[]{:S(2)}) collective-permute-start(bf16[2,64,256]{2,1,0:T(8,128)(2,1)S(1)} %get-tuple-element.105), channel_id=1, source_target_pairs={{0,2},{1,3},{2,0},{3,1},{4,6},{5,7},{6,4},{7,5},{8,10},{9,11},{10,... | collective-permute-start | bytes 196616 | tf_op jit(solution)/shard_map/ppermute | solution.py:325
  58.7 6.5 %collective-permute-start.23 = (bf16[4,64,256]{2,1,0:T(8,128)(2,1)S(1)}, bf16[4,64,256]{2,1,0:T(8,128)(2,1)S(1)}, u32[]{:S(2)}, u32[]{:S(2)}) collective-permute-start(bf16[4,64,256]{2,1,0:T(8,128)(2,1)S(1)} %mate_terms.15), channel_id=1, source_target_pairs={{0,6},{1,7},{2,4},{3,5},{4,2},{5,3},{6,0},{7,1},{8,14},{9,15},{10,... | collective-permute-start | bytes 393224 | tf_op jit(solution)/shard_map/ppermute | solution.py:325
  59.7 5.9 %collective-permute-start.22 = (bf16[4,64,256]{2,1,0:T(8,128)(2,1)S(1)}, bf16[4,64,256]{2,1,0:T(8,128)(2,1)S(1)}, u32[]{:S(2)}, u32[]{:S(2)}) collective-permute-start(bf16[4,64,256]{2,1,0:T(8,128)(2,1)S(1)} %mate_terms.14), channel_id=1, source_target_pairs={{0,4},{1,5},{2,6},{3,7},{4,0},{5,1},{6,2},{7,3},{8,12},{9,13},{10,... | collective-permute-start | bytes 393224 | tf_op jit(solution)/shard_map/ppermute | solution.py:325
  62.1 5.0 %collective-permute-start.21 = (bf16[4,64,256]{2,1,0:T(8,128)(2,1)S(1)}, bf16[4,64,256]{2,1,0:T(8,128)(2,1)S(1)}, u32[]{:S(2)}, u32[]{:S(2)}) collective-permute-start(bf16[4,64,256]{2,1,0:T(8,128)(2,1)S(1)} %mate_terms.13), channel_id=1, source_target_pairs={{0,2},{1,3},{2,0},{3,1},{4,6},{5,7},{6,4},{7,5},{8,10},{9,11},{10,... | collective-permute-start | bytes 393224 | tf_op jit(solution)/shard_map/ppermute | solution.py:325
  67.5 1.5 %collective-permute-start.24 = (bf16[2,64,640]{2,1,0:T(8,128)(2,1)S(1)}, bf16[2,64,640]{2,1,0:T(8,128)(2,1)S(1)}, u32[]{:S(2)}, u32[]{:S(2)}) collective-permute-start(bf16[2,64,640]{2,1,0:T(8,128)(2,1)S(1)} %mates_sum.6.refs_4_), channel_id=1, source_target_pairs={{0,1},{1,0},{2,3},{3,2},{4,5},{5,4},{6,7},{7,6},{8,9},{9,8},{10,11... | collective-permute-start | bytes 491528 | tf_op jit(solution)/shard_map/ppermute | solution.py:325
  68.9 7.2 %collective-permute-start.25 = (bf16[64,640]{1,0:T(8,128)(2,1)S(1)}, bf16[64,640]{1,0:T(8,128)(2,1)S(1)}, u32[]{:S(2)}, u32[]{:S(2)}) collective-permute-start(bf16[64,640]{1,0:T(8,128)(2,1)S(1)} %fusion.6), channel_id=1, source_target_pairs={{0,8},{1,9},{2,10},{3,11},{4,12},{5,13},{6,14},{7,15},{8,0},{9,1},... | collective-permute-start | bytes 245768 | tf_op jit(solution)/shard_map/ppermute | solution.py:325

commit v12 on v11

--- a/solution.py
+++ b/solution.py
@@ -133,7 +133,7 @@
 
 
 def product_kernel(turns, mate, first, rows, pos_ref, geno, packet, *refs):
-    before, (gradient, gram) = refs[:-2], refs[-2:]
+    before, (gradient, gram) = refs[:2], refs[-2:]
     pos = pos_ref[0]
     width = packet.shape[2]
     total = None if first else before[1][...]
@@ -286,17 +286,17 @@
         name="owners_update",
     )
 
-    def product(mate, group, panel, before):
+    def product(mate, group, panel, before, after):
         share = samples_here * snps_here // len(MATES) // 2
         return pl.pallas_call(
             functools.partial(product_kernel, [turns[t] for t in group], mate, not before, 256),
             out_shape=(by_samples, square),
-            in_specs=[smem] + [vmem] * (2 + len(before)),
+            in_specs=[smem] + [vmem] * (2 + len(before)) + [anywhere] * len(after),
             out_specs=(vmem, vmem),
             compiler_params=params,
             cost_estimate=cost(8 * rank * share, 2 * share),
             name="panel_product",
-        )(pos, geno, panel, *before)
+        )(pos, geno, panel, *before, *after)
 
     def sample_update(samples, gradient, gram, outs):
         return pl.pallas_call(
@@ -354,8 +354,9 @@
             ]
         panels = [[to_mate(x, mate) for x, mate in zip(packets, MATES)] for packets in picked]
         partial = ()
-        for g, m in ((0, 0), (1, 0), (0, 3), (0, 2), (0, 1), (1, 3), (1, 2), (1, 1)):
-            partial = product(MATES[m], groups[g], panels[g][m], partial)
+        for g, m in ((0, 0), (0, 3), (0, 2), (0, 1), (1, 0), (1, 3), (1, 2), (1, 1)):
+            after = [panels[1][0]] if (g, m) == (0, 3) else []
+            partial = product(MATES[m], groups[g], panels[g][m], partial, after)
         rounded = (jax.ShapeDtypeStruct((rank, samples_here), jnp.bfloat16), square)
         if not last:
             samples, *current = sample_update(samples, *partial, (by_samples,) + rounded)

time: 77.1 us -> 76.2 us (0.988)
  waiting for transfers between devices: 24.1 us -> 22.7 us
    ppermute x26, waiting for transfers between devices: 24.1 us -> 22.7 us  [swap(): return lax.ppermute(x, 'rows', [(r, r ^ turn) for r in range(devices)])]
  transfers between devices with their start and end apart: 26 -> 26, of which waited for: 13 -> 14; matrix products, arithmetic and copies ran while one was open for 0% -> 0% of each run, Pallas kernels for 21% -> 21%
where the time goes in v12:
time: 76.2 us; the launch traced here: 76 us
  starting transfers between devices  30.7 us (40%)
  waiting for transfers between devices  22.7 us (30%)
  Pallas kernels  19.9 us (26%)
  other arithmetic  1.65 us (2%)
  between operations  0.95 us (1%)
    ppermute x26, starting transfers between devices, swap(): return lax.ppermute(x, 'rows', [(r, r ^ turn) for r in range(devices)])  30.7 us
    ppermute x26, waiting for transfers between devices, swap(): return lax.ppermute(x, 'rows', [(r, r ^ turn) for r in range(devices)])  22.7 us
    pallas_call x16, Pallas kernels, product(): pl.pallas_call(functools.partial(product_kernel, [turns[t] for t in group...  7.44 us
    pallas_call x8, Pallas kernels, terms_for(): pl.pallas_call(functools.partial(term_kernel, turns, groups, mate), out_s...  4.9 us
    pallas_call x1, Pallas kernels, on_device(): pl.pallas_call(functools.partial(load_kernel, turns, per_owner, own_block...  3.51 us
    pallas_call x3, Pallas kernels, sample_update(): pl.pallas_call(functools.partial(sample_kernel, sample_step), out_shape=o...  1.76 us
  transfers between devices with their start and end apart: 26, of which 14 were waited for; matrix products, arithmetic and copies ran while one was open for 0% of the time, Pallas kernels for 21%

profile of v12, /device:TPU:0, one launch (start us, length us, event | category | flops | bytes accessed | tf_op | source)
XLA Modules:
  0.0 76.0 jit_solution(16147896280133700295)
XLA Ops:
  0.6 0.9 %bitcast_convert_fusion.refs_0_ = bf16[64,640]{1,0:T(8,128)(2,1)S(1)} fusion(f32[640,64]{0,1:T(8,128)} %param.6), kind=kLoop, calls=%fused_computation.9 | loop fusion | flops 40960 | bytes 245760 | tf_op jit(solution)/shard_map/convert_element_type | solution.py:335
  1.6 4.1 %collective-permute-start = (bf16[64,640]{1,0:T(8,128)(2,1)S(1)}, bf16[64,640]{1,0:T(8,128)(2,1)S(1)}, u32[]{:S(2)}, u32[]{:S(2)}) collective-permute-start(bf16[64,640]{1,0:T(8,128)(2,1)S(1)} %bitcast_convert_fusion.refs_0_), channel_id=1, source_target_pairs={{0,8},{1,9},{2,10},{3,11},{4,12},{5,13},{6,14},{7,15},{8,0},{9,1},... | collective-permute-start | bytes 245768 | tf_op jit(solution)/shard_map/ppermute | solution.py:325
  5.7 3.5 %load_batch.1 = (bf16[1024,4096]{1,0:T(8,128)(2,1)S(1)}, f32[64,1024]{1,0:T(8,128)S(1)}, s32[16,4]{1,0:T(8,128)S(4)}) custom-call(s32[1]{0:T(128)} %bitcast.pos_ref, s32[16,64]{1,0:T(8,128)} %cov.3, bf16[1024,4096]{1,0:T(8,128)(2,1)} %geno.1, f32[64,1024]{1,0:T(8,128)} %bitcast.20), custom_call_target="tpu_custom_call" | custom-call | bytes 8388608 | tf_op jit(solution)/shard_map/load_batch/pallas_call | solution.py:215
  9.2 0.7 collective-permute-done.refs_0_.other_snps
  10.0 2.5 %collective-permute-start.8 = (bf16[2,64,256]{2,1,0:T(8,128)(2,1)S(1)}, bf16[2,64,256]{2,1,0:T(8,128)(2,1)S(1)}, u32[]{:S(2)}, u32[]{:S(2)}) collective-permute-start(bf16[2,64,256]{2,1,0:T(8,128)(2,1)S(1)} %get-tuple-element.78), channel_id=1, source_target_pairs={{0,6},{1,7},{2,4},{3,5},{4,2},{5,3},{6,0},{7,1},{8,14},{9,15},{10,... | collective-permute-start | bytes 196616 | tf_op jit(solution)/shard_map/ppermute | solution.py:325
  12.5 0.7 collective-permute-start.7
  14.2 2.5 %collective-permute-start.4 = (bf16[2,64,256]{2,1,0:T(8,128)(2,1)S(1)}, bf16[2,64,256]{2,1,0:T(8,128)(2,1)S(1)}, u32[]{:S(2)}, u32[]{:S(2)}) collective-permute-start(bf16[2,64,256]{2,1,0:T(8,128)(2,1)S(1)} %get-tuple-element.74), channel_id=1, source_target_pairs={{0,6},{1,7},{2,4},{3,5},{4,2},{5,3},{6,0},{7,1},{8,14},{9,15},{10,... | collective-permute-start | bytes 196616 | tf_op jit(solution)/shard_map/ppermute | solution.py:325
  16.7 0.7 collective-permute-start.3
  20.2 0.8 %collective-permute-done.3.packet.refs_1_ = bf16[2,64,256]{2,1,0:T(8,128)(2,1)S(1)} collective-permute-done((bf16[2,64,256]{2,1,0:T(8,128)(2,1)S(1)}, bf16[2,64,256]{2,1,0:T(8,128)(2,1)S(1)}, u32[]{:S(2)}, u32[]{:S(2)}) %collective-permute-start.3) | collective-permute-done | bytes 65568 | tf_op jit(solution)/shard_map/ppermute | solution.py:325
  23.3 1.4 %collective-permute-start.11 = (bf16[4,64,256]{2,1,0:T(8,128)(2,1)S(1)}, bf16[4,64,256]{2,1,0:T(8,128)(2,1)S(1)}, u32[]{:S(2)}, u32[]{:S(2)}) collective-permute-start(bf16[4,64,256]{2,1,0:T(8,128)(2,1)S(1)} %mate_terms.11), channel_id=1, source_target_pairs={{0,6},{1,7},{2,4},{3,5},{4,2},{5,3},{6,0},{7,1},{8,14},{9,15},{10,... | collective-permute-start | bytes 393224 | tf_op jit(solution)/shard_map/ppermute | solution.py:325
  25.3 0.8 %collective-permute-start.10 = (bf16[4,64,256]{2,1,0:T(8,128)(2,1)S(1)}, bf16[4,64,256]{2,1,0:T(8,128)(2,1)S(1)}, u32[]{:S(2)}, u32[]{:S(2)}) collective-permute-start(bf16[4,64,256]{2,1,0:T(8,128)(2,1)S(1)} %mate_terms.10), channel_id=1, source_target_pairs={{0,4},{1,5},{2,6},{3,7},{4,0},{5,1},{6,2},{7,3},{8,12},{9,13},{10,... | collective-permute-start | bytes 393224 | tf_op jit(solution)/shard_map/ppermute | solution.py:325
  26.7 1.5 %collective-permute-start.9 = (bf16[4,64,256]{2,1,0:T(8,128)(2,1)S(1)}, bf16[4,64,256]{2,1,0:T(8,128)(2,1)S(1)}, u32[]{:S(2)}, u32[]{:S(2)}) collective-permute-start(bf16[4,64,256]{2,1,0:T(8,128)(2,1)S(1)} %mate_terms.9), channel_id=1, source_target_pairs={{0,2},{1,3},{2,0},{3,1},{4,6},{5,7},{6,4},{7,5},{8,10},{9,11},{10,... | collective-permute-start | bytes 393224 | tf_op jit(solution)/shard_map/ppermute | solution.py:325
  28.8 1.1 %collective-permute-done.11.refs_3_ = bf16[4,64,256]{2,1,0:T(8,128)(2,1)S(1)} collective-permute-done((bf16[4,64,256]{2,1,0:T(8,128)(2,1)S(1)}, bf16[4,64,256]{2,1,0:T(8,128)(2,1)S(1)}, u32[]{:S(2)}, u32[]{:S(2)}) %collective-permute-start.11) | collective-permute-done | bytes 131104 | tf_op jit(solution)/shard_map/ppermute | solution.py:325
  30.4 1.4 %collective-permute-done.9.refs_1_ = bf16[4,64,256]{2,1,0:T(8,128)(2,1)S(1)} collective-permute-done((bf16[4,64,256]{2,1,0:T(8,128)(2,1)S(1)}, bf16[4,64,256]{2,1,0:T(8,128)(2,1)S(1)}, u32[]{:S(2)}, u32[]{:S(2)}) %collective-permute-start.9) | collective-permute-done | bytes 131104 | tf_op jit(solution)/shard_map/ppermute | solution.py:325
  32.7 1.0 %collective-permute-done.12.arrived = bf16[2,64,640]{2,1,0:T(8,128)(2,1)S(1)} collective-permute-done((bf16[2,64,640]{2,1,0:T(8,128)(2,1)S(1)}, bf16[2,64,640]{2,1,0:T(8,128)(2,1)S(1)}, u32[]{:S(2)}, u32[]{:S(2)}) %collective-permute-start.12) | collective-permute-done | bytes 163872 | tf_op jit(solution)/shard_map/ppermute | solution.py:325
  33.7 2.4 %collective-permute-start.13 = (bf16[2,64,640]{2,1,0:T(8,128)(2,1)S(1)}, bf16[2,64,640]{2,1,0:T(8,128)(2,1)S(1)}, u32[]{:S(2)}, u32[]{:S(2)}) collective-permute-start(bf16[2,64,640]{2,1,0:T(8,128)(2,1)S(1)} %get-tuple-element.101), channel_id=1, source_target_pairs={{0,8},{1,9},{2,10},{3,11},{4,12},{5,13},{6,14},{7,15},{8,0},{9,1},... | collective-permute-start | bytes 491528 | tf_op jit(solution)/shard_map/ppermute | solution.py:325
  36.3 8.2 %collective-permute-done.13.arrived = bf16[2,64,640]{2,1,0:T(8,128)(2,1)S(1)} collective-permute-done((bf16[2,64,640]{2,1,0:T(8,128)(2,1)S(1)}, bf16[2,64,640]{2,1,0:T(8,128)(2,1)S(1)}, u32[]{:S(2)}, u32[]{:S(2)}) %collective-permute-start.13) | collective-permute-done | bytes 163872 | tf_op jit(solution)/shard_map/ppermute | solution.py:325
  44.8 1.3 %collective-permute-start.20 = (bf16[2,64,256]{2,1,0:T(8,128)(2,1)S(1)}, bf16[2,64,256]{2,1,0:T(8,128)(2,1)S(1)}, u32[]{:S(2)}, u32[]{:S(2)}) collective-permute-start(bf16[2,64,256]{2,1,0:T(8,128)(2,1)S(1)} %get-tuple-element.111), channel_id=1, source_target_pairs={{0,6},{1,7},{2,4},{3,5},{4,2},{5,3},{6,0},{7,1},{8,14},{9,15},{10,... | collective-permute-start | bytes 196616 | tf_op jit(solution)/shard_map/ppermute | solution.py:325
  46.1 1.6 %collective-permute-start.19 = (bf16[2,64,256]{2,1,0:T(8,128)(2,1)S(1)}, bf16[2,64,256]{2,1,0:T(8,128)(2,1)S(1)}, u32[]{:S(2)}, u32[]{:S(2)}) collective-permute-start(bf16[2,64,256]{2,1,0:T(8,128)(2,1)S(1)} %get-tuple-element.110), channel_id=1, source_target_pairs={{0,4},{1,5},{2,6},{3,7},{4,0},{5,1},{6,2},{7,3},{8,12},{9,13},{10,... | collective-permute-start | bytes 196616 | tf_op jit(solution)/shard_map/ppermute | solution.py:325
  47.6 0.7 collective-permute-start.18
  49.0 1.3 %collective-permute-start.17 = (bf16[2,64,256]{2,1,0:T(8,128)(2,1)S(1)}, bf16[2,64,256]{2,1,0:T(8,128)(2,1)S(1)}, u32[]{:S(2)}, u32[]{:S(2)}) collective-permute-start(bf16[2,64,256]{2,1,0:T(8,128)(2,1)S(1)} %get-tuple-element.107), channel_id=1, source_target_pairs={{0,6},{1,7},{2,4},{3,5},{4,2},{5,3},{6,0},{7,1},{8,14},{9,15},{10,... | collective-permute-start | bytes 196616 | tf_op jit(solution)/shard_map/ppermute | solution.py:325
  50.3 1.6 %collective-permute-start.16 = (bf16[2,64,256]{2,1,0:T(8,128)(2,1)S(1)}, bf16[2,64,256]{2,1,0:T(8,128)(2,1)S(1)}, u32[]{:S(2)}, u32[]{:S(2)}) collective-permute-start(bf16[2,64,256]{2,1,0:T(8,128)(2,1)S(1)} %get-tuple-element.106), channel_id=1, source_target_pairs={{0,4},{1,5},{2,6},{3,7},{4,0},{5,1},{6,2},{7,3},{8,12},{9,13},{10,... | collective-permute-start | bytes 196616 | tf_op jit(solution)/shard_map/ppermute | solution.py:325
  51.9 0.7 collective-permute-start.15
  57.6 1.1 %collective-permute-start.23 = (bf16[4,64,256]{2,1,0:T(8,128)(2,1)S(1)}, bf16[4,64,256]{2,1,0:T(8,128)(2,1)S(1)}, u32[]{:S(2)}, u32[]{:S(2)}) collective-permute-start(bf16[4,64,256]{2,1,0:T(8,128)(2,1)S(1)} %mate_terms.15), channel_id=1, source_target_pairs={{0,6},{1,7},{2,4},{3,5},{4,2},{5,3},{6,0},{7,1},{8,14},{9,15},{10,... | collective-permute-start | bytes 393224 | tf_op jit(solution)/shard_map/ppermute | solution.py:325
  59.4 1.2 %collective-permute-start.22 = (bf16[4,64,256]{2,1,0:T(8,128)(2,1)S(1)}, bf16[4,64,256]{2,1,0:T(8,128)(2,1)S(1)}, u32[]{:S(2)}, u32[]{:S(2)}) collective-permute-start(bf16[4,64,256]{2,1,0:T(8,128)(2,1)S(1)} %mate_terms.14), channel_id=1, source_target_pairs={{0,4},{1,5},{2,6},{3,7},{4,0},{5,1},{6,2},{7,3},{8,12},{9,13},{10,... | collective-permute-start | bytes 393224 | tf_op jit(solution)/shard_map/ppermute | solution.py:325
  61.2 1.4 %collective-permute-start.21 = (bf16[4,64,256]{2,1,0:T(8,128)(2,1)S(1)}, bf16[4,64,256]{2,1,0:T(8,128)(2,1)S(1)}, u32[]{:S(2)}, u32[]{:S(2)}) collective-permute-start(bf16[4,64,256]{2,1,0:T(8,128)(2,1)S(1)} %mate_terms.13), channel_id=1, source_target_pairs={{0,2},{1,3},{2,0},{3,1},{4,6},{5,7},{6,4},{7,5},{8,10},{9,11},{10,... | collective-permute-start | bytes 393224 | tf_op jit(solution)/shard_map/ppermute | solution.py:325
  62.6 0.9 %sample_update.4 = (f32[64,1024]{1,0:T(8,128)}, f32[8,128]{1,0:T(8,128)S(1)}) custom-call(f32[64,1024]{1,0:T(8,128)S(1)} %get-tuple-element.96.samples, f32[64,1024]{1,0:T(8,128)S(1)} %get-tuple-element.127.gradient, f32[64,64]{1,0:T(8,128)S(1)} %get-tuple-element.128.gram), custom_call_target="tpu_custom_call" | custom-call | bytes 2097152 | tf_op jit(solution)/shard_map/sample_update/pallas_call | solution.py:302
  64.8 1.4 %collective-permute-done.21.refs_1_ = bf16[4,64,256]{2,1,0:T(8,128)(2,1)S(1)} collective-permute-done((bf16[4,64,256]{2,1,0:T(8,128)(2,1)S(1)}, bf16[4,64,256]{2,1,0:T(8,128)(2,1)S(1)}, u32[]{:S(2)}, u32[]{:S(2)}) %collective-permute-start.21) | collective-permute-done | bytes 131104 | tf_op jit(solution)/shard_map/ppermute | solution.py:325
  67.0 1.0 %collective-permute-done.24 = bf16[2,64,640]{2,1,0:T(8,128)(2,1)S(1)} collective-permute-done((bf16[2,64,640]{2,1,0:T(8,128)(2,1)S(1)}, bf16[2,64,640]{2,1,0:T(8,128)(2,1)S(1)}, u32[]{:S(2)}, u32[]{:S(2)}) %collective-permute-start.24) | collective-permute-done | bytes 163872 | tf_op jit(solution)/shard_map/ppermute | solution.py:325
  68.0 2.4 %collective-permute-start.25 = (bf16[64,640]{1,0:T(8,128)(2,1)S(1)}, bf16[64,640]{1,0:T(8,128)(2,1)S(1)}, u32[]{:S(2)}, u32[]{:S(2)}) collective-permute-start(bf16[64,640]{1,0:T(8,128)(2,1)S(1)} %fusion.6), channel_id=1, source_target_pairs={{0,8},{1,9},{2,10},{3,11},{4,12},{5,13},{6,14},{7,15},{8,0},{9,1},... | collective-permute-start | bytes 245768 | tf_op jit(solution)/shard_map/ppermute | solution.py:325
  70.5 4.8 %collective-permute-done.25 = bf16[64,640]{1,0:T(8,128)(2,1)S(1)} collective-permute-done((bf16[64,640]{1,0:T(8,128)(2,1)S(1)}, bf16[64,640]{1,0:T(8,128)(2,1)S(1)}, u32[]{:S(2)}, u32[]{:S(2)}) %collective-permute-start.25) | collective-permute-done | bytes 81952 | tf_op jit(solution)/shard_map/ppermute | solution.py:325
  75.3 0.7 fusion.5
  (66 shorter events, 18.6 us)
Async XLA Ops:
  1.6 8.3 %collective-permute-start = (bf16[64,640]{1,0:T(8,128)(2,1)S(1)}, bf16[64,640]{1,0:T(8,128)(2,1)S(1)}, u32[]{:S(2)}, u32[]{:S(2)}) collective-permute-start(bf16[64,640]{1,0:T(8,128)(2,1)S(1)} %bitcast_convert_fusion.refs_0_), channel_id=1, source_target_pairs={{0,8},{1,9},{2,10},{3,11},{4,12},{5,13},{6,14},{7,15},{8,0},{9,1},... | collective-permute-start | bytes 245768 | tf_op jit(solution)/shard_map/ppermute | solution.py:325
  5.7 4.2 %collective-permute-start.5 = (bf16[64,640]{1,0:T(8,128)(2,1)S(1)}, bf16[64,640]{1,0:T(8,128)(2,1)S(1)}, u32[]{:S(2)}, u32[]{:S(2)}) collective-permute-start(bf16[64,640]{1,0:T(8,128)(2,1)S(1)} %bitcast_convert_fusion.refs_0_), channel_id=1, source_target_pairs={{0,1},{1,0},{2,3},{3,2},{4,5},{5,4},{6,7},{7,6},{8,9},{9,8},{10,11... | collective-permute-start | bytes 245768 | tf_op jit(solution)/shard_map/ppermute | solution.py:325
  9.9 4.2 %collective-permute-start.1 = (bf16[64,640]{1,0:T(8,128)(2,1)S(1)}, bf16[64,640]{1,0:T(8,128)(2,1)S(1)}, u32[]{:S(2)}, u32[]{:S(2)}) collective-permute-start(bf16[64,640]{1,0:T(8,128)(2,1)S(1)} %collective-permute-done.refs_0_.other_snps), channel_id=1, source_target_pairs={{0,1},{1,0},{2,3},{3,2},{4,5},{5,4},{6,7},{7,6},{8,9},{9,8},{10,11... | collective-permute-start | bytes 245768 | tf_op jit(solution)/shard_map/ppermute | solution.py:325
  10.0 7.4 %collective-permute-start.8 = (bf16[2,64,256]{2,1,0:T(8,128)(2,1)S(1)}, bf16[2,64,256]{2,1,0:T(8,128)(2,1)S(1)}, u32[]{:S(2)}, u32[]{:S(2)}) collective-permute-start(bf16[2,64,256]{2,1,0:T(8,128)(2,1)S(1)} %get-tuple-element.78), channel_id=1, source_target_pairs={{0,6},{1,7},{2,4},{3,5},{4,2},{5,3},{6,0},{7,1},{8,14},{9,15},{10,... | collective-permute-start | bytes 196616 | tf_op jit(solution)/shard_map/ppermute | solution.py:325
  12.5 5.7 %collective-permute-start.7 = (bf16[2,64,256]{2,1,0:T(8,128)(2,1)S(1)}, bf16[2,64,256]{2,1,0:T(8,128)(2,1)S(1)}, u32[]{:S(2)}, u32[]{:S(2)}) collective-permute-start(bf16[2,64,256]{2,1,0:T(8,128)(2,1)S(1)} %get-tuple-element.77), channel_id=1, source_target_pairs={{0,4},{1,5},{2,6},{3,7},{4,0},{5,1},{6,2},{7,3},{8,12},{9,13},{10,... | collective-permute-start | bytes 196616 | tf_op jit(solution)/shard_map/ppermute | solution.py:325
  13.3 5.5 %collective-permute-start.6 = (bf16[2,64,256]{2,1,0:T(8,128)(2,1)S(1)}, bf16[2,64,256]{2,1,0:T(8,128)(2,1)S(1)}, u32[]{:S(2)}, u32[]{:S(2)}) collective-permute-start(bf16[2,64,256]{2,1,0:T(8,128)(2,1)S(1)} %get-tuple-element.76), channel_id=1, source_target_pairs={{0,2},{1,3},{2,0},{3,1},{4,6},{5,7},{6,4},{7,5},{8,10},{9,11},{10,... | collective-permute-start | bytes 196616 | tf_op jit(solution)/shard_map/ppermute | solution.py:325
  14.2 5.5 %collective-permute-start.4 = (bf16[2,64,256]{2,1,0:T(8,128)(2,1)S(1)}, bf16[2,64,256]{2,1,0:T(8,128)(2,1)S(1)}, u32[]{:S(2)}, u32[]{:S(2)}) collective-permute-start(bf16[2,64,256]{2,1,0:T(8,128)(2,1)S(1)} %get-tuple-element.74), channel_id=1, source_target_pairs={{0,6},{1,7},{2,4},{3,5},{4,2},{5,3},{6,0},{7,1},{8,14},{9,15},{10,... | collective-permute-start | bytes 196616 | tf_op jit(solution)/shard_map/ppermute | solution.py:325
  16.7 4.3 %collective-permute-start.3 = (bf16[2,64,256]{2,1,0:T(8,128)(2,1)S(1)}, bf16[2,64,256]{2,1,0:T(8,128)(2,1)S(1)}, u32[]{:S(2)}, u32[]{:S(2)}) collective-permute-start(bf16[2,64,256]{2,1,0:T(8,128)(2,1)S(1)} %get-tuple-element.73), channel_id=1, source_target_pairs={{0,4},{1,5},{2,6},{3,7},{4,0},{5,1},{6,2},{7,3},{8,12},{9,13},{10,... | collective-permute-start | bytes 196616 | tf_op jit(solution)/shard_map/ppermute | solution.py:325
  17.5 4.3 %collective-permute-start.2 = (bf16[2,64,256]{2,1,0:T(8,128)(2,1)S(1)}, bf16[2,64,256]{2,1,0:T(8,128)(2,1)S(1)}, u32[]{:S(2)}, u32[]{:S(2)}) collective-permute-start(bf16[2,64,256]{2,1,0:T(8,128)(2,1)S(1)} %get-tuple-element.72), channel_id=1, source_target_pairs={{0,2},{1,3},{2,0},{3,1},{4,6},{5,7},{6,4},{7,5},{8,10},{9,11},{10,... | collective-permute-start | bytes 196616 | tf_op jit(solution)/shard_map/ppermute | solution.py:325
  23.3 6.6 %collective-permute-start.11 = (bf16[4,64,256]{2,1,0:T(8,128)(2,1)S(1)}, bf16[4,64,256]{2,1,0:T(8,128)(2,1)S(1)}, u32[]{:S(2)}, u32[]{:S(2)}) collective-permute-start(bf16[4,64,256]{2,1,0:T(8,128)(2,1)S(1)} %mate_terms.11), channel_id=1, source_target_pairs={{0,6},{1,7},{2,4},{3,5},{4,2},{5,3},{6,0},{7,1},{8,14},{9,15},{10,... | collective-permute-start | bytes 393224 | tf_op jit(solution)/shard_map/ppermute | solution.py:325
  25.3 10.9 %copy-start.1 = (s32[16,64]{1,0:T(8,128)S(1)}, s32[16,64]{1,0:T(8,128)}, u32[]{:S(2)}) copy-start(s32[16,64]{1,0:T(8,128)} %cov.3) | copy-start | bytes 12292
  25.3 19.2 %copy-start = (f32[640,64]{0,1:T(8,128)S(1)}, f32[640,64]{0,1:T(8,128)}, u32[]{:S(2)}) copy-start(f32[640,64]{0,1:T(8,128)} %param.6) | copy-start | bytes 491524
  25.3 5.1 %collective-permute-start.10 = (bf16[4,64,256]{2,1,0:T(8,128)(2,1)S(1)}, bf16[4,64,256]{2,1,0:T(8,128)(2,1)S(1)}, u32[]{:S(2)}, u32[]{:S(2)}) collective-permute-start(bf16[4,64,256]{2,1,0:T(8,128)(2,1)S(1)} %mate_terms.10), channel_id=1, source_target_pairs={{0,4},{1,5},{2,6},{3,7},{4,0},{5,1},{6,2},{7,3},{8,12},{9,13},{10,... | collective-permute-start | bytes 393224 | tf_op jit(solution)/shard_map/ppermute | solution.py:325
  26.7 5.1 %collective-permute-start.9 = (bf16[4,64,256]{2,1,0:T(8,128)(2,1)S(1)}, bf16[4,64,256]{2,1,0:T(8,128)(2,1)S(1)}, u32[]{:S(2)}, u32[]{:S(2)}) collective-permute-start(bf16[4,64,256]{2,1,0:T(8,128)(2,1)S(1)} %mate_terms.9), channel_id=1, source_target_pairs={{0,2},{1,3},{2,0},{3,1},{4,6},{5,7},{6,4},{7,5},{8,10},{9,11},{10,... | collective-permute-start | bytes 393224 | tf_op jit(solution)/shard_map/ppermute | solution.py:325
  32.2 1.5 %collective-permute-start.12 = (bf16[2,64,640]{2,1,0:T(8,128)(2,1)S(1)}, bf16[2,64,640]{2,1,0:T(8,128)(2,1)S(1)}, u32[]{:S(2)}, u32[]{:S(2)}) collective-permute-start(bf16[2,64,640]{2,1,0:T(8,128)(2,1)S(1)} %mates_sum.4.refs_4_), channel_id=1, source_target_pairs={{0,1},{1,0},{2,3},{3,2},{4,5},{5,4},{6,7},{7,6},{8,9},{9,8},{10,11... | collective-permute-start | bytes 491528 | tf_op jit(solution)/shard_map/ppermute | solution.py:325
  33.7 10.7 %collective-permute-start.13 = (bf16[2,64,640]{2,1,0:T(8,128)(2,1)S(1)}, bf16[2,64,640]{2,1,0:T(8,128)(2,1)S(1)}, u32[]{:S(2)}, u32[]{:S(2)}) collective-permute-start(bf16[2,64,640]{2,1,0:T(8,128)(2,1)S(1)} %get-tuple-element.101), channel_id=1, source_target_pairs={{0,8},{1,9},{2,10},{3,11},{4,12},{5,13},{6,14},{7,15},{8,0},{9,1},... | collective-permute-start | bytes 491528 | tf_op jit(solution)/shard_map/ppermute | solution.py:325
  44.6 4.3 %collective-permute-start.14 = (bf16[2,64,640]{2,1,0:T(8,128)(2,1)S(1)}, bf16[2,64,640]{2,1,0:T(8,128)(2,1)S(1)}, u32[]{:S(2)}, u32[]{:S(2)}) collective-permute-start(bf16[2,64,640]{2,1,0:T(8,128)(2,1)S(1)} %get-tuple-element.104.refs_0_), channel_id=1, source_target_pairs={{0,1},{1,0},{2,3},{3,2},{4,5},{5,4},{6,7},{7,6},{8,9},{9,8},{10,11... | collective-permute-start | bytes 491528 | tf_op jit(solution)/shard_map/ppermute | solution.py:325
  44.8 7.0 %collective-permute-start.20 = (bf16[2,64,256]{2,1,0:T(8,128)(2,1)S(1)}, bf16[2,64,256]{2,1,0:T(8,128)(2,1)S(1)}, u32[]{:S(2)}, u32[]{:S(2)}) collective-permute-start(bf16[2,64,256]{2,1,0:T(8,128)(2,1)S(1)} %get-tuple-element.111), channel_id=1, source_target_pairs={{0,6},{1,7},{2,4},{3,5},{4,2},{5,3},{6,0},{7,1},{8,14},{9,15},{10,... | collective-permute-start | bytes 196616 | tf_op jit(solution)/shard_map/ppermute | solution.py:325
  46.1 7.0 %collective-permute-start.19 = (bf16[2,64,256]{2,1,0:T(8,128)(2,1)S(1)}, bf16[2,64,256]{2,1,0:T(8,128)(2,1)S(1)}, u32[]{:S(2)}, u32[]{:S(2)}) collective-permute-start(bf16[2,64,256]{2,1,0:T(8,128)(2,1)S(1)} %get-tuple-element.110), channel_id=1, source_target_pairs={{0,4},{1,5},{2,6},{3,7},{4,0},{5,1},{6,2},{7,3},{8,12},{9,13},{10,... | collective-permute-start | bytes 196616 | tf_op jit(solution)/shard_map/ppermute | solution.py:325
  47.6 5.9 %collective-permute-start.18 = (bf16[2,64,256]{2,1,0:T(8,128)(2,1)S(1)}, bf16[2,64,256]{2,1,0:T(8,128)(2,1)S(1)}, u32[]{:S(2)}, u32[]{:S(2)}) collective-permute-start(bf16[2,64,256]{2,1,0:T(8,128)(2,1)S(1)} %get-tuple-element.109), channel_id=1, source_target_pairs={{0,2},{1,3},{2,0},{3,1},{4,6},{5,7},{6,4},{7,5},{8,10},{9,11},{10,... | collective-permute-start | bytes 196616 | tf_op jit(solution)/shard_map/ppermute | solution.py:325
  49.0 5.5 %collective-permute-start.17 = (bf16[2,64,256]{2,1,0:T(8,128)(2,1)S(1)}, bf16[2,64,256]{2,1,0:T(8,128)(2,1)S(1)}, u32[]{:S(2)}, u32[]{:S(2)}) collective-permute-start(bf16[2,64,256]{2,1,0:T(8,128)(2,1)S(1)} %get-tuple-element.107), channel_id=1, source_target_pairs={{0,6},{1,7},{2,4},{3,5},{4,2},{5,3},{6,0},{7,1},{8,14},{9,15},{10,... | collective-permute-start | bytes 196616 | tf_op jit(solution)/shard_map/ppermute | solution.py:325
  50.3 4.7 %collective-permute-start.16 = (bf16[2,64,256]{2,1,0:T(8,128)(2,1)S(1)}, bf16[2,64,256]{2,1,0:T(8,128)(2,1)S(1)}, u32[]{:S(2)}, u32[]{:S(2)}) collective-permute-start(bf16[2,64,256]{2,1,0:T(8,128)(2,1)S(1)} %get-tuple-element.106), channel_id=1, source_target_pairs={{0,4},{1,5},{2,6},{3,7},{4,0},{5,1},{6,2},{7,3},{8,12},{9,13},{10,... | collective-permute-start | bytes 196616 | tf_op jit(solution)/shard_map/ppermute | solution.py:325
  51.9 4.3 %collective-permute-start.15 = (bf16[2,64,256]{2,1,0:T(8,128)(2,1)S(1)}, bf16[2,64,256]{2,1,0:T(8,128)(2,1)S(1)}, u32[]{:S(2)}, u32[]{:S(2)}) collective-permute-start(bf16[2,64,256]{2,1,0:T(8,128)(2,1)S(1)} %get-tuple-element.105), channel_id=1, source_target_pairs={{0,2},{1,3},{2,0},{3,1},{4,6},{5,7},{6,4},{7,5},{8,10},{9,11},{10,... | collective-permute-start | bytes 196616 | tf_op jit(solution)/shard_map/ppermute | solution.py:325
  57.6 6.8 %collective-permute-start.23 = (bf16[4,64,256]{2,1,0:T(8,128)(2,1)S(1)}, bf16[4,64,256]{2,1,0:T(8,128)(2,1)S(1)}, u32[]{:S(2)}, u32[]{:S(2)}) collective-permute-start(bf16[4,64,256]{2,1,0:T(8,128)(2,1)S(1)} %mate_terms.15), channel_id=1, source_target_pairs={{0,6},{1,7},{2,4},{3,5},{4,2},{5,3},{6,0},{7,1},{8,14},{9,15},{10,... | collective-permute-start | bytes 393224 | tf_op jit(solution)/shard_map/ppermute | solution.py:325
  59.4 5.4 %collective-permute-start.22 = (bf16[4,64,256]{2,1,0:T(8,128)(2,1)S(1)}, bf16[4,64,256]{2,1,0:T(8,128)(2,1)S(1)}, u32[]{:S(2)}, u32[]{:S(2)}) collective-permute-start(bf16[4,64,256]{2,1,0:T(8,128)(2,1)S(1)} %mate_terms.14), channel_id=1, source_target_pairs={{0,4},{1,5},{2,6},{3,7},{4,0},{5,1},{6,2},{7,3},{8,12},{9,13},{10,... | collective-permute-start | bytes 393224 | tf_op jit(solution)/shard_map/ppermute | solution.py:325
  61.2 5.0 %collective-permute-start.21 = (bf16[4,64,256]{2,1,0:T(8,128)(2,1)S(1)}, bf16[4,64,256]{2,1,0:T(8,128)(2,1)S(1)}, u32[]{:S(2)}, u32[]{:S(2)}) collective-permute-start(bf16[4,64,256]{2,1,0:T(8,128)(2,1)S(1)} %mate_terms.13), channel_id=1, source_target_pairs={{0,2},{1,3},{2,0},{3,1},{4,6},{5,7},{6,4},{7,5},{8,10},{9,11},{10,... | collective-permute-start | bytes 393224 | tf_op jit(solution)/shard_map/ppermute | solution.py:325
  66.6 1.5 %collective-permute-start.24 = (bf16[2,64,640]{2,1,0:T(8,128)(2,1)S(1)}, bf16[2,64,640]{2,1,0:T(8,128)(2,1)S(1)}, u32[]{:S(2)}, u32[]{:S(2)}) collective-permute-start(bf16[2,64,640]{2,1,0:T(8,128)(2,1)S(1)} %mates_sum.6.refs_4_), channel_id=1, source_target_pairs={{0,1},{1,0},{2,3},{3,2},{4,5},{5,4},{6,7},{7,6},{8,9},{9,8},{10,11... | collective-permute-start | bytes 491528 | tf_op jit(solution)/shard_map/ppermute | solution.py:325
  68.0 7.2 %collective-permute-start.25 = (bf16[64,640]{1,0:T(8,128)(2,1)S(1)}, bf16[64,640]{1,0:T(8,128)(2,1)S(1)}, u32[]{:S(2)}, u32[]{:S(2)}) collective-permute-start(bf16[64,640]{1,0:T(8,128)(2,1)S(1)} %fusion.6), channel_id=1, source_target_pairs={{0,8},{1,9},{2,10},{3,11},{4,12},{5,13},{6,14},{7,15},{8,0},{9,1},... | collective-permute-start | bytes 245768 | tf_op jit(solution)/shard_map/ppermute | solution.py:325

commit v13 on v12

--- a/solution.py
+++ b/solution.py
@@ -23,12 +23,18 @@
     return lax.dot_general(a, b, dims, preferred_element_type=jnp.float32)
 
 
-def split3(x):
+def stacked3(x):
     hi = x.astype(jnp.bfloat16)
     rest = x - hi.astype(jnp.float32)
     mid = rest.astype(jnp.bfloat16)
     lo = (rest - mid.astype(jnp.float32)).astype(jnp.bfloat16)
-    return hi, mid, lo
+    return jnp.concatenate([hi, mid, lo], axis=0)
+
+
+def dot3(parts, b):
+    products = dot(parts, b, NN)
+    rows = parts.shape[0] // 3
+    return products[:rows] + (products[rows:2 * rows] + products[2 * rows:])
 
 
 def low_half(rows):
@@ -154,8 +160,7 @@
     old = samples[...]
     old_bf16 = old.astype(jnp.bfloat16)
     total = gradient[...]
-    for part in split3(gram[...]):
-        total -= dot(part, old_bf16, NN)
+    total -= dot3(stacked3(gram[...]), old_bf16)
     new = (1.0 - weight_decay) * old + sample_step * total
     *full, last = outs
     rounded = new.astype(jnp.bfloat16)
@@ -171,12 +176,11 @@
     packets, terms = refs[:-1], refs[-1]
     pos = pos_ref[0]
     width = terms.shape[2]
-    parts = split3(gram[...])
+    parts = stacked3(gram[...])
     for packet, group in zip(packets, groups):
         for i, t in enumerate(group):
             term = dot(samples[...], geno[:, columns_of(pos, turns[t], mate, width)], NN)
-            for part in parts:
-                term -= dot(part, packet[i], NN)
+            term -= dot3(parts, packet[i])
             terms[t] = term.astype(jnp.bfloat16)
 
 

time: 76.2 us -> 75.8 us (level)
  no operation moved by 1% of the time
where the time goes in v13:
time: 75.8 us; the launch traced here: 75.6 us
  starting transfers between devices  30.8 us (41%)
  waiting for transfers between devices  22.7 us (30%)
  Pallas kernels  19.4 us (26%)
  other arithmetic  1.65 us (2%)
  between operations  0.96 us (1%)
    ppermute x26, starting transfers between devices, swap(): return lax.ppermute(x, 'rows', [(r, r ^ turn) for r in range(devices)])  30.8 us
    ppermute x26, waiting for transfers between devices, swap(): return lax.ppermute(x, 'rows', [(r, r ^ turn) for r in range(devices)])  22.7 us
    pallas_call x16, Pallas kernels, product(): pl.pallas_call(functools.partial(product_kernel, [turns[t] for t in group...  7.44 us
    pallas_call x8, Pallas kernels, terms_for(): pl.pallas_call(functools.partial(term_kernel, turns, groups, mate), out_s...  4.37 us
    pallas_call x1, Pallas kernels, on_device(): pl.pallas_call(functools.partial(load_kernel, turns, per_owner, own_block...  3.51 us
    pallas_call x3, Pallas kernels, sample_update(): pl.pallas_call(functools.partial(sample_kernel, sample_step), out_shape=o...  1.74 us
  transfers between devices with their start and end apart: 26, of which 14 were waited for; matrix products, arithmetic and copies ran while one was open for 0% of the time, Pallas kernels for 21%

profile of v13, /device:TPU:0, one launch (start us, length us, event | category | flops | bytes accessed | tf_op | source)
XLA Modules:
  0.0 75.6 jit_solution(5950238637793402227)
XLA Ops:
  0.6 0.9 %bitcast_convert_fusion.refs_0_ = bf16[64,640]{1,0:T(8,128)(2,1)S(1)} fusion(f32[640,64]{0,1:T(8,128)} %param.6), kind=kLoop, calls=%fused_computation.9 | loop fusion | flops 40960 | bytes 245760 | tf_op jit(solution)/shard_map/convert_element_type | solution.py:339
  1.6 4.1 %collective-permute-start = (bf16[64,640]{1,0:T(8,128)(2,1)S(1)}, bf16[64,640]{1,0:T(8,128)(2,1)S(1)}, u32[]{:S(2)}, u32[]{:S(2)}) collective-permute-start(bf16[64,640]{1,0:T(8,128)(2,1)S(1)} %bitcast_convert_fusion.refs_0_), channel_id=1, source_target_pairs={{0,8},{1,9},{2,10},{3,11},{4,12},{5,13},{6,14},{7,15},{8,0},{9,1},... | collective-permute-start | bytes 245768 | tf_op jit(solution)/shard_map/ppermute | solution.py:329
  5.7 3.5 %load_batch.1 = (bf16[1024,4096]{1,0:T(8,128)(2,1)S(1)}, f32[64,1024]{1,0:T(8,128)S(1)}, s32[16,4]{1,0:T(8,128)S(4)}) custom-call(s32[1]{0:T(128)} %bitcast.pos_ref, s32[16,64]{1,0:T(8,128)} %cov.3, bf16[1024,4096]{1,0:T(8,128)(2,1)} %geno.1, f32[64,1024]{1,0:T(8,128)} %bitcast.20), custom_call_target="tpu_custom_call" | custom-call | bytes 8388608 | tf_op jit(solution)/shard_map/load_batch/pallas_call | solution.py:219
  9.2 0.7 collective-permute-done.refs_0_.other_snps
  10.0 2.5 %collective-permute-start.8 = (bf16[2,64,256]{2,1,0:T(8,128)(2,1)S(1)}, bf16[2,64,256]{2,1,0:T(8,128)(2,1)S(1)}, u32[]{:S(2)}, u32[]{:S(2)}) collective-permute-start(bf16[2,64,256]{2,1,0:T(8,128)(2,1)S(1)} %get-tuple-element.78), channel_id=1, source_target_pairs={{0,6},{1,7},{2,4},{3,5},{4,2},{5,3},{6,0},{7,1},{8,14},{9,15},{10,... | collective-permute-start | bytes 196616 | tf_op jit(solution)/shard_map/ppermute | solution.py:329
  12.5 0.7 collective-permute-start.7
  14.2 2.5 %collective-permute-start.4 = (bf16[2,64,256]{2,1,0:T(8,128)(2,1)S(1)}, bf16[2,64,256]{2,1,0:T(8,128)(2,1)S(1)}, u32[]{:S(2)}, u32[]{:S(2)}) collective-permute-start(bf16[2,64,256]{2,1,0:T(8,128)(2,1)S(1)} %get-tuple-element.74), channel_id=1, source_target_pairs={{0,6},{1,7},{2,4},{3,5},{4,2},{5,3},{6,0},{7,1},{8,14},{9,15},{10,... | collective-permute-start | bytes 196616 | tf_op jit(solution)/shard_map/ppermute | solution.py:329
  16.7 0.7 collective-permute-start.3
  20.2 0.8 %collective-permute-done.3.packet.refs_1_ = bf16[2,64,256]{2,1,0:T(8,128)(2,1)S(1)} collective-permute-done((bf16[2,64,256]{2,1,0:T(8,128)(2,1)S(1)}, bf16[2,64,256]{2,1,0:T(8,128)(2,1)S(1)}, u32[]{:S(2)}, u32[]{:S(2)}) %collective-permute-start.3) | collective-permute-done | bytes 65568 | tf_op jit(solution)/shard_map/ppermute | solution.py:329
  23.2 1.4 %collective-permute-start.11 = (bf16[4,64,256]{2,1,0:T(8,128)(2,1)S(1)}, bf16[4,64,256]{2,1,0:T(8,128)(2,1)S(1)}, u32[]{:S(2)}, u32[]{:S(2)}) collective-permute-start(bf16[4,64,256]{2,1,0:T(8,128)(2,1)S(1)} %mate_terms.11), channel_id=1, source_target_pairs={{0,6},{1,7},{2,4},{3,5},{4,2},{5,3},{6,0},{7,1},{8,14},{9,15},{10,... | collective-permute-start | bytes 393224 | tf_op jit(solution)/shard_map/ppermute | solution.py:329
  25.2 0.8 %collective-permute-start.10 = (bf16[4,64,256]{2,1,0:T(8,128)(2,1)S(1)}, bf16[4,64,256]{2,1,0:T(8,128)(2,1)S(1)}, u32[]{:S(2)}, u32[]{:S(2)}) collective-permute-start(bf16[4,64,256]{2,1,0:T(8,128)(2,1)S(1)} %mate_terms.10), channel_id=1, source_target_pairs={{0,4},{1,5},{2,6},{3,7},{4,0},{5,1},{6,2},{7,3},{8,12},{9,13},{10,... | collective-permute-start | bytes 393224 | tf_op jit(solution)/shard_map/ppermute | solution.py:329
  26.5 1.5 %collective-permute-start.9 = (bf16[4,64,256]{2,1,0:T(8,128)(2,1)S(1)}, bf16[4,64,256]{2,1,0:T(8,128)(2,1)S(1)}, u32[]{:S(2)}, u32[]{:S(2)}) collective-permute-start(bf16[4,64,256]{2,1,0:T(8,128)(2,1)S(1)} %mate_terms.9), channel_id=1, source_target_pairs={{0,2},{1,3},{2,0},{3,1},{4,6},{5,7},{6,4},{7,5},{8,10},{9,11},{10,... | collective-permute-start | bytes 393224 | tf_op jit(solution)/shard_map/ppermute | solution.py:329
  28.5 1.2 %collective-permute-done.11.refs_3_ = bf16[4,64,256]{2,1,0:T(8,128)(2,1)S(1)} collective-permute-done((bf16[4,64,256]{2,1,0:T(8,128)(2,1)S(1)}, bf16[4,64,256]{2,1,0:T(8,128)(2,1)S(1)}, u32[]{:S(2)}, u32[]{:S(2)}) %collective-permute-start.11) | collective-permute-done | bytes 131104 | tf_op jit(solution)/shard_map/ppermute | solution.py:329
  30.4 1.3 %collective-permute-done.9.refs_1_ = bf16[4,64,256]{2,1,0:T(8,128)(2,1)S(1)} collective-permute-done((bf16[4,64,256]{2,1,0:T(8,128)(2,1)S(1)}, bf16[4,64,256]{2,1,0:T(8,128)(2,1)S(1)}, u32[]{:S(2)}, u32[]{:S(2)}) %collective-permute-start.9) | collective-permute-done | bytes 131104 | tf_op jit(solution)/shard_map/ppermute | solution.py:329
  32.5 1.0 %collective-permute-done.12.arrived = bf16[2,64,640]{2,1,0:T(8,128)(2,1)S(1)} collective-permute-done((bf16[2,64,640]{2,1,0:T(8,128)(2,1)S(1)}, bf16[2,64,640]{2,1,0:T(8,128)(2,1)S(1)}, u32[]{:S(2)}, u32[]{:S(2)}) %collective-permute-start.12) | collective-permute-done | bytes 163872 | tf_op jit(solution)/shard_map/ppermute | solution.py:329
  33.5 2.4 %collective-permute-start.13 = (bf16[2,64,640]{2,1,0:T(8,128)(2,1)S(1)}, bf16[2,64,640]{2,1,0:T(8,128)(2,1)S(1)}, u32[]{:S(2)}, u32[]{:S(2)}) collective-permute-start(bf16[2,64,640]{2,1,0:T(8,128)(2,1)S(1)} %get-tuple-element.101), channel_id=1, source_target_pairs={{0,8},{1,9},{2,10},{3,11},{4,12},{5,13},{6,14},{7,15},{8,0},{9,1},... | collective-permute-start | bytes 491528 | tf_op jit(solution)/shard_map/ppermute | solution.py:329
  36.1 8.1 %collective-permute-done.13.arrived = bf16[2,64,640]{2,1,0:T(8,128)(2,1)S(1)} collective-permute-done((bf16[2,64,640]{2,1,0:T(8,128)(2,1)S(1)}, bf16[2,64,640]{2,1,0:T(8,128)(2,1)S(1)}, u32[]{:S(2)}, u32[]{:S(2)}) %collective-permute-start.13) | collective-permute-done | bytes 163872 | tf_op jit(solution)/shard_map/ppermute | solution.py:329
  44.6 1.3 %collective-permute-start.20 = (bf16[2,64,256]{2,1,0:T(8,128)(2,1)S(1)}, bf16[2,64,256]{2,1,0:T(8,128)(2,1)S(1)}, u32[]{:S(2)}, u32[]{:S(2)}) collective-permute-start(bf16[2,64,256]{2,1,0:T(8,128)(2,1)S(1)} %get-tuple-element.111), channel_id=1, source_target_pairs={{0,6},{1,7},{2,4},{3,5},{4,2},{5,3},{6,0},{7,1},{8,14},{9,15},{10,... | collective-permute-start | bytes 196616 | tf_op jit(solution)/shard_map/ppermute | solution.py:329
  45.9 1.6 %collective-permute-start.19 = (bf16[2,64,256]{2,1,0:T(8,128)(2,1)S(1)}, bf16[2,64,256]{2,1,0:T(8,128)(2,1)S(1)}, u32[]{:S(2)}, u32[]{:S(2)}) collective-permute-start(bf16[2,64,256]{2,1,0:T(8,128)(2,1)S(1)} %get-tuple-element.110), channel_id=1, source_target_pairs={{0,4},{1,5},{2,6},{3,7},{4,0},{5,1},{6,2},{7,3},{8,12},{9,13},{10,... | collective-permute-start | bytes 196616 | tf_op jit(solution)/shard_map/ppermute | solution.py:329
  47.4 0.7 collective-permute-start.18
  48.8 1.3 %collective-permute-start.17 = (bf16[2,64,256]{2,1,0:T(8,128)(2,1)S(1)}, bf16[2,64,256]{2,1,0:T(8,128)(2,1)S(1)}, u32[]{:S(2)}, u32[]{:S(2)}) collective-permute-start(bf16[2,64,256]{2,1,0:T(8,128)(2,1)S(1)} %get-tuple-element.107), channel_id=1, source_target_pairs={{0,6},{1,7},{2,4},{3,5},{4,2},{5,3},{6,0},{7,1},{8,14},{9,15},{10,... | collective-permute-start | bytes 196616 | tf_op jit(solution)/shard_map/ppermute | solution.py:329
  50.1 1.6 %collective-permute-start.16 = (bf16[2,64,256]{2,1,0:T(8,128)(2,1)S(1)}, bf16[2,64,256]{2,1,0:T(8,128)(2,1)S(1)}, u32[]{:S(2)}, u32[]{:S(2)}) collective-permute-start(bf16[2,64,256]{2,1,0:T(8,128)(2,1)S(1)} %get-tuple-element.106), channel_id=1, source_target_pairs={{0,4},{1,5},{2,6},{3,7},{4,0},{5,1},{6,2},{7,3},{8,12},{9,13},{10,... | collective-permute-start | bytes 196616 | tf_op jit(solution)/shard_map/ppermute | solution.py:329
  51.6 0.7 collective-permute-start.15
  57.4 1.1 %collective-permute-start.23 = (bf16[4,64,256]{2,1,0:T(8,128)(2,1)S(1)}, bf16[4,64,256]{2,1,0:T(8,128)(2,1)S(1)}, u32[]{:S(2)}, u32[]{:S(2)}) collective-permute-start(bf16[4,64,256]{2,1,0:T(8,128)(2,1)S(1)} %mate_terms.15), channel_id=1, source_target_pairs={{0,6},{1,7},{2,4},{3,5},{4,2},{5,3},{6,0},{7,1},{8,14},{9,15},{10,... | collective-permute-start | bytes 393224 | tf_op jit(solution)/shard_map/ppermute | solution.py:329
  59.0 1.2 %collective-permute-start.22 = (bf16[4,64,256]{2,1,0:T(8,128)(2,1)S(1)}, bf16[4,64,256]{2,1,0:T(8,128)(2,1)S(1)}, u32[]{:S(2)}, u32[]{:S(2)}) collective-permute-start(bf16[4,64,256]{2,1,0:T(8,128)(2,1)S(1)} %mate_terms.14), channel_id=1, source_target_pairs={{0,4},{1,5},{2,6},{3,7},{4,0},{5,1},{6,2},{7,3},{8,12},{9,13},{10,... | collective-permute-start | bytes 393224 | tf_op jit(solution)/shard_map/ppermute | solution.py:329
  60.8 1.4 %collective-permute-start.21 = (bf16[4,64,256]{2,1,0:T(8,128)(2,1)S(1)}, bf16[4,64,256]{2,1,0:T(8,128)(2,1)S(1)}, u32[]{:S(2)}, u32[]{:S(2)}) collective-permute-start(bf16[4,64,256]{2,1,0:T(8,128)(2,1)S(1)} %mate_terms.13), channel_id=1, source_target_pairs={{0,2},{1,3},{2,0},{3,1},{4,6},{5,7},{6,4},{7,5},{8,10},{9,11},{10,... | collective-permute-start | bytes 393224 | tf_op jit(solution)/shard_map/ppermute | solution.py:329
  62.1 0.9 %sample_update.4 = (f32[64,1024]{1,0:T(8,128)}, f32[8,128]{1,0:T(8,128)S(1)}) custom-call(f32[64,1024]{1,0:T(8,128)S(1)} %get-tuple-element.96.samples, f32[64,1024]{1,0:T(8,128)S(1)} %get-tuple-element.127.gradient, f32[64,64]{1,0:T(8,128)S(1)} %get-tuple-element.128.gram), custom_call_target="tpu_custom_call" | custom-call | bytes 2097152 | tf_op jit(solution)/shard_map/sample_update/pallas_call | solution.py:306
  64.5 1.3 %collective-permute-done.21.refs_1_ = bf16[4,64,256]{2,1,0:T(8,128)(2,1)S(1)} collective-permute-done((bf16[4,64,256]{2,1,0:T(8,128)(2,1)S(1)}, bf16[4,64,256]{2,1,0:T(8,128)(2,1)S(1)}, u32[]{:S(2)}, u32[]{:S(2)}) %collective-permute-start.21) | collective-permute-done | bytes 131104 | tf_op jit(solution)/shard_map/ppermute | solution.py:329
  66.6 1.0 %collective-permute-done.24 = bf16[2,64,640]{2,1,0:T(8,128)(2,1)S(1)} collective-permute-done((bf16[2,64,640]{2,1,0:T(8,128)(2,1)S(1)}, bf16[2,64,640]{2,1,0:T(8,128)(2,1)S(1)}, u32[]{:S(2)}, u32[]{:S(2)}) %collective-permute-start.24) | collective-permute-done | bytes 163872 | tf_op jit(solution)/shard_map/ppermute | solution.py:329
  67.6 2.4 %collective-permute-start.25 = (bf16[64,640]{1,0:T(8,128)(2,1)S(1)}, bf16[64,640]{1,0:T(8,128)(2,1)S(1)}, u32[]{:S(2)}, u32[]{:S(2)}) collective-permute-start(bf16[64,640]{1,0:T(8,128)(2,1)S(1)} %fusion.6), channel_id=1, source_target_pairs={{0,8},{1,9},{2,10},{3,11},{4,12},{5,13},{6,14},{7,15},{8,0},{9,1},... | collective-permute-start | bytes 245768 | tf_op jit(solution)/shard_map/ppermute | solution.py:329
  70.1 4.8 %collective-permute-done.25 = bf16[64,640]{1,0:T(8,128)(2,1)S(1)} collective-permute-done((bf16[64,640]{1,0:T(8,128)(2,1)S(1)}, bf16[64,640]{1,0:T(8,128)(2,1)S(1)}, u32[]{:S(2)}, u32[]{:S(2)}) %collective-permute-start.25) | collective-permute-done | bytes 81952 | tf_op jit(solution)/shard_map/ppermute | solution.py:329
  74.8 0.7 fusion.5
  (66 shorter events, 18.3 us)
Async XLA Ops:
  1.6 8.3 %collective-permute-start = (bf16[64,640]{1,0:T(8,128)(2,1)S(1)}, bf16[64,640]{1,0:T(8,128)(2,1)S(1)}, u32[]{:S(2)}, u32[]{:S(2)}) collective-permute-start(bf16[64,640]{1,0:T(8,128)(2,1)S(1)} %bitcast_convert_fusion.refs_0_), channel_id=1, source_target_pairs={{0,8},{1,9},{2,10},{3,11},{4,12},{5,13},{6,14},{7,15},{8,0},{9,1},... | collective-permute-start | bytes 245768 | tf_op jit(solution)/shard_map/ppermute | solution.py:329
  5.7 4.2 %collective-permute-start.5 = (bf16[64,640]{1,0:T(8,128)(2,1)S(1)}, bf16[64,640]{1,0:T(8,128)(2,1)S(1)}, u32[]{:S(2)}, u32[]{:S(2)}) collective-permute-start(bf16[64,640]{1,0:T(8,128)(2,1)S(1)} %bitcast_convert_fusion.refs_0_), channel_id=1, source_target_pairs={{0,1},{1,0},{2,3},{3,2},{4,5},{5,4},{6,7},{7,6},{8,9},{9,8},{10,11... | collective-permute-start | bytes 245768 | tf_op jit(solution)/shard_map/ppermute | solution.py:329
  9.9 4.2 %collective-permute-start.1 = (bf16[64,640]{1,0:T(8,128)(2,1)S(1)}, bf16[64,640]{1,0:T(8,128)(2,1)S(1)}, u32[]{:S(2)}, u32[]{:S(2)}) collective-permute-start(bf16[64,640]{1,0:T(8,128)(2,1)S(1)} %collective-permute-done.refs_0_.other_snps), channel_id=1, source_target_pairs={{0,1},{1,0},{2,3},{3,2},{4,5},{5,4},{6,7},{7,6},{8,9},{9,8},{10,11... | collective-permute-start | bytes 245768 | tf_op jit(solution)/shard_map/ppermute | solution.py:329
  10.0 7.4 %collective-permute-start.8 = (bf16[2,64,256]{2,1,0:T(8,128)(2,1)S(1)}, bf16[2,64,256]{2,1,0:T(8,128)(2,1)S(1)}, u32[]{:S(2)}, u32[]{:S(2)}) collective-permute-start(bf16[2,64,256]{2,1,0:T(8,128)(2,1)S(1)} %get-tuple-element.78), channel_id=1, source_target_pairs={{0,6},{1,7},{2,4},{3,5},{4,2},{5,3},{6,0},{7,1},{8,14},{9,15},{10,... | collective-permute-start | bytes 196616 | tf_op jit(solution)/shard_map/ppermute | solution.py:329
  12.5 5.7 %collective-permute-start.7 = (bf16[2,64,256]{2,1,0:T(8,128)(2,1)S(1)}, bf16[2,64,256]{2,1,0:T(8,128)(2,1)S(1)}, u32[]{:S(2)}, u32[]{:S(2)}) collective-permute-start(bf16[2,64,256]{2,1,0:T(8,128)(2,1)S(1)} %get-tuple-element.77), channel_id=1, source_target_pairs={{0,4},{1,5},{2,6},{3,7},{4,0},{5,1},{6,2},{7,3},{8,12},{9,13},{10,... | collective-permute-start | bytes 196616 | tf_op jit(solution)/shard_map/ppermute | solution.py:329
  13.3 5.5 %collective-permute-start.6 = (bf16[2,64,256]{2,1,0:T(8,128)(2,1)S(1)}, bf16[2,64,256]{2,1,0:T(8,128)(2,1)S(1)}, u32[]{:S(2)}, u32[]{:S(2)}) collective-permute-start(bf16[2,64,256]{2,1,0:T(8,128)(2,1)S(1)} %get-tuple-element.76), channel_id=1, source_target_pairs={{0,2},{1,3},{2,0},{3,1},{4,6},{5,7},{6,4},{7,5},{8,10},{9,11},{10,... | collective-permute-start | bytes 196616 | tf_op jit(solution)/shard_map/ppermute | solution.py:329
  14.2 5.5 %collective-permute-start.4 = (bf16[2,64,256]{2,1,0:T(8,128)(2,1)S(1)}, bf16[2,64,256]{2,1,0:T(8,128)(2,1)S(1)}, u32[]{:S(2)}, u32[]{:S(2)}) collective-permute-start(bf16[2,64,256]{2,1,0:T(8,128)(2,1)S(1)} %get-tuple-element.74), channel_id=1, source_target_pairs={{0,6},{1,7},{2,4},{3,5},{4,2},{5,3},{6,0},{7,1},{8,14},{9,15},{10,... | collective-permute-start | bytes 196616 | tf_op jit(solution)/shard_map/ppermute | solution.py:329
  16.7 4.3 %collective-permute-start.3 = (bf16[2,64,256]{2,1,0:T(8,128)(2,1)S(1)}, bf16[2,64,256]{2,1,0:T(8,128)(2,1)S(1)}, u32[]{:S(2)}, u32[]{:S(2)}) collective-permute-start(bf16[2,64,256]{2,1,0:T(8,128)(2,1)S(1)} %get-tuple-element.73), channel_id=1, source_target_pairs={{0,4},{1,5},{2,6},{3,7},{4,0},{5,1},{6,2},{7,3},{8,12},{9,13},{10,... | collective-permute-start | bytes 196616 | tf_op jit(solution)/shard_map/ppermute | solution.py:329
  17.5 4.3 %collective-permute-start.2 = (bf16[2,64,256]{2,1,0:T(8,128)(2,1)S(1)}, bf16[2,64,256]{2,1,0:T(8,128)(2,1)S(1)}, u32[]{:S(2)}, u32[]{:S(2)}) collective-permute-start(bf16[2,64,256]{2,1,0:T(8,128)(2,1)S(1)} %get-tuple-element.72), channel_id=1, source_target_pairs={{0,2},{1,3},{2,0},{3,1},{4,6},{5,7},{6,4},{7,5},{8,10},{9,11},{10,... | collective-permute-start | bytes 196616 | tf_op jit(solution)/shard_map/ppermute | solution.py:329
  23.2 6.5 %collective-permute-start.11 = (bf16[4,64,256]{2,1,0:T(8,128)(2,1)S(1)}, bf16[4,64,256]{2,1,0:T(8,128)(2,1)S(1)}, u32[]{:S(2)}, u32[]{:S(2)}) collective-permute-start(bf16[4,64,256]{2,1,0:T(8,128)(2,1)S(1)} %mate_terms.11), channel_id=1, source_target_pairs={{0,6},{1,7},{2,4},{3,5},{4,2},{5,3},{6,0},{7,1},{8,14},{9,15},{10,... | collective-permute-start | bytes 393224 | tf_op jit(solution)/shard_map/ppermute | solution.py:329
  25.1 10.8 %copy-start.1 = (s32[16,64]{1,0:T(8,128)S(1)}, s32[16,64]{1,0:T(8,128)}, u32[]{:S(2)}) copy-start(s32[16,64]{1,0:T(8,128)} %cov.3) | copy-start | bytes 12292
  25.2 19.1 %copy-start = (f32[640,64]{0,1:T(8,128)S(1)}, f32[640,64]{0,1:T(8,128)}, u32[]{:S(2)}) copy-start(f32[640,64]{0,1:T(8,128)} %param.6) | copy-start | bytes 491524
  25.2 5.2 %collective-permute-start.10 = (bf16[4,64,256]{2,1,0:T(8,128)(2,1)S(1)}, bf16[4,64,256]{2,1,0:T(8,128)(2,1)S(1)}, u32[]{:S(2)}, u32[]{:S(2)}) collective-permute-start(bf16[4,64,256]{2,1,0:T(8,128)(2,1)S(1)} %mate_terms.10), channel_id=1, source_target_pairs={{0,4},{1,5},{2,6},{3,7},{4,0},{5,1},{6,2},{7,3},{8,12},{9,13},{10,... | collective-permute-start | bytes 393224 | tf_op jit(solution)/shard_map/ppermute | solution.py:329
  26.5 5.1 %collective-permute-start.9 = (bf16[4,64,256]{2,1,0:T(8,128)(2,1)S(1)}, bf16[4,64,256]{2,1,0:T(8,128)(2,1)S(1)}, u32[]{:S(2)}, u32[]{:S(2)}) collective-permute-start(bf16[4,64,256]{2,1,0:T(8,128)(2,1)S(1)} %mate_terms.9), channel_id=1, source_target_pairs={{0,2},{1,3},{2,0},{3,1},{4,6},{5,7},{6,4},{7,5},{8,10},{9,11},{10,... | collective-permute-start | bytes 393224 | tf_op jit(solution)/shard_map/ppermute | solution.py:329
  32.0 1.5 %collective-permute-start.12 = (bf16[2,64,640]{2,1,0:T(8,128)(2,1)S(1)}, bf16[2,64,640]{2,1,0:T(8,128)(2,1)S(1)}, u32[]{:S(2)}, u32[]{:S(2)}) collective-permute-start(bf16[2,64,640]{2,1,0:T(8,128)(2,1)S(1)} %mates_sum.4.refs_4_), channel_id=1, source_target_pairs={{0,1},{1,0},{2,3},{3,2},{4,5},{5,4},{6,7},{7,6},{8,9},{9,8},{10,11... | collective-permute-start | bytes 491528 | tf_op jit(solution)/shard_map/ppermute | solution.py:329
  33.5 10.7 %collective-permute-start.13 = (bf16[2,64,640]{2,1,0:T(8,128)(2,1)S(1)}, bf16[2,64,640]{2,1,0:T(8,128)(2,1)S(1)}, u32[]{:S(2)}, u32[]{:S(2)}) collective-permute-start(bf16[2,64,640]{2,1,0:T(8,128)(2,1)S(1)} %get-tuple-element.101), channel_id=1, source_target_pairs={{0,8},{1,9},{2,10},{3,11},{4,12},{5,13},{6,14},{7,15},{8,0},{9,1},... | collective-permute-start | bytes 491528 | tf_op jit(solution)/shard_map/ppermute | solution.py:329
  44.4 4.3 %collective-permute-start.14 = (bf16[2,64,640]{2,1,0:T(8,128)(2,1)S(1)}, bf16[2,64,640]{2,1,0:T(8,128)(2,1)S(1)}, u32[]{:S(2)}, u32[]{:S(2)}) collective-permute-start(bf16[2,64,640]{2,1,0:T(8,128)(2,1)S(1)} %get-tuple-element.104.refs_0_), channel_id=1, source_target_pairs={{0,1},{1,0},{2,3},{3,2},{4,5},{5,4},{6,7},{7,6},{8,9},{9,8},{10,11... | collective-permute-start | bytes 491528 | tf_op jit(solution)/shard_map/ppermute | solution.py:329
  44.6 7.0 %collective-permute-start.20 = (bf16[2,64,256]{2,1,0:T(8,128)(2,1)S(1)}, bf16[2,64,256]{2,1,0:T(8,128)(2,1)S(1)}, u32[]{:S(2)}, u32[]{:S(2)}) collective-permute-start(bf16[2,64,256]{2,1,0:T(8,128)(2,1)S(1)} %get-tuple-element.111), channel_id=1, source_target_pairs={{0,6},{1,7},{2,4},{3,5},{4,2},{5,3},{6,0},{7,1},{8,14},{9,15},{10,... | collective-permute-start | bytes 196616 | tf_op jit(solution)/shard_map/ppermute | solution.py:329
  45.9 7.0 %collective-permute-start.19 = (bf16[2,64,256]{2,1,0:T(8,128)(2,1)S(1)}, bf16[2,64,256]{2,1,0:T(8,128)(2,1)S(1)}, u32[]{:S(2)}, u32[]{:S(2)}) collective-permute-start(bf16[2,64,256]{2,1,0:T(8,128)(2,1)S(1)} %get-tuple-element.110), channel_id=1, source_target_pairs={{0,4},{1,5},{2,6},{3,7},{4,0},{5,1},{6,2},{7,3},{8,12},{9,13},{10,... | collective-permute-start | bytes 196616 | tf_op jit(solution)/shard_map/ppermute | solution.py:329
  47.4 5.9 %collective-permute-start.18 = (bf16[2,64,256]{2,1,0:T(8,128)(2,1)S(1)}, bf16[2,64,256]{2,1,0:T(8,128)(2,1)S(1)}, u32[]{:S(2)}, u32[]{:S(2)}) collective-permute-start(bf16[2,64,256]{2,1,0:T(8,128)(2,1)S(1)} %get-tuple-element.109), channel_id=1, source_target_pairs={{0,2},{1,3},{2,0},{3,1},{4,6},{5,7},{6,4},{7,5},{8,10},{9,11},{10,... | collective-permute-start | bytes 196616 | tf_op jit(solution)/shard_map/ppermute | solution.py:329
  48.8 5.5 %collective-permute-start.17 = (bf16[2,64,256]{2,1,0:T(8,128)(2,1)S(1)}, bf16[2,64,256]{2,1,0:T(8,128)(2,1)S(1)}, u32[]{:S(2)}, u32[]{:S(2)}) collective-permute-start(bf16[2,64,256]{2,1,0:T(8,128)(2,1)S(1)} %get-tuple-element.107), channel_id=1, source_target_pairs={{0,6},{1,7},{2,4},{3,5},{4,2},{5,3},{6,0},{7,1},{8,14},{9,15},{10,... | collective-permute-start | bytes 196616 | tf_op jit(solution)/shard_map/ppermute | solution.py:329
  50.1 4.7 %collective-permute-start.16 = (bf16[2,64,256]{2,1,0:T(8,128)(2,1)S(1)}, bf16[2,64,256]{2,1,0:T(8,128)(2,1)S(1)}, u32[]{:S(2)}, u32[]{:S(2)}) collective-permute-start(bf16[2,64,256]{2,1,0:T(8,128)(2,1)S(1)} %get-tuple-element.106), channel_id=1, source_target_pairs={{0,4},{1,5},{2,6},{3,7},{4,0},{5,1},{6,2},{7,3},{8,12},{9,13},{10,... | collective-permute-start | bytes 196616 | tf_op jit(solution)/shard_map/ppermute | solution.py:329
  51.6 4.3 %collective-permute-start.15 = (bf16[2,64,256]{2,1,0:T(8,128)(2,1)S(1)}, bf16[2,64,256]{2,1,0:T(8,128)(2,1)S(1)}, u32[]{:S(2)}, u32[]{:S(2)}) collective-permute-start(bf16[2,64,256]{2,1,0:T(8,128)(2,1)S(1)} %get-tuple-element.105), channel_id=1, source_target_pairs={{0,2},{1,3},{2,0},{3,1},{4,6},{5,7},{6,4},{7,5},{8,10},{9,11},{10,... | collective-permute-start | bytes 196616 | tf_op jit(solution)/shard_map/ppermute | solution.py:329
  57.4 6.7 %collective-permute-start.23 = (bf16[4,64,256]{2,1,0:T(8,128)(2,1)S(1)}, bf16[4,64,256]{2,1,0:T(8,128)(2,1)S(1)}, u32[]{:S(2)}, u32[]{:S(2)}) collective-permute-start(bf16[4,64,256]{2,1,0:T(8,128)(2,1)S(1)} %mate_terms.15), channel_id=1, source_target_pairs={{0,6},{1,7},{2,4},{3,5},{4,2},{5,3},{6,0},{7,1},{8,14},{9,15},{10,... | collective-permute-start | bytes 393224 | tf_op jit(solution)/shard_map/ppermute | solution.py:329
  59.0 5.5 %collective-permute-start.22 = (bf16[4,64,256]{2,1,0:T(8,128)(2,1)S(1)}, bf16[4,64,256]{2,1,0:T(8,128)(2,1)S(1)}, u32[]{:S(2)}, u32[]{:S(2)}) collective-permute-start(bf16[4,64,256]{2,1,0:T(8,128)(2,1)S(1)} %mate_terms.14), channel_id=1, source_target_pairs={{0,4},{1,5},{2,6},{3,7},{4,0},{5,1},{6,2},{7,3},{8,12},{9,13},{10,... | collective-permute-start | bytes 393224 | tf_op jit(solution)/shard_map/ppermute | solution.py:329
  60.8 5.0 %collective-permute-start.21 = (bf16[4,64,256]{2,1,0:T(8,128)(2,1)S(1)}, bf16[4,64,256]{2,1,0:T(8,128)(2,1)S(1)}, u32[]{:S(2)}, u32[]{:S(2)}) collective-permute-start(bf16[4,64,256]{2,1,0:T(8,128)(2,1)S(1)} %mate_terms.13), channel_id=1, source_target_pairs={{0,2},{1,3},{2,0},{3,1},{4,6},{5,7},{6,4},{7,5},{8,10},{9,11},{10,... | collective-permute-start | bytes 393224 | tf_op jit(solution)/shard_map/ppermute | solution.py:329
  66.2 1.5 %collective-permute-start.24 = (bf16[2,64,640]{2,1,0:T(8,128)(2,1)S(1)}, bf16[2,64,640]{2,1,0:T(8,128)(2,1)S(1)}, u32[]{:S(2)}, u32[]{:S(2)}) collective-permute-start(bf16[2,64,640]{2,1,0:T(8,128)(2,1)S(1)} %mates_sum.6.refs_4_), channel_id=1, source_target_pairs={{0,1},{1,0},{2,3},{3,2},{4,5},{5,4},{6,7},{7,6},{8,9},{9,8},{10,11... | collective-permute-start | bytes 491528 | tf_op jit(solution)/shard_map/ppermute | solution.py:329
  67.6 7.2 %collective-permute-start.25 = (bf16[64,640]{1,0:T(8,128)(2,1)S(1)}, bf16[64,640]{1,0:T(8,128)(2,1)S(1)}, u32[]{:S(2)}, u32[]{:S(2)}) collective-permute-start(bf16[64,640]{1,0:T(8,128)(2,1)S(1)} %fusion.6), channel_id=1, source_target_pairs={{0,8},{1,9},{2,10},{3,11},{4,12},{5,13},{6,14},{7,15},{8,0},{9,1},... | collective-permute-start | bytes 245768 | tf_op jit(solution)/shard_map/ppermute | solution.py:329

commit v14 on v13

--- a/solution.py
+++ b/solution.py
@@ -293,7 +293,7 @@
     def product(mate, group, panel, before, after):
         share = samples_here * snps_here // len(MATES) // 2
         return pl.pallas_call(
-            functools.partial(product_kernel, [turns[t] for t in group], mate, not before, 256),
+            functools.partial(product_kernel, [turns[t] for t in group], mate, not before, 512),
             out_shape=(by_samples, square),
             in_specs=[smem] + [vmem] * (2 + len(before)) + [anywhere] * len(after),
             out_specs=(vmem, vmem),

time: 75.8 us -> 75.8 us (level)
  no operation moved by 1% of the time
where the time goes in v14:
time: 75.8 us; the launch traced here: 75.6 us
  starting transfers between devices  30.8 us (41%)
  waiting for transfers between devices  22.8 us (30%)
  Pallas kernels  19.4 us (26%)
  other arithmetic  1.65 us (2%)
  between operations  0.97 us (1%)
    ppermute x26, starting transfers between devices, swap(): return lax.ppermute(x, 'rows', [(r, r ^ turn) for r in range(devices)])  30.8 us
    ppermute x26, waiting for transfers between devices, swap(): return lax.ppermute(x, 'rows', [(r, r ^ turn) for r in range(devices)])  22.8 us
    pallas_call x16, Pallas kernels, product(): pl.pallas_call(functools.partial(product_kernel, [turns[t] for t in group...  7.42 us
    pallas_call x8, Pallas kernels, terms_for(): pl.pallas_call(functools.partial(term_kernel, turns, groups, mate), out_s...  4.37 us
    pallas_call x1, Pallas kernels, on_device(): pl.pallas_call(functools.partial(load_kernel, turns, per_owner, own_block...  3.51 us
    pallas_call x3, Pallas kernels, sample_update(): pl.pallas_call(functools.partial(sample_kernel, sample_step), out_shape=o...  1.74 us
  transfers between devices with their start and end apart: 26, of which 14 were waited for; matrix products, arithmetic and copies ran while one was open for 0% of the time, Pallas kernels for 21%

profile of v14, /device:TPU:0, one launch (start us, length us, event | category | flops | bytes accessed | tf_op | source)
XLA Modules:
  0.0 75.6 jit_solution(3748099913447091613)
XLA Ops:
  0.6 0.9 %bitcast_convert_fusion.refs_0_ = bf16[64,640]{1,0:T(8,128)(2,1)S(1)} fusion(f32[640,64]{0,1:T(8,128)} %param.6), kind=kLoop, calls=%fused_computation.9 | loop fusion | flops 40960 | bytes 245760 | tf_op jit(solution)/shard_map/convert_element_type | solution.py:339
  1.6 4.1 %collective-permute-start = (bf16[64,640]{1,0:T(8,128)(2,1)S(1)}, bf16[64,640]{1,0:T(8,128)(2,1)S(1)}, u32[]{:S(2)}, u32[]{:S(2)}) collective-permute-start(bf16[64,640]{1,0:T(8,128)(2,1)S(1)} %bitcast_convert_fusion.refs_0_), channel_id=1, source_target_pairs={{0,8},{1,9},{2,10},{3,11},{4,12},{5,13},{6,14},{7,15},{8,0},{9,1},... | collective-permute-start | bytes 245768 | tf_op jit(solution)/shard_map/ppermute | solution.py:329
  5.7 3.5 %load_batch.1 = (bf16[1024,4096]{1,0:T(8,128)(2,1)S(1)}, f32[64,1024]{1,0:T(8,128)S(1)}, s32[16,4]{1,0:T(8,128)S(4)}) custom-call(s32[1]{0:T(128)} %bitcast.pos_ref, s32[16,64]{1,0:T(8,128)} %cov.3, bf16[1024,4096]{1,0:T(8,128)(2,1)} %geno.1, f32[64,1024]{1,0:T(8,128)} %bitcast.20), custom_call_target="tpu_custom_call" | custom-call | bytes 8388608 | tf_op jit(solution)/shard_map/load_batch/pallas_call | solution.py:219
  9.2 0.7 collective-permute-done.refs_0_.other_snps
  10.0 2.5 %collective-permute-start.8 = (bf16[2,64,256]{2,1,0:T(8,128)(2,1)S(1)}, bf16[2,64,256]{2,1,0:T(8,128)(2,1)S(1)}, u32[]{:S(2)}, u32[]{:S(2)}) collective-permute-start(bf16[2,64,256]{2,1,0:T(8,128)(2,1)S(1)} %get-tuple-element.78), channel_id=1, source_target_pairs={{0,6},{1,7},{2,4},{3,5},{4,2},{5,3},{6,0},{7,1},{8,14},{9,15},{10,... | collective-permute-start | bytes 196616 | tf_op jit(solution)/shard_map/ppermute | solution.py:329
  12.5 0.7 collective-permute-start.7
  14.2 2.5 %collective-permute-start.4 = (bf16[2,64,256]{2,1,0:T(8,128)(2,1)S(1)}, bf16[2,64,256]{2,1,0:T(8,128)(2,1)S(1)}, u32[]{:S(2)}, u32[]{:S(2)}) collective-permute-start(bf16[2,64,256]{2,1,0:T(8,128)(2,1)S(1)} %get-tuple-element.74), channel_id=1, source_target_pairs={{0,6},{1,7},{2,4},{3,5},{4,2},{5,3},{6,0},{7,1},{8,14},{9,15},{10,... | collective-permute-start | bytes 196616 | tf_op jit(solution)/shard_map/ppermute | solution.py:329
  16.7 0.7 collective-permute-start.3
  20.2 0.8 %collective-permute-done.3.packet.refs_1_ = bf16[2,64,256]{2,1,0:T(8,128)(2,1)S(1)} collective-permute-done((bf16[2,64,256]{2,1,0:T(8,128)(2,1)S(1)}, bf16[2,64,256]{2,1,0:T(8,128)(2,1)S(1)}, u32[]{:S(2)}, u32[]{:S(2)}) %collective-permute-start.3) | collective-permute-done | bytes 65568 | tf_op jit(solution)/shard_map/ppermute | solution.py:329
  23.2 1.4 %collective-permute-start.11 = (bf16[4,64,256]{2,1,0:T(8,128)(2,1)S(1)}, bf16[4,64,256]{2,1,0:T(8,128)(2,1)S(1)}, u32[]{:S(2)}, u32[]{:S(2)}) collective-permute-start(bf16[4,64,256]{2,1,0:T(8,128)(2,1)S(1)} %mate_terms.11), channel_id=1, source_target_pairs={{0,6},{1,7},{2,4},{3,5},{4,2},{5,3},{6,0},{7,1},{8,14},{9,15},{10,... | collective-permute-start | bytes 393224 | tf_op jit(solution)/shard_map/ppermute | solution.py:329
  25.2 0.8 %collective-permute-start.10 = (bf16[4,64,256]{2,1,0:T(8,128)(2,1)S(1)}, bf16[4,64,256]{2,1,0:T(8,128)(2,1)S(1)}, u32[]{:S(2)}, u32[]{:S(2)}) collective-permute-start(bf16[4,64,256]{2,1,0:T(8,128)(2,1)S(1)} %mate_terms.10), channel_id=1, source_target_pairs={{0,4},{1,5},{2,6},{3,7},{4,0},{5,1},{6,2},{7,3},{8,12},{9,13},{10,... | collective-permute-start | bytes 393224 | tf_op jit(solution)/shard_map/ppermute | solution.py:329
  26.5 1.5 %collective-permute-start.9 = (bf16[4,64,256]{2,1,0:T(8,128)(2,1)S(1)}, bf16[4,64,256]{2,1,0:T(8,128)(2,1)S(1)}, u32[]{:S(2)}, u32[]{:S(2)}) collective-permute-start(bf16[4,64,256]{2,1,0:T(8,128)(2,1)S(1)} %mate_terms.9), channel_id=1, source_target_pairs={{0,2},{1,3},{2,0},{3,1},{4,6},{5,7},{6,4},{7,5},{8,10},{9,11},{10,... | collective-permute-start | bytes 393224 | tf_op jit(solution)/shard_map/ppermute | solution.py:329
  28.5 1.2 %collective-permute-done.11.refs_3_ = bf16[4,64,256]{2,1,0:T(8,128)(2,1)S(1)} collective-permute-done((bf16[4,64,256]{2,1,0:T(8,128)(2,1)S(1)}, bf16[4,64,256]{2,1,0:T(8,128)(2,1)S(1)}, u32[]{:S(2)}, u32[]{:S(2)}) %collective-permute-start.11) | collective-permute-done | bytes 131104 | tf_op jit(solution)/shard_map/ppermute | solution.py:329
  30.4 1.3 %collective-permute-done.9.refs_1_ = bf16[4,64,256]{2,1,0:T(8,128)(2,1)S(1)} collective-permute-done((bf16[4,64,256]{2,1,0:T(8,128)(2,1)S(1)}, bf16[4,64,256]{2,1,0:T(8,128)(2,1)S(1)}, u32[]{:S(2)}, u32[]{:S(2)}) %collective-permute-start.9) | collective-permute-done | bytes 131104 | tf_op jit(solution)/shard_map/ppermute | solution.py:329
  32.5 1.0 %collective-permute-done.12.arrived = bf16[2,64,640]{2,1,0:T(8,128)(2,1)S(1)} collective-permute-done((bf16[2,64,640]{2,1,0:T(8,128)(2,1)S(1)}, bf16[2,64,640]{2,1,0:T(8,128)(2,1)S(1)}, u32[]{:S(2)}, u32[]{:S(2)}) %collective-permute-start.12) | collective-permute-done | bytes 163872 | tf_op jit(solution)/shard_map/ppermute | solution.py:329
  33.5 2.4 %collective-permute-start.13 = (bf16[2,64,640]{2,1,0:T(8,128)(2,1)S(1)}, bf16[2,64,640]{2,1,0:T(8,128)(2,1)S(1)}, u32[]{:S(2)}, u32[]{:S(2)}) collective-permute-start(bf16[2,64,640]{2,1,0:T(8,128)(2,1)S(1)} %get-tuple-element.101), channel_id=1, source_target_pairs={{0,8},{1,9},{2,10},{3,11},{4,12},{5,13},{6,14},{7,15},{8,0},{9,1},... | collective-permute-start | bytes 491528 | tf_op jit(solution)/shard_map/ppermute | solution.py:329
  36.1 8.1 %collective-permute-done.13.arrived = bf16[2,64,640]{2,1,0:T(8,128)(2,1)S(1)} collective-permute-done((bf16[2,64,640]{2,1,0:T(8,128)(2,1)S(1)}, bf16[2,64,640]{2,1,0:T(8,128)(2,1)S(1)}, u32[]{:S(2)}, u32[]{:S(2)}) %collective-permute-start.13) | collective-permute-done | bytes 163872 | tf_op jit(solution)/shard_map/ppermute | solution.py:329
  44.6 1.3 %collective-permute-start.20 = (bf16[2,64,256]{2,1,0:T(8,128)(2,1)S(1)}, bf16[2,64,256]{2,1,0:T(8,128)(2,1)S(1)}, u32[]{:S(2)}, u32[]{:S(2)}) collective-permute-start(bf16[2,64,256]{2,1,0:T(8,128)(2,1)S(1)} %get-tuple-element.111), channel_id=1, source_target_pairs={{0,6},{1,7},{2,4},{3,5},{4,2},{5,3},{6,0},{7,1},{8,14},{9,15},{10,... | collective-permute-start | bytes 196616 | tf_op jit(solution)/shard_map/ppermute | solution.py:329
  45.9 1.6 %collective-permute-start.19 = (bf16[2,64,256]{2,1,0:T(8,128)(2,1)S(1)}, bf16[2,64,256]{2,1,0:T(8,128)(2,1)S(1)}, u32[]{:S(2)}, u32[]{:S(2)}) collective-permute-start(bf16[2,64,256]{2,1,0:T(8,128)(2,1)S(1)} %get-tuple-element.110), channel_id=1, source_target_pairs={{0,4},{1,5},{2,6},{3,7},{4,0},{5,1},{6,2},{7,3},{8,12},{9,13},{10,... | collective-permute-start | bytes 196616 | tf_op jit(solution)/shard_map/ppermute | solution.py:329
  47.4 0.7 collective-permute-start.18
  48.8 1.3 %collective-permute-start.17 = (bf16[2,64,256]{2,1,0:T(8,128)(2,1)S(1)}, bf16[2,64,256]{2,1,0:T(8,128)(2,1)S(1)}, u32[]{:S(2)}, u32[]{:S(2)}) collective-permute-start(bf16[2,64,256]{2,1,0:T(8,128)(2,1)S(1)} %get-tuple-element.107), channel_id=1, source_target_pairs={{0,6},{1,7},{2,4},{3,5},{4,2},{5,3},{6,0},{7,1},{8,14},{9,15},{10,... | collective-permute-start | bytes 196616 | tf_op jit(solution)/shard_map/ppermute | solution.py:329
  50.1 1.6 %collective-permute-start.16 = (bf16[2,64,256]{2,1,0:T(8,128)(2,1)S(1)}, bf16[2,64,256]{2,1,0:T(8,128)(2,1)S(1)}, u32[]{:S(2)}, u32[]{:S(2)}) collective-permute-start(bf16[2,64,256]{2,1,0:T(8,128)(2,1)S(1)} %get-tuple-element.106), channel_id=1, source_target_pairs={{0,4},{1,5},{2,6},{3,7},{4,0},{5,1},{6,2},{7,3},{8,12},{9,13},{10,... | collective-permute-start | bytes 196616 | tf_op jit(solution)/shard_map/ppermute | solution.py:329
  51.6 0.7 collective-permute-start.15
  57.4 1.1 %collective-permute-start.23 = (bf16[4,64,256]{2,1,0:T(8,128)(2,1)S(1)}, bf16[4,64,256]{2,1,0:T(8,128)(2,1)S(1)}, u32[]{:S(2)}, u32[]{:S(2)}) collective-permute-start(bf16[4,64,256]{2,1,0:T(8,128)(2,1)S(1)} %mate_terms.15), channel_id=1, source_target_pairs={{0,6},{1,7},{2,4},{3,5},{4,2},{5,3},{6,0},{7,1},{8,14},{9,15},{10,... | collective-permute-start | bytes 393224 | tf_op jit(solution)/shard_map/ppermute | solution.py:329
  59.0 1.2 %collective-permute-start.22 = (bf16[4,64,256]{2,1,0:T(8,128)(2,1)S(1)}, bf16[4,64,256]{2,1,0:T(8,128)(2,1)S(1)}, u32[]{:S(2)}, u32[]{:S(2)}) collective-permute-start(bf16[4,64,256]{2,1,0:T(8,128)(2,1)S(1)} %mate_terms.14), channel_id=1, source_target_pairs={{0,4},{1,5},{2,6},{3,7},{4,0},{5,1},{6,2},{7,3},{8,12},{9,13},{10,... | collective-permute-start | bytes 393224 | tf_op jit(solution)/shard_map/ppermute | solution.py:329
  60.8 1.4 %collective-permute-start.21 = (bf16[4,64,256]{2,1,0:T(8,128)(2,1)S(1)}, bf16[4,64,256]{2,1,0:T(8,128)(2,1)S(1)}, u32[]{:S(2)}, u32[]{:S(2)}) collective-permute-start(bf16[4,64,256]{2,1,0:T(8,128)(2,1)S(1)} %mate_terms.13), channel_id=1, source_target_pairs={{0,2},{1,3},{2,0},{3,1},{4,6},{5,7},{6,4},{7,5},{8,10},{9,11},{10,... | collective-permute-start | bytes 393224 | tf_op jit(solution)/shard_map/ppermute | solution.py:329
  62.1 0.9 %sample_update.4 = (f32[64,1024]{1,0:T(8,128)}, f32[8,128]{1,0:T(8,128)S(1)}) custom-call(f32[64,1024]{1,0:T(8,128)S(1)} %get-tuple-element.96.samples, f32[64,1024]{1,0:T(8,128)S(1)} %get-tuple-element.127.gradient, f32[64,64]{1,0:T(8,128)S(1)} %get-tuple-element.128.gram), custom_call_target="tpu_custom_call" | custom-call | bytes 2097152 | tf_op jit(solution)/shard_map/sample_update/pallas_call | solution.py:306
  64.5 1.3 %collective-permute-done.21.refs_1_ = bf16[4,64,256]{2,1,0:T(8,128)(2,1)S(1)} collective-permute-done((bf16[4,64,256]{2,1,0:T(8,128)(2,1)S(1)}, bf16[4,64,256]{2,1,0:T(8,128)(2,1)S(1)}, u32[]{:S(2)}, u32[]{:S(2)}) %collective-permute-start.21) | collective-permute-done | bytes 131104 | tf_op jit(solution)/shard_map/ppermute | solution.py:329
  66.6 1.0 %collective-permute-done.24 = bf16[2,64,640]{2,1,0:T(8,128)(2,1)S(1)} collective-permute-done((bf16[2,64,640]{2,1,0:T(8,128)(2,1)S(1)}, bf16[2,64,640]{2,1,0:T(8,128)(2,1)S(1)}, u32[]{:S(2)}, u32[]{:S(2)}) %collective-permute-start.24) | collective-permute-done | bytes 163872 | tf_op jit(solution)/shard_map/ppermute | solution.py:329
  67.6 2.4 %collective-permute-start.25 = (bf16[64,640]{1,0:T(8,128)(2,1)S(1)}, bf16[64,640]{1,0:T(8,128)(2,1)S(1)}, u32[]{:S(2)}, u32[]{:S(2)}) collective-permute-start(bf16[64,640]{1,0:T(8,128)(2,1)S(1)} %fusion.6), channel_id=1, source_target_pairs={{0,8},{1,9},{2,10},{3,11},{4,12},{5,13},{6,14},{7,15},{8,0},{9,1},... | collective-permute-start | bytes 245768 | tf_op jit(solution)/shard_map/ppermute | solution.py:329
  70.1 4.8 %collective-permute-done.25 = bf16[64,640]{1,0:T(8,128)(2,1)S(1)} collective-permute-done((bf16[64,640]{1,0:T(8,128)(2,1)S(1)}, bf16[64,640]{1,0:T(8,128)(2,1)S(1)}, u32[]{:S(2)}, u32[]{:S(2)}) %collective-permute-start.25) | collective-permute-done | bytes 81952 | tf_op jit(solution)/shard_map/ppermute | solution.py:329
  74.9 0.7 fusion.5
  (66 shorter events, 18.3 us)
Async XLA Ops:
  1.6 8.3 %collective-permute-start = (bf16[64,640]{1,0:T(8,128)(2,1)S(1)}, bf16[64,640]{1,0:T(8,128)(2,1)S(1)}, u32[]{:S(2)}, u32[]{:S(2)}) collective-permute-start(bf16[64,640]{1,0:T(8,128)(2,1)S(1)} %bitcast_convert_fusion.refs_0_), channel_id=1, source_target_pairs={{0,8},{1,9},{2,10},{3,11},{4,12},{5,13},{6,14},{7,15},{8,0},{9,1},... | collective-permute-start | bytes 245768 | tf_op jit(solution)/shard_map/ppermute | solution.py:329
  5.7 4.2 %collective-permute-start.5 = (bf16[64,640]{1,0:T(8,128)(2,1)S(1)}, bf16[64,640]{1,0:T(8,128)(2,1)S(1)}, u32[]{:S(2)}, u32[]{:S(2)}) collective-permute-start(bf16[64,640]{1,0:T(8,128)(2,1)S(1)} %bitcast_convert_fusion.refs_0_), channel_id=1, source_target_pairs={{0,1},{1,0},{2,3},{3,2},{4,5},{5,4},{6,7},{7,6},{8,9},{9,8},{10,11... | collective-permute-start | bytes 245768 | tf_op jit(solution)/shard_map/ppermute | solution.py:329
  9.9 4.2 %collective-permute-start.1 = (bf16[64,640]{1,0:T(8,128)(2,1)S(1)}, bf16[64,640]{1,0:T(8,128)(2,1)S(1)}, u32[]{:S(2)}, u32[]{:S(2)}) collective-permute-start(bf16[64,640]{1,0:T(8,128)(2,1)S(1)} %collective-permute-done.refs_0_.other_snps), channel_id=1, source_target_pairs={{0,1},{1,0},{2,3},{3,2},{4,5},{5,4},{6,7},{7,6},{8,9},{9,8},{10,11... | collective-permute-start | bytes 245768 | tf_op jit(solution)/shard_map/ppermute | solution.py:329
  10.0 7.4 %collective-permute-start.8 = (bf16[2,64,256]{2,1,0:T(8,128)(2,1)S(1)}, bf16[2,64,256]{2,1,0:T(8,128)(2,1)S(1)}, u32[]{:S(2)}, u32[]{:S(2)}) collective-permute-start(bf16[2,64,256]{2,1,0:T(8,128)(2,1)S(1)} %get-tuple-element.78), channel_id=1, source_target_pairs={{0,6},{1,7},{2,4},{3,5},{4,2},{5,3},{6,0},{7,1},{8,14},{9,15},{10,... | collective-permute-start | bytes 196616 | tf_op jit(solution)/shard_map/ppermute | solution.py:329
  12.5 5.7 %collective-permute-start.7 = (bf16[2,64,256]{2,1,0:T(8,128)(2,1)S(1)}, bf16[2,64,256]{2,1,0:T(8,128)(2,1)S(1)}, u32[]{:S(2)}, u32[]{:S(2)}) collective-permute-start(bf16[2,64,256]{2,1,0:T(8,128)(2,1)S(1)} %get-tuple-element.77), channel_id=1, source_target_pairs={{0,4},{1,5},{2,6},{3,7},{4,0},{5,1},{6,2},{7,3},{8,12},{9,13},{10,... | collective-permute-start | bytes 196616 | tf_op jit(solution)/shard_map/ppermute | solution.py:329
  13.3 5.5 %collective-permute-start.6 = (bf16[2,64,256]{2,1,0:T(8,128)(2,1)S(1)}, bf16[2,64,256]{2,1,0:T(8,128)(2,1)S(1)}, u32[]{:S(2)}, u32[]{:S(2)}) collective-permute-start(bf16[2,64,256]{2,1,0:T(8,128)(2,1)S(1)} %get-tuple-element.76), channel_id=1, source_target_pairs={{0,2},{1,3},{2,0},{3,1},{4,6},{5,7},{6,4},{7,5},{8,10},{9,11},{10,... | collective-permute-start | bytes 196616 | tf_op jit(solution)/shard_map/ppermute | solution.py:329
  14.2 5.5 %collective-permute-start.4 = (bf16[2,64,256]{2,1,0:T(8,128)(2,1)S(1)}, bf16[2,64,256]{2,1,0:T(8,128)(2,1)S(1)}, u32[]{:S(2)}, u32[]{:S(2)}) collective-permute-start(bf16[2,64,256]{2,1,0:T(8,128)(2,1)S(1)} %get-tuple-element.74), channel_id=1, source_target_pairs={{0,6},{1,7},{2,4},{3,5},{4,2},{5,3},{6,0},{7,1},{8,14},{9,15},{10,... | collective-permute-start | bytes 196616 | tf_op jit(solution)/shard_map/ppermute | solution.py:329
  16.7 4.3 %collective-permute-start.3 = (bf16[2,64,256]{2,1,0:T(8,128)(2,1)S(1)}, bf16[2,64,256]{2,1,0:T(8,128)(2,1)S(1)}, u32[]{:S(2)}, u32[]{:S(2)}) collective-permute-start(bf16[2,64,256]{2,1,0:T(8,128)(2,1)S(1)} %get-tuple-element.73), channel_id=1, source_target_pairs={{0,4},{1,5},{2,6},{3,7},{4,0},{5,1},{6,2},{7,3},{8,12},{9,13},{10,... | collective-permute-start | bytes 196616 | tf_op jit(solution)/shard_map/ppermute | solution.py:329
  17.5 4.3 %collective-permute-start.2 = (bf16[2,64,256]{2,1,0:T(8,128)(2,1)S(1)}, bf16[2,64,256]{2,1,0:T(8,128)(2,1)S(1)}, u32[]{:S(2)}, u32[]{:S(2)}) collective-permute-start(bf16[2,64,256]{2,1,0:T(8,128)(2,1)S(1)} %get-tuple-element.72), channel_id=1, source_target_pairs={{0,2},{1,3},{2,0},{3,1},{4,6},{5,7},{6,4},{7,5},{8,10},{9,11},{10,... | collective-permute-start | bytes 196616 | tf_op jit(solution)/shard_map/ppermute | solution.py:329
  23.2 6.5 %collective-permute-start.11 = (bf16[4,64,256]{2,1,0:T(8,128)(2,1)S(1)}, bf16[4,64,256]{2,1,0:T(8,128)(2,1)S(1)}, u32[]{:S(2)}, u32[]{:S(2)}) collective-permute-start(bf16[4,64,256]{2,1,0:T(8,128)(2,1)S(1)} %mate_terms.11), channel_id=1, source_target_pairs={{0,6},{1,7},{2,4},{3,5},{4,2},{5,3},{6,0},{7,1},{8,14},{9,15},{10,... | collective-permute-start | bytes 393224 | tf_op jit(solution)/shard_map/ppermute | solution.py:329
  25.1 10.8 %copy-start.1 = (s32[16,64]{1,0:T(8,128)S(1)}, s32[16,64]{1,0:T(8,128)}, u32[]{:S(2)}) copy-start(s32[16,64]{1,0:T(8,128)} %cov.3) | copy-start | bytes 12292
  25.2 19.1 %copy-start = (f32[640,64]{0,1:T(8,128)S(1)}, f32[640,64]{0,1:T(8,128)}, u32[]{:S(2)}) copy-start(f32[640,64]{0,1:T(8,128)} %param.6) | copy-start | bytes 491524
  25.2 5.2 %collective-permute-start.10 = (bf16[4,64,256]{2,1,0:T(8,128)(2,1)S(1)}, bf16[4,64,256]{2,1,0:T(8,128)(2,1)S(1)}, u32[]{:S(2)}, u32[]{:S(2)}) collective-permute-start(bf16[4,64,256]{2,1,0:T(8,128)(2,1)S(1)} %mate_terms.10), channel_id=1, source_target_pairs={{0,4},{1,5},{2,6},{3,7},{4,0},{5,1},{6,2},{7,3},{8,12},{9,13},{10,... | collective-permute-start | bytes 393224 | tf_op jit(solution)/shard_map/ppermute | solution.py:329
  26.5 5.1 %collective-permute-start.9 = (bf16[4,64,256]{2,1,0:T(8,128)(2,1)S(1)}, bf16[4,64,256]{2,1,0:T(8,128)(2,1)S(1)}, u32[]{:S(2)}, u32[]{:S(2)}) collective-permute-start(bf16[4,64,256]{2,1,0:T(8,128)(2,1)S(1)} %mate_terms.9), channel_id=1, source_target_pairs={{0,2},{1,3},{2,0},{3,1},{4,6},{5,7},{6,4},{7,5},{8,10},{9,11},{10,... | collective-permute-start | bytes 393224 | tf_op jit(solution)/shard_map/ppermute | solution.py:329
  32.0 1.5 %collective-permute-start.12 = (bf16[2,64,640]{2,1,0:T(8,128)(2,1)S(1)}, bf16[2,64,640]{2,1,0:T(8,128)(2,1)S(1)}, u32[]{:S(2)}, u32[]{:S(2)}) collective-permute-start(bf16[2,64,640]{2,1,0:T(8,128)(2,1)S(1)} %mates_sum.4.refs_4_), channel_id=1, source_target_pairs={{0,1},{1,0},{2,3},{3,2},{4,5},{5,4},{6,7},{7,6},{8,9},{9,8},{10,11... | collective-permute-start | bytes 491528 | tf_op jit(solution)/shard_map/ppermute | solution.py:329
  33.5 10.7 %collective-permute-start.13 = (bf16[2,64,640]{2,1,0:T(8,128)(2,1)S(1)}, bf16[2,64,640]{2,1,0:T(8,128)(2,1)S(1)}, u32[]{:S(2)}, u32[]{:S(2)}) collective-permute-start(bf16[2,64,640]{2,1,0:T(8,128)(2,1)S(1)} %get-tuple-element.101), channel_id=1, source_target_pairs={{0,8},{1,9},{2,10},{3,11},{4,12},{5,13},{6,14},{7,15},{8,0},{9,1},... | collective-permute-start | bytes 491528 | tf_op jit(solution)/shard_map/ppermute | solution.py:329
  44.4 4.3 %collective-permute-start.14 = (bf16[2,64,640]{2,1,0:T(8,128)(2,1)S(1)}, bf16[2,64,640]{2,1,0:T(8,128)(2,1)S(1)}, u32[]{:S(2)}, u32[]{:S(2)}) collective-permute-start(bf16[2,64,640]{2,1,0:T(8,128)(2,1)S(1)} %get-tuple-element.104.refs_0_), channel_id=1, source_target_pairs={{0,1},{1,0},{2,3},{3,2},{4,5},{5,4},{6,7},{7,6},{8,9},{9,8},{10,11... | collective-permute-start | bytes 491528 | tf_op jit(solution)/shard_map/ppermute | solution.py:329
  44.6 7.0 %collective-permute-start.20 = (bf16[2,64,256]{2,1,0:T(8,128)(2,1)S(1)}, bf16[2,64,256]{2,1,0:T(8,128)(2,1)S(1)}, u32[]{:S(2)}, u32[]{:S(2)}) collective-permute-start(bf16[2,64,256]{2,1,0:T(8,128)(2,1)S(1)} %get-tuple-element.111), channel_id=1, source_target_pairs={{0,6},{1,7},{2,4},{3,5},{4,2},{5,3},{6,0},{7,1},{8,14},{9,15},{10,... | collective-permute-start | bytes 196616 | tf_op jit(solution)/shard_map/ppermute | solution.py:329
  45.9 7.0 %collective-permute-start.19 = (bf16[2,64,256]{2,1,0:T(8,128)(2,1)S(1)}, bf16[2,64,256]{2,1,0:T(8,128)(2,1)S(1)}, u32[]{:S(2)}, u32[]{:S(2)}) collective-permute-start(bf16[2,64,256]{2,1,0:T(8,128)(2,1)S(1)} %get-tuple-element.110), channel_id=1, source_target_pairs={{0,4},{1,5},{2,6},{3,7},{4,0},{5,1},{6,2},{7,3},{8,12},{9,13},{10,... | collective-permute-start | bytes 196616 | tf_op jit(solution)/shard_map/ppermute | solution.py:329
  47.4 5.9 %collective-permute-start.18 = (bf16[2,64,256]{2,1,0:T(8,128)(2,1)S(1)}, bf16[2,64,256]{2,1,0:T(8,128)(2,1)S(1)}, u32[]{:S(2)}, u32[]{:S(2)}) collective-permute-start(bf16[2,64,256]{2,1,0:T(8,128)(2,1)S(1)} %get-tuple-element.109), channel_id=1, source_target_pairs={{0,2},{1,3},{2,0},{3,1},{4,6},{5,7},{6,4},{7,5},{8,10},{9,11},{10,... | collective-permute-start | bytes 196616 | tf_op jit(solution)/shard_map/ppermute | solution.py:329
  48.8 5.5 %collective-permute-start.17 = (bf16[2,64,256]{2,1,0:T(8,128)(2,1)S(1)}, bf16[2,64,256]{2,1,0:T(8,128)(2,1)S(1)}, u32[]{:S(2)}, u32[]{:S(2)}) collective-permute-start(bf16[2,64,256]{2,1,0:T(8,128)(2,1)S(1)} %get-tuple-element.107), channel_id=1, source_target_pairs={{0,6},{1,7},{2,4},{3,5},{4,2},{5,3},{6,0},{7,1},{8,14},{9,15},{10,... | collective-permute-start | bytes 196616 | tf_op jit(solution)/shard_map/ppermute | solution.py:329
  50.1 4.7 %collective-permute-start.16 = (bf16[2,64,256]{2,1,0:T(8,128)(2,1)S(1)}, bf16[2,64,256]{2,1,0:T(8,128)(2,1)S(1)}, u32[]{:S(2)}, u32[]{:S(2)}) collective-permute-start(bf16[2,64,256]{2,1,0:T(8,128)(2,1)S(1)} %get-tuple-element.106), channel_id=1, source_target_pairs={{0,4},{1,5},{2,6},{3,7},{4,0},{5,1},{6,2},{7,3},{8,12},{9,13},{10,... | collective-permute-start | bytes 196616 | tf_op jit(solution)/shard_map/ppermute | solution.py:329
  51.6 4.3 %collective-permute-start.15 = (bf16[2,64,256]{2,1,0:T(8,128)(2,1)S(1)}, bf16[2,64,256]{2,1,0:T(8,128)(2,1)S(1)}, u32[]{:S(2)}, u32[]{:S(2)}) collective-permute-start(bf16[2,64,256]{2,1,0:T(8,128)(2,1)S(1)} %get-tuple-element.105), channel_id=1, source_target_pairs={{0,2},{1,3},{2,0},{3,1},{4,6},{5,7},{6,4},{7,5},{8,10},{9,11},{10,... | collective-permute-start | bytes 196616 | tf_op jit(solution)/shard_map/ppermute | solution.py:329
  57.4 6.8 %collective-permute-start.23 = (bf16[4,64,256]{2,1,0:T(8,128)(2,1)S(1)}, bf16[4,64,256]{2,1,0:T(8,128)(2,1)S(1)}, u32[]{:S(2)}, u32[]{:S(2)}) collective-permute-start(bf16[4,64,256]{2,1,0:T(8,128)(2,1)S(1)} %mate_terms.15), channel_id=1, source_target_pairs={{0,6},{1,7},{2,4},{3,5},{4,2},{5,3},{6,0},{7,1},{8,14},{9,15},{10,... | collective-permute-start | bytes 393224 | tf_op jit(solution)/shard_map/ppermute | solution.py:329
  59.0 5.5 %collective-permute-start.22 = (bf16[4,64,256]{2,1,0:T(8,128)(2,1)S(1)}, bf16[4,64,256]{2,1,0:T(8,128)(2,1)S(1)}, u32[]{:S(2)}, u32[]{:S(2)}) collective-permute-start(bf16[4,64,256]{2,1,0:T(8,128)(2,1)S(1)} %mate_terms.14), channel_id=1, source_target_pairs={{0,4},{1,5},{2,6},{3,7},{4,0},{5,1},{6,2},{7,3},{8,12},{9,13},{10,... | collective-permute-start | bytes 393224 | tf_op jit(solution)/shard_map/ppermute | solution.py:329
  60.8 5.0 %collective-permute-start.21 = (bf16[4,64,256]{2,1,0:T(8,128)(2,1)S(1)}, bf16[4,64,256]{2,1,0:T(8,128)(2,1)S(1)}, u32[]{:S(2)}, u32[]{:S(2)}) collective-permute-start(bf16[4,64,256]{2,1,0:T(8,128)(2,1)S(1)} %mate_terms.13), channel_id=1, source_target_pairs={{0,2},{1,3},{2,0},{3,1},{4,6},{5,7},{6,4},{7,5},{8,10},{9,11},{10,... | collective-permute-start | bytes 393224 | tf_op jit(solution)/shard_map/ppermute | solution.py:329
  66.2 1.5 %collective-permute-start.24 = (bf16[2,64,640]{2,1,0:T(8,128)(2,1)S(1)}, bf16[2,64,640]{2,1,0:T(8,128)(2,1)S(1)}, u32[]{:S(2)}, u32[]{:S(2)}) collective-permute-start(bf16[2,64,640]{2,1,0:T(8,128)(2,1)S(1)} %mates_sum.6.refs_4_), channel_id=1, source_target_pairs={{0,1},{1,0},{2,3},{3,2},{4,5},{5,4},{6,7},{7,6},{8,9},{9,8},{10,11... | collective-permute-start | bytes 491528 | tf_op jit(solution)/shard_map/ppermute | solution.py:329
  67.6 7.2 %collective-permute-start.25 = (bf16[64,640]{1,0:T(8,128)(2,1)S(1)}, bf16[64,640]{1,0:T(8,128)(2,1)S(1)}, u32[]{:S(2)}, u32[]{:S(2)}) collective-permute-start(bf16[64,640]{1,0:T(8,128)(2,1)S(1)} %fusion.6), channel_id=1, source_target_pairs={{0,8},{1,9},{2,10},{3,11},{4,12},{5,13},{6,14},{7,15},{8,0},{9,1},... | collective-permute-start | bytes 245768 | tf_op jit(solution)/shard_map/ppermute | solution.py:329
